TPU v7x, 32 devices: a whole 2x2x4 slice. The times are simulated.
32 devices in a mesh: rep: 4 (over y, x), grp: 8 (over z, core).
Axes of the slice: x: 2, y: 2, z: 4, core: 2. Of those that a mesh axis runs over, the one named last changes fastest.
Arguments:
- tokens: bfloat16 [32768, 768], P(('rep', 'grp')), may hold values from -6 to 6
- segments: int32 [32768], P(('rep', 'grp')), may hold values from 0 to 17, as said below
- routes: int32 [32768, 2], P(('rep', 'grp')), may hold values from 0 to 15, all different within a row; in each aligned block of 1024 rows (0 to 1023, 1024 to 2047, ...) at most 256 rows name the same one
- gain_attn: bfloat16 [768], P('grp'), may hold values from 0.5 to 1.5
- w_query: bfloat16 [768, 768], P('grp'), may hold values from -0.21875 to 0.21875
- w_key: bfloat16 [768, 768], P('grp'), may hold values from -0.21875 to 0.21875
- w_value: bfloat16 [768, 768], P('grp'), may hold values from -0.21875 to 0.21875
- w_output: bfloat16 [768, 768], P('grp'), may hold values from -1.75 to 1.75
- rel_bias: bfloat16 [32, 12], P('grp'), may hold values from -4 to 4
- gain_ffn: bfloat16 [768], P('grp'), may hold values from 0.5 to 1.5
- router: bfloat16 [768, 16], P('grp'), may hold values from -0.21875 to 0.21875
- w_in: bfloat16 [16, 768, 3072], P('grp'), may hold values from -0.21875 to 0.21875
- w_out: bfloat16 [16, 3072, 768], P('grp'), may hold values from -0.109375 to 0.109375
- cotangent: bfloat16 [32768, 768], P(('rep', 'grp')), may hold values from -6 to 6
Outputs:
- out: bfloat16 [32768, 768], P(('rep', 'grp'))
- loss: float32 [], replicated
- balance_terms: float32 [16], replicated
- x_grad: float32 [32768, 768], P(('rep', 'grp'))
- gain_attn_grad: float32 [768], P('grp')
- w_query_grad: float32 [768, 768], P('grp')
- w_key_grad: float32 [768, 768], P('grp')
- w_value_grad: float32 [768, 768], P('grp')
- w_output_grad: float32 [768, 768], P('grp')
- rel_bias_grad: float32 [32, 12], P('grp')
- gain_ffn_grad: float32 [768], P('grp')
- router_grad: float32 [768, 16], P('grp')
- w_in_grad: float32 [16, 768, 3072], P('grp', 'rep')
- w_out_grad: float32 [16, 3072, 768], P('grp', 'rep')
Inputs may be any that keep to these rules, and one draw needn't show every extreme that they name: `segments`: within each sequence of 1024 tokens, documents carry ids 1, 2, 3 in order, each of 60 to 800 tokens; id 0 marks padding after the last document. The first sequence holds documents of exactly 60 tokens. `routes`: A token's 2 experts differ. In the rows of one device no expert is named more than 256 times, and this bound is reached.
All inputs are finite; a program needn't handle non-finite values.
Results may differ from a plain program's by a relative error of at most 0.013.
Values may be sent and summed in bfloat16 or wider, within the bound.
A program may use at most 384 MiB of HBM per device.

v0:
```python
from functools import partial

import jax
import jax.numpy as jnp
from jax import lax
from jax.sharding import PartitionSpec as P

HEADS = 12
HEAD_DIM = 64
TOP = 2
SEQ = 1024
QBLK = 512


norm_eps = 1e-06
aux_weight = 0.01
masked_score = -1e30
far_marks = (18, 20, 23, 26, 30, 34, 39, 45, 51, 58, 66, 76, 86, 98, 112)


def rms_scale(values):
    return lax.rsqrt(jnp.mean(values * values, axis=-1, keepdims=True) + norm_eps)


def positions_of(seg_row):
    length = seg_row.shape[0]
    places = lax.iota(jnp.int32, length)
    before = jnp.concatenate([seg_row[:1] - 1, seg_row[:-1]])
    starts = jnp.where(seg_row != before, places, 0)
    return places - lax.cummax(starts, axis=0)


def bucket_of(distance):
    far_part = jnp.zeros_like(distance)
    for far_mark in far_marks:
        far_part = far_part + (distance >= far_mark).astype(jnp.int32)
    return jnp.minimum(distance, 16) + far_part


def outer_sum(left_rows, right_rows):
    return lax.dot_general(
        left_rows, right_rows, (((0,), (0,)), ((), ())), preferred_element_type=jnp.float32
    )


def back_proj(grad_rows, weight):
    return lax.dot_general(
        grad_rows, weight, (((1,), (1,)), ((), ())), preferred_element_type=jnp.float32
    )


def block_scores(
    query_blk, key_seq, seg_query, seg_key, pos_query, pos_key, row_start, table_heads
):
    query_count = query_blk.shape[0]
    key_count = key_seq.shape[0]
    distance = jnp.maximum(pos_query[:, None] - pos_key[None, :], 0)
    flat_bucket = bucket_of(distance).reshape(1, query_count * key_count)
    bucket_ids = lax.iota(jnp.int32, table_heads.shape[1])[:, None]
    one_hot = (flat_bucket == bucket_ids).astype(jnp.bfloat16)
    biases = jnp.dot(table_heads, one_hot, preferred_element_type=jnp.float32).reshape(
        -1, query_count, key_count
    )
    scaling = query_blk.shape[2] ** (-0.5)
    scores = (
        jnp.einsum("qhd,khd->hqk", query_blk, key_seq, preferred_element_type=jnp.float32) * scaling
        + biases
    )
    query_place = row_start + lax.iota(jnp.int32, query_count)
    key_place = lax.iota(jnp.int32, key_count)
    same_doc = seg_query[:, None] == seg_key[None, :]
    causal = key_place[None, :] <= query_place[:, None]
    own_place = key_place[None, :] == query_place[:, None]
    allowed = same_doc & causal & ((seg_query[:, None] != 0) | own_place)
    return (scores, allowed, one_hot)


def shards(
    tokens,
    segments,
    routes,
    gain_attn,
    w_query,
    w_key,
    w_value,
    w_output,
    rel_bias,
    gain_ffn,
    router,
    w_in,
    w_out,
    cotangent,
):
    dense_full = (
        lax.all_gather(gain_attn, "grp", axis=0, tiled=True),
        lax.all_gather(w_query, "grp", axis=0, tiled=True),
        lax.all_gather(w_key, "grp", axis=0, tiled=True),
        lax.all_gather(w_value, "grp", axis=0, tiled=True),
        lax.all_gather(w_output, "grp", axis=0, tiled=True),
        lax.all_gather(rel_bias, "grp", axis=0, tiled=True),
        lax.all_gather(gain_ffn, "grp", axis=0, tiled=True),
        lax.all_gather(router, "grp", axis=0, tiled=True),
    )
    gain_one, query_full, key_full, value_full, output_full, table_full, gain_two, router_full = (
        dense_full
    )
    tok_rows = tokens.shape[0]
    width = tokens.shape[1]
    seq_count = tok_rows // SEQ
    block_count = SEQ // QBLK
    scaling = HEAD_DIM ** (-0.5)
    inputs = tokens.astype(jnp.float32)
    scale_one = rms_scale(inputs)
    normed_one = (inputs * scale_one * gain_one.astype(jnp.float32)).astype(jnp.bfloat16)
    query_rows = jnp.dot(normed_one, query_full, preferred_element_type=jnp.float32).astype(
        jnp.bfloat16
    )
    key_rows = jnp.dot(normed_one, key_full, preferred_element_type=jnp.float32).astype(
        jnp.bfloat16
    )
    value_rows = jnp.dot(normed_one, value_full, preferred_element_type=jnp.float32).astype(
        jnp.bfloat16
    )
    head_query = query_rows.reshape(tok_rows, HEADS, HEAD_DIM)
    head_key = key_rows.reshape(tok_rows, HEADS, HEAD_DIM)
    head_value = value_rows.reshape(tok_rows, HEADS, HEAD_DIM)
    seg_rows = segments.reshape(seq_count, SEQ)
    pos_rows = jax.vmap(positions_of)(seg_rows)
    table_heads = table_full.T

    def forward_block(block_id):
        seq_id = block_id // block_count
        row_start = block_id % block_count * QBLK
        seq_base = seq_id * SEQ
        query_blk = lax.dynamic_slice_in_dim(head_query, seq_base + row_start, QBLK, 0)
        seg_seq = lax.dynamic_index_in_dim(seg_rows, seq_id, 0, keepdims=False)
        pos_seq = lax.dynamic_index_in_dim(pos_rows, seq_id, 0, keepdims=False)
        seg_query = lax.dynamic_slice_in_dim(seg_seq, row_start, QBLK, 0)
        pos_query = lax.dynamic_slice_in_dim(pos_seq, row_start, QBLK, 0)
        scores, allowed, unused_hot = block_scores(
            query_blk, head_key, seg_query, seg_seq, pos_query, pos_seq, row_start, table_heads
        )
        scores = jnp.where(allowed[None], scores, masked_score)
        highest = jnp.max(scores, axis=-1, keepdims=True)
        expos = jnp.exp(scores - highest)
        totals = jnp.sum(expos, axis=-1, keepdims=True)
        weights = (expos / totals).astype(jnp.bfloat16)
        context_blk = jnp.einsum(
            "hqk,khd->qhd", weights, head_value, preferred_element_type=jnp.float32
        )
        return (
            context_blk.reshape(QBLK, width).astype(jnp.bfloat16),
            (highest + jnp.log(totals))[:, :, 0],
        )

    context_blocks, lse_blocks = lax.map(
        forward_block, jnp.arange(seq_count * block_count, dtype=jnp.int32)
    )
    context = context_blocks.reshape(tok_rows, width)
    hidden_one = inputs + jnp.dot(context, output_full, preferred_element_type=jnp.float32)
    scale_two = rms_scale(hidden_one)
    normed_two = (hidden_one * scale_two * gain_two.astype(jnp.float32)).astype(jnp.bfloat16)
    logits = jnp.dot(normed_two, router_full, preferred_element_type=jnp.float32)
    router_prob = jax.nn.softmax(logits, axis=-1)
    exp_local = w_in.shape[0]
    groups = lax.axis_size("grp")
    experts = exp_local * groups
    capacity = 2 * tok_rows * TOP // experts
    choose = routes[:, :, None] == lax.iota(jnp.int32, experts)[None, None, :]
    picked_prob = jnp.sum(jnp.where(choose, router_prob[:, None, :], 0.0), axis=-1)
    prob_sum = jnp.sum(picked_prob, axis=-1, keepdims=True)
    gates = picked_prob / prob_sum
    counts, prob_totals = lax.psum(
        (jnp.sum(choose.astype(jnp.float32), axis=(0, 1)), jnp.sum(router_prob, axis=0)),
        ("rep", "grp"),
    )
    all_tokens = tok_rows * lax.axis_size("rep") * groups
    fraction = counts / (TOP * all_tokens)
    balance_terms = experts * experts * fraction * (prob_totals / all_tokens)
    loss = aux_weight / experts * jnp.sum(balance_terms)
    flat_routes = routes.reshape(tok_rows * TOP)
    flat_hot = (flat_routes[:, None] == lax.iota(jnp.int32, experts)[None, :]).astype(jnp.int32)
    slots = jnp.sum((jnp.cumsum(flat_hot, axis=0) - flat_hot) * flat_hot, axis=1)
    copies = jnp.repeat(normed_two, TOP, axis=0)
    send_rows = (
        jnp.zeros((experts, capacity, width), jnp.bfloat16).at[flat_routes, slots].set(copies)
    )
    received = lax.all_to_all(
        send_rows.reshape(groups, exp_local, capacity, width),
        "grp",
        split_axis=0,
        concat_axis=0,
        tiled=True,
    )
    pre_act = jnp.einsum("gecd,edf->gecf", received, w_in, preferred_element_type=jnp.float32)
    activated = jax.nn.gelu(pre_act, approximate=True).astype(jnp.bfloat16)
    expert_out = jnp.einsum(
        "gecf,efd->gecd", activated, w_out, preferred_element_type=jnp.float32
    ).astype(jnp.bfloat16)
    returned = lax.all_to_all(expert_out, "grp", split_axis=0, concat_axis=0, tiled=True).reshape(
        experts, capacity, width
    )
    picked_out = returned[flat_routes, slots].astype(jnp.float32).reshape(tok_rows, TOP, width)
    hidden_two = hidden_one + jnp.sum(gates[:, :, None] * picked_out, axis=1)
    output = hidden_two.astype(jnp.bfloat16)
    gain_one, query_full, key_full, value_full, output_full, table_full, gain_two, router_full = (
        dense_full
    )
    grad_out = cotangent.astype(jnp.float32) * (segments != 0).astype(jnp.float32)[:, None]
    grad_gate = jnp.sum(grad_out[:, None, :] * picked_out, axis=-1)
    grad_mix = (
        (gates[:, :, None] * grad_out[:, None, :])
        .astype(jnp.bfloat16)
        .reshape(tok_rows * TOP, width)
    )
    grad_send = (
        jnp.zeros((experts, capacity, width), jnp.bfloat16).at[flat_routes, slots].set(grad_mix)
    )
    grad_received = lax.all_to_all(
        grad_send.reshape(groups, exp_local, capacity, width),
        "grp",
        split_axis=0,
        concat_axis=0,
        tiled=True,
    )
    grad_act = jnp.einsum(
        "gecd,efd->gecf", grad_received, w_out, preferred_element_type=jnp.float32
    )
    down_grad = jnp.einsum(
        "gecf,gecd->efd", activated, grad_received, preferred_element_type=jnp.float32
    )
    unused_out, gelu_back = jax.vjp(partial(jax.nn.gelu, approximate=True), pre_act)
    grad_pre = gelu_back(grad_act)[0].astype(jnp.bfloat16)
    up_grad = jnp.einsum("gecd,gecf->edf", received, grad_pre, preferred_element_type=jnp.float32)
    grad_rows = jnp.einsum(
        "gecf,edf->gecd", grad_pre, w_in, preferred_element_type=jnp.float32
    ).astype(jnp.bfloat16)
    up_share, down_share = (
        lax.psum_scatter(up_grad, "rep", scatter_dimension=1, tiled=True),
        lax.psum_scatter(down_grad, "rep", scatter_dimension=1, tiled=True),
    )
    grad_back = lax.all_to_all(grad_rows, "grp", split_axis=0, concat_axis=0, tiled=True).reshape(
        experts, capacity, width
    )
    grad_norm_two = jnp.sum(
        grad_back[flat_routes, slots].astype(jnp.float32).reshape(tok_rows, TOP, width), axis=1
    )
    grad_picked = grad_gate / prob_sum - jnp.sum(
        grad_gate * picked_prob, axis=-1, keepdims=True
    ) / (prob_sum * prob_sum)
    grad_router_prob = (
        jnp.sum(jnp.where(choose, grad_picked[:, :, None], 0.0), axis=1)
        + aux_weight * experts * fraction / all_tokens
    )
    grad_logits = (
        router_prob
        * (grad_router_prob - jnp.sum(router_prob * grad_router_prob, axis=-1, keepdims=True))
    ).astype(jnp.bfloat16)
    router_grad = outer_sum(normed_two, grad_logits)
    grad_norm_two = grad_norm_two + back_proj(grad_logits, router_full)
    gain_two_grad = jnp.sum(grad_norm_two * (hidden_one * scale_two), axis=0)
    scaled_two = grad_norm_two * gain_two.astype(jnp.float32)
    grad_hidden_one = (
        grad_out
        + scale_two * scaled_two
        - hidden_one * scale_two**3 * jnp.mean(scaled_two * hidden_one, axis=-1, keepdims=True)
    )
    grad_attn = grad_hidden_one.astype(jnp.bfloat16)
    output_grad = outer_sum(context, grad_attn)
    grad_context = back_proj(grad_attn, output_full).astype(jnp.bfloat16)
    head_grad_ctx = grad_context.reshape(tok_rows, HEADS, HEAD_DIM)
    table_heads = table_full.T

    def backward_seq(seq_id):
        seq_base = seq_id * SEQ
        seg_seq = lax.dynamic_index_in_dim(seg_rows, seq_id, 0, keepdims=False)
        pos_seq = lax.dynamic_index_in_dim(pos_rows, seq_id, 0, keepdims=False)

        def block_step(carry_in, block_idx):
            grad_key, grad_value, grad_table = carry_in
            row_start = block_idx * QBLK
            query_blk = lax.dynamic_slice_in_dim(head_query, seq_base + row_start, QBLK, 0)
            ctx_grad_blk = lax.dynamic_slice_in_dim(head_grad_ctx, seq_base + row_start, QBLK, 0)
            lse_blk = lax.dynamic_index_in_dim(
                lse_blocks, seq_id * block_count + block_idx, 0, keepdims=False
            )
            seg_query = lax.dynamic_slice_in_dim(seg_seq, row_start, QBLK, 0)
            pos_query = lax.dynamic_slice_in_dim(pos_seq, row_start, QBLK, 0)
            scores, allowed, one_hot = block_scores(
                query_blk, head_key, seg_query, seg_seq, pos_query, pos_seq, row_start, table_heads
            )
            prob_blk = jnp.where(allowed[None], jnp.exp(scores - lse_blk[:, :, None]), 0.0)
            grad_prob = jnp.einsum(
                "qhd,khd->hqk", ctx_grad_blk, head_value, preferred_element_type=jnp.float32
            )
            centre = jnp.sum(prob_blk * grad_prob, axis=-1, keepdims=True)
            grad_score = (prob_blk * (grad_prob - centre)).astype(jnp.bfloat16)
            grad_query = (
                jnp.einsum("hqk,khd->qhd", grad_score, head_key, preferred_element_type=jnp.float32)
                * scaling
            ).astype(jnp.bfloat16)
            grad_key = grad_key + jnp.einsum(
                "hqk,qhd->khd", grad_score, query_blk, preferred_element_type=jnp.float32
            )
            grad_value = grad_value + jnp.einsum(
                "hqk,qhd->khd",
                prob_blk.astype(jnp.bfloat16),
                ctx_grad_blk,
                preferred_element_type=jnp.float32,
            )
            grad_table = grad_table + lax.dot_general(
                grad_score.reshape(HEADS, QBLK * SEQ),
                one_hot,
                (((1,), (1,)), ((), ())),
                preferred_element_type=jnp.float32,
            )
            return ((grad_key, grad_value, grad_table), grad_query)

        start_carry = (
            jnp.zeros((SEQ, HEADS, HEAD_DIM), jnp.float32),
            jnp.zeros((SEQ, HEADS, HEAD_DIM), jnp.float32),
            jnp.zeros((HEADS, table_heads.shape[1]), jnp.float32),
        )
        (grad_key, grad_value, grad_table), grad_query = lax.scan(
            block_step, start_carry, jnp.arange(block_count, dtype=jnp.int32)
        )
        return (
            grad_query.reshape(SEQ, width),
            (grad_key * scaling).astype(jnp.bfloat16).reshape(SEQ, width),
            grad_value.astype(jnp.bfloat16).reshape(SEQ, width),
            grad_table,
        )

    grad_q_seq, grad_k_seq, grad_v_seq, table_parts = lax.map(
        backward_seq, jnp.arange(seq_count, dtype=jnp.int32)
    )
    grad_query_rows = grad_q_seq.reshape(tok_rows, width)
    grad_key_rows = grad_k_seq.reshape(tok_rows, width)
    grad_value_rows = grad_v_seq.reshape(tok_rows, width)
    query_grad = outer_sum(normed_one, grad_query_rows)
    key_grad = outer_sum(normed_one, grad_key_rows)
    value_grad = outer_sum(normed_one, grad_value_rows)
    grad_norm_one = (
        back_proj(grad_query_rows, query_full)
        + back_proj(grad_key_rows, key_full)
        + back_proj(grad_value_rows, value_full)
    )
    gain_one_grad = jnp.sum(grad_norm_one * (inputs * scale_one), axis=0)
    scaled_one = grad_norm_one * gain_one.astype(jnp.float32)
    grad_input = (
        grad_hidden_one
        + scale_one * scaled_one
        - inputs * scale_one**3 * jnp.mean(scaled_one * inputs, axis=-1, keepdims=True)
    )
    table_grad = jnp.sum(table_parts, axis=0).T
    shares = (
        lax.psum_scatter(gain_one_grad, "grp", scatter_dimension=0, tiled=True),
        lax.psum_scatter(query_grad, "grp", scatter_dimension=0, tiled=True),
        lax.psum_scatter(key_grad, "grp", scatter_dimension=0, tiled=True),
        lax.psum_scatter(value_grad, "grp", scatter_dimension=0, tiled=True),
        lax.psum_scatter(output_grad, "grp", scatter_dimension=0, tiled=True),
        lax.psum_scatter(table_grad, "grp", scatter_dimension=0, tiled=True),
        lax.psum_scatter(gain_two_grad, "grp", scatter_dimension=0, tiled=True),
        lax.psum_scatter(router_grad, "grp", scatter_dimension=0, tiled=True),
    )
    summed = lax.psum(
        (shares[0], shares[1], shares[2], shares[3], shares[4], shares[5], shares[6], shares[7]),
        "rep",
    )
    return (
        output,
        loss,
        balance_terms,
        grad_input,
        summed[0],
        summed[1],
        summed[2],
        summed[3],
        summed[4],
        summed[5],
        summed[6],
        summed[7],
        up_share,
        down_share,
    )


def solution(mesh):
    return jax.shard_map(
        shards,
        mesh=mesh,
        in_specs=(
            P(("rep", "grp"), None),
            P(("rep", "grp")),
            P(("rep", "grp"), None),
            P("grp"),
            P("grp", None),
            P("grp", None),
            P("grp", None),
            P("grp", None),
            P("grp", None),
            P("grp"),
            P("grp", None),
            P("grp", None, None),
            P("grp", None, None),
            P(("rep", "grp"), None),
        ),
        out_specs=(
            P(("rep", "grp"), None),
            P(),
            P(),
            P(("rep", "grp"), None),
            P("grp"),
            P("grp", None),
            P("grp", None),
            P("grp", None),
            P("grp", None),
            P("grp", None),
            P("grp"),
            P("grp", None),
            P("grp", "rep", None),
            P("grp", "rep", None),
        ),
        check_vma=False,
    )
```

profile of v0, /device:TPU:0, one launch (start us, length us, event | category | flops | bytes accessed | tf_op | source)
XLA Modules:
  0.0 2033.5 jit_solution(12784509609773973087)
XLA Ops:
  16.6 18.2 all-reduce.8
  62.6 20.5 %all-gather.7.cloned.1.call-done = bf16[768,768]{1,0:T(8,128)(2,1)} async-done(((bf16[96,768]{1,0:T(8,128)(2,1)}), bf16[768,768]{1,0:T(8,128)(2,1)}) %all-gather.7.cloned.1.call-update) | async-done | bytes 1179664 | tf_op jit(solution)/shard_map/all_gather | solution.py:96
  87.5 204.0 %while.47 = (s32[]{:T(128)}, bf16[2,512,768]{2,1,0:T(8,128)(2,1)}, f32[2,12,512]{2,1,0:T(8,128)S(1)}, s32[2]{0:T(128)S(1)}, s32[1,1024]{1,0:T(1,128)S(1)}, /*ind...) while((s32[]{:T(128)}, bf16[2,512,768]{2,1,0:T(8,128)(2,1)}, ...), condition=%wide.region_6.7_spmd, body=%wide.region_3.6_spmd.sunk | while | flops 2116414464 | bytes 248244464 | solution.py:156
  98.8 16.1 fusion.201
  114.9 31.8 %copy.219 = f32[2,8,512,1024]{3,2,1,0:T(8,128)} copy(f32[2,8,512,1024]{3,1,2,0:T(8,128)} %bitcast.303) | data formatting | bytes 67108864 | tf_op jit(solution)/shard_map/while
  146.7 16.2 fusion.203
  200.5 16.1 fusion.201
  216.6 31.8 %copy.219 = f32[2,8,512,1024]{3,2,1,0:T(8,128)} copy(f32[2,8,512,1024]{3,1,2,0:T(8,128)} %bitcast.303) | data formatting | bytes 67108864 | tf_op jit(solution)/shard_map/while
  248.4 16.2 fusion.203
  310.1 14.0 scatter_custom_fusion
  329.1 144.9 %all-gather.1 = bf16[8,96,16]{1,2,0:T(8,128)(2,1)S(1)} all-gather(bf16[1,96,16]{1,2,0:T(8,128)(2,1)S(1)} %bitcast.353), channel_id=1, replica_groups=mesh['rep'=4,'grp'=8] {'grp'}, dimensions={0}, use_global_device_ids=true | all-gather | bytes 27648 | tf_op jit(solution)/shard_map/all_gather | solution.py:102
  497.9 14.9 scatter_custom_fusion.1
  517.7 29.8 %fusion.84 = f32[2,8,256,3072]{3,2,1,0:T(8,128)} fusion(bf16[2,768,3072]{2,1,0:T(8,128)(2,1)} %param.29, bf16[8,2,256,768]{3,2,1,0:T(8,128)(2,1)} %all-to-all-done), kind=kOutput, calls=%fused_computation.129 | convolution fusion | flops 19327352832 | bytes 66060288 | tf_op jit(solution)/shard_map/gecd,edf->gecf/dot_general | solution.py:195
  547.6 30.5 %convert_bitcast_fusion.7 = bf16[8,2,256,768]{3,2,0,1:T(8,128)(2,1)S(1)} fusion(bf16[2,3072,768]{2,1,0:T(8,128)(2,1)} %param.30, f32[2,8,256,3072]{3,2,1,0:T(8,128)} %fusion.84), kind=kOutput, calls=%fused_computation.141 | convolution fusion | flops 19443744768 | bytes 66060288 | tf_op jit(solution)/shard_map/gecf,efd->gecd/dot_general | solution.py:197
  581.1 75.6 %all-to-all-done.2 = bf16[8,2,256,768]{3,2,1,0:T(8,128)(2,1)} async-done(((bf16[8,2,256,768]{3,2,1,0:T(8,128)(2,1)}), bf16[8,2,256,768]{3,2,1,0:T(8,128)(2,1)}, u32[]{:S(2)}, u32[]{:S(2)}) %all-to-all-start.2) | async-done | bytes 6291488 | tf_op jit(solution)/shard_map/all_to_all | solution.py:219
  661.8 56.8 %fusion.75 = bf16[8,2,256,3072]{3,2,0,1:T(8,128)(2,1)} fusion(f32[2,8,256,3072]{3,2,1,0:T(8,128)} %fusion.84, bf16[2,3072,768]{2,1,0:T(8,128)(2,1)} %param.30, bf16[8,2,256,768]{3,2,1,0:T(8,128)(2,1)} %all-to-all-done.2), kind=kOutput, calls=%fused_computation.117 | convolution fusion | flops 19579011072 | bytes 91226112 | tf_op jit(solution)/shard_map/gecd,efd->gecf/dot_general | solution.py:226
  718.6 26.0 %convert_bitcast_fusion.6 = bf16[8,2,256,768]{3,2,0,1:T(8,128)(2,1)S(1)} fusion(bf16[8,2,256,3072]{3,2,0,1:T(8,128)(2,1)} %fusion.75, bf16[2,768,3072]{2,1,0:T(8,128)(2,1)} %param.29), kind=kOutput, calls=%fused_computation.138 | convolution fusion | flops 19330498560 | bytes 40894464 | tf_op jit(solution)/shard_map/gecf,edf->gecd/dot_general | solution.py:235
  747.8 53.0 %all-to-all-done.1 = bf16[8,2,256,768]{3,2,1,0:T(8,128)(2,1)} async-done(((bf16[8,2,256,768]{3,2,1,0:T(8,128)(2,1)}), bf16[8,2,256,768]{3,2,1,0:T(8,128)(2,1)}, u32[]{:S(2)}, u32[]{:S(2)}) %all-to-all-start.1) | async-done | bytes 6291488 | tf_op jit(solution)/shard_map/all_to_all | solution.py:200
  805.7 38.8 %gather_fusion = bf16[2048,768]{1,0:T(8,128)(2,1)} fusion(bf16[16,256,768]{2,1,0:T(8,128)(2,1)} %bitcast.34, s32[2048]{0:T(1024)S(1)} %bitcast.307), kind=kCustom, calls=%fused_computation | custom fusion | bytes 6307840 | tf_op jit(solution)/shard_map/gather | solution.py:203
  852.5 17.2 multiply_reduce_fusion.1
  871.1 93.5 %psum.70 = f32[16]{0:T(128)S(1)} all-reduce(f32[16]{0:T(128)S(1)} %get-tuple-element.540), channel_id=1, replica_groups=mesh['rep'=4,'grp'=8] {'rep','grp'}, use_global_device_ids=true, to_apply=%region_18.19 | all-reduce | flops 16 | bytes 128 | tf_op jit(solution)/shard_map/psum | solution.py:173
  969.1 28.3 %gather_fusion.1 = bf16[2048,768]{1,0:T(8,128)(2,1)S(1)} fusion(bf16[16,256,768]{2,1,0:T(8,128)(2,1)} %bitcast.41, s32[2048]{0:T(1024)S(1)} %bitcast.308), kind=kCustom, calls=%fused_computation.1 | custom fusion | bytes 6307840 | tf_op jit(solution)/shard_map/gather | solution.py:246
  1002.1 11.9 reduce_sum.213
  1033.9 426.0 %while.48 = (s32[]{:T(128)}, f32[1024,12,64]{0,2,1:T(8,128)}, f32[1024,12,64]{0,2,1:T(8,128)}, f32[12,32]{1,0:T(8,128)}, bf16[2,512,12,64]{1,3,2,0:T(8,128)(2,1)...) while((s32[]{:T(128)}, f32[1024,12,64]{0,2,1:T(8,128)}, ...), condition=%wide.region_31.32_spmd.clone, body=%wide.region_29.31_spmd.clone.sunk | while | flops 4961595392 | bytes 488095232 | solution.py:324
  1079.0 16.0 fusion.218
  1095.0 31.9 %copy.226 = f32[2,8,512,1024]{3,2,1,0:T(8,128)} copy(f32[2,8,512,1024]{3,1,2,0:T(8,128)} %bitcast.304) | data formatting | bytes 67108864 | tf_op jit(solution)/shard_map/while/body/eval_jaxpr/while
  1127.0 25.1 %multiply_reduce_fusion.10 = (f32[12,512]{1,0:T(8,128)S(1)}, f32[12,512,1024]{2,1,0:T(8,128)}) fusion(f32[12,512,1024]{2,1,0:T(8,128)} %fusion.217, f32[12,512]{1,0:T(8,128)S(1)} %dynamic-slice_bitcast_fusion.2, f32[16,512,1024]{2,1,0:T(8,128)} %bitcast.302, bf16[1024,12,64]{0,2,1:T(8,128)(2,1)S(1)} %get-tuple-element.917, ...), kind=kOutput, calls=%fused_computation.60.clone.1 | convolution fusion | flops 843048960 | bytes 78438400 | tf_op jit(solution)/shard_map/while/body/eval_jaxpr/while/body/eval_jaxpr/qhd,khd->hqk/dot_general | solution.py:66
  1152.1 21.2 %multiply_convert_fusion.8 = bf16[12,512,1024]{2,1,0:T(8,128)(2,1)} fusion(f32[12,512,1024]{2,1,0:T(8,128)} %get-tuple-element.819, f32[12,512,1024]{2,1,0:T(8,128)} %fusion.217, f32[12,512]{1,0:T(8,128)S(1)} %get-tuple-element.820), kind=kLoop, calls=%fused_computation.59.clone.1 | loop fusion | flops 18874368 | bytes 62939136 | tf_op jit(solution)/shard_map/while/body/eval_jaxpr/while/body/eval_jaxpr/convert_element_type | solution.py:297
  1173.3 12.1 bitcast_add_fusion.5
  1209.4 31.0 %copy.227 = bf16[2,8,512,1024]{3,1,2,0:T(8,128)(2,1)} copy(bf16[2,8,512,1024]{3,2,1,0:T(8,128)(2,1)S(1)} %bitcast.306) | data formatting | bytes 33554432 | tf_op jit(solution)/shard_map/while/body/eval_jaxpr/while
  1240.4 13.7 fusion.220
  1277.2 16.0 fusion.218
  1293.2 31.9 %copy.226 = f32[2,8,512,1024]{3,2,1,0:T(8,128)} copy(f32[2,8,512,1024]{3,1,2,0:T(8,128)} %bitcast.304) | data formatting | bytes 67108864 | tf_op jit(solution)/shard_map/while/body/eval_jaxpr/while
  1325.1 25.1 %multiply_reduce_fusion.10 = (f32[12,512]{1,0:T(8,128)S(1)}, f32[12,512,1024]{2,1,0:T(8,128)}) fusion(f32[12,512,1024]{2,1,0:T(8,128)} %fusion.217, f32[12,512]{1,0:T(8,128)S(1)} %dynamic-slice_bitcast_fusion.2, f32[16,512,1024]{2,1,0:T(8,128)} %bitcast.302, bf16[1024,12,64]{0,2,1:T(8,128)(2,1)S(1)} %get-tuple-element.917, ...), kind=kOutput, calls=%fused_computation.60.clone.1 | convolution fusion | flops 843048960 | bytes 78438400 | tf_op jit(solution)/shard_map/while/body/eval_jaxpr/while/body/eval_jaxpr/qhd,khd->hqk/dot_general | solution.py:66
  1350.3 21.2 %multiply_convert_fusion.8 = bf16[12,512,1024]{2,1,0:T(8,128)(2,1)} fusion(f32[12,512,1024]{2,1,0:T(8,128)} %get-tuple-element.819, f32[12,512,1024]{2,1,0:T(8,128)} %fusion.217, f32[12,512]{1,0:T(8,128)S(1)} %get-tuple-element.820), kind=kLoop, calls=%fused_computation.59.clone.1 | loop fusion | flops 18874368 | bytes 62939136 | tf_op jit(solution)/shard_map/while/body/eval_jaxpr/while/body/eval_jaxpr/convert_element_type | solution.py:297
  1371.5 13.0 bitcast_add_fusion.5
  1409.4 31.0 %copy.227 = bf16[2,8,512,1024]{3,1,2,0:T(8,128)(2,1)} copy(bf16[2,8,512,1024]{3,2,1,0:T(8,128)(2,1)S(1)} %bitcast.306) | data formatting | bytes 33554432 | tf_op jit(solution)/shard_map/while/body/eval_jaxpr/while
  1440.4 13.7 fusion.220
  1481.6 21.3 %reduce-scatter.12.cloned.1.call-done = f32[96,768]{1,0:T(8,128)} async-done(((f32[768,768]{1,0:T(8,128)}), f32[96,768]{1,0:T(8,128)}) %reduce-scatter.12.cloned.1.call-update) | async-done | bytes 294928 | tf_op jit(solution)/shard_map/reduce_scatter | solution.py:359
  1502.9 38.4 %reduce-scatter.10.cloned.1.call-done = f32[96,768]{1,0:T(8,128)} async-done(((f32[768,768]{1,0:T(8,128)}), f32[96,768]{1,0:T(8,128)}) %reduce-scatter.10.cloned.1.call-update) | async-done | bytes 294928 | tf_op jit(solution)/shard_map/reduce_scatter | solution.py:358
  1541.3 37.9 %reduce-scatter.14.cloned.1.call-done = f32[96,768]{1,0:T(8,128)} async-done(((f32[768,768]{1,0:T(8,128)}), f32[96,768]{1,0:T(8,128)}) %reduce-scatter.14.cloned.1.call-update) | async-done | bytes 294928 | tf_op jit(solution)/shard_map/reduce_scatter | solution.py:360
  1579.2 40.0 %convolution_bitcast_fusion = f32[2,3072,768]{2,1,0:T(8,128)} fusion(bf16[8,2,256,768]{3,2,1,0:T(8,128)(2,1)} %all-to-all-done.2, f32[2,8,256,3072]{3,2,1,0:T(8,128)} %fusion.84), kind=kOutput, calls=%fused_computation.134 | convolution fusion | flops 19440599040 | bytes 75497472 | tf_op jit(solution)/shard_map/gecf,gecd->efd/dot_general | solution.py:229
  1619.3 27.9 %fusion.89 = f32[2,768,3072]{2,1,0:T(8,128)} fusion(bf16[8,2,256,768]{3,2,1,0:T(8,128)(2,1)} %all-to-all-done, bf16[8,2,256,3072]{3,2,0,1:T(8,128)(2,1)} %fusion.75), kind=kOutput, calls=%fused_computation.135 | convolution fusion | flops 19327352832 | bytes 50331648 | tf_op jit(solution)/shard_map/gecd,gecf->edf/dot_general | solution.py:234
  1648.6 38.0 %psum.71 = f32[16]{0:T(128)S(1)} all-reduce(f32[16]{0:T(128)S(1)} %copy-done.78), channel_id=1, replica_groups=mesh['rep'=4,'grp'=8] {'rep','grp'}, use_global_device_ids=true, to_apply=%region_20.21 | all-reduce | flops 16 | bytes 128 | tf_op jit(solution)/shard_map/psum | solution.py:173
  1697.4 27.3 %all-reduce.5 = (f32[768]{0:T(1024)S(1)}, f32[32,12]{1,0:T(8,128)S(1)}, f32[768]{0:T(1024)S(1)}) all-reduce(f32[768]{0:T(1024)S(1)} %get-tuple-element.533, f32[32,12]{1,0:T(8,128)S(1)} %bitcast.347, f32[768]{0:T(1024)S(1)} %copy-done.71), channel_id=2, replica_groups=mesh['rep'=4,'grp'=8] {'grp'}, use_global_device_ids=true, to_apply=%region_34.35.clone | all-reduce | flops 1920 | bytes 15360
  1736.6 16.1 all-reduce.6
  1752.7 91.0 %reduce-scatter.20.cloned.1.call-done = f32[2,768,768]{2,1,0:T(8,128)} async-done(((f32[2,3072,768]{2,1,0:T(8,128)}), f32[2,768,768]{2,1,0:T(8,128)}) %reduce-scatter.20.cloned.1.call-update) | async-done | bytes 4718608 | tf_op jit(solution)/shard_map/reduce_scatter | solution.py:240
  1843.8 174.8 %reduce-scatter.18.cloned.1.call-done = f32[2,192,3072]{2,1,0:T(8,128)} async-done(((f32[2,768,3072]{2,1,0:T(8,128)}), f32[2,192,3072]{2,1,0:T(8,128)}) %reduce-scatter.18.cloned.1.call-update) | async-done | bytes 4718608 | tf_op jit(solution)/shard_map/reduce_scatter | solution.py:239
  (419 shorter events, 356.0 us)
Async XLA Ops:
  7.2 45.2 %copy-start.80 = (s32[2]{0:T(128)S(1)}, s32[2]{0:T(128)}, u32[]{:S(2)}) copy-start(s32[2]{0:T(128)} %constant.425) | copy-start | bytes 28
  7.2 45.3 %copy-start.79 = (s32[2]{0:T(128)S(1)}, s32[2]{0:T(128)}, u32[]{:S(2)}) copy-start(s32[2]{0:T(128)} %constant.422) | copy-start | bytes 28
  7.2 49.0 %all-gather.9.cloned.1.call-start = ((), (), s32[]{:S(2)}) async-start(), calls=%async_computation.12 | async-start | bytes 1327104 | tf_op jit(solution)/shard_map/all_gather | solution.py:97
  7.9 51.4 %all-gather.11.cloned.1.call-start = ((), (), s32[]{:S(2)}) async-start(), calls=%async_computation.13 | async-start | bytes 1327104 | tf_op jit(solution)/shard_map/all_gather | solution.py:98
  8.7 74.4 %all-gather.7.cloned.1.call-start = ((), (), s32[]{:S(2)}) async-start(), calls=%async_computation.11 | async-start | bytes 1327104 | tf_op jit(solution)/shard_map/all_gather | solution.py:96
  9.4 282.1 %all-gather.13.cloned.1.call-start = ((), (), s32[]{:S(2)}) async-start(), calls=%async_computation.14 | async-start | bytes 1327104 | tf_op jit(solution)/shard_map/all_gather | solution.py:99
  34.9 48.2 %copy-start.65 = (f32[768]{0:T(1024)}, f32[768]{0:T(1024)S(1)}, u32[]{:S(2)}) copy-start(f32[768]{0:T(1024)S(1)} %convert_element_type.559) | copy-start | bytes 9220
  36.7 22.3 %copy-start.59 = (s32[1,8,128]{2,1,0:T(8,128)}, s32[1,8,128]{2,1,0:T(8,128)S(1)}, u32[]{:S(2)}) copy-start(s32[1,8,128]{2,1,0:T(8,128)S(1)} %reduce-window.14) | copy-start | bytes 12292
  37.0 18.5 copy-start.76
  55.5 27.6 %copy-start.63 = (f32[1024]{0:T(1024)}, f32[1024]{0:T(1024)S(1)}, u32[]{:S(2)}) copy-start(f32[1024]{0:T(1024)S(1)} %get-tuple-element.628) | copy-start | bytes 12292
  62.5 24.9 %copy-start.33 = (s32[1024]{0:T(1024)S(1)}, s32[1024]{0:T(1024)}, u32[]{:S(2)}) copy-start(s32[1024]{0:T(1024)} %param.19) | copy-start | bytes 12292
  324.1 149.9 %copy-start.28 = (bf16[1024,768]{1,0:T(8,128)(2,1)S(1)}, bf16[1024,768]{1,0:T(8,128)(2,1)}, u32[]{:S(2)}) copy-start(bf16[1024,768]{1,0:T(8,128)(2,1)} %param.31) | copy-start | bytes 4718596
  324.1 188.6 %all-to-all-start = ((bf16[8,2,256,768]{3,2,1,0:T(8,128)(2,1)}), bf16[8,2,256,768]{3,2,1,0:T(8,128)(2,1)}, u32[]{:S(2)}, u32[]{:S(2)}) async-start(bf16[8,2,256,768]{3,2,1,0:T(8,128)(2,1)} %bitcast.324), calls=%async_computation | async-start | bytes 12582912 | tf_op jit(solution)/shard_map/all_to_all | solution.py:188
  474.1 20.2 copy-start.45
  497.6 15.2 copy-start.25
  512.8 143.9 %all-to-all-start.2 = ((bf16[8,2,256,768]{3,2,1,0:T(8,128)(2,1)}), bf16[8,2,256,768]{3,2,1,0:T(8,128)(2,1)}, u32[]{:S(2)}, u32[]{:S(2)}) async-start(bf16[8,2,256,768]{3,2,1,0:T(8,128)(2,1)} %bitcast.325), calls=%async_computation.2 | async-start | bytes 12582912 | tf_op jit(solution)/shard_map/all_to_all | solution.py:219
  656.7 144.1 %all-to-all-start.1 = ((bf16[8,2,256,768]{3,2,1,0:T(8,128)(2,1)}), bf16[8,2,256,768]{3,2,1,0:T(8,128)(2,1)}, u32[]{:S(2)}, u32[]{:S(2)}) async-start(bf16[8,2,256,768]{3,2,1,0:T(8,128)(2,1)} %copy.139), calls=%async_computation.1 | async-start | bytes 12582912 | tf_op jit(solution)/shard_map/all_to_all | solution.py:200
  747.8 57.8 %copy-start.60 = (s32[1,8,128]{2,1,0:T(8,128)S(1)}, s32[1,8,128]{2,1,0:T(8,128)}, u32[]{:S(2)}) copy-start(s32[1,8,128]{2,1,0:T(8,128)} %copy-done.59) | copy-start | bytes 12292
  747.8 57.8 %copy-start.77 = (s32[8]{0:T(128)S(1)}, s32[8]{0:T(128)}, u32[]{:S(2)}) copy-start(s32[8]{0:T(128)} %copy-done.76) | copy-start | bytes 100
  747.8 57.9 %copy-start = (s32[2048,1]{0,1:T(1,128)S(1)}, s32[2048,1]{0,1:T(1,128)}, u32[]{:S(2)}) copy-start(s32[2048,1]{0,1:T(1,128)} %get-tuple-element.624) | copy-start | bytes 24580
  800.8 168.3 %all-to-all-start.3 = ((bf16[8,2,256,768]{3,2,1,0:T(8,128)(2,1)}), bf16[8,2,256,768]{3,2,1,0:T(8,128)(2,1)}, u32[]{:S(2)}, u32[]{:S(2)}) async-start(bf16[8,2,256,768]{3,2,1,0:T(8,128)(2,1)} %copy.145), calls=%async_computation.3 | async-start | bytes 12582912 | tf_op jit(solution)/shard_map/all_to_all | solution.py:242
  805.6 676.0 %reduce-scatter.16.cloned.1.call-start = ((), (), s32[]{:S(2)}) async-start(), calls=%async_computation.18 | async-start | bytes 2654208 | tf_op jit(solution)/shard_map/reduce_scatter | solution.py:361
  852.5 18.4 copy-start.52
  852.5 18.5 copy-start.62
  852.5 18.5 copy-start.50
  969.0 49.0 %copy-start.43 = (bf16[1024,16]{0,1:T(8,128)(2,1)}, bf16[1024,16]{0,1:T(8,128)(2,1)S(1)}, u32[]{:S(2)}) copy-start(bf16[1024,16]{0,1:T(8,128)(2,1)S(1)} %multiply_convert_fusion.6) | copy-start | bytes 98308
  1028.9 474.0 %reduce-scatter.12.cloned.1.call-start = ((), (), s32[]{:S(2)}) async-start(), calls=%async_computation.16 | async-start | bytes 2654208 | tf_op jit(solution)/shard_map/reduce_scatter | solution.py:359
  1095.0 31.9 %copy-start.7 = (bf16[1024,12,64]{0,2,1:T(8,128)(2,1)S(1)}, bf16[1024,12,64]{0,2,1:T(8,128)(2,1)}, u32[]{:S(2)}) copy-start(bf16[1024,12,64]{0,2,1:T(8,128)(2,1)} %get-tuple-element.915) | copy-start | bytes 4718596 | tf_op jit(solution)/shard_map/while/body/eval_jaxpr/while
  1152.1 21.2 %copy-start.9 = (bf16[1024,12,64]{0,2,1:T(8,128)(2,1)S(1)}, bf16[1024,12,64]{0,2,1:T(8,128)(2,1)}, u32[]{:S(2)}) copy-start(bf16[1024,12,64]{0,2,1:T(8,128)(2,1)} %get-tuple-element.921) | copy-start | bytes 4718596 | tf_op jit(solution)/shard_map/while/body/eval_jaxpr/while
  1209.4 31.0 %copy-start.4 = (s32[524288]{0:T(1024)S(1)}, s32[524288]{0:T(1024)}, u32[]{:S(2)}) copy-start(s32[524288]{0:T(1024)} %copy-done.3) | copy-start | bytes 6291460 | tf_op jit(solution)/shard_map/while/body/eval_jaxpr/while
  1209.4 31.0 %copy-start.72 = (f32[12,32]{1,0:T(8,128)S(1)}, f32[12,32]{1,0:T(8,128)}, u32[]{:S(2)}) copy-start(f32[12,32]{1,0:T(8,128)} %get-tuple-element.892) | copy-start | bytes 4612 | tf_op jit(solution)/shard_map/while/body/eval_jaxpr/while
  1240.4 14.4 copy-start.36
  1240.4 14.4 copy-start.39
  1293.2 31.9 %copy-start.7 = (bf16[1024,12,64]{0,2,1:T(8,128)(2,1)S(1)}, bf16[1024,12,64]{0,2,1:T(8,128)(2,1)}, u32[]{:S(2)}) copy-start(bf16[1024,12,64]{0,2,1:T(8,128)(2,1)} %get-tuple-element.915) | copy-start | bytes 4718596 | tf_op jit(solution)/shard_map/while/body/eval_jaxpr/while
  1350.3 21.2 %copy-start.9 = (bf16[1024,12,64]{0,2,1:T(8,128)(2,1)S(1)}, bf16[1024,12,64]{0,2,1:T(8,128)(2,1)}, u32[]{:S(2)}) copy-start(bf16[1024,12,64]{0,2,1:T(8,128)(2,1)} %get-tuple-element.921) | copy-start | bytes 4718596 | tf_op jit(solution)/shard_map/while/body/eval_jaxpr/while
  1409.4 31.0 %copy-start.4 = (s32[524288]{0:T(1024)S(1)}, s32[524288]{0:T(1024)}, u32[]{:S(2)}) copy-start(s32[524288]{0:T(1024)} %copy-done.3) | copy-start | bytes 6291460 | tf_op jit(solution)/shard_map/while/body/eval_jaxpr/while
  1409.4 31.0 %copy-start.72 = (f32[12,32]{1,0:T(8,128)S(1)}, f32[12,32]{1,0:T(8,128)}, u32[]{:S(2)}) copy-start(f32[12,32]{1,0:T(8,128)} %get-tuple-element.892) | copy-start | bytes 4612 | tf_op jit(solution)/shard_map/while/body/eval_jaxpr/while
  1440.4 14.4 copy-start.36
  1440.4 14.4 copy-start.39
  1466.4 74.9 %reduce-scatter.10.cloned.1.call-start = ((), (), s32[]{:S(2)}) async-start(), calls=%async_computation.15 | async-start | bytes 2654208 | tf_op jit(solution)/shard_map/reduce_scatter | solution.py:358
  1473.8 105.3 %reduce-scatter.14.cloned.1.call-start = ((), (), s32[]{:S(2)}) async-start(), calls=%async_computation.17 | async-start | bytes 2654208 | tf_op jit(solution)/shard_map/reduce_scatter | solution.py:360
  1480.1 255.7 %reduce-scatter.22.cloned.1.call-start = ((), (), s32[]{:S(2)}) async-start(), calls=%async_computation.21 | async-start | bytes 442368
  1481.5 271.2 %all-reduce.11.cloned.1.call-start = ((), (), s32[]{:S(2)}) async-start(), calls=%async_computation.22 | async-start | bytes 2359296 | tf_op jit(solution)/shard_map/psum | solution.py:366
  1579.2 264.6 %reduce-scatter.20.cloned.1.call-start = ((), (), s32[]{:S(2)}) async-start(), calls=%async_computation.20 | async-start | bytes 23592960 | tf_op jit(solution)/shard_map/reduce_scatter | solution.py:240
  1619.2 399.3 %reduce-scatter.18.cloned.1.call-start = ((), (), s32[]{:S(2)}) async-start(), calls=%async_computation.19 | async-start | bytes 23592960 | tf_op jit(solution)/shard_map/reduce_scatter | solution.py:239
  1647.2 39.5 %copy-start.22 = (bf16[1024,768]{0,1:T(8,128)(2,1)S(1)}, bf16[1024,768]{0,1:T(8,128)(2,1)}, u32[]{:S(2)}) copy-start(bf16[1024,768]{0,1:T(8,128)(2,1)} %get-tuple-element.623) | copy-start | bytes 4718596
  1647.2 41.0 %copy-start.74 = (f32[12,32]{1,0:T(8,128)S(1)}, f32[12,32]{1,0:T(8,128)}, u32[]{:S(2)}) copy-start(f32[12,32]{1,0:T(8,128)} %get-tuple-element.413) | copy-start | bytes 4612
  1693.8 31.1 %copy-start.69 = (f32[1024]{0:T(1024)S(1)}, f32[1024]{0:T(1024)}, u32[]{:S(2)}) copy-start(f32[1024]{0:T(1024)} %get-tuple-element.627) | copy-start | bytes 12292
  (68 other events, 292.1 us)
Sparse Core Ops, SparseCore 0:
  9.7 25.5 all-gather.8
  36.9 22.3 all-gather.10
  60.9 22.0 all-gather.6
  84.6 22.4 all-gather.12
  1029.0 36.4 reduce-scatter.15
  1466.5 36.3 reduce-scatter.11
  1505.8 35.4 reduce-scatter.9
  1543.6 35.5 reduce-scatter.13
  1581.4 29.7 reduce-scatter.21
  1614.7 53.5 all-reduce.10
  1672.0 171.7 reduce-scatter.19
  1847.6 170.8 reduce-scatter.17
where the time goes:
time: 2040 us; the launch traced here: 2030 us
  matrix products  537 us (26%)
  waiting for transfers between devices  515 us (25%)
  local copies, waits for them, and re-layouts  398 us (20%)
  blocking collectives  347 us (17%)
  other arithmetic  156 us (8%)
  loops' own time  39.4 us (2%)
    while x80, local copies, waits for them, and re-layouts  214 us
    reduce_scatter x1, waiting for transfers between devices, shards(): lax.psum_scatter(up_grad, 'rep', scatter_dimension=1, tiled=True)  175 us
    all_gather x1, blocking collectives, shards(): lax.all_gather(router, 'grp', axis=0, tiled=True)  145 us
    psum x2, blocking collectives, shards(): lax.psum((jnp.sum(choose.astype(jnp.float32), axis=(0, 1)), jnp.sum(route...  132 us
    reduce_scatter x1, waiting for transfers between devices, shards(): lax.psum_scatter(down_grad, 'rep', scatter_dimension=1, tiled=True)  91 us
    dot_general x4, matrix products, block_scores(): jnp.einsum('qhd,khd->hqk', query_blk, key_seq, preferred_element_type=jnp...  82.6 us
    all_to_all x1, waiting for transfers between devices, shards(): lax.all_to_all(grad_send.reshape(groups, exp_local, capacity, width), 'gr...  75.6 us
    dot_general x4, matrix products, block_scores(): jnp.dot(table_heads, one_hot, preferred_element_type=jnp.float32)  64.3 us
  transfers between devices with their start and end apart: 16, of which 9 were waited for; matrix products, arithmetic and copies ran while one was open for 48% of the time, Pallas kernels for 0%

commit v1 on v0

--- a/solution.py
+++ b/solution.py
@@ -3,38 +3,250 @@
 import jax
 import jax.numpy as jnp
 from jax import lax
+from jax.experimental import pallas as pl
+from jax.experimental.pallas import tpu as pltpu
 from jax.sharding import PartitionSpec as P
 
-HEADS = 12
-HEAD_DIM = 64
 TOP = 2
-SEQ = 1024
-QBLK = 512
-
-
+QB = 128
+PAIR = 128
+NEAR = 2 * QB
+SPAN = 3 * QB
+OUT_OF_DOC = -1e30
+FAR_MARKS = (18, 20, 23, 26, 30, 34, 39, 45, 51, 58, 66, 76, 86, 98, 112)
 norm_eps = 1e-06
 aux_weight = 0.01
-masked_score = -1e30
-far_marks = (18, 20, 23, 26, 30, 34, 39, 45, 51, 58, 66, 76, 86, 98, 112)
+f32, bf16 = jnp.float32, jnp.bfloat16
 
 
 def rms_scale(values):
     return lax.rsqrt(jnp.mean(values * values, axis=-1, keepdims=True) + norm_eps)
 
 
-def positions_of(seg_row):
-    length = seg_row.shape[0]
-    places = lax.iota(jnp.int32, length)
-    before = jnp.concatenate([seg_row[:1] - 1, seg_row[:-1]])
-    starts = jnp.where(seg_row != before, places, 0)
-    return places - lax.cummax(starts, axis=0)
-
-
 def bucket_of(distance):
     far_part = jnp.zeros_like(distance)
-    for far_mark in far_marks:
+    for far_mark in FAR_MARKS:
         far_part = far_part + (distance >= far_mark).astype(jnp.int32)
     return jnp.minimum(distance, 16) + far_part
+
+
+def band_hot(buckets):
+    lane = lax.broadcasted_iota(jnp.int32, (8, SPAN), 1)
+    row = lax.broadcasted_iota(jnp.int32, (8, SPAN), 0)
+    turn = (lane - row + SPAN) % SPAN
+    diff = jnp.where(turn < QB, turn, turn - SPAN) + QB
+    bucket = bucket_of(jnp.maximum(diff, 0)).reshape(1, 8 * SPAN)
+    return bucket == lax.iota(jnp.int32, buckets)[:, None]
+
+
+def split_pair(rows, low_lanes):
+    zero = jnp.zeros_like(rows)
+    return jnp.concatenate(
+        [jnp.where(low_lanes, rows, zero), jnp.where(low_lanes, zero, rows)], axis=0
+    )
+
+
+def fill_mask(seg_col, seg_row, mask):
+    seq = mask.shape[0]
+    for i in range(seq // QB):
+        length = (i + 1) * QB
+        sk = seg_col[0:length, :]
+        sq = seg_row[:, i * QB:(i + 1) * QB]
+        kp = lax.broadcasted_iota(jnp.int32, (length, QB), 0)
+        qp = lax.broadcasted_iota(jnp.int32, (length, QB), 1) + i * QB
+        ok = (sk == sq) & (kp <= qp) & ((sq != 0) | (kp == qp))
+        mask[0:length, i * QB:(i + 1) * QB] = jnp.where(ok, 0.0, OUT_OF_DOC).astype(f32)
+
+
+def fill_near(base, near):
+    for head in range(2):
+        rows = base[head]
+        for a in range(NEAR // 8):
+            turned = rows if a == 0 else pltpu.roll(rows, 8 * a, 1)
+            near[8 * a:8 * a + 8, head * QB:(head + 1) * QB] = turned[:, 0:QB]
+
+
+def scores_chunk(k, lo, hi, qcat, mask, near, i):
+    s = lax.dot_general(k[lo:hi, :], qcat, (((1,), (1,)), ((), ())), preferred_element_type=f32)
+    m = mask[lo:hi, i * QB:(i + 1) * QB]
+    s = s + jnp.concatenate([m, m], axis=1)
+    start = (i - 1) * QB
+    if lo >= start:
+        s = s + near[lo - start:hi - start, :]
+    return s
+
+
+def fwd_kernel(base, seg_col, seg_row, q, k, v, ctx, lse, mask, near, scores, probs, v_t):
+    seq = q.shape[0]
+
+    @pl.when(pl.program_id(0) == 0)
+    def _():
+        fill_mask(seg_col, seg_row, mask)
+
+    fill_near(base, near)
+    v_t[...] = v[...].T
+    low_lanes = lax.broadcasted_iota(jnp.int32, (QB, PAIR), 1) < PAIR // 2
+    scale = (PAIR // 2) ** -0.5
+    for i in range(seq // QB):
+        qs = slice(i * QB, (i + 1) * QB)
+        qcat = split_pair(q[qs, :] * jnp.asarray(scale, bf16), low_lanes)
+        top = None
+        for c in range(i + 1):
+            s = scores_chunk(k, c * QB, (c + 1) * QB, qcat, mask, near, i)
+            scores[c * QB:(c + 1) * QB, :] = s
+            here = jnp.max(s.reshape(QB // 8, 8, NEAR), axis=0)
+            top = here if top is None else jnp.maximum(top, here)
+        top = jnp.max(top, axis=0, keepdims=True)
+        total = jnp.zeros((8, NEAR), f32)
+        for c in range(i + 1):
+            p = jnp.exp(scores[c * QB:(c + 1) * QB, :] - top)
+            total = total + jnp.sum(p.reshape(QB // 8, 8, NEAR), axis=0)
+            probs[c * QB:(c + 1) * QB, :] = p.astype(bf16)
+        total = jnp.sum(total, axis=0, keepdims=True)
+        length = (i + 1) * QB
+        out = jnp.dot(v_t[:, 0:length], probs[0:length, :], preferred_element_type=f32) / total
+        half = PAIR // 2
+        both = jnp.concatenate([out[0:half, 0:QB], out[half:PAIR, QB:NEAR]], axis=0)
+        ctx[qs, :] = both.T.astype(bf16)
+        lse[0, i:i + 1, :] = top + jnp.log(total)
+
+
+def attend(q, k, v, seg, base):
+    seq, width = q.shape
+    pairs = width // PAIR
+    col = pl.BlockSpec((seq, PAIR), lambda h: (0, h))
+    whole = lambda *shape: pl.BlockSpec(shape, lambda h: (0,) * len(shape))
+    return pl.pallas_call(
+        fwd_kernel,
+        grid=(pairs,),
+        in_specs=[pl.BlockSpec((2, 8, SPAN), lambda h: (h, 0, 0)), whole(seq, 1), whole(1, seq), col, col, col],
+        out_specs=[col, pl.BlockSpec((1, seq // QB, NEAR), lambda h: (h, 0, 0))],
+        out_shape=[
+            jax.ShapeDtypeStruct((seq, width), bf16),
+            jax.ShapeDtypeStruct((pairs, seq // QB, NEAR), f32),
+        ],
+        scratch_shapes=[
+            pltpu.VMEM((seq, seq), f32),
+            pltpu.VMEM((NEAR, NEAR), f32),
+            pltpu.VMEM((seq, NEAR), f32),
+            pltpu.VMEM((seq, NEAR), bf16),
+            pltpu.VMEM((PAIR, seq), bf16),
+        ],
+        compiler_params=pltpu.CompilerParams(vmem_limit_bytes=32 * 1024 * 1024),
+        cost_estimate=pl.CostEstimate(flops=seq * seq * width * 4, bytes_accessed=8 * seq * width, transcendentals=6 * seq * seq),
+        name="attend",
+    )(base, seg.reshape(seq, 1), seg.reshape(1, seq), q, k, v)
+
+
+def bwd_kernel(base, seg_col, seg_row, q, k, v, ctx, dctx, lse, dq, dk, dv, dnear, dfar,
+               mask, near, ds_all, p_all, k_t, dk_sum, dv_sum, dnear_sum, dfar_sum):
+    seq = q.shape[0]
+
+    @pl.when(pl.program_id(0) == 0)
+    def _():
+        fill_mask(seg_col, seg_row, mask)
+
+    fill_near(base, near)
+    k_t[...] = k[...].T
+    low_lanes = lax.broadcasted_iota(jnp.int32, (QB, PAIR), 1) < PAIR // 2
+    half = PAIR // 2
+    scale = half ** -0.5
+    dnear_sum[...] = jnp.zeros_like(dnear_sum)
+    dfar_sum[...] = jnp.zeros_like(dfar_sum)
+    for i in reversed(range(seq // QB)):
+        qs = slice(i * QB, (i + 1) * QB)
+        length = (i + 1) * QB
+        qcat = split_pair(q[qs, :] * jnp.asarray(scale, bf16), low_lanes)
+        dcat = split_pair(dctx[qs, :], low_lanes)
+        dots = (ctx[qs, :].astype(f32) * dctx[qs, :].astype(f32)).T
+        centre = jnp.concatenate(
+            [jnp.sum(dots[0:half], axis=0, keepdims=True), jnp.sum(dots[half:], axis=0, keepdims=True)], axis=1
+        )
+        norm = lse[0, i:i + 1, :]
+        for c in range(i + 1):
+            lo, hi = c * QB, (c + 1) * QB
+            s = scores_chunk(k, lo, hi, qcat, mask, near, i)
+            p = jnp.exp(s - norm)
+            p_all[lo:hi, :] = p.astype(bf16)
+            dp = lax.dot_general(v[lo:hi, :], dcat, (((1,), (1,)), ((), ())), preferred_element_type=f32)
+            ds = p * (dp - centre)
+            ds_all[lo:hi, :] = ds.astype(bf16)
+            start = (i - 1) * QB
+            if lo >= start:
+                dnear_sum[lo - start:hi - start, :] += ds
+            else:
+                dfar_sum[...] += jnp.sum(ds.reshape(QB // 8, 8, NEAR), axis=0)
+        out = jnp.dot(k_t[:, 0:length], ds_all[0:length, :], preferred_element_type=f32)
+        both = jnp.concatenate([out[0:half, 0:QB], out[half:PAIR, QB:NEAR]], axis=0)
+        dq[qs, :] = (both.T * scale).astype(bf16)
+        dk_part = jnp.dot(ds_all[0:length, :], qcat, preferred_element_type=f32)
+        dv_part = jnp.dot(p_all[0:length, :], dcat, preferred_element_type=f32)
+        if i == seq // QB - 1:
+            dk_sum[0:length, :] = dk_part
+            dv_sum[0:length, :] = dv_part
+        else:
+            dk_sum[0:length, :] += dk_part
+            dv_sum[0:length, :] += dv_part
+    dk[...] = dk_sum[...].astype(bf16)
+    dv[...] = dv_sum[...].astype(bf16)
+    for head in range(2):
+        total = jnp.zeros((8, SPAN), f32)
+        for a in range(NEAR // 8):
+            rows = dnear_sum[8 * a:8 * a + 8, head * QB:(head + 1) * QB]
+            rows = jnp.concatenate([rows, jnp.zeros((8, SPAN - QB), f32)], axis=1)
+            total = total + (rows if a == 0 else pltpu.roll(rows, SPAN - 8 * a, 1))
+        dnear[head] = total
+    dfar[0] = dfar_sum[...]
+
+
+def attend_back(q, k, v, seg, base, ctx, dctx, lse):
+    seq, width = q.shape
+    pairs = width // PAIR
+    col = pl.BlockSpec((seq, PAIR), lambda h: (0, h))
+    band = pl.BlockSpec((2, 8, SPAN), lambda h: (h, 0, 0))
+    whole = lambda *shape: pl.BlockSpec(shape, lambda h: (0,) * len(shape))
+    rows = jax.ShapeDtypeStruct((seq, width), bf16)
+    return pl.pallas_call(
+        bwd_kernel,
+        grid=(pairs,),
+        in_specs=[band, whole(seq, 1), whole(1, seq), col, col, col, col, col,
+                  pl.BlockSpec((1, seq // QB, NEAR), lambda h: (h, 0, 0))],
+        out_specs=[col, col, col, band, pl.BlockSpec((1, 8, NEAR), lambda h: (h, 0, 0))],
+        out_shape=[rows, rows, rows, jax.ShapeDtypeStruct((2 * pairs, 8, SPAN), f32),
+                   jax.ShapeDtypeStruct((pairs, 8, NEAR), f32)],
+        scratch_shapes=[
+            pltpu.VMEM((seq, seq), f32),
+            pltpu.VMEM((NEAR, NEAR), f32),
+            pltpu.VMEM((seq, NEAR), bf16),
+            pltpu.VMEM((seq, NEAR), bf16),
+            pltpu.VMEM((PAIR, seq), bf16),
+            pltpu.VMEM((seq, PAIR), f32),
+            pltpu.VMEM((seq, PAIR), f32),
+            pltpu.VMEM((NEAR, NEAR), f32),
+            pltpu.VMEM((8, NEAR), f32),
+        ],
+        compiler_params=pltpu.CompilerParams(vmem_limit_bytes=40 * 1024 * 1024),
+        cost_estimate=pl.CostEstimate(flops=seq * seq * width * 10, bytes_accessed=16 * seq * width, transcendentals=6 * seq * seq),
+        name="attend_back",
+    )(base, seg.reshape(seq, 1), seg.reshape(1, seq), q, k, v, ctx, dctx, lse)
+
+
+def bias_base(table):
+    buckets, heads = table.shape
+    hot = band_hot(buckets).astype(bf16)
+    base = lax.dot_general(table, hot, (((0,), (0,)), ((), ())), preferred_element_type=f32)
+    last = table[buckets - 1].astype(f32)
+    return base.reshape(heads, 8, SPAN) - last[:, None, None]
+
+
+def table_back(dnear, dfar, buckets):
+    heads = dnear.shape[0]
+    hot = band_hot(buckets).astype(f32)
+    grad = lax.dot_general(hot, dnear.reshape(heads, 8 * SPAN), (((1,), (1,)), ((), ())),
+                           preferred_element_type=f32, precision=lax.Precision.HIGHEST)
+    far = jnp.sum(dfar.reshape(heads // 2, 8, 2, QB), axis=(1, 3)).reshape(1, heads)
+    last = (lax.iota(jnp.int32, buckets) == buckets - 1)[:, None]
+    return grad + jnp.where(last, far, 0.0)
 
 
 def outer_sum(left_rows, right_rows):
@@ -47,32 +259,6 @@
     return lax.dot_general(
         grad_rows, weight, (((1,), (1,)), ((), ())), preferred_element_type=jnp.float32
     )
-
-
-def block_scores(
-    query_blk, key_seq, seg_query, seg_key, pos_query, pos_key, row_start, table_heads
-):
-    query_count = query_blk.shape[0]
-    key_count = key_seq.shape[0]
-    distance = jnp.maximum(pos_query[:, None] - pos_key[None, :], 0)
-    flat_bucket = bucket_of(distance).reshape(1, query_count * key_count)
-    bucket_ids = lax.iota(jnp.int32, table_heads.shape[1])[:, None]
-    one_hot = (flat_bucket == bucket_ids).astype(jnp.bfloat16)
-    biases = jnp.dot(table_heads, one_hot, preferred_element_type=jnp.float32).reshape(
-        -1, query_count, key_count
-    )
-    scaling = query_blk.shape[2] ** (-0.5)
-    scores = (
-        jnp.einsum("qhd,khd->hqk", query_blk, key_seq, preferred_element_type=jnp.float32) * scaling
-        + biases
-    )
-    query_place = row_start + lax.iota(jnp.int32, query_count)
-    key_place = lax.iota(jnp.int32, key_count)
-    same_doc = seg_query[:, None] == seg_key[None, :]
-    causal = key_place[None, :] <= query_place[:, None]
-    own_place = key_place[None, :] == query_place[:, None]
-    allowed = same_doc & causal & ((seg_query[:, None] != 0) | own_place)
-    return (scores, allowed, one_hot)
 
 
 def shards(
@@ -106,9 +292,6 @@
     )
     tok_rows = tokens.shape[0]
     width = tokens.shape[1]
-    seq_count = tok_rows // SEQ
-    block_count = SEQ // QBLK
-    scaling = HEAD_DIM ** (-0.5)
     inputs = tokens.astype(jnp.float32)
     scale_one = rms_scale(inputs)
     normed_one = (inputs * scale_one * gain_one.astype(jnp.float32)).astype(jnp.bfloat16)
@@ -121,42 +304,8 @@
     value_rows = jnp.dot(normed_one, value_full, preferred_element_type=jnp.float32).astype(
         jnp.bfloat16
     )
-    head_query = query_rows.reshape(tok_rows, HEADS, HEAD_DIM)
-    head_key = key_rows.reshape(tok_rows, HEADS, HEAD_DIM)
-    head_value = value_rows.reshape(tok_rows, HEADS, HEAD_DIM)
-    seg_rows = segments.reshape(seq_count, SEQ)
-    pos_rows = jax.vmap(positions_of)(seg_rows)
-    table_heads = table_full.T
-
-    def forward_block(block_id):
-        seq_id = block_id // block_count
-        row_start = block_id % block_count * QBLK
-        seq_base = seq_id * SEQ
-        query_blk = lax.dynamic_slice_in_dim(head_query, seq_base + row_start, QBLK, 0)
-        seg_seq = lax.dynamic_index_in_dim(seg_rows, seq_id, 0, keepdims=False)
-        pos_seq = lax.dynamic_index_in_dim(pos_rows, seq_id, 0, keepdims=False)
-        seg_query = lax.dynamic_slice_in_dim(seg_seq, row_start, QBLK, 0)
-        pos_query = lax.dynamic_slice_in_dim(pos_seq, row_start, QBLK, 0)
-        scores, allowed, unused_hot = block_scores(
-            query_blk, head_key, seg_query, seg_seq, pos_query, pos_seq, row_start, table_heads
-        )
-        scores = jnp.where(allowed[None], scores, masked_score)
-        highest = jnp.max(scores, axis=-1, keepdims=True)
-        expos = jnp.exp(scores - highest)
-        totals = jnp.sum(expos, axis=-1, keepdims=True)
-        weights = (expos / totals).astype(jnp.bfloat16)
-        context_blk = jnp.einsum(
-            "hqk,khd->qhd", weights, head_value, preferred_element_type=jnp.float32
-        )
-        return (
-            context_blk.reshape(QBLK, width).astype(jnp.bfloat16),
-            (highest + jnp.log(totals))[:, :, 0],
-        )
-
-    context_blocks, lse_blocks = lax.map(
-        forward_block, jnp.arange(seq_count * block_count, dtype=jnp.int32)
-    )
-    context = context_blocks.reshape(tok_rows, width)
+    base = bias_base(table_full)
+    context, lse = attend(query_rows, key_rows, value_rows, segments, base)
     hidden_one = inputs + jnp.dot(context, output_full, preferred_element_type=jnp.float32)
     scale_two = rms_scale(hidden_one)
     normed_two = (hidden_one * scale_two * gain_two.astype(jnp.float32)).astype(jnp.bfloat16)
@@ -268,75 +417,9 @@
     grad_attn = grad_hidden_one.astype(jnp.bfloat16)
     output_grad = outer_sum(context, grad_attn)
     grad_context = back_proj(grad_attn, output_full).astype(jnp.bfloat16)
-    head_grad_ctx = grad_context.reshape(tok_rows, HEADS, HEAD_DIM)
-    table_heads = table_full.T
-
-    def backward_seq(seq_id):
-        seq_base = seq_id * SEQ
-        seg_seq = lax.dynamic_index_in_dim(seg_rows, seq_id, 0, keepdims=False)
-        pos_seq = lax.dynamic_index_in_dim(pos_rows, seq_id, 0, keepdims=False)
-
-        def block_step(carry_in, block_idx):
-            grad_key, grad_value, grad_table = carry_in
-            row_start = block_idx * QBLK
-            query_blk = lax.dynamic_slice_in_dim(head_query, seq_base + row_start, QBLK, 0)
-            ctx_grad_blk = lax.dynamic_slice_in_dim(head_grad_ctx, seq_base + row_start, QBLK, 0)
-            lse_blk = lax.dynamic_index_in_dim(
-                lse_blocks, seq_id * block_count + block_idx, 0, keepdims=False
-            )
-            seg_query = lax.dynamic_slice_in_dim(seg_seq, row_start, QBLK, 0)
-            pos_query = lax.dynamic_slice_in_dim(pos_seq, row_start, QBLK, 0)
-            scores, allowed, one_hot = block_scores(
-                query_blk, head_key, seg_query, seg_seq, pos_query, pos_seq, row_start, table_heads
-            )
-            prob_blk = jnp.where(allowed[None], jnp.exp(scores - lse_blk[:, :, None]), 0.0)
-            grad_prob = jnp.einsum(
-                "qhd,khd->hqk", ctx_grad_blk, head_value, preferred_element_type=jnp.float32
-            )
-            centre = jnp.sum(prob_blk * grad_prob, axis=-1, keepdims=True)
-            grad_score = (prob_blk * (grad_prob - centre)).astype(jnp.bfloat16)
-            grad_query = (
-                jnp.einsum("hqk,khd->qhd", grad_score, head_key, preferred_element_type=jnp.float32)
-                * scaling
-            ).astype(jnp.bfloat16)
-            grad_key = grad_key + jnp.einsum(
-                "hqk,qhd->khd", grad_score, query_blk, preferred_element_type=jnp.float32
-            )
-            grad_value = grad_value + jnp.einsum(
-                "hqk,qhd->khd",
-                prob_blk.astype(jnp.bfloat16),
-                ctx_grad_blk,
-                preferred_element_type=jnp.float32,
-            )
-            grad_table = grad_table + lax.dot_general(
-                grad_score.reshape(HEADS, QBLK * SEQ),
-                one_hot,
-                (((1,), (1,)), ((), ())),
-                preferred_element_type=jnp.float32,
-            )
-            return ((grad_key, grad_value, grad_table), grad_query)
-
-        start_carry = (
-            jnp.zeros((SEQ, HEADS, HEAD_DIM), jnp.float32),
-            jnp.zeros((SEQ, HEADS, HEAD_DIM), jnp.float32),
-            jnp.zeros((HEADS, table_heads.shape[1]), jnp.float32),
-        )
-        (grad_key, grad_value, grad_table), grad_query = lax.scan(
-            block_step, start_carry, jnp.arange(block_count, dtype=jnp.int32)
-        )
-        return (
-            grad_query.reshape(SEQ, width),
-            (grad_key * scaling).astype(jnp.bfloat16).reshape(SEQ, width),
-            grad_value.astype(jnp.bfloat16).reshape(SEQ, width),
-            grad_table,
-        )
-
-    grad_q_seq, grad_k_seq, grad_v_seq, table_parts = lax.map(
-        backward_seq, jnp.arange(seq_count, dtype=jnp.int32)
-    )
-    grad_query_rows = grad_q_seq.reshape(tok_rows, width)
-    grad_key_rows = grad_k_seq.reshape(tok_rows, width)
-    grad_value_rows = grad_v_seq.reshape(tok_rows, width)
+    grad_query_rows, grad_key_rows, grad_value_rows, near_grad, far_grad = attend_back(
+        query_rows, key_rows, value_rows, segments, base, context, grad_context, lse
+    )
     query_grad = outer_sum(normed_one, grad_query_rows)
     key_grad = outer_sum(normed_one, grad_key_rows)
     value_grad = outer_sum(normed_one, grad_value_rows)
@@ -352,7 +435,7 @@
         + scale_one * scaled_one
         - inputs * scale_one**3 * jnp.mean(scaled_one * inputs, axis=-1, keepdims=True)
     )
-    table_grad = jnp.sum(table_parts, axis=0).T
+    table_grad = table_back(near_grad, far_grad, table_full.shape[0])
     shares = (
         lax.psum_scatter(gain_one_grad, "grp", scatter_dimension=0, tiled=True),
         lax.psum_scatter(query_grad, "grp", scatter_dimension=0, tiled=True),

time: 2040 us -> 1510 us (0.74)
  matrix products: 537 us -> 265 us
  local copies, waits for them, and re-layouts: 398 us -> 183 us
  other arithmetic: 156 us -> 67.9 us
  Pallas kernels: 0 us -> 46 us
  loops' own time: 39.4 us -> 0 us
  waiting for transfers between devices: 515 us -> 548 us
    dot_general x20 -> x2, matrix products: 279 us -> 1.8 us  [the longest x1 1.59 us: table_back(): lax.dot_general(hot, dnear.reshape(heads, 8 * SPAN), (((1,), (1,)), ((),...]
    while x82 -> x0, local copies, waits for them, and re-layouts: 215 us -> none
    convert_element_type x4 -> x1, other arithmetic: 47 us -> 0.01 us  [bias_base(): last = table[buckets - 1].astype(f32)]
    pallas_call x0 -> x2, Pallas kernels: none -> 46 us  [the longest x1 25.9 us: attend_back(): pl.pallas_call(bwd_kernel, grid=(pairs,), in_specs=[band, whole(seq, 1),...]
    another operation x2 -> x0, loops' own time: 39.4 us -> none  [the longest x1 33.4 us: backward_seq(): lax.scan(block_step, start_carry, jnp.arange(block_count, dtype=jnp.int32))]
    reduce_scatter x1, waiting for transfers between devices: 0.02 us -> 37.9 us  [shards(): lax.psum_scatter(output_grad, 'grp', scatter_dimension=0, tiled=True)]
    reduce_sum x2, other arithmetic: 21.8 us -> 0.1 us  [table_back(): jnp.sum(dfar.reshape(heads // 2, 8, 2, QB), axis=(1, 3)).reshape(1, heads)]
    unnamed x170 -> x173, local copies, waits for them, and re-layouts: 44.6 us -> 40.9 us
  transfers between devices with their start and end apart: 16 -> 16, of which waited for: 9 -> 10; matrix products, arithmetic and copies ran while one was open for 48% -> 26% of each run, Pallas kernels for 0% -> 1%
where the time goes in v1:
time: 1510 us; the launch traced here: 1500 us
  waiting for transfers between devices  548 us (36%)
  blocking collectives  350 us (23%)
  matrix products  265 us (18%)
  local copies, waits for them, and re-layouts  183 us (12%)
  other arithmetic  67.9 us (4%)
  Pallas kernels  46 us (3%)
  starting transfers between devices  20.6 us (1%)
  between operations  19.2 us (1%)
    reduce_scatter x1, waiting for transfers between devices, shards(): lax.psum_scatter(up_grad, 'rep', scatter_dimension=1, tiled=True)  175 us
    all_gather x1, blocking collectives, shards(): lax.all_gather(router, 'grp', axis=0, tiled=True)  145 us
    psum x2, blocking collectives, shards(): lax.psum((jnp.sum(choose.astype(jnp.float32), axis=(0, 1)), jnp.sum(route...  133 us
    reduce_scatter x1, waiting for transfers between devices, shards(): lax.psum_scatter(down_grad, 'rep', scatter_dimension=1, tiled=True)  88.5 us
    all_to_all x1, waiting for transfers between devices, shards(): lax.all_to_all(grad_send.reshape(groups, exp_local, capacity, width), 'gr...  70.9 us
    dot_general x1, matrix products, shards(): jnp.einsum('gecd,efd->gecf', grad_received, w_out, preferred_element_type...  56.8 us
    all_to_all x1, waiting for transfers between devices, shards(): lax.all_to_all(expert_out, 'grp', split_axis=0, concat_axis=0, tiled=True)  52.6 us
    unnamed x2, blocking collectives  42.1 us
  transfers between devices with their start and end apart: 16, of which 10 were waited for; matrix products, arithmetic and copies ran while one was open for 26% of the time, Pallas kernels for 1%

profile of v1, /device:TPU:0, one launch (start us, length us, event | category | flops | bytes accessed | tf_op | source)
XLA Modules:
  0.0 1499.6 jit_solution(5824677461544436127)
XLA Ops:
  13.8 13.5 all-gather
  27.5 4.5 reduce-window.6
  35.4 14.1 all-reduce.8
  54.1 5.0 all-gather.9.cloned.1.call-done
  63.1 20.1 %all-gather.7.cloned.1.call-done = bf16[768,768]{1,0:T(8,128)(2,1)} async-done(((bf16[96,768]{1,0:T(8,128)(2,1)}), bf16[768,768]{1,0:T(8,128)(2,1)}) %all-gather.7.cloned.1.call-update) | async-done | bytes 1179664 | tf_op jit(solution)/shard_map/all_gather | solution.py:282
  86.3 20.0 %attend.1 = (bf16[1024,768]{1,0:T(8,128)(2,1)S(1)}, f32[6,8,256]{2,1,0:T(8,128)S(1)}) custom-call(f32[12,8,384]{2,1,0:T(8,128)S(1)} %slice_subtract_fusion.base, s32[1024,1]{1,0:T(8,128)S(1)} %copy.122.seg_col, s32[1,1024]{1,0:T(1,128)S(1)} %bitcast.128, bf16[1024,768]{1,0:T(8,128)(2,1)S(1)} %convolution_convert_fusion.3.q, ...), custom_call_target="tpu_custom_call" | custom-call | flops 3221225472 | bytes 6291456 | tf_op jit(solution)/shard_map/attend/pallas_call | solution.py:119
  117.7 7.5 reshape.381
  125.3 14.0 scatter_custom_fusion
  139.3 4.9 all-to-all-start
  144.2 144.9 %all-gather.1 = bf16[8,96,16]{1,2,0:T(8,128)(2,1)S(1)} all-gather(bf16[1,96,16]{1,2,0:T(8,128)(2,1)S(1)} %bitcast.143), channel_id=1, replica_groups=mesh['rep'=4,'grp'=8] {'grp'}, dimensions={0}, use_global_device_ids=true | all-gather | bytes 27648 | tf_op jit(solution)/shard_map/all_gather | solution.py:288
  297.1 6.7 mul.255
  303.8 8.5 mul.256
  314.0 14.9 scatter_custom_fusion.1
  328.9 4.9 all-to-all-start.2
  333.8 30.1 %fusion.15 = f32[2,8,256,3072]{3,2,1,0:T(8,128)} fusion(bf16[2,768,3072]{2,1,0:T(8,128)(2,1)} %param.25, bf16[8,2,256,768]{3,2,1,0:T(8,128)(2,1)} %all-to-all-done), kind=kOutput, calls=%fused_computation.24 | convolution fusion | flops 19327352832 | bytes 66060288 | tf_op jit(solution)/shard_map/gecd,edf->gecf/dot_general | solution.py:344
  363.9 32.0 %convert_bitcast_fusion.1 = bf16[8,2,256,768]{3,2,0,1:T(8,128)(2,1)} fusion(bf16[2,3072,768]{2,1,0:T(8,128)(2,1)} %param.26, f32[2,8,256,3072]{3,2,1,0:T(8,128)} %fusion.15), kind=kOutput, calls=%fused_computation.36 | convolution fusion | flops 19443744768 | bytes 66060288 | tf_op jit(solution)/shard_map/gecf,efd->gecd/dot_general | solution.py:346
  395.9 6.0 copy.130
  401.9 70.9 %all-to-all-done.2 = bf16[8,2,256,768]{3,2,1,0:T(8,128)(2,1)} async-done(((bf16[8,2,256,768]{3,2,1,0:T(8,128)(2,1)}), bf16[8,2,256,768]{3,2,1,0:T(8,128)(2,1)}, u32[]{:S(2)}, u32[]{:S(2)}) %all-to-all-start.2) | async-done | bytes 6291488 | tf_op jit(solution)/shard_map/all_to_all | solution.py:368
  472.8 5.0 all-to-all-start.1
  477.7 56.8 %fusion.6 = bf16[8,2,256,3072]{3,2,0,1:T(8,128)(2,1)} fusion(f32[2,8,256,3072]{3,2,1,0:T(8,128)} %fusion.15, bf16[2,3072,768]{2,1,0:T(8,128)(2,1)} %param.26, bf16[8,2,256,768]{3,2,1,0:T(8,128)(2,1)} %all-to-all-done.2), kind=kOutput, calls=%fused_computation.12 | convolution fusion | flops 19579011072 | bytes 91226112 | tf_op jit(solution)/shard_map/gecd,efd->gecf/dot_general | solution.py:375
  534.5 26.3 %convert_bitcast_fusion = bf16[8,2,256,768]{3,2,0,1:T(8,128)(2,1)S(1)} fusion(bf16[8,2,256,3072]{3,2,0,1:T(8,128)(2,1)} %fusion.6, bf16[2,768,3072]{2,1,0:T(8,128)(2,1)} %param.25), kind=kOutput, calls=%fused_computation.33 | convolution fusion | flops 19330498560 | bytes 40894464 | tf_op jit(solution)/shard_map/gecf,edf->gecd/dot_general | solution.py:384
  564.1 52.6 %all-to-all-done.1 = bf16[8,2,256,768]{3,2,1,0:T(8,128)(2,1)} async-done(((bf16[8,2,256,768]{3,2,1,0:T(8,128)(2,1)}), bf16[8,2,256,768]{3,2,1,0:T(8,128)(2,1)}, u32[]{:S(2)}, u32[]{:S(2)}) %all-to-all-start.1) | async-done | bytes 6291488 | tf_op jit(solution)/shard_map/all_to_all | solution.py:349
  616.7 4.7 all-to-all-start.3
  621.5 38.7 %gather_fusion = bf16[2048,768]{1,0:T(8,128)(2,1)} fusion(bf16[16,256,768]{2,1,0:T(8,128)(2,1)} %bitcast.17, s32[2048]{0:T(1024)S(1)} %bitcast.130), kind=kCustom, calls=%fused_computation | custom fusion | bytes 6307840 | tf_op jit(solution)/shard_map/gather | solution.py:352
  660.2 7.8 reshape.365
  668.1 17.2 %multiply_reduce_fusion = (f32[1024,2]{1,0:T(8,128)S(1)}, f32[1024,768]{1,0:T(8,128)}) fusion(f32[1024,2,768]{2,1,0:T(2,128)} %reshape.365, f32[1024,768]{1,0:T(8,128)} %copy.134, f32[1024,2]{1,0:T(8,128)S(1)} %copy-done.29), kind=kLoop, calls=%fused_computation.32 | loop fusion | flops 5502976 | bytes 12599296 | tf_op jit(solution)/shard_map/reduce_sum | solution.py:359
  685.7 94.9 %psum.70 = f32[16]{0:T(128)S(1)} all-reduce(f32[16]{0:T(128)S(1)} %get-tuple-element.109), channel_id=1, replica_groups=mesh['rep'=4,'grp'=8] {'rep','grp'}, use_global_device_ids=true, to_apply=%region_12.13 | all-reduce | flops 16 | bytes 128 | tf_op jit(solution)/shard_map/psum | solution.py:322
  781.3 38.7 %gather_fusion.1 = bf16[2048,768]{1,0:T(8,128)(2,1)} fusion(bf16[16,256,768]{2,1,0:T(8,128)(2,1)} %bitcast.24, s32[2048]{0:T(1024)S(1)} %bitcast.131), kind=kCustom, calls=%fused_computation.1 | custom fusion | bytes 6307840 | tf_op jit(solution)/shard_map/gather | solution.py:395
  820.1 7.8 reshape.366
  827.8 11.9 reduce_sum.200
  843.6 6.1 multiply_reduce_fusion.2
  853.4 6.0 multiply_subtract_fusion
  863.6 25.9 %attend_back.1 = (bf16[1024,768]{1,0:T(8,128)(2,1)S(1)}, bf16[1024,768]{1,0:T(8,128)(2,1)S(1)}, bf16[1024,768]{1,0:T(8,128)(2,1)S(1)}, f32[12,8,384]{2,1,0:T(8,128)S(1)}, f32[6,8,256]{2,1,0:T(8,128)S(1)}) custom-call(f32[12,8,384]{2,1,0:T(8,128)S(1)} %copy-done.3, s32[1024,1]{1,0:T(8,128)S(1)} %copy-done.1, s32[1,1024]{1,0:T(1,128)S(1)} %bitcast.129, ...), custom_call_target="tpu_custom_call" | custom-call | flops 8053063680 | bytes 12582912 | tf_op jit(solution)/shard_map/attend_back/pallas_call | solution.py:209
  894.8 4.7 fusion.59
  899.6 4.3 fusion.57
  904.3 4.8 fusion.43
  912.1 19.1 %reduce-scatter.10.cloned.1.call-done = f32[96,768]{1,0:T(8,128)} async-done(((f32[768,768]{1,0:T(8,128)}), f32[96,768]{1,0:T(8,128)}) %reduce-scatter.10.cloned.1.call-update) | async-done | bytes 294928 | tf_op jit(solution)/shard_map/reduce_scatter | solution.py:441
  931.2 38.4 %reduce-scatter.12.cloned.1.call-done = f32[96,768]{1,0:T(8,128)} async-done(((f32[768,768]{1,0:T(8,128)}), f32[96,768]{1,0:T(8,128)}) %reduce-scatter.12.cloned.1.call-update) | async-done | bytes 294928 | tf_op jit(solution)/shard_map/reduce_scatter | solution.py:442
  969.6 37.9 %reduce-scatter.14.cloned.1.call-done = f32[96,768]{1,0:T(8,128)} async-done(((f32[768,768]{1,0:T(8,128)}), f32[96,768]{1,0:T(8,128)}) %reduce-scatter.14.cloned.1.call-update) | async-done | bytes 294928 | tf_op jit(solution)/shard_map/reduce_scatter | solution.py:443
  1007.5 37.9 %reduce-scatter.16.cloned.1.call-done = f32[96,768]{1,0:T(8,128)} async-done(((f32[768,768]{1,0:T(8,128)}), f32[96,768]{1,0:T(8,128)}) %reduce-scatter.16.cloned.1.call-update) | async-done | bytes 294928 | tf_op jit(solution)/shard_map/reduce_scatter | solution.py:444
  1045.4 39.8 %convolution_bitcast_fusion = f32[2,3072,768]{2,1,0:T(8,128)} fusion(bf16[8,2,256,768]{3,2,1,0:T(8,128)(2,1)} %all-to-all-done.2, f32[2,8,256,3072]{3,2,1,0:T(8,128)} %fusion.15), kind=kOutput, calls=%fused_computation.29 | convolution fusion | flops 19440599040 | bytes 75497472 | tf_op jit(solution)/shard_map/gecf,gecd->efd/dot_general | solution.py:378
  1085.5 28.0 %fusion.20 = f32[2,768,3072]{2,1,0:T(8,128)} fusion(bf16[8,2,256,768]{3,2,1,0:T(8,128)(2,1)} %all-to-all-done, bf16[8,2,256,3072]{3,2,0,1:T(8,128)(2,1)} %fusion.6), kind=kOutput, calls=%fused_computation.30 | convolution fusion | flops 19327352832 | bytes 50331648 | tf_op jit(solution)/shard_map/gecd,gecf->edf/dot_general | solution.py:383
  1115.4 38.1 %psum.71 = f32[16]{0:T(128)} all-reduce(f32[16]{0:T(128)S(1)} %get-tuple-element.107), channel_id=1, replica_groups=mesh['rep'=4,'grp'=8] {'rep','grp'}, use_global_device_ids=true, to_apply=%region_14.15 | all-reduce | flops 16 | bytes 128 | tf_op jit(solution)/shard_map/psum | solution.py:322
  1163.7 28.0 %all-reduce.5 = (f32[768]{0:T(1024)S(1)}, f32[32,12]{1,0:T(8,128)S(1)}, f32[768]{0:T(1024)S(1)}) all-reduce(f32[768]{0:T(1024)S(1)} %get-tuple-element.102, f32[32,12]{1,0:T(8,128)S(1)} %copy-done.55, f32[768]{0:T(1024)S(1)} %copy-done.62), channel_id=2, replica_groups=mesh['rep'=4,'grp'=8] {'grp'}, use_global_device_ids=true, to_apply=%region_25.26.clone | all-reduce | flops 1920 | bytes 15360
  1191.9 5.6 fusion.36
  1205.4 16.1 %all-reduce.6 = (f32[96]{0:T(128)}, f32[4,12]{1,0:T(4,128)}, f32[96]{0:T(128)}, f32[96,16]{0,1:T(8,128)}) all-reduce(f32[96]{0:T(128)S(1)} %dynamic-slice.3, f32[4,12]{1,0:T(4,128)S(1)} %constant_dynamic-slice_fusion, f32[96]{0:T(128)S(1)} %dynamic-slice.7, f32[96,16]{0,1:T(8,128)S(1)} %copy.161), channel_id=1, replica_groups=mesh['rep'=4,'grp'=8] {'rep'}, use_global_device_ids=true, to_apply=%region_26.27 | all-reduce | flops 1776 | bytes 14208 | tf_op jit(solution)/shard_map/psum | solution.py:449
  1221.5 88.5 %reduce-scatter.20.cloned.1.call-done = f32[2,768,768]{2,1,0:T(8,128)} async-done(((f32[2,3072,768]{2,1,0:T(8,128)}), f32[2,768,768]{2,1,0:T(8,128)}) %reduce-scatter.20.cloned.1.call-update) | async-done | bytes 4718608 | tf_op jit(solution)/shard_map/reduce_scatter | solution.py:389
  1309.9 174.7 %reduce-scatter.18.cloned.1.call-done = f32[2,192,3072]{2,1,0:T(8,128)} async-done(((f32[2,768,3072]{2,1,0:T(8,128)}), f32[2,192,3072]{2,1,0:T(8,128)}) %reduce-scatter.18.cloned.1.call-update) | async-done | bytes 4718608 | tf_op jit(solution)/shard_map/reduce_scatter | solution.py:388
  (270 shorter events, 91.3 us)
Async XLA Ops:
  7.2 42.9 %all-gather.11.cloned.1.call-start = ((), (), s32[]{:S(2)}) async-start(), calls=%async_computation.13 | async-start | bytes 1327104 | tf_op jit(solution)/shard_map/all_gather | solution.py:284
  7.9 51.2 %all-gather.9.cloned.1.call-start = ((), (), s32[]{:S(2)}) async-start(), calls=%async_computation.12 | async-start | bytes 1327104 | tf_op jit(solution)/shard_map/all_gather | solution.py:283
  8.7 74.6 %all-gather.7.cloned.1.call-start = ((), (), s32[]{:S(2)}) async-start(), calls=%async_computation.11 | async-start | bytes 1327104 | tf_op jit(solution)/shard_map/all_gather | solution.py:282
  9.4 98.1 %all-gather.13.cloned.1.call-start = ((), (), s32[]{:S(2)}) async-start(), calls=%async_computation.14 | async-start | bytes 1327104 | tf_op jit(solution)/shard_map/all_gather | solution.py:285
  11.8 21.7 %copy-start.67 = (s32[2]{0:T(128)S(1)}, s32[2]{0:T(128)}, u32[]{:S(2)}) copy-start(s32[2]{0:T(128)} %constant.110) | copy-start | bytes 28
  11.8 21.8 %copy-start.64 = (u32[32]{0:T(128)S(1)}, u32[32]{0:T(128)}, u32[]{:S(2)}) copy-start(u32[32]{0:T(128)} %constant.153) | copy-start | bytes 388
  11.8 23.1 %copy-start.73 = (bf16[96]{0:T(256)(128)(2,1)S(1)}, bf16[96]{0:T(256)(128)(2,1)}, u32[]{:S(2)}) copy-start(bf16[96]{0:T(256)(128)(2,1)} %param.17) | copy-start | bytes 580
  11.8 23.3 %copy-start.74 = (bf16[96]{0:T(256)(128)(2,1)S(1)}, bf16[96]{0:T(256)(128)(2,1)}, u32[]{:S(2)}) copy-start(bf16[96]{0:T(256)(128)(2,1)} %param.23) | copy-start | bytes 580
  11.8 37.7 %copy-start.4 = (s32[1024]{0:T(1024)S(1)}, s32[1024]{0:T(1024)}, u32[]{:S(2)}) copy-start(s32[1024]{0:T(1024)} %param.15) | copy-start | bytes 12292
  11.9 38.0 %copy-start.66 = (s32[2]{0:T(128)S(1)}, s32[2]{0:T(128)}, u32[]{:S(2)}) copy-start(s32[2]{0:T(128)} %constant.113) | copy-start | bytes 28
  12.6 70.6 %copy-start.19 = (bf16[1024,768]{0,1:T(8,128)(2,1)}, bf16[1024,768]{0,1:T(8,128)(2,1)S(1)}, u32[]{:S(2)}) copy-start(bf16[1024,768]{0,1:T(8,128)(2,1)S(1)} %copy.121) | copy-start | bytes 4718596
  13.8 69.5 %copy-start.36 = (f32[1024]{0:T(1024)}, f32[1024]{0:T(1024)S(1)}, u32[]{:S(2)}) copy-start(f32[1024]{0:T(1024)S(1)} %get-tuple-element.131) | copy-start | bytes 12292
  49.5 33.7 %copy-start.48 = (f32[768]{0:T(1024)}, f32[768]{0:T(1024)S(1)}, u32[]{:S(2)}) copy-start(f32[768]{0:T(1024)S(1)} %convert_element_type.274) | copy-start | bytes 9220
  49.8 36.5 %copy-start = (s32[1024,1]{1,0:T(8,128)}, s32[1024,1]{1,0:T(8,128)S(1)}, u32[]{:S(2)}) copy-start(s32[1024,1]{1,0:T(8,128)S(1)} %copy.122.seg_col) | copy-start | bytes 12292
  49.8 62.3 %copy-start.51 = (f32[768]{0:T(1024)}, f32[768]{0:T(1024)S(1)}, u32[]{:S(2)}) copy-start(f32[768]{0:T(1024)S(1)} %convert_element_type.279) | copy-start | bytes 9220
  50.0 36.2 %copy-start.2 = (f32[12,8,384]{2,1,0:T(8,128)}, f32[12,8,384]{2,1,0:T(8,128)S(1)}, u32[]{:S(2)}) copy-start(f32[12,8,384]{2,1,0:T(8,128)S(1)} %slice_subtract_fusion.base) | copy-start | bytes 442372
  113.4 198.9 %copy-start.23 = (bf16[1024,768]{0,1:T(8,128)(2,1)}, bf16[1024,768]{0,1:T(8,128)(2,1)S(1)}, u32[]{:S(2)}) copy-start(bf16[1024,768]{0,1:T(8,128)(2,1)S(1)} %multiply_convert_fusion.2) | copy-start | bytes 4718596
  139.3 189.6 %all-to-all-start = ((bf16[8,2,256,768]{3,2,1,0:T(8,128)(2,1)}), bf16[8,2,256,768]{3,2,1,0:T(8,128)(2,1)}, u32[]{:S(2)}, u32[]{:S(2)}) async-start(bf16[8,2,256,768]{3,2,1,0:T(8,128)(2,1)} %bitcast.132), calls=%async_computation | async-start | bytes 12582912 | tf_op jit(solution)/shard_map/all_to_all | solution.py:337
  289.2 23.2 %copy-start.34 = (bf16[768,16]{0,1:T(8,128)(2,1)}, bf16[768,16]{0,1:T(8,128)(2,1)S(1)}, u32[]{:S(2)}) copy-start(bf16[768,16]{0,1:T(8,128)(2,1)S(1)} %reshape.400) | copy-start | bytes 73732
  312.7 16.2 %copy-start.30 = (f32[1024,16]{0,1:T(8,128)}, f32[1024,16]{0,1:T(8,128)S(1)}, u32[]{:S(2)}) copy-start(f32[1024,16]{0,1:T(8,128)S(1)} %get-tuple-element.139) | copy-start | bytes 196612
  312.7 16.2 %copy-start.40 = (f32[1024]{0:T(1024)}, f32[1024]{0:T(1024)S(1)}, u32[]{:S(2)}) copy-start(f32[1024]{0:T(1024)S(1)} %get-tuple-element.138) | copy-start | bytes 12292
  313.4 15.4 %copy-start.44 = (f32[1024,2]{0,1:T(2,128)}, f32[1024,2]{0,1:T(2,128)S(1)}, u32[]{:S(2)}) copy-start(f32[1024,2]{0,1:T(2,128)S(1)} %get-tuple-element.105) | copy-start | bytes 24580
  313.4 15.4 %copy-start.56 = (f32[1024]{0:T(1024)}, f32[1024]{0:T(1024)S(1)}, u32[]{:S(2)}) copy-start(f32[1024]{0:T(1024)S(1)} %get-tuple-element.104) | copy-start | bytes 12292
  313.7 15.2 %copy-start.28 = (f32[1024,2]{1,0:T(8,128)}, f32[1024,2]{1,0:T(8,128)S(1)}, u32[]{:S(2)}) copy-start(f32[1024,2]{1,0:T(8,128)S(1)} %copy.124) | copy-start | bytes 24580
  328.9 143.9 %all-to-all-start.2 = ((bf16[8,2,256,768]{3,2,1,0:T(8,128)(2,1)}), bf16[8,2,256,768]{3,2,1,0:T(8,128)(2,1)}, u32[]{:S(2)}, u32[]{:S(2)}) async-start(bf16[8,2,256,768]{3,2,1,0:T(8,128)(2,1)} %bitcast.133), calls=%async_computation.2 | async-start | bytes 12582912 | tf_op jit(solution)/shard_map/all_to_all | solution.py:368
  472.8 143.9 %all-to-all-start.1 = ((bf16[8,2,256,768]{3,2,1,0:T(8,128)(2,1)}), bf16[8,2,256,768]{3,2,1,0:T(8,128)(2,1)}, u32[]{:S(2)}, u32[]{:S(2)}) async-start(bf16[8,2,256,768]{3,2,1,0:T(8,128)(2,1)} %copy.130), calls=%async_computation.1 | async-start | bytes 12582912 | tf_op jit(solution)/shard_map/all_to_all | solution.py:349
  564.1 57.4 %copy-start.18 = (s32[2048,1]{0,1:T(1,128)S(1)}, s32[2048,1]{0,1:T(1,128)}, u32[]{:S(2)}) copy-start(s32[2048,1]{0,1:T(1,128)} %get-tuple-element.127) | copy-start | bytes 24580
  616.7 164.6 %all-to-all-start.3 = ((bf16[8,2,256,768]{3,2,1,0:T(8,128)(2,1)}), bf16[8,2,256,768]{3,2,1,0:T(8,128)(2,1)}, u32[]{:S(2)}, u32[]{:S(2)}) async-start(bf16[8,2,256,768]{3,2,1,0:T(8,128)(2,1)} %copy.136), calls=%async_computation.3 | async-start | bytes 12582912 | tf_op jit(solution)/shard_map/all_to_all | solution.py:391
  621.4 309.7 %reduce-scatter.10.cloned.1.call-start = ((), (), s32[]{:S(2)}) async-start(), calls=%async_computation.15 | async-start | bytes 2654208 | tf_op jit(solution)/shard_map/reduce_scatter | solution.py:441
  668.1 17.4 %copy-start.45 = (f32[1024,2]{0,1:T(2,128)S(1)}, f32[1024,2]{0,1:T(2,128)}, u32[]{:S(2)}) copy-start(f32[1024,2]{0,1:T(2,128)} %copy-done.44) | copy-start | bytes 24580
  668.1 17.4 %copy-start.57 = (f32[1024]{0:T(1024)S(1)}, f32[1024]{0:T(1024)}, u32[]{:S(2)}) copy-start(f32[1024]{0:T(1024)} %copy-done.56) | copy-start | bytes 12292
  668.1 17.5 %copy-start.43 = (s32[1024,2]{0,1:T(2,128)S(1)}, s32[1024,2]{0,1:T(2,128)}, u32[]{:S(2)}) copy-start(s32[1024,2]{0,1:T(2,128)} %param.16) | copy-start | bytes 24580
  668.1 113.0 %copy-start.31 = (f32[1024,16]{0,1:T(8,128)S(1)}, f32[1024,16]{0,1:T(8,128)}, u32[]{:S(2)}) copy-start(f32[1024,16]{0,1:T(8,128)} %copy-done.30) | copy-start | bytes 196612
  668.1 113.0 %copy-start.41 = (f32[1024]{0:T(1024)S(1)}, f32[1024]{0:T(1024)}, u32[]{:S(2)}) copy-start(f32[1024]{0:T(1024)} %copy-done.40) | copy-start | bytes 12292
  668.1 113.0 %copy-start.54 = (f32[1024]{0:T(1024)S(1)}, f32[1024]{0:T(1024)}, u32[]{:S(2)}) copy-start(f32[1024]{0:T(1024)} %copy-done.53) | copy-start | bytes 12292
  863.6 28.3 %copy-start.20 = (bf16[1024,768]{0,1:T(8,128)(2,1)S(1)}, bf16[1024,768]{0,1:T(8,128)(2,1)}, u32[]{:S(2)}) copy-start(bf16[1024,768]{0,1:T(8,128)(2,1)} %copy-done.19) | copy-start | bytes 4718596
  863.6 28.3 %copy-start.37 = (f32[1024]{0:T(1024)S(1)}, f32[1024]{0:T(1024)}, u32[]{:S(2)}) copy-start(f32[1024]{0:T(1024)} %copy-done.36) | copy-start | bytes 12292
  863.6 28.3 %copy-start.49 = (f32[768]{0:T(1024)S(1)}, f32[768]{0:T(1024)}, u32[]{:S(2)}) copy-start(f32[768]{0:T(1024)} %copy-done.48) | copy-start | bytes 9220
  894.7 74.8 %reduce-scatter.12.cloned.1.call-start = ((), (), s32[]{:S(2)}) async-start(), calls=%async_computation.16 | async-start | bytes 2654208 | tf_op jit(solution)/shard_map/reduce_scatter | solution.py:442
  899.5 107.9 %reduce-scatter.14.cloned.1.call-start = ((), (), s32[]{:S(2)}) async-start(), calls=%async_computation.17 | async-start | bytes 2654208 | tf_op jit(solution)/shard_map/reduce_scatter | solution.py:443
  903.9 141.5 %reduce-scatter.16.cloned.1.call-start = ((), (), s32[]{:S(2)}) async-start(), calls=%async_computation.18 | async-start | bytes 2654208 | tf_op jit(solution)/shard_map/reduce_scatter | solution.py:444
  909.2 295.3 %reduce-scatter.22.cloned.1.call-start = ((), (), s32[]{:S(2)}) async-start(), calls=%async_computation.21 | async-start | bytes 442368
  912.0 309.5 %all-reduce.11.cloned.1.call-start = ((), (), s32[]{:S(2)}) async-start(), calls=%async_computation.22 | async-start | bytes 2359296 | tf_op jit(solution)/shard_map/psum | solution.py:449
  1045.4 264.6 %reduce-scatter.20.cloned.1.call-start = ((), (), s32[]{:S(2)}) async-start(), calls=%async_computation.20 | async-start | bytes 23592960 | tf_op jit(solution)/shard_map/reduce_scatter | solution.py:389
  1085.3 399.4 %reduce-scatter.18.cloned.1.call-start = ((), (), s32[]{:S(2)}) async-start(), calls=%async_computation.19 | async-start | bytes 23592960 | tf_op jit(solution)/shard_map/reduce_scatter | solution.py:388
  1113.4 40.4 %copy-start.39 = (s32[3072]{0:T(1024)S(1)}, s32[3072]{0:T(1024)}, u32[]{:S(2)}) copy-start(s32[3072]{0:T(1024)} %copy-done.38) | copy-start | bytes 36868
  1113.4 41.9 %copy-start.11 = (bf16[1024,768]{1,0:T(8,128)(2,1)S(1)}, bf16[1024,768]{1,0:T(8,128)(2,1)}, u32[]{:S(2)}) copy-start(bf16[1024,768]{1,0:T(8,128)(2,1)} %copy-done.10) | copy-start | bytes 4718596
  1160.1 31.8 %copy-start.60 = (f32[1024]{0:T(1024)S(1)}, f32[1024]{0:T(1024)}, u32[]{:S(2)}) copy-start(f32[1024]{0:T(1024)} %get-tuple-element.130) | copy-start | bytes 12292
  (43 other events, 147.2 us)
Sparse Core Ops, SparseCore 0:
  9.7 25.3 all-gather.10
  36.7 22.3 all-gather.8
  60.8 22.4 all-gather.6
  84.7 22.4 all-gather.12
  894.8 36.2 reduce-scatter.9
  933.9 35.5 reduce-scatter.11
  971.9 35.5 reduce-scatter.13
  1009.8 35.5 reduce-scatter.15
  1047.6 29.9 reduce-scatter.21
  1081.0 53.3 all-reduce.10
  1138.1 171.7 reduce-scatter.19
  1313.8 170.8 reduce-scatter.17

commit v2 on v1

--- a/solution.py
+++ b/solution.py
@@ -249,6 +249,346 @@
     return grad + jnp.where(last, far, 0.0)
 
 
+def gelu_and_slope(u):
+    root = (2.0 / jnp.pi) ** 0.5
+    square = u * u
+    bent = jnp.tanh(u * (root + (root * 0.044715) * square))
+    rise = 0.5 + 0.5 * bent
+    slope = rise + (0.5 * u) * (1.0 - bent * bent) * (root + (root * 3 * 0.044715) * square)
+    return u * rise, slope
+
+
+def expert_kernel(first, n_a, n_b, g_a, g_b, info, router_t, w_in, w_out, *rest):
+    (y_a, y_b, r_a, r_b, act_out, dpre_out, x_out, dy_out,
+     hot, x_s, g_s, dy_s, gate_s, y_sum, d_sum, y_all, d_all, dgate_c) = rest[-18:]
+    e, f = pl.program_id(0), pl.program_id(1)
+    rows, width = n_a.shape
+    cap = x_s.shape[0] // 2
+    expert = first[0] + e
+    sources = ((n_a, g_a), (n_b, g_b))
+
+    @pl.when((e == 0) & (f == 0))
+    def _():
+        dgate_c[...] = jnp.zeros_like(dgate_c)
+
+    @pl.when(f == 0)
+    def _():
+        for s, (n_ref, g_ref) in enumerate(sources):
+            logits = lax.dot_general(router_t[...], n_ref[...], (((1,), (1,)), ((), ())), preferred_element_type=f32)
+            ids = lax.broadcasted_iota(jnp.int32, logits.shape, 0)
+            power = jnp.exp(logits - jnp.max(logits, axis=0, keepdims=True))
+            prob = power / jnp.sum(power, axis=0, keepdims=True)
+            chosen = (ids == info[4 * s + 2:4 * s + 3, :]) | (ids == info[4 * s + 3:4 * s + 4, :])
+            both = jnp.sum(jnp.where(chosen, prob, 0.0), axis=0, keepdims=True)
+            gate_row = jnp.sum(jnp.where(ids == expert, prob, 0.0), axis=0, keepdims=True) / both
+            slot_row = jnp.where(e == 0, info[4 * s:4 * s + 1, :], info[4 * s + 1:4 * s + 2, :])
+            match = slot_row == lax.broadcasted_iota(jnp.int32, (cap, rows), 0)
+            one_hot = jnp.where(match, 1.0, 0.0).astype(bf16)
+            part = slice(s * cap, (s + 1) * cap)
+            gate_s[part, :] = jnp.sum(jnp.where(match, gate_row, 0.0), axis=1, keepdims=True)
+            hot[s, pl.ds(pl.multiple_of(e * cap, cap), cap), :] = one_hot
+            x_s[part, :] = jnp.dot(one_hot, n_ref[...], preferred_element_type=f32).astype(bf16)
+            g_rows = jnp.dot(one_hot, g_ref[...], preferred_element_type=f32)
+            g_s[part, :] = g_rows.astype(bf16)
+            dy_s[part, :] = (gate_s[part, :] * g_rows).astype(bf16)
+        x_out[0] = x_s[...]
+        dy_out[0] = dy_s[...]
+
+    pre = jnp.dot(x_s[...], w_in[0], preferred_element_type=f32)
+    act, slope = gelu_and_slope(pre)
+    act = act.astype(bf16)
+    act_out[0] = act
+    dact = lax.dot_general(dy_s[...], w_out[0], (((1,), (1,)), ((), ())), preferred_element_type=f32)
+    dpre = (dact * slope).astype(bf16)
+    dpre_out[0] = dpre
+    y_part = jnp.dot(act, w_out[0], preferred_element_type=f32)
+    d_part = lax.dot_general(dpre, w_in[0], (((1,), (1,)), ((), ())), preferred_element_type=f32)
+
+    @pl.when(f == 0)
+    def _():
+        y_sum[...] = y_part
+        d_sum[...] = d_part
+
+    @pl.when(f != 0)
+    def _():
+        y_sum[...] += y_part
+        d_sum[...] += d_part
+
+    @pl.when(f == pl.num_programs(1) - 1)
+    def _():
+        y_rows = y_sum[...].astype(bf16).astype(f32)
+        dgate = jnp.sum(y_rows * g_s[...].astype(f32), axis=1, keepdims=True)
+        y_rows = (gate_s[...] * y_rows).astype(bf16)
+        d_rows = d_sum[...].astype(bf16)
+        for s in range(2):
+            part = slice(s * cap, (s + 1) * cap)
+            here = pl.ds(pl.multiple_of(e * cap, cap), cap)
+            y_all[s, here, :] = y_rows[part]
+            d_all[s, here, :] = d_rows[part]
+            slot_row = jnp.where(e == 0, info[4 * s:4 * s + 1, :], info[4 * s + 1:4 * s + 2, :])
+            match = slot_row == lax.broadcasted_iota(jnp.int32, (cap, rows), 0)
+            row = jnp.sum(jnp.where(match, dgate[part], 0.0), axis=0, keepdims=True)
+            for c in range(TOP):
+                routed = info[4 * s + 2 + c:4 * s + 3 + c, :] == expert
+                dgate_c[TOP * s + c:TOP * s + c + 1, :] += jnp.where(routed, row, 0.0)
+
+    @pl.when((e == pl.num_programs(0) - 1) & (f == pl.num_programs(1) - 1))
+    def _():
+        turn = (((0,), (0,)), ((), ()))
+        for s, (y_ref, r_ref) in enumerate(((y_a, r_a), (y_b, r_b))):
+            y_ref[...] = lax.dot_general(hot[s], y_all[s], turn, preferred_element_type=f32).astype(bf16)
+            r_ref[0:rows, :] = lax.dot_general(hot[s], d_all[s], turn, preferred_element_type=f32).astype(bf16)
+            value = dgate_c[TOP * s:TOP * s + TOP, :]
+            high = value.astype(bf16)
+            value = value - high.astype(f32)
+            middle = value.astype(bf16)
+            low = (value - middle.astype(f32)).astype(bf16)
+            pieces = jnp.concatenate([high.astype(f32), middle.astype(f32), low.astype(f32), jnp.zeros((2, rows), f32)], axis=0)
+            over = jnp.concatenate([pieces[:, width:], jnp.zeros((8, 2 * width - rows), f32)], axis=1)
+            r_ref[rows:rows + 16, :] = jnp.concatenate([pieces[:, 0:width], over], axis=0).astype(bf16)
+
+
+def unpack_dgate(tail, rows):
+    tail = tail.astype(f32)
+    pieces = jnp.concatenate([tail[0:8], tail[8:16]], axis=1)[:, 0:rows]
+    return pieces[0:2] + pieces[2:4] + pieces[4:6]
+
+
+def expert_block(k, blocks, first, n_a, n_b, g_a, g_b, info, router_t, w_in, w_out, cap, kept):
+    rows, width = n_a.shape
+    local, _, hidden = w_in.shape
+    part = 768 if hidden % 768 == 0 else hidden
+    once = pl.Buffered(1)
+    whole = lambda *shape: pl.BlockSpec(shape, lambda e, f: (0,) * len(shape), pipeline_mode=once)
+    wide = pl.BlockSpec((1, 2 * cap, part), lambda e, f: (e, k, f))
+    slim = pl.BlockSpec((1, 2 * cap, width), lambda e, f: (e, k, 0))
+    slots = blocks * 2 * cap
+    shapes = [
+        jax.ShapeDtypeStruct((rows, width), bf16), jax.ShapeDtypeStruct((rows, width), bf16),
+        jax.ShapeDtypeStruct((rows + 16, width), bf16), jax.ShapeDtypeStruct((rows + 16, width), bf16),
+        jax.ShapeDtypeStruct((local, slots, hidden), bf16), jax.ShapeDtypeStruct((local, slots, hidden), bf16),
+        jax.ShapeDtypeStruct((local, slots, width), bf16), jax.ShapeDtypeStruct((local, slots, width), bf16),
+    ]
+    in_specs = [
+        pl.BlockSpec(memory_space=pltpu.SMEM), whole(rows, width), whole(rows, width), whole(rows, width), whole(rows, width),
+        whole(8, rows), whole(*router_t.shape),
+        pl.BlockSpec((1, width, part), lambda e, f: (e, 0, f)), pl.BlockSpec((1, part, width), lambda e, f: (e, f, 0)),
+    ]
+    args = [first, n_a, n_b, g_a, g_b, info, router_t, w_in, w_out]
+    alias = {}
+    if kept is not None:
+        alias = {len(args) + i: 4 + i for i in range(4)}
+        in_specs += [pl.BlockSpec(memory_space=pl.ANY)] * 4
+        args += list(kept)
+    out = pl.pallas_call(
+        expert_kernel,
+        grid=(local, hidden // part),
+        in_specs=in_specs,
+        out_specs=[whole(rows, width), whole(rows, width), whole(rows + 16, width), whole(rows + 16, width), wide, wide, slim, slim],
+        out_shape=shapes,
+        scratch_shapes=[
+            pltpu.VMEM((2, local * cap, rows), bf16),
+            pltpu.VMEM((2 * cap, width), bf16), pltpu.VMEM((2 * cap, width), bf16), pltpu.VMEM((2 * cap, width), bf16),
+            pltpu.VMEM((2 * cap, 1), f32),
+            pltpu.VMEM((2 * cap, width), f32), pltpu.VMEM((2 * cap, width), f32),
+            pltpu.VMEM((2, local * cap, width), bf16), pltpu.VMEM((2, local * cap, width), bf16),
+            pltpu.VMEM((8, rows), f32),
+        ],
+        input_output_aliases=alias,
+        compiler_params=pltpu.CompilerParams(vmem_limit_bytes=48 * 1024 * 1024),
+        cost_estimate=pl.CostEstimate(flops=2 * local * cap * (8 * width * hidden + 8 * width * rows), bytes_accessed=60 * 1024 * 1024, transcendentals=2 * local * cap * hidden),
+        name="expert_block",
+    )(*args)
+    return out[:4], out[4:]
+
+
+def chip_ring(chips):
+    return [0] + list(range(1, chips, 2)) + [z for z in range(chips - 1, 0, -1) if z % 2 == 0]
+
+
+class Group:
+    def __init__(self):
+        self.size = lax.axis_size("grp")
+        self.chips = self.size // 2
+        self.order = chip_ring(self.chips)
+        me = lax.axis_index("grp")
+        self.me, self.chip, self.core = me, me // 2, me % 2
+
+    def onward(self, x):
+        pairs = []
+        for i, z in enumerate(self.order):
+            after = self.order[(i + 1) % self.chips]
+            pairs += [(2 * z, 2 * after), (2 * z + 1, 2 * after + 1)]
+        return lax.ppermute(x, "grp", pairs)
+
+    def swap(self, x):
+        return lax.ppermute(x, "grp", [(i, i ^ 1) for i in range(self.size)])
+
+    def source_chip(self, k):
+        table = [0] * self.chips
+        for i, z in enumerate(self.order):
+            table[z] = self.order[(i - k) % self.chips]
+        return jnp.asarray(table, jnp.int32)[self.chip]
+
+
+def pick_constant(table, index):
+    value = jnp.int32(table[0])
+    for i in range(1, len(table)):
+        value = jnp.where(index == i, jnp.int32(table[i]), value)
+    return value
+
+
+def gather_kernel(chips, reps, *refs):
+    count = 5
+    shard, tally = refs[:count], refs[count]
+    full, tally_all = refs[count + 1:2 * count + 1], refs[2 * count + 1]
+    own_sem, ring_send, ring_recv, core_send, core_recv, rep_send, rep_recv, tally_in, tally_sum, tally_vmem = refs[2 * count + 2:]
+    order = chip_ring(chips)
+    rep, me = lax.axis_index("rep"), lax.axis_index("grp")
+    chip, core = me // 2, me % 2
+    after, before = [0] * chips, [0] * chips
+    for i, z in enumerate(order):
+        after[z], before[z] = order[(i + 1) % chips], order[(i - 1) % chips]
+    after = 2 * pick_constant(after, chip) + core
+    before = 2 * pick_constant(before, chip) + core
+    sibling = 2 * chip + 1 - core
+    mesh_id = pl.DeviceIdType.MESH
+
+    barrier = pltpu.get_barrier_semaphore()
+    peers = [(rep, after), (rep, before), (rep, sibling)]
+    peers += [(lax.rem(rep + k, reps), me) for k in range(1, reps)]
+    for peer in peers:
+        pl.semaphore_signal(barrier, inc=1, device_id=peer, device_id_type=mesh_id)
+    pl.semaphore_wait(barrier, len(peers))
+
+    def place(a, owner):
+        if a == count:
+            return tally_all.at[owner]
+        rows = shard[a].shape[0]
+        return full[a].at[pl.ds(pl.multiple_of(owner * rows, rows), rows), :]
+
+    def remote(src, dst, send, recv, target):
+        return pltpu.make_async_remote_copy(
+            src_ref=src, dst_ref=dst, send_sem=send, recv_sem=recv, device_id=target, device_id_type=mesh_id
+        )
+
+    tallies = [
+        remote(tally, tally_in.at[k - 1], rep_send.at[k - 1], rep_recv.at[k - 1], (lax.rem(rep + k, reps), me))
+        for k in range(1, reps)
+    ]
+    for copy in tallies:
+        copy.start()
+    own_tally = pltpu.make_async_copy(tally, tally_vmem, own_sem.at[count])
+    own_tally.start()
+
+    pending = []
+    moved = [None] * (count + 1)
+    own = []
+    for a in range(count):
+        keep = pltpu.make_async_copy(shard[a], place(a, me), own_sem.at[a])
+        keep.start()
+        own.append(keep)
+        ring = remote(shard[a], place(a, me), ring_send.at[0, a], ring_recv.at[0, a], (rep, after))
+        ring.start()
+        across = remote(shard[a], place(a, me), core_send.at[0, a], core_recv.at[0, a], (rep, sibling))
+        across.start()
+        moved[a] = ring
+        pending += [ring, across]
+
+    own_tally.wait()
+    total = tally_vmem[...]
+    for k, copy in enumerate(tallies):
+        copy.wait_recv()
+        total = total + tally_in[k]
+    tally_sum[...] = total
+    keep = pltpu.make_async_copy(tally_sum, place(count, me), own_sem.at[count + 1])
+    keep.start()
+    own.append(keep)
+    ring = remote(tally_sum, place(count, me), ring_send.at[0, count], ring_recv.at[0, count], (rep, after))
+    ring.start()
+    across = remote(tally_sum, place(count, me), core_send.at[0, count], core_recv.at[0, count], (rep, sibling))
+    across.start()
+    moved[count] = ring
+    pending += [ring, across]
+
+    for k in range(1, chips):
+        source = [0] * chips
+        for i, z in enumerate(order):
+            source[z] = order[(i - k) % chips]
+        owner = 2 * pick_constant(source, chip) + core
+        for a in range(count + 1):
+            moved[a].wait_recv()
+            block = place(a, owner)
+            if k < chips - 1:
+                ring = remote(block, block, ring_send.at[k, a], ring_recv.at[k, a], (rep, after))
+                ring.start()
+                moved[a] = ring
+                pending.append(ring)
+            across = remote(block, block, core_send.at[k, a], core_recv.at[k, a], (rep, sibling))
+            across.start()
+            pending.append(across)
+    for copy in pending:
+        copy.wait_send()
+    for copy in tallies:
+        copy.wait_send()
+    for keep in own:
+        keep.wait()
+    for k in range(chips):
+        source = [0] * chips
+        for i, z in enumerate(order):
+            source[z] = order[(i - k) % chips]
+        owner = 2 * pick_constant(source, chip) + 1 - core
+        for a in range(count + 1):
+            block = place(a, owner)
+            remote(block, block, core_send.at[k, a], core_recv.at[k, a], (rep, sibling)).wait_recv()
+
+
+def gather_group(arrays, tally):
+    size, reps = lax.axis_size("grp"), lax.axis_size("rep")
+    chips = size // 2
+    count = len(arrays)
+    hbm = pl.BlockSpec(memory_space=pl.ANY)
+    dma = pltpu.SemaphoreType.DMA
+    return pl.pallas_call(
+        partial(gather_kernel, chips, reps),
+        in_specs=[hbm] * (count + 1),
+        out_specs=[hbm] * (count + 1),
+        out_shape=[jax.ShapeDtypeStruct((size * x.shape[0], x.shape[1]), x.dtype) for x in arrays]
+        + [jax.ShapeDtypeStruct((size,) + tally.shape, f32)],
+        scratch_shapes=[
+            dma((count + 2,)), dma((chips, count + 1)), dma((chips, count + 1)), dma((chips, count + 1)), dma((chips, count + 1)),
+            dma((reps,)), dma((reps,)),
+            pltpu.VMEM((reps - 1,) + tally.shape, f32), pltpu.VMEM(tally.shape, f32), pltpu.VMEM(tally.shape, f32),
+        ],
+        compiler_params=pltpu.CompilerParams(collective_id=0, has_side_effects=True),
+        cost_estimate=pl.CostEstimate(flops=0, bytes_accessed=16 * 1024 * 1024, transcendentals=0),
+        name="gather_group",
+    )(*arrays, tally)
+
+
+def pack_small(gain_attn, gain_ffn, router, rel_bias, routes):
+    def lanes(x):
+        return jnp.pad(x, ((0, 0), (0, 128 - x.shape[1])))
+
+    rows = jnp.concatenate([
+        lanes(gain_attn[None]), lanes(gain_ffn[None]), lanes(rel_bias), lanes(router.T),
+        routes.T.astype(bf16).reshape(-1, 128),
+    ], axis=0)
+    return jnp.pad(rows, ((0, -rows.shape[0] % 16), (0, 0)))
+
+
+def unpack_small(packed, size, shard, bias_rows, heads, experts, tokens):
+    blocks = packed.reshape(size, -1, 128)
+    gain_one = blocks[:, 0, 0:shard].reshape(-1)
+    gain_two = blocks[:, 1, 0:shard].reshape(-1)
+    at = 2 + bias_rows
+    table = blocks[:, 2:at, 0:heads].reshape(-1, heads)
+    router_t = jnp.transpose(blocks[:, at:at + experts, 0:shard], (1, 0, 2)).reshape(experts, -1)
+    at += experts
+    routes = blocks[:, at:at + TOP * tokens // 128].reshape(size, TOP, tokens).astype(jnp.int32)
+    return gain_one, gain_two, table, router_t, routes
+
+
 def outer_sum(left_rows, right_rows):
     return lax.dot_general(
         left_rows, right_rows, (((0,), (0,)), ((), ())), preferred_element_type=jnp.float32
@@ -259,6 +599,31 @@
     return lax.dot_general(
         grad_rows, weight, (((1,), (1,)), ((), ())), preferred_element_type=jnp.float32
     )
+
+
+def rep_moved(whole):
+    count = lax.axis_size("rep")
+    me = lax.axis_index("rep")
+    rows = whole.shape[1] // count
+    moved = []
+    for k in range(1, count):
+        piece = lax.dynamic_slice_in_dim(whole, (me ^ k) * rows, rows, 1)
+        moved.append(lax.ppermute(piece, "rep", [(i, i ^ k) for i in range(count)]))
+    return moved
+
+
+def rep_sum(whole, moved):
+    rows = moved[0].shape[1]
+    total = lax.dynamic_slice_in_dim(whole, lax.axis_index("rep") * rows, rows, 1).astype(f32)
+    for piece in moved:
+        total = total + piece.astype(f32)
+    return total
+
+
+def local_slots(routes_all, first, local):
+    ids = first + lax.iota(jnp.int32, local)
+    hot = jnp.any(routes_all[:, None, :, :] == ids[None, :, None, None], axis=2).astype(jnp.int32)
+    return jnp.where(hot != 0, jnp.cumsum(hot, axis=2) - hot, -1)
 
 
 def shards(
@@ -277,123 +642,100 @@
     w_out,
     cotangent,
 ):
-    dense_full = (
-        lax.all_gather(gain_attn, "grp", axis=0, tiled=True),
-        lax.all_gather(w_query, "grp", axis=0, tiled=True),
-        lax.all_gather(w_key, "grp", axis=0, tiled=True),
-        lax.all_gather(w_value, "grp", axis=0, tiled=True),
-        lax.all_gather(w_output, "grp", axis=0, tiled=True),
-        lax.all_gather(rel_bias, "grp", axis=0, tiled=True),
-        lax.all_gather(gain_ffn, "grp", axis=0, tiled=True),
-        lax.all_gather(router, "grp", axis=0, tiled=True),
-    )
-    gain_one, query_full, key_full, value_full, output_full, table_full, gain_two, router_full = (
-        dense_full
-    )
-    tok_rows = tokens.shape[0]
-    width = tokens.shape[1]
-    inputs = tokens.astype(jnp.float32)
-    scale_one = rms_scale(inputs)
-    normed_one = (inputs * scale_one * gain_one.astype(jnp.float32)).astype(jnp.bfloat16)
-    query_rows = jnp.dot(normed_one, query_full, preferred_element_type=jnp.float32).astype(
-        jnp.bfloat16
-    )
-    key_rows = jnp.dot(normed_one, key_full, preferred_element_type=jnp.float32).astype(
-        jnp.bfloat16
-    )
-    value_rows = jnp.dot(normed_one, value_full, preferred_element_type=jnp.float32).astype(
-        jnp.bfloat16
-    )
-    base = bias_base(table_full)
-    context, lse = attend(query_rows, key_rows, value_rows, segments, base)
-    hidden_one = inputs + jnp.dot(context, output_full, preferred_element_type=jnp.float32)
-    scale_two = rms_scale(hidden_one)
-    normed_two = (hidden_one * scale_two * gain_two.astype(jnp.float32)).astype(jnp.bfloat16)
-    logits = jnp.dot(normed_two, router_full, preferred_element_type=jnp.float32)
-    router_prob = jax.nn.softmax(logits, axis=-1)
+    group = Group()
+    tok_rows, width = tokens.shape
     exp_local = w_in.shape[0]
-    groups = lax.axis_size("grp")
+    groups = group.size
     experts = exp_local * groups
     capacity = 2 * tok_rows * TOP // experts
     choose = routes[:, :, None] == lax.iota(jnp.int32, experts)[None, None, :]
+    tally = jnp.pad(jnp.sum(choose.astype(f32), axis=(0, 1))[None], ((0, 7), (0, 128 - experts)))
+    small = pack_small(gain_attn, gain_ffn, router, rel_bias, routes)
+    query_full, key_full, value_full, output_full, small_all, tally_all = gather_group(
+        (w_query, w_key, w_value, w_output, small), tally
+    )
+    gain_one, gain_two, table_full, router_t, routes_all = unpack_small(
+        small_all, groups, gain_attn.shape[0], rel_bias.shape[0], rel_bias.shape[1], experts, tok_rows
+    )
+    router_full = router_t.T
+    counts = jnp.sum(tally_all[:, 0, 0:experts], axis=0)
+    first = (group.me * exp_local).astype(jnp.int32)
+    cotangent, small_all = lax.optimization_barrier((cotangent, small_all))
+    slots_all = local_slots(routes_all, first, exp_local)
+
+    kept_grad = jnp.where((segments != 0)[:, None], cotangent, jnp.zeros_like(cotangent))
+    grad_own = [kept_grad]
+    for k in range(1, group.chips):
+        grad_own.append(group.onward(grad_own[-1]))
+    grad_sib = [group.swap(block) for block in grad_own]
+
+    inputs = tokens.astype(f32)
+    scale_one = rms_scale(inputs)
+    normed_one = (inputs * scale_one * gain_one.astype(f32)).astype(bf16)
+    query_rows = jnp.dot(normed_one, query_full, preferred_element_type=f32).astype(bf16)
+    key_rows = jnp.dot(normed_one, key_full, preferred_element_type=f32).astype(bf16)
+    value_rows = jnp.dot(normed_one, value_full, preferred_element_type=f32).astype(bf16)
+    base = bias_base(table_full)
+    context, lse = attend(query_rows, key_rows, value_rows, segments, base)
+    hidden_one = inputs + jnp.dot(context, output_full, preferred_element_type=f32)
+    scale_two = rms_scale(hidden_one)
+    normed_two = (hidden_one * scale_two * gain_two.astype(f32)).astype(bf16)
+
+    norm_own = [normed_two]
+    for k in range(1, group.chips):
+        norm_own.append(group.onward(norm_own[-1]))
+    norm_sib = [group.swap(block) for block in norm_own]
+
+    kept = None
+    results = []
+    for k in range(group.chips):
+        chip = group.source_chip(k)
+        info = jnp.concatenate(
+            [
+                lax.dynamic_index_in_dim(rows, 2 * chip + core, 0, keepdims=False)
+                for core in (group.core, 1 - group.core)
+                for rows in (slots_all, routes_all)
+            ],
+            axis=0,
+        )
+        outs, kept = expert_block(
+            k, group.chips, first.reshape(1), norm_own[k], norm_sib[k], grad_own[k], grad_sib[k],
+            info, router_t, w_in, w_out, capacity, kept,
+        )
+        results.append(outs)
+
+    def reduce_blocks(own, sibling):
+        moving = None
+        for k in list(range(1, group.chips)) + [0]:
+            total = own[k].astype(f32) + group.swap(sibling[k]).astype(f32)
+            if moving is not None:
+                total = total + moving.astype(f32)
+            if k != 0:
+                moving = group.onward(total.astype(bf16))
+        return total
+
+    act_all, dpre_all, x_all, dy_all = kept
+    up_grad = jnp.einsum("ekd,ekf->edf", x_all, dpre_all, preferred_element_type=f32).astype(bf16)
+    down_grad = jnp.einsum("ekf,ekd->efd", act_all, dy_all, preferred_element_type=f32).astype(bf16)
+    up_moved, down_moved = rep_moved(up_grad), rep_moved(down_grad)
+
+    back = reduce_blocks([r[2] for r in results], [r[3] for r in results])
+    y_own, y_sib = [r[0] for r in results], [r[1] for r in results]
+    back, up_grad, down_grad, y_own, y_sib = lax.optimization_barrier((back, up_grad, down_grad, y_own, y_sib))
+    mixed = reduce_blocks(y_own, y_sib)
+    up_share, down_share = rep_sum(up_grad, up_moved), rep_sum(down_grad, down_moved)
+
+    logits = jnp.dot(normed_two, router_full, preferred_element_type=f32)
+    router_prob = jax.nn.softmax(logits, axis=-1)
     picked_prob = jnp.sum(jnp.where(choose, router_prob[:, None, :], 0.0), axis=-1)
     prob_sum = jnp.sum(picked_prob, axis=-1, keepdims=True)
-    gates = picked_prob / prob_sum
-    counts, prob_totals = lax.psum(
-        (jnp.sum(choose.astype(jnp.float32), axis=(0, 1)), jnp.sum(router_prob, axis=0)),
-        ("rep", "grp"),
-    )
     all_tokens = tok_rows * lax.axis_size("rep") * groups
     fraction = counts / (TOP * all_tokens)
-    balance_terms = experts * experts * fraction * (prob_totals / all_tokens)
-    loss = aux_weight / experts * jnp.sum(balance_terms)
-    flat_routes = routes.reshape(tok_rows * TOP)
-    flat_hot = (flat_routes[:, None] == lax.iota(jnp.int32, experts)[None, :]).astype(jnp.int32)
-    slots = jnp.sum((jnp.cumsum(flat_hot, axis=0) - flat_hot) * flat_hot, axis=1)
-    copies = jnp.repeat(normed_two, TOP, axis=0)
-    send_rows = (
-        jnp.zeros((experts, capacity, width), jnp.bfloat16).at[flat_routes, slots].set(copies)
-    )
-    received = lax.all_to_all(
-        send_rows.reshape(groups, exp_local, capacity, width),
-        "grp",
-        split_axis=0,
-        concat_axis=0,
-        tiled=True,
-    )
-    pre_act = jnp.einsum("gecd,edf->gecf", received, w_in, preferred_element_type=jnp.float32)
-    activated = jax.nn.gelu(pre_act, approximate=True).astype(jnp.bfloat16)
-    expert_out = jnp.einsum(
-        "gecf,efd->gecd", activated, w_out, preferred_element_type=jnp.float32
-    ).astype(jnp.bfloat16)
-    returned = lax.all_to_all(expert_out, "grp", split_axis=0, concat_axis=0, tiled=True).reshape(
-        experts, capacity, width
-    )
-    picked_out = returned[flat_routes, slots].astype(jnp.float32).reshape(tok_rows, TOP, width)
-    hidden_two = hidden_one + jnp.sum(gates[:, :, None] * picked_out, axis=1)
-    output = hidden_two.astype(jnp.bfloat16)
-    gain_one, query_full, key_full, value_full, output_full, table_full, gain_two, router_full = (
-        dense_full
-    )
-    grad_out = cotangent.astype(jnp.float32) * (segments != 0).astype(jnp.float32)[:, None]
-    grad_gate = jnp.sum(grad_out[:, None, :] * picked_out, axis=-1)
-    grad_mix = (
-        (gates[:, :, None] * grad_out[:, None, :])
-        .astype(jnp.bfloat16)
-        .reshape(tok_rows * TOP, width)
-    )
-    grad_send = (
-        jnp.zeros((experts, capacity, width), jnp.bfloat16).at[flat_routes, slots].set(grad_mix)
-    )
-    grad_received = lax.all_to_all(
-        grad_send.reshape(groups, exp_local, capacity, width),
-        "grp",
-        split_axis=0,
-        concat_axis=0,
-        tiled=True,
-    )
-    grad_act = jnp.einsum(
-        "gecd,efd->gecf", grad_received, w_out, preferred_element_type=jnp.float32
-    )
-    down_grad = jnp.einsum(
-        "gecf,gecd->efd", activated, grad_received, preferred_element_type=jnp.float32
-    )
-    unused_out, gelu_back = jax.vjp(partial(jax.nn.gelu, approximate=True), pre_act)
-    grad_pre = gelu_back(grad_act)[0].astype(jnp.bfloat16)
-    up_grad = jnp.einsum("gecd,gecf->edf", received, grad_pre, preferred_element_type=jnp.float32)
-    grad_rows = jnp.einsum(
-        "gecf,edf->gecd", grad_pre, w_in, preferred_element_type=jnp.float32
-    ).astype(jnp.bfloat16)
-    up_share, down_share = (
-        lax.psum_scatter(up_grad, "rep", scatter_dimension=1, tiled=True),
-        lax.psum_scatter(down_grad, "rep", scatter_dimension=1, tiled=True),
-    )
-    grad_back = lax.all_to_all(grad_rows, "grp", split_axis=0, concat_axis=0, tiled=True).reshape(
-        experts, capacity, width
-    )
-    grad_norm_two = jnp.sum(
-        grad_back[flat_routes, slots].astype(jnp.float32).reshape(tok_rows, TOP, width), axis=1
-    )
+
+    output = (hidden_one + mixed[0:tok_rows]).astype(bf16)
+    grad_out = kept_grad.astype(f32)
+    grad_gate = unpack_dgate(back[tok_rows:], tok_rows).T
+    grad_norm_two = back[0:tok_rows]
     grad_picked = grad_gate / prob_sum - jnp.sum(
         grad_gate * picked_prob, axis=-1, keepdims=True
     ) / (prob_sum * prob_sum)
@@ -436,33 +778,42 @@
         - inputs * scale_one**3 * jnp.mean(scaled_one * inputs, axis=-1, keepdims=True)
     )
     table_grad = table_back(near_grad, far_grad, table_full.shape[0])
-    shares = (
-        lax.psum_scatter(gain_one_grad, "grp", scatter_dimension=0, tiled=True),
-        lax.psum_scatter(query_grad, "grp", scatter_dimension=0, tiled=True),
-        lax.psum_scatter(key_grad, "grp", scatter_dimension=0, tiled=True),
-        lax.psum_scatter(value_grad, "grp", scatter_dimension=0, tiled=True),
-        lax.psum_scatter(output_grad, "grp", scatter_dimension=0, tiled=True),
-        lax.psum_scatter(table_grad, "grp", scatter_dimension=0, tiled=True),
-        lax.psum_scatter(gain_two_grad, "grp", scatter_dimension=0, tiled=True),
-        lax.psum_scatter(router_grad, "grp", scatter_dimension=0, tiled=True),
-    )
-    summed = lax.psum(
-        (shares[0], shares[1], shares[2], shares[3], shares[4], shares[5], shares[6], shares[7]),
-        "rep",
-    )
+    heads = table_grad.shape[1]
+    flat = jnp.concatenate([
+        gain_one_grad, gain_two_grad, table_grad.reshape(-1), router_grad.T.reshape(-1), jnp.sum(router_prob, axis=0)
+    ])
+    flat = lax.psum(flat, ("rep", "grp"))
+    at = 2 * width
+    table_sum = flat[at:at + table_grad.size].reshape(-1, heads)
+    at += table_grad.size
+    router_sum = flat[at:at + router_grad.size].reshape(experts, width).T
+    at += router_grad.size
+    prob_totals = flat[at:at + experts]
+    balance_terms = experts * experts * fraction * (prob_totals / all_tokens)
+    loss = aux_weight / experts * jnp.sum(balance_terms)
+
+    def mine(x):
+        rows = x.shape[0] // groups
+        return lax.dynamic_slice_in_dim(x, group.me * rows, rows, 0)
+
+    dense = [
+        lax.psum_scatter(x, "grp", scatter_dimension=0, tiled=True)
+        for x in (query_grad, key_grad, value_grad, output_grad)
+    ]
+    dense = lax.psum(tuple(dense), "rep")
     return (
         output,
         loss,
         balance_terms,
         grad_input,
-        summed[0],
-        summed[1],
-        summed[2],
-        summed[3],
-        summed[4],
-        summed[5],
-        summed[6],
-        summed[7],
+        mine(flat[0:width]),
+        dense[0],
+        dense[1],
+        dense[2],
+        dense[3],
+        mine(table_sum),
+        mine(flat[width:2 * width]),
+        mine(router_sum),
         up_share,
         down_share,
     )

time: 1510 us -> 986 us (0.65)
  blocking collectives: 350 us -> 38.2 us
  Pallas kernels: 46 us -> 264 us
  matrix products: 265 us -> 92.6 us
  local copies, waits for them, and re-layouts: 183 us -> 41.8 us
  waiting for transfers between devices: 548 us -> 452 us
  other arithmetic: 67.9 us -> 51.1 us
    ppermute x0 -> x34, waiting for transfers between devices: none -> 405 us  [the longest x12 221 us: onward(): return lax.ppermute(x, 'grp', pairs)]
    reduce_scatter x6 -> x4, waiting for transfers between devices: 396 us -> 0.08 us  [shards(): lax.psum_scatter(x, 'grp', scatter_dimension=0, tiled=True)]
    pallas_call x0 -> x5, Pallas kernels: none -> 218 us  [the longest x4 170 us: expert_block(): pl.pallas_call(expert_kernel, grid=(local, hidden // part), in_specs=in_s...]
    dot_general x11 -> x7, matrix products: 228 us -> 65.7 us  [the longest x1 28.5 us: shards(): jnp.einsum('ekf,ekd->efd', act_all, dy_all, preferred_element_type=f32)]
    all_gather x2 -> x0, blocking collectives: 158 us -> none  [the longest x1 145 us: shards(): lax.all_gather(router, 'grp', axis=0, tiled=True)]
    all_to_all x4 -> x0, waiting for transfers between devices: 124 us -> none  [the longest x1 70.9 us: shards(): lax.all_to_all(grad_send.reshape(groups, exp_local, capacity, width), 'gr...]
    psum x3 -> x1, blocking collectives: 149 us -> 38.2 us  [shards(): flat = lax.psum(flat, ('rep', 'grp'))]
    gather x2 -> x0, local copies, waits for them, and re-layouts: 77.4 us -> none  [the longest x1 38.7 us: shards(): returned[flat_routes, slots].astype(jnp.float32)]
  transfers between devices with their start and end apart: 16 -> 39, of which waited for: 10 -> 16; matrix products, arithmetic and copies ran while one was open for 26% -> 14% of each run, Pallas kernels for 1% -> 17%
where the time goes in v2:
time: 986 us; the launch traced here: 976 us
  waiting for transfers between devices  452 us (46%)
  Pallas kernels  264 us (27%)
  matrix products  92.6 us (9%)
  other arithmetic  51.1 us (5%)
  local copies, waits for them, and re-layouts  41.8 us (4%)
  blocking collectives  38.2 us (4%)
  between operations  19.4 us (2%)
  starting transfers between devices  17.5 us (2%)
    ppermute x12, waiting for transfers between devices, onward(): return lax.ppermute(x, 'grp', pairs)  221 us
    ppermute x6, waiting for transfers between devices, rep_moved(): moved.append(lax.ppermute(piece, 'rep', [(i, i ^ k) for i in range(count)]))  179 us
    pallas_call x4, Pallas kernels, expert_block(): pl.pallas_call(expert_kernel, grid=(local, hidden // part), in_specs=in_s...  170 us
    pallas_call x1, Pallas kernels, gather_group(): pl.pallas_call(partial(gather_kernel, chips, reps), in_specs=[hbm] * (cou...  48.4 us
    psum x1, waiting for transfers between devices, shards(): dense = lax.psum(tuple(dense), 'rep')  46.7 us
    psum x1, blocking collectives, shards(): flat = lax.psum(flat, ('rep', 'grp'))  38.2 us
    dot_general x1, matrix products, shards(): jnp.einsum('ekf,ekd->efd', act_all, dy_all, preferred_element_type=f32)  28.5 us
    dot_general x1, matrix products, shards(): jnp.einsum('ekd,ekf->edf', x_all, dpre_all, preferred_element_type=f32)  27.9 us
  transfers between devices with their start and end apart: 39, of which 16 were waited for; matrix products, arithmetic and copies ran while one was open for 14% of the time, Pallas kernels for 17%

profile of v2, /device:TPU:0, one launch (start us, length us, event | category | flops | bytes accessed | tf_op | source)
XLA Modules:
  0.0 976.3 jit_solution(17174438577029629938)
XLA Ops:
  13.1 48.4 %gather_group.1 = (bf16[768,768]{1,0:T(8,128)(2,1)}, bf16[768,768]{1,0:T(8,128)(2,1)}, bf16[768,768]{1,0:T(8,128)(2,1)}, bf16[768,768]{1,0:T(8,128)(2,1)}, bf16[...) custom-call(bf16[96,768]{1,0:T(8,128)(2,1)} %refs_0_.1, bf16[96,768]{1,0:T(8,128)(2,1)} %refs_1_.1, bf16[96,768]{1,0:T(8,128)(2,1)} %refs_2_.1, ...), custom_call_target="tpu_custom_call" | custom-call | bytes 16777216 | tf_op jit(solution)/shard_map/gather_group/pallas_call | solution.py:552
  64.1 1.9 fusion.4
  66.6 2.8 convolution_convert_fusion.5.q
  73.1 20.0 %attend.1 = (bf16[1024,768]{1,0:T(8,128)(2,1)S(1)}, f32[6,8,256]{2,1,0:T(8,128)S(1)}) custom-call(f32[12,8,384]{2,1,0:T(8,128)S(1)} %copy_subtract_fusion.base, s32[1024,1]{1,0:T(8,128)S(1)} %copy.71.seg_col, s32[1,1024]{1,0:T(1,128)S(1)} %bitcast.101, bf16[1024,768]{1,0:T(8,128)(2,1)S(1)} %convolution_convert_fusion.5.q, ...), custom_call_target="tpu_custom_call" | custom-call | flops 3221225472 | bytes 6291456 | tf_op jit(solution)/shard_map/attend/pallas_call | solution.py:119
  93.2 3.1 multiply_reduce_fusion.2
  97.0 2.3 multiply_convert_fusion.n_a
  100.1 1.8 collective-permute-start.7
  106.2 4.5 reduce-window.6
  111.8 25.8 %collective-permute-done.3.n_a = bf16[1024,768]{1,0:T(8,128)(2,1)} collective-permute-done((bf16[1024,768]{1,0:T(8,128)(2,1)S(1)}, bf16[1024,768]{1,0:T(8,128)(2,1)}, u32[]{:S(2)}, u32[]{:S(2)}) %collective-permute-start.3) | collective-permute-done | bytes 1572896 | tf_op jit(solution)/shard_map/ppermute | solution.py:422
  137.7 33.7 %collective-permute-done.7.g_a = bf16[1024,768]{1,0:T(8,128)(2,1)} collective-permute-done((bf16[1024,768]{1,0:T(8,128)(2,1)S(1)}, bf16[1024,768]{1,0:T(8,128)(2,1)}, u32[]{:S(2)}, u32[]{:S(2)}) %collective-permute-start.7) | collective-permute-done | bytes 1572896 | tf_op jit(solution)/shard_map/ppermute | solution.py:422
  171.6 42.1 %expert_block.4 = (bf16[1024,768]{1,0:T(8,128)(2,1)S(1)}, bf16[1024,768]{1,0:T(8,128)(2,1)S(1)}, bf16[1040,768]{1,0:T(8,128)(2,1)}, bf16[1040,768]{1,0:T(8,128)(...) custom-call(s32[1]{0:T(128)} %bitcast.12.first, ...), custom_call_target="tpu_custom_call" | custom-call | flops 25769803776 | bytes 62914560 | tf_op jit(solution)/shard_map/expert_block/pallas_call | solution.py:383
  215.4 2.0 collective-permute-start.5
  217.4 21.3 %collective-permute-done.8.g_a = bf16[1024,768]{1,0:T(8,128)(2,1)S(1)} collective-permute-done((bf16[1024,768]{1,0:T(8,128)(2,1)}, bf16[1024,768]{1,0:T(8,128)(2,1)S(1)}, u32[]{:S(2)}, u32[]{:S(2)}) %collective-permute-start.8) | collective-permute-done | bytes 1572896 | tf_op jit(solution)/shard_map/ppermute | solution.py:422
  239.9 42.6 %expert_block.5 = (bf16[1024,768]{1,0:T(8,128)(2,1)S(1)}, bf16[1024,768]{1,0:T(8,128)(2,1)S(1)}, bf16[1040,768]{1,0:T(8,128)(2,1)}, bf16[1040,768]{1,0:T(8,128)(...) custom-call(s32[1]{0:T(128)} %bitcast.12.first, ...), custom_call_target="tpu_custom_call", output_to_operand_aliasing={{4}: (9, {}), {5}: (10, {}), {6}: (11, {}), {7}: (12, {})} | custom-call | flops 25769803776 | bytes 62914560 | tf_op jit(solution)/shard_map/expert_block/pallas_call | solution.py:383
  285.5 20.1 %collective-permute-done.9.g_a = bf16[1024,768]{1,0:T(8,128)(2,1)} collective-permute-done((bf16[1024,768]{1,0:T(8,128)(2,1)S(1)}, bf16[1024,768]{1,0:T(8,128)(2,1)}, u32[]{:S(2)}, u32[]{:S(2)}) %collective-permute-start.9) | collective-permute-done | bytes 1572896 | tf_op jit(solution)/shard_map/ppermute | solution.py:422
  305.6 42.4 %expert_block.6 = (bf16[1024,768]{1,0:T(8,128)(2,1)S(1)}, bf16[1024,768]{1,0:T(8,128)(2,1)S(1)}, bf16[1040,768]{1,0:T(8,128)(2,1)}, bf16[1040,768]{1,0:T(8,128)(...) custom-call(s32[1]{0:T(128)} %bitcast.12.first, ...), custom_call_target="tpu_custom_call", output_to_operand_aliasing={{4}: (9, {}), {5}: (10, {}), {6}: (11, {}), {7}: (12, {})} | custom-call | flops 25769803776 | bytes 62914560 | tf_op jit(solution)/shard_map/expert_block/pallas_call | solution.py:383
  349.7 42.5 %expert_block.7 = (bf16[1024,768]{1,0:T(8,128)(2,1)S(1)}, bf16[1024,768]{1,0:T(8,128)(2,1)S(1)}, bf16[1040,768]{1,0:T(8,128)(2,1)}, bf16[1040,768]{1,0:T(8,128)(...) custom-call(s32[1]{0:T(128)} %bitcast.12.first, ...), custom_call_target="tpu_custom_call", output_to_operand_aliasing={{4}: (9, {}), {5}: (10, {}), {6}: (11, {}), {7}: (12, {})} | custom-call | flops 25769803776 | bytes 62914560 | tf_op jit(solution)/shard_map/expert_block/pallas_call | solution.py:383
  392.7 1.8 add_convert_fusion.1
  394.6 1.9 collective-permute-start.19
  396.5 27.9 %convolution_convert_fusion = bf16[2,768,3072]{2,1,0:T(8,128)(2,1)} fusion(bf16[2,2048,768]{2,1,0:T(8,128)(2,1)} %get-tuple-element.98, bf16[2,2048,3072]{2,1,0:T(8,128)(2,1)} %get-tuple-element.99), kind=kOutput, calls=%fused_computation | convolution fusion | flops 19332071424 | bytes 40894464 | tf_op jit(solution)/shard_map/ekd,ekf->edf/dot_general | solution.py:718
  424.4 8.6 collective-permute-done.19
  433.0 4.1 add_convert_fusion
  438.0 28.5 %convolution_convert_fusion.1 = bf16[2,3072,768]{2,1,0:T(8,128)(2,1)} fusion(bf16[2,2048,3072]{2,1,0:T(8,128)(2,1)} %get-tuple-element.100, bf16[2,2048,768]{2,1,0:T(8,128)(2,1)} %get-tuple-element.101), kind=kOutput, calls=%fused_computation.1 | convolution fusion | flops 19332071424 | bytes 40894464 | tf_op jit(solution)/shard_map/ekf,ekd->efd/dot_general | solution.py:719
  466.5 8.2 collective-permute-done.20
  474.7 3.0 convert_add_fusion.3
  478.4 2.9 collective-permute-done.24
  483.5 35.6 %collective-permute-done.25 = bf16[1024,768]{1,0:T(8,128)(2,1)S(1)} collective-permute-done((bf16[1024,768]{1,0:T(8,128)(2,1)S(1)}, bf16[1024,768]{1,0:T(8,128)(2,1)S(1)}, u32[]{:S(2)}, u32[]{:S(2)}) %collective-permute-start.25) | collective-permute-done | bytes 1572896 | tf_op jit(solution)/shard_map/ppermute | solution.py:422
  521.5 34.7 %collective-permute-done.26 = bf16[1024,768]{1,0:T(8,128)(2,1)S(1)} collective-permute-done((bf16[1024,768]{1,0:T(8,128)(2,1)S(1)}, bf16[1024,768]{1,0:T(8,128)(2,1)S(1)}, u32[]{:S(2)}, u32[]{:S(2)}) %collective-permute-start.26) | collective-permute-done | bytes 1572896 | tf_op jit(solution)/shard_map/ppermute | solution.py:422
  559.4 33.0 %collective-permute-done.27 = bf16[1024,768]{1,0:T(8,128)(2,1)S(1)} collective-permute-done((bf16[1024,768]{1,0:T(8,128)(2,1)S(1)}, bf16[1024,768]{1,0:T(8,128)(2,1)S(1)}, u32[]{:S(2)}, u32[]{:S(2)}) %collective-permute-start.27) | collective-permute-done | bytes 1572896 | tf_op jit(solution)/shard_map/ppermute | solution.py:422
  592.4 3.1 multiply_subtract_fusion
  599.7 25.9 %attend_back.1 = (bf16[1024,768]{1,0:T(8,128)(2,1)S(1)}, bf16[1024,768]{1,0:T(8,128)(2,1)S(1)}, bf16[1024,768]{1,0:T(8,128)(2,1)S(1)}, f32[12,8,384]{2,1,0:T(8,128)S(1)}, f32[6,8,256]{2,1,0:T(8,128)S(1)}) custom-call(f32[12,8,384]{2,1,0:T(8,128)S(1)} %copy-done.9, s32[1024,1]{1,0:T(8,128)S(1)} %copy-done.7, s32[1,1024]{1,0:T(1,128)S(1)} %bitcast.102, ...), custom_call_target="tpu_custom_call" | custom-call | flops 8053063680 | bytes 12582912 | tf_op jit(solution)/shard_map/attend_back/pallas_call | solution.py:209
  628.0 3.0 fusion.31
  631.1 4.9 fusion.29
  636.1 4.4 fusion.27
  640.8 6.3 constant_dynamic-slice_fusion.2
  650.6 6.5 constant_dynamic-slice_fusion.5
  659.1 43.4 %collective-permute-done.33 = bf16[2,768,768]{2,1,0:T(8,128)(2,1)} collective-permute-done((bf16[2,768,768]{2,1,0:T(8,128)(2,1)}, bf16[2,768,768]{2,1,0:T(8,128)(2,1)}, u32[]{:S(2)}, u32[]{:S(2)}) %collective-permute-start.33) | collective-permute-done | bytes 2359328 | tf_op jit(solution)/shard_map/ppermute | solution.py:611
  703.1 2.9 fusion.8
  707.6 45.5 %collective-permute-done.32 = bf16[2,768,768]{2,1,0:T(8,128)(2,1)} collective-permute-done((bf16[2,768,768]{2,1,0:T(8,128)(2,1)}, bf16[2,768,768]{2,1,0:T(8,128)(2,1)}, u32[]{:S(2)}, u32[]{:S(2)}) %collective-permute-start.32) | collective-permute-done | bytes 2359328 | tf_op jit(solution)/shard_map/ppermute | solution.py:611
  753.1 7.1 convert_add_fusion.1
  760.2 43.5 %collective-permute-done.30 = bf16[2,192,3072]{2,1,0:T(8,128)(2,1)} collective-permute-done((bf16[2,192,3072]{2,1,0:T(8,128)(2,1)}, bf16[2,192,3072]{2,1,0:T(8,128)(2,1)}, u32[]{:S(2)}, u32[]{:S(2)}) %collective-permute-start.30) | collective-permute-done | bytes 2359328 | tf_op jit(solution)/shard_map/ppermute | solution.py:611
  803.6 46.9 %collective-permute-done.29 = bf16[2,192,3072]{2,1,0:T(8,128)(2,1)} collective-permute-done((bf16[2,192,3072]{2,1,0:T(8,128)(2,1)}, bf16[2,192,3072]{2,1,0:T(8,128)(2,1)}, u32[]{:S(2)}, u32[]{:S(2)}) %collective-permute-start.29) | collective-permute-done | bytes 2359328 | tf_op jit(solution)/shard_map/ppermute | solution.py:611
  850.6 7.6 convert_add_fusion.2
  859.0 2.8 fusion.43
  863.6 3.5 fusion.7
  867.2 38.2 %psum.35 = f32[14224]{0:T(1024)S(1)} all-reduce(f32[14224]{0:T(1024)S(1)} %constant_dynamic-update-slice_fusion), channel_id=1, replica_groups=mesh['rep'=4,'grp'=8] {'rep','grp'}, use_global_device_ids=true, to_apply=%region_20.21 | all-reduce | flops 14224 | bytes 113792 | tf_op jit(solution)/shard_map/psum | solution.py:785
  909.9 4.8 fusion.6
  914.7 46.7 %all-reduce.9.cloned.1.call-done = (f32[96,768]{1,0:T(8,128)}, f32[96,768]{1,0:T(8,128)}, f32[96,768]{1,0:T(8,128)}, f32[96,768]{1,0:T(8,128)}) async-done(((f32[96,768]{1,0:T(8,128)}, f32[96,768]{1,0:T(8,128)}, f32[96,768]{1,0:T(8,128)}, f32[96,768]{1,0:T(8,128)}), (f32[96,768]{1,0:T(8,128)}, f32[96,768]{1,0:T(8,128)}, f32[96,768]{1,0:T(8,128)}, f32[96,768]{1,0:T(8,128)})) %all-reduce.9.cloned.1.call-update) | async-done | bytes 1179664 | tf_op jit(solution)/shard_map/psum | solution.py:803
  (331 shorter events, 62.1 us)
Async XLA Ops:
  7.2 59.4 %copy-start.34 = (bf16[1024,768]{1,0:T(8,128)(2,1)S(1)}, bf16[1024,768]{1,0:T(8,128)(2,1)}, u32[]{:S(2)}) copy-start(bf16[1024,768]{1,0:T(8,128)(2,1)} %param.18) | copy-start | bytes 4718596
  7.2 898.2 %reduce-scatter.5.cloned.1.call-start = ((), (), s32[]{:S(2)}) async-start(), calls=%async_computation.4 | async-start | bytes 2654208 | tf_op jit(solution)/shard_map/reduce_scatter | solution.py:800
  99.4 38.3 %collective-permute-start.3 = (bf16[1024,768]{1,0:T(8,128)(2,1)S(1)}, bf16[1024,768]{1,0:T(8,128)(2,1)}, u32[]{:S(2)}, u32[]{:S(2)}) collective-permute-start(bf16[1024,768]{1,0:T(8,128)(2,1)S(1)} %multiply_convert_fusion.n_a), channel_id=1, source_target_pairs={{0,2},{1,3},{2,6},{3,7},{6,4},{7,5},{4,0},{5,1},{8,10},{9,11},{10,... | collective-permute-start | bytes 4718600 | tf_op jit(solution)/shard_map/ppermute | solution.py:422
  99.5 71.9 %collective-permute-start = (bf16[1024,768]{1,0:T(8,128)(2,1)S(1)}, bf16[1024,768]{1,0:T(8,128)(2,1)}, u32[]{:S(2)}, u32[]{:S(2)}) collective-permute-start(bf16[1024,768]{1,0:T(8,128)(2,1)S(1)} %multiply_convert_fusion.n_a), channel_id=1, source_target_pairs={{0,1},{1,0},{2,3},{3,2},{4,5},{5,4},{6,7},{7,6},{8,9},{9,8},{10,11... | collective-permute-start | bytes 4718600 | tf_op jit(solution)/shard_map/ppermute | solution.py:425
  100.1 71.5 %copy-start.43 = (bf16[1024,768]{1,0:T(8,128)(2,1)}, bf16[1024,768]{1,0:T(8,128)(2,1)S(1)}, u32[]{:S(2)}) copy-start(bf16[1024,768]{1,0:T(8,128)(2,1)S(1)} %broadcast_select_fusion.g_a) | copy-start | bytes 4718596
  100.1 71.3 %collective-permute-start.7 = (bf16[1024,768]{1,0:T(8,128)(2,1)S(1)}, bf16[1024,768]{1,0:T(8,128)(2,1)}, u32[]{:S(2)}, u32[]{:S(2)}) collective-permute-start(bf16[1024,768]{1,0:T(8,128)(2,1)S(1)} %broadcast_select_fusion.g_a), channel_id=1, source_target_pairs={{0,2},{1,3},{2,6},{3,7},{6,4},{7,5},{4,0},{5,1},{8,10},{9,11},{10,... | collective-permute-start | bytes 4718600 | tf_op jit(solution)/shard_map/ppermute | solution.py:422
  101.8 69.7 %collective-permute-start.1 = (bf16[1024,768]{1,0:T(8,128)(2,1)S(1)}, bf16[1024,768]{1,0:T(8,128)(2,1)}, u32[]{:S(2)}, u32[]{:S(2)}) collective-permute-start(bf16[1024,768]{1,0:T(8,128)(2,1)S(1)} %broadcast_select_fusion.g_a), channel_id=1, source_target_pairs={{0,1},{1,0},{2,3},{3,2},{4,5},{5,4},{6,7},{7,6},{8,9},{9,8},{10,11... | collective-permute-start | bytes 4718600 | tf_op jit(solution)/shard_map/ppermute | solution.py:425
  137.7 77.7 %collective-permute-start.13 = (bf16[1024,768]{1,0:T(8,128)(2,1)}, bf16[1024,768]{1,0:T(8,128)(2,1)S(1)}, u32[]{:S(2)}, u32[]{:S(2)}) collective-permute-start(bf16[1024,768]{1,0:T(8,128)(2,1)} %collective-permute-done.3.n_a), channel_id=1, source_target_pairs={{0,1},{1,0},{2,3},{3,2},{4,5},{5,4},{6,7},{7,6},{8,9},{9,8},{10,11... | collective-permute-start | bytes 4718600 | tf_op jit(solution)/shard_map/ppermute | solution.py:425
  137.7 77.7 %collective-permute-start.4 = (bf16[1024,768]{1,0:T(8,128)(2,1)}, bf16[1024,768]{1,0:T(8,128)(2,1)S(1)}, u32[]{:S(2)}, u32[]{:S(2)}) collective-permute-start(bf16[1024,768]{1,0:T(8,128)(2,1)} %collective-permute-done.3.n_a), channel_id=1, source_target_pairs={{0,2},{1,3},{2,6},{3,7},{6,4},{7,5},{4,0},{5,1},{8,10},{9,11},{10,... | collective-permute-start | bytes 4718600 | tf_op jit(solution)/shard_map/ppermute | solution.py:422
  171.4 67.3 %collective-permute-start.14 = (bf16[1024,768]{1,0:T(8,128)(2,1)}, bf16[1024,768]{1,0:T(8,128)(2,1)S(1)}, u32[]{:S(2)}, u32[]{:S(2)}) collective-permute-start(bf16[1024,768]{1,0:T(8,128)(2,1)} %collective-permute-done.7.g_a), channel_id=1, source_target_pairs={{0,1},{1,0},{2,3},{3,2},{4,5},{5,4},{6,7},{7,6},{8,9},{9,8},{10,11... | collective-permute-start | bytes 4718600 | tf_op jit(solution)/shard_map/ppermute | solution.py:425
  171.4 67.3 %collective-permute-start.8 = (bf16[1024,768]{1,0:T(8,128)(2,1)}, bf16[1024,768]{1,0:T(8,128)(2,1)S(1)}, u32[]{:S(2)}, u32[]{:S(2)}) collective-permute-start(bf16[1024,768]{1,0:T(8,128)(2,1)} %collective-permute-done.7.g_a), channel_id=1, source_target_pairs={{0,2},{1,3},{2,6},{3,7},{6,4},{7,5},{4,0},{5,1},{8,10},{9,11},{10,... | collective-permute-start | bytes 4718600 | tf_op jit(solution)/shard_map/ppermute | solution.py:422
  214.8 251.6 %collective-permute-start.2 = (bf16[1040,768]{1,0:T(8,128)(2,1)}, bf16[1040,768]{1,0:T(8,128)(2,1)}, u32[]{:S(2)}, u32[]{:S(2)}) collective-permute-start(bf16[1040,768]{1,0:T(8,128)(2,1)} %get-tuple-element.79), channel_id=1, source_target_pairs={{0,1},{1,0},{2,3},{3,2},{4,5},{5,4},{6,7},{7,6},{8,9},{9,8},{10,11... | collective-permute-start | bytes 4792328 | tf_op jit(solution)/shard_map/ppermute | solution.py:425
  215.4 69.6 %collective-permute-start.11 = (bf16[1024,768]{1,0:T(8,128)(2,1)S(1)}, bf16[1024,768]{1,0:T(8,128)(2,1)S(1)}, u32[]{:S(2)}, u32[]{:S(2)}) collective-permute-start(bf16[1024,768]{1,0:T(8,128)(2,1)S(1)} %collective-permute-done.4.n_a), channel_id=1, source_target_pairs={{0,1},{1,0},{2,3},{3,2},{4,5},{5,4},{6,7},{7,6},{8,9},{9,8},{10,11... | collective-permute-start | bytes 4718600 | tf_op jit(solution)/shard_map/ppermute | solution.py:425
  215.4 70.0 %collective-permute-start.5 = (bf16[1024,768]{1,0:T(8,128)(2,1)S(1)}, bf16[1024,768]{1,0:T(8,128)(2,1)S(1)}, u32[]{:S(2)}, u32[]{:S(2)}) collective-permute-start(bf16[1024,768]{1,0:T(8,128)(2,1)S(1)} %collective-permute-done.4.n_a), channel_id=1, source_target_pairs={{0,2},{1,3},{2,6},{3,7},{6,4},{7,5},{4,0},{5,1},{8,10},{9,11},{10,... | collective-permute-start | bytes 4718600 | tf_op jit(solution)/shard_map/ppermute | solution.py:422
  238.7 43.9 %copy-start.66 = (bf16[1024,768]{1,0:T(8,128)(2,1)}, bf16[1024,768]{1,0:T(8,128)(2,1)S(1)}, u32[]{:S(2)}) copy-start(bf16[1024,768]{1,0:T(8,128)(2,1)S(1)} %collective-permute-done.8.g_a) | copy-start | bytes 4718596
  238.7 66.9 %collective-permute-start.12 = (bf16[1024,768]{1,0:T(8,128)(2,1)S(1)}, bf16[1024,768]{1,0:T(8,128)(2,1)}, u32[]{:S(2)}, u32[]{:S(2)}) collective-permute-start(bf16[1024,768]{1,0:T(8,128)(2,1)S(1)} %collective-permute-done.8.g_a), channel_id=1, source_target_pairs={{0,1},{1,0},{2,3},{3,2},{4,5},{5,4},{6,7},{7,6},{8,9},{9,8},{10,11... | collective-permute-start | bytes 4718600 | tf_op jit(solution)/shard_map/ppermute | solution.py:425
  238.7 66.9 %collective-permute-start.9 = (bf16[1024,768]{1,0:T(8,128)(2,1)S(1)}, bf16[1024,768]{1,0:T(8,128)(2,1)}, u32[]{:S(2)}, u32[]{:S(2)}) collective-permute-start(bf16[1024,768]{1,0:T(8,128)(2,1)S(1)} %collective-permute-done.8.g_a), channel_id=1, source_target_pairs={{0,2},{1,3},{2,6},{3,7},{6,4},{7,5},{4,0},{5,1},{8,10},{9,11},{10,... | collective-permute-start | bytes 4718600 | tf_op jit(solution)/shard_map/ppermute | solution.py:422
  284.9 63.6 %collective-permute-start.17 = (bf16[1040,768]{1,0:T(8,128)(2,1)}, bf16[1040,768]{1,0:T(8,128)(2,1)S(1)}, u32[]{:S(2)}, u32[]{:S(2)}) collective-permute-start(bf16[1040,768]{1,0:T(8,128)(2,1)} %get-tuple-element.97), channel_id=1, source_target_pairs={{0,1},{1,0},{2,3},{3,2},{4,5},{5,4},{6,7},{7,6},{8,9},{9,8},{10,11... | collective-permute-start | bytes 4792328 | tf_op jit(solution)/shard_map/ppermute | solution.py:425
  285.4 64.3 %collective-permute-start.6 = (bf16[1024,768]{1,0:T(8,128)(2,1)S(1)}, bf16[1024,768]{1,0:T(8,128)(2,1)}, u32[]{:S(2)}, u32[]{:S(2)}) collective-permute-start(bf16[1024,768]{1,0:T(8,128)(2,1)S(1)} %collective-permute-done.5.n_a), channel_id=1, source_target_pairs={{0,1},{1,0},{2,3},{3,2},{4,5},{5,4},{6,7},{7,6},{8,9},{9,8},{10,11... | collective-permute-start | bytes 4718600 | tf_op jit(solution)/shard_map/ppermute | solution.py:425
  305.6 44.1 %collective-permute-start.10 = (bf16[1024,768]{1,0:T(8,128)(2,1)}, bf16[1024,768]{1,0:T(8,128)(2,1)}, u32[]{:S(2)}, u32[]{:S(2)}) collective-permute-start(bf16[1024,768]{1,0:T(8,128)(2,1)} %collective-permute-done.9.g_a), channel_id=1, source_target_pairs={{0,1},{1,0},{2,3},{3,2},{4,5},{5,4},{6,7},{7,6},{8,9},{9,8},{10,11... | collective-permute-start | bytes 4718600 | tf_op jit(solution)/shard_map/ppermute | solution.py:425
  348.0 44.7 %collective-permute-start.16 = (bf16[1040,768]{1,0:T(8,128)(2,1)}, bf16[1040,768]{1,0:T(8,128)(2,1)S(1)}, u32[]{:S(2)}, u32[]{:S(2)}) collective-permute-start(bf16[1040,768]{1,0:T(8,128)(2,1)} %get-tuple-element.95), channel_id=1, source_target_pairs={{0,1},{1,0},{2,3},{3,2},{4,5},{5,4},{6,7},{7,6},{8,9},{9,8},{10,11... | collective-permute-start | bytes 4792328 | tf_op jit(solution)/shard_map/ppermute | solution.py:425
  349.7 43.1 %collective-permute-start.18 = (bf16[1040,768]{1,0:T(8,128)(2,1)S(1)}, bf16[1040,768]{1,0:T(8,128)(2,1)S(1)}, u32[]{:S(2)}, u32[]{:S(2)}) collective-permute-start(bf16[1040,768]{1,0:T(8,128)(2,1)S(1)} %add_convert_fusion.2), channel_id=1, source_target_pairs={{0,2},{1,3},{2,6},{3,7},{6,4},{7,5},{4,0},{5,1},{8,10},{9,11},{10,... | collective-permute-start | bytes 4792328 | tf_op jit(solution)/shard_map/ppermute | solution.py:422
  392.2 32.2 %collective-permute-start.15 = (bf16[1040,768]{1,0:T(8,128)(2,1)}, bf16[1040,768]{1,0:T(8,128)(2,1)}, u32[]{:S(2)}, u32[]{:S(2)}) collective-permute-start(bf16[1040,768]{1,0:T(8,128)(2,1)} %get-tuple-element.93), channel_id=1, source_target_pairs={{0,1},{1,0},{2,3},{3,2},{4,5},{5,4},{6,7},{7,6},{8,9},{9,8},{10,11... | collective-permute-start | bytes 4792328 | tf_op jit(solution)/shard_map/ppermute | solution.py:425
  394.6 38.4 %collective-permute-start.19 = (bf16[1040,768]{1,0:T(8,128)(2,1)}, bf16[1040,768]{1,0:T(8,128)(2,1)}, u32[]{:S(2)}, u32[]{:S(2)}) collective-permute-start(bf16[1040,768]{1,0:T(8,128)(2,1)} %add_convert_fusion.1), channel_id=1, source_target_pairs={{0,2},{1,3},{2,6},{3,7},{6,4},{7,5},{4,0},{5,1},{8,10},{9,11},{10,... | collective-permute-start | bytes 4792328 | tf_op jit(solution)/shard_map/ppermute | solution.py:422
  437.1 37.6 %collective-permute-start.20 = (bf16[1040,768]{1,0:T(8,128)(2,1)}, bf16[1040,768]{1,0:T(8,128)(2,1)}, u32[]{:S(2)}, u32[]{:S(2)}) collective-permute-start(bf16[1040,768]{1,0:T(8,128)(2,1)} %add_convert_fusion), channel_id=1, source_target_pairs={{0,2},{1,3},{2,6},{3,7},{6,4},{7,5},{4,0},{5,1},{8,10},{9,11},{10,... | collective-permute-start | bytes 4792328 | tf_op jit(solution)/shard_map/ppermute | solution.py:422
  477.8 3.5 collective-permute-start.24
  478.0 5.5 collective-permute-start.23
  481.7 37.4 %collective-permute-start.25 = (bf16[1024,768]{1,0:T(8,128)(2,1)S(1)}, bf16[1024,768]{1,0:T(8,128)(2,1)S(1)}, u32[]{:S(2)}, u32[]{:S(2)}) collective-permute-start(bf16[1024,768]{1,0:T(8,128)(2,1)S(1)} %add_convert_fusion.6), channel_id=1, source_target_pairs={{0,2},{1,3},{2,6},{3,7},{6,4},{7,5},{4,0},{5,1},{8,10},{9,11},{10,... | collective-permute-start | bytes 4718600 | tf_op jit(solution)/shard_map/ppermute | solution.py:422
  481.7 39.7 %collective-permute-start.22 = (bf16[1024,768]{1,0:T(8,128)(2,1)S(1)}, bf16[1024,768]{1,0:T(8,128)(2,1)S(1)}, u32[]{:S(2)}, u32[]{:S(2)}) collective-permute-start(bf16[1024,768]{1,0:T(8,128)(2,1)S(1)} %copy-done.17), channel_id=1, source_target_pairs={{0,1},{1,0},{2,3},{3,2},{4,5},{5,4},{6,7},{7,6},{8,9},{9,8},{10,11... | collective-permute-start | bytes 4718600 | tf_op jit(solution)/shard_map/ppermute | solution.py:425
  519.6 36.6 %collective-permute-start.26 = (bf16[1024,768]{1,0:T(8,128)(2,1)S(1)}, bf16[1024,768]{1,0:T(8,128)(2,1)S(1)}, u32[]{:S(2)}, u32[]{:S(2)}) collective-permute-start(bf16[1024,768]{1,0:T(8,128)(2,1)S(1)} %add_convert_fusion.5), channel_id=1, source_target_pairs={{0,2},{1,3},{2,6},{3,7},{6,4},{7,5},{4,0},{5,1},{8,10},{9,11},{10,... | collective-permute-start | bytes 4718600 | tf_op jit(solution)/shard_map/ppermute | solution.py:422
  521.3 38.1 %collective-permute-start.21 = (bf16[1024,768]{1,0:T(8,128)(2,1)S(1)}, bf16[1024,768]{1,0:T(8,128)(2,1)S(1)}, u32[]{:S(2)}, u32[]{:S(2)}) collective-permute-start(bf16[1024,768]{1,0:T(8,128)(2,1)S(1)} %copy-done.13), channel_id=1, source_target_pairs={{0,1},{1,0},{2,3},{3,2},{4,5},{5,4},{6,7},{7,6},{8,9},{9,8},{10,11... | collective-permute-start | bytes 4718600 | tf_op jit(solution)/shard_map/ppermute | solution.py:425
  556.8 35.6 %collective-permute-start.27 = (bf16[1024,768]{1,0:T(8,128)(2,1)S(1)}, bf16[1024,768]{1,0:T(8,128)(2,1)S(1)}, u32[]{:S(2)}, u32[]{:S(2)}) collective-permute-start(bf16[1024,768]{1,0:T(8,128)(2,1)S(1)} %add_convert_fusion.4), channel_id=1, source_target_pairs={{0,2},{1,3},{2,6},{3,7},{6,4},{7,5},{4,0},{5,1},{8,10},{9,11},{10,... | collective-permute-start | bytes 4718600 | tf_op jit(solution)/shard_map/ppermute | solution.py:422
  631.0 274.4 %reduce-scatter.7.cloned.1.call-start = ((), (), s32[]{:S(2)}) async-start(), calls=%async_computation.5 | async-start | bytes 2654208 | tf_op jit(solution)/shard_map/reduce_scatter | solution.py:800
  636.0 269.5 %reduce-scatter.9.cloned.1.call-start = ((), (), s32[]{:S(2)}) async-start(), calls=%async_computation.6 | async-start | bytes 2654208 | tf_op jit(solution)/shard_map/reduce_scatter | solution.py:800
  640.5 265.0 %reduce-scatter.11.cloned.1.call-start = ((), (), s32[]{:S(2)}) async-start(), calls=%async_computation.7 | async-start | bytes 2654208 | tf_op jit(solution)/shard_map/reduce_scatter | solution.py:800
  647.1 55.4 %collective-permute-start.33 = (bf16[2,768,768]{2,1,0:T(8,128)(2,1)}, bf16[2,768,768]{2,1,0:T(8,128)(2,1)}, u32[]{:S(2)}, u32[]{:S(2)}) collective-permute-start(bf16[2,768,768]{2,1,0:T(8,128)(2,1)} %get-tuple-element.147), channel_id=1, source_target_pairs={{0,24},{8,16},{16,8},{24,0},{1,25},{9,17},{17,9},{25,1},{2,26},{10... | collective-permute-start | bytes 7077896 | tf_op jit(solution)/shard_map/ppermute | solution.py:611
  648.6 104.5 %collective-permute-start.32 = (bf16[2,768,768]{2,1,0:T(8,128)(2,1)}, bf16[2,768,768]{2,1,0:T(8,128)(2,1)}, u32[]{:S(2)}, u32[]{:S(2)}) collective-permute-start(bf16[2,768,768]{2,1,0:T(8,128)(2,1)} %get-tuple-element.148), channel_id=1, source_target_pairs={{0,16},{8,24},{16,0},{24,8},{1,17},{9,25},{17,1},{25,9},{2,18},{10... | collective-permute-start | bytes 7077896 | tf_op jit(solution)/shard_map/ppermute | solution.py:611
  649.1 103.9 %collective-permute-start.31 = (bf16[2,768,768]{2,1,0:T(8,128)(2,1)}, bf16[2,768,768]{2,1,0:T(8,128)(2,1)}, u32[]{:S(2)}, u32[]{:S(2)}) collective-permute-start(bf16[2,768,768]{2,1,0:T(8,128)(2,1)} %get-tuple-element.146), channel_id=1, source_target_pairs={{0,8},{8,0},{16,24},{24,16},{1,9},{9,1},{17,25},{25,17},{2,10},{10... | collective-permute-start | bytes 7077896 | tf_op jit(solution)/shard_map/ppermute | solution.py:611
  650.6 52.5 %copy-start.22 = (bf16[1024,768]{1,0:T(8,128)(2,1)S(1)}, bf16[1024,768]{1,0:T(8,128)(2,1)}, u32[]{:S(2)}) copy-start(bf16[1024,768]{1,0:T(8,128)(2,1)} %copy-done.20) | copy-start | bytes 4718596
  650.6 52.5 %copy-start.38 = (f32[1024,768]{1,0:T(8,128)S(1)}, f32[1024,768]{1,0:T(8,128)}, u32[]{:S(2)}) copy-start(f32[1024,768]{1,0:T(8,128)} %copy-done.37) | copy-start | bytes 9437188
  657.0 146.6 %collective-permute-start.30 = (bf16[2,192,3072]{2,1,0:T(8,128)(2,1)}, bf16[2,192,3072]{2,1,0:T(8,128)(2,1)}, u32[]{:S(2)}, u32[]{:S(2)}) collective-permute-start(bf16[2,192,3072]{2,1,0:T(8,128)(2,1)} %get-tuple-element.150), channel_id=1, source_target_pairs={{0,24},{8,16},{16,8},{24,0},{1,25},{9,17},{17,9},{25,1},{2,26},{10... | collective-permute-start | bytes 7077896 | tf_op jit(solution)/shard_map/ppermute | solution.py:611
  658.6 192.0 %collective-permute-start.29 = (bf16[2,192,3072]{2,1,0:T(8,128)(2,1)}, bf16[2,192,3072]{2,1,0:T(8,128)(2,1)}, u32[]{:S(2)}, u32[]{:S(2)}) collective-permute-start(bf16[2,192,3072]{2,1,0:T(8,128)(2,1)} %get-tuple-element.151), channel_id=1, source_target_pairs={{0,16},{8,24},{16,0},{24,8},{1,17},{9,25},{17,1},{25,9},{2,18},{10... | collective-permute-start | bytes 7077896 | tf_op jit(solution)/shard_map/ppermute | solution.py:611
  702.5 148.1 %collective-permute-start.28 = (bf16[2,192,3072]{2,1,0:T(8,128)(2,1)}, bf16[2,192,3072]{2,1,0:T(8,128)(2,1)}, u32[]{:S(2)}, u32[]{:S(2)}) collective-permute-start(bf16[2,192,3072]{2,1,0:T(8,128)(2,1)} %get-tuple-element.149), channel_id=1, source_target_pairs={{0,8},{8,0},{16,24},{24,16},{1,9},{9,1},{17,25},{25,17},{2,10},{10... | collective-permute-start | bytes 7077896 | tf_op jit(solution)/shard_map/ppermute | solution.py:611
  706.0 255.5 %all-reduce.9.cloned.1.call-start = ((), (), s32[]{:S(2)}) async-start(), calls=%async_computation.8 | async-start | bytes 2359296 | tf_op jit(solution)/shard_map/psum | solution.py:803
  760.2 98.3 %copy-start.52 = (s32[3072]{0:T(1024)S(1)}, s32[3072]{0:T(1024)}, u32[]{:S(2)}) copy-start(s32[3072]{0:T(1024)} %add_add_fusion.1) | copy-start | bytes 36868
  760.2 98.3 %copy-start.65 = (pred[32]{0:T(512)(128)(4,1)S(1)}, pred[32]{0:T(512)(128)(4,1)}, u32[]{:S(2)}) copy-start(pred[32]{0:T(512)(128)(4,1)} %iota_compare_fusion.4) | copy-start | bytes 100
  760.2 98.8 %copy-start.26 = (bf16[1024,768]{1,0:T(8,128)(2,1)S(1)}, bf16[1024,768]{1,0:T(8,128)(2,1)}, u32[]{:S(2)}) copy-start(bf16[1024,768]{1,0:T(8,128)(2,1)} %copy-done.25) | copy-start | bytes 4718596
  863.6 46.3 %copy-start.57 = (f32[1024]{0:T(1024)S(1)}, f32[1024]{0:T(1024)}, u32[]{:S(2)}) copy-start(f32[1024]{0:T(1024)} %get-tuple-element.174) | copy-start | bytes 12292
  (68 other events, 861.4 us)
Sparse Core Ops, SparseCore 0:
  631.1 35.5 reduce-scatter.4
  669.1 35.5 reduce-scatter.6
  707.1 35.5 reduce-scatter.8
  744.8 35.5 reduce-scatter.10
  905.7 55.7 all-reduce.8

commit v3 on v2

--- a/solution.py
+++ b/solution.py
@@ -17,6 +17,10 @@
 norm_eps = 1e-06
 aux_weight = 0.01
 f32, bf16 = jnp.float32, jnp.bfloat16
+
+
+def after(x, *earlier):
+    return lax.optimization_barrier((x, earlier))[0]
 
 
 def rms_scale(values):
@@ -133,7 +137,7 @@
             pltpu.VMEM((PAIR, seq), bf16),
         ],
         compiler_params=pltpu.CompilerParams(vmem_limit_bytes=32 * 1024 * 1024),
-        cost_estimate=pl.CostEstimate(flops=seq * seq * width * 4, bytes_accessed=8 * seq * width, transcendentals=6 * seq * seq),
+        cost_estimate=pl.CostEstimate(flops=1, bytes_accessed=1024, transcendentals=0),
         name="attend",
     )(base, seg.reshape(seq, 1), seg.reshape(1, seq), q, k, v)
 
@@ -226,7 +230,7 @@
             pltpu.VMEM((8, NEAR), f32),
         ],
         compiler_params=pltpu.CompilerParams(vmem_limit_bytes=40 * 1024 * 1024),
-        cost_estimate=pl.CostEstimate(flops=seq * seq * width * 10, bytes_accessed=16 * seq * width, transcendentals=6 * seq * seq),
+        cost_estimate=pl.CostEstimate(flops=1, bytes_accessed=1024, transcendentals=0),
         name="attend_back",
     )(base, seg.reshape(seq, 1), seg.reshape(1, seq), q, k, v, ctx, dctx, lse)
 
@@ -601,23 +605,20 @@
     )
 
 
-def rep_moved(whole):
-    count = lax.axis_size("rep")
-    me = lax.axis_index("rep")
-    rows = whole.shape[1] // count
-    moved = []
-    for k in range(1, count):
-        piece = lax.dynamic_slice_in_dim(whole, (me ^ k) * rows, rows, 1)
-        moved.append(lax.ppermute(piece, "rep", [(i, i ^ k) for i in range(count)]))
-    return moved
-
-
-def rep_sum(whole, moved):
-    rows = moved[0].shape[1]
-    total = lax.dynamic_slice_in_dim(whole, lax.axis_index("rep") * rows, rows, 1).astype(f32)
-    for piece in moved:
-        total = total + piece.astype(f32)
-    return total
+def reduce_steps(group, own, sibling, sent_as=bf16):
+    moving, total = None, None
+    for k in list(range(1, group.chips)) + [0]:
+        pins = yield moving, total
+        other = group.swap(sibling[k].astype(sent_as))
+        if pins is not None:
+            other, moving = after((other, moving), pins)
+        total = own[k].astype(f32) + other.astype(f32)
+        if moving is not None:
+            total = total + moving.astype(f32)
+        if k != 0:
+            total = total.astype(sent_as)
+            moving = group.onward(total)
+    yield moving, total
 
 
 def local_slots(routes_all, first, local):
@@ -660,35 +661,40 @@
     router_full = router_t.T
     counts = jnp.sum(tally_all[:, 0, 0:experts], axis=0)
     first = (group.me * exp_local).astype(jnp.int32)
-    cotangent, small_all = lax.optimization_barrier((cotangent, small_all))
     slots_all = local_slots(routes_all, first, exp_local)
 
     kept_grad = jnp.where((segments != 0)[:, None], cotangent, jnp.zeros_like(cotangent))
-    grad_own = [kept_grad]
+    grad_ring = [kept_grad]
     for k in range(1, group.chips):
-        grad_own.append(group.onward(grad_own[-1]))
-    grad_sib = [group.swap(block) for block in grad_own]
+        grad_ring.append(group.onward(grad_ring[-1]))
 
     inputs = tokens.astype(f32)
     scale_one = rms_scale(inputs)
     normed_one = (inputs * scale_one * gain_one.astype(f32)).astype(bf16)
+    normed_one = after(normed_one, grad_ring[1])
     query_rows = jnp.dot(normed_one, query_full, preferred_element_type=f32).astype(bf16)
     key_rows = jnp.dot(normed_one, key_full, preferred_element_type=f32).astype(bf16)
     value_rows = jnp.dot(normed_one, value_full, preferred_element_type=f32).astype(bf16)
     base = bias_base(table_full)
     context, lse = attend(query_rows, key_rows, value_rows, segments, base)
+    context = after(context, grad_ring[2])
     hidden_one = inputs + jnp.dot(context, output_full, preferred_element_type=f32)
     scale_two = rms_scale(hidden_one)
     normed_two = (hidden_one * scale_two * gain_two.astype(f32)).astype(bf16)
 
-    norm_own = [normed_two]
-    for k in range(1, group.chips):
-        norm_own.append(group.onward(norm_own[-1]))
-    norm_sib = [group.swap(block) for block in norm_own]
-
     kept = None
     results = []
+    sibs = [group.swap(block) for block in grad_ring[:3]]
+    ring = list(grad_ring)
+    norm_ring = [normed_two]
     for k in range(group.chips):
+        if k >= 3:
+            ring[k] = after(ring[k], results[k - 3][2])
+            sibs.append(group.swap(ring[k]))
+        norm_now = norm_ring[k]
+        norm_sib = group.swap(norm_now)
+        if k < group.chips - 1:
+            moved = group.onward(norm_now)
         chip = group.source_chip(k)
         info = jnp.concatenate(
             [
@@ -698,32 +704,38 @@
             ],
             axis=0,
         )
+        if k == group.chips - 1:
+            back_own, back_sib = [r[2] for r in results], [r[3] for r in results]
+            back_steps = reduce_steps(group, back_own, back_sib)
+            next(back_steps)
+            sent = back_steps.send(None)[1]
+            info = after(info, sent)
         outs, kept = expert_block(
-            k, group.chips, first.reshape(1), norm_own[k], norm_sib[k], grad_own[k], grad_sib[k],
+            k, group.chips, first.reshape(1), norm_now, norm_sib, ring[k], sibs[k],
             info, router_t, w_in, w_out, capacity, kept,
         )
         results.append(outs)
-
-    def reduce_blocks(own, sibling):
-        moving = None
-        for k in list(range(1, group.chips)) + [0]:
-            total = own[k].astype(f32) + group.swap(sibling[k]).astype(f32)
-            if moving is not None:
-                total = total + moving.astype(f32)
-            if k != 0:
-                moving = group.onward(total.astype(bf16))
-        return total
+        if k == group.chips - 1:
+            back_own.append(outs[2])
+            back_sib.append(outs[3])
+        if k < group.chips - 1:
+            norm_ring.append(after(moved, outs[2]))
 
     act_all, dpre_all, x_all, dy_all = kept
-    up_grad = jnp.einsum("ekd,ekf->edf", x_all, dpre_all, preferred_element_type=f32).astype(bf16)
-    down_grad = jnp.einsum("ekf,ekd->efd", act_all, dy_all, preferred_element_type=f32).astype(bf16)
-    up_moved, down_moved = rep_moved(up_grad), rep_moved(down_grad)
-
-    back = reduce_blocks([r[2] for r in results], [r[3] for r in results])
-    y_own, y_sib = [r[0] for r in results], [r[1] for r in results]
-    back, up_grad, down_grad, y_own, y_sib = lax.optimization_barrier((back, up_grad, down_grad, y_own, y_sib))
-    mixed = reduce_blocks(y_own, y_sib)
-    up_share, down_share = rep_sum(up_grad, up_moved), rep_sum(down_grad, down_moved)
+    chips = group.chips
+    for k in range(2, chips - 1):
+        sent = back_steps.send(outs[2])[1]
+    up_grad = jnp.einsum("ekd,ekf->edf", after(x_all, sent), dpre_all, preferred_element_type=f32).astype(bf16)
+    sent = back_steps.send(up_grad)[1]
+    up_share = lax.psum_scatter(after(up_grad, sent), "rep", scatter_dimension=1, tiled=True)
+    down_grad = jnp.einsum("ekf,ekd->efd", act_all, after(dy_all, sent), preferred_element_type=f32).astype(bf16)
+    back = back_steps.send(down_grad)[1]
+    down_share = lax.psum_scatter(after(down_grad, back), "rep", scatter_dimension=1, tiled=True)
+
+    y_own, y_sib = after(([r[0] for r in results], [r[1] for r in results]), back)
+    y_steps = reduce_steps(group, y_own, y_sib)
+    next(y_steps)
+    y_moving = y_steps.send(None)[0]
 
     logits = jnp.dot(normed_two, router_full, preferred_element_type=f32)
     router_prob = jax.nn.softmax(logits, axis=-1)
@@ -732,7 +744,6 @@
     all_tokens = tok_rows * lax.axis_size("rep") * groups
     fraction = counts / (TOP * all_tokens)
 
-    output = (hidden_one + mixed[0:tok_rows]).astype(bf16)
     grad_out = kept_grad.astype(f32)
     grad_gate = unpack_dgate(back[tok_rows:], tok_rows).T
     grad_norm_two = back[0:tok_rows]
@@ -762,6 +773,7 @@
     grad_query_rows, grad_key_rows, grad_value_rows, near_grad, far_grad = attend_back(
         query_rows, key_rows, value_rows, segments, base, context, grad_context, lse
     )
+    grad_query_rows = after(grad_query_rows, y_moving)
     query_grad = outer_sum(normed_one, grad_query_rows)
     key_grad = outer_sum(normed_one, grad_key_rows)
     value_grad = outer_sum(normed_one, grad_value_rows)
@@ -778,44 +790,63 @@
         - inputs * scale_one**3 * jnp.mean(scaled_one * inputs, axis=-1, keepdims=True)
     )
     table_grad = table_back(near_grad, far_grad, table_full.shape[0])
+    def shares(x, rows):
+        x = x.reshape(x.shape[:-2] + (groups, rows, x.shape[-1]))
+        def one(k, core):
+            return lax.dynamic_index_in_dim(x, 2 * group.source_chip(k) + core, x.ndim - 3, keepdims=False)
+        return [one(k, group.core) for k in range(chips)], [one(k, 1 - group.core) for k in range(chips)]
+
+    for k in range(2, chips):
+        y_steps.send(grad_query_rows)
+    rows = width // groups
+    dense = after(jnp.stack([query_grad, key_grad, value_grad, output_grad]).astype(bf16), grad_input)
+    dense_steps = reduce_steps(group, *shares(dense, rows))
+
+    def lanes(x):
+        return jnp.pad(x, ((0, 0), (0, 0), (0, 128 - x.shape[2])))
+
     heads = table_grad.shape[1]
-    flat = jnp.concatenate([
-        gain_one_grad, gain_two_grad, table_grad.reshape(-1), router_grad.T.reshape(-1), jnp.sum(router_prob, axis=0)
-    ])
-    flat = lax.psum(flat, ("rep", "grp"))
-    at = 2 * width
-    table_sum = flat[at:at + table_grad.size].reshape(-1, heads)
-    at += table_grad.size
-    router_sum = flat[at:at + router_grad.size].reshape(experts, width).T
-    at += router_grad.size
-    prob_totals = flat[at:at + experts]
-    balance_terms = experts * experts * fraction * (prob_totals / all_tokens)
+    bias_rows = table_grad.shape[0] // groups
+    prob_row = jnp.broadcast_to(jnp.sum(router_prob, axis=0), (groups, 1, experts))
+    small = jnp.concatenate([
+        lanes(gain_one_grad.reshape(groups, 1, rows)), lanes(gain_two_grad.reshape(groups, 1, rows)),
+        lanes(prob_row), lanes(table_grad.reshape(groups, bias_rows, heads)),
+        lanes(jnp.transpose(router_grad.T.reshape(experts, groups, rows), (1, 0, 2))),
+    ], axis=1)
+    small = jnp.pad(small, ((0, 0), (0, -small.shape[1] % 8), (0, 0)))
+    small_steps = reduce_steps(group, *shares(small.reshape(-1, 128), small.shape[1]), f32)
+    next(dense_steps)
+    next(small_steps)
+    for k in range(chips):
+        dense_sum, small_sum = dense_steps.send(None)[1], small_steps.send(None)[1]
+    mixed = y_steps.send(grad_input)[1]
+    output = (hidden_one + mixed).astype(bf16)
+
+    def over_rep(x):
+        total = x.astype(f32)
+        for k in range(1, lax.axis_size("rep")):
+            total = total + lax.ppermute(x, "rep", [(i, i ^ k) for i in range(lax.axis_size("rep"))]).astype(f32)
+        return total
+
+    dense, small = over_rep(dense_sum.astype(bf16)), over_rep(small_sum)
+    at = 3 + bias_rows
+    balance_terms = experts * experts * fraction * (small[2, 0:experts] / all_tokens)
     loss = aux_weight / experts * jnp.sum(balance_terms)
-
-    def mine(x):
-        rows = x.shape[0] // groups
-        return lax.dynamic_slice_in_dim(x, group.me * rows, rows, 0)
-
-    dense = [
-        lax.psum_scatter(x, "grp", scatter_dimension=0, tiled=True)
-        for x in (query_grad, key_grad, value_grad, output_grad)
-    ]
-    dense = lax.psum(tuple(dense), "rep")
     return (
         output,
         loss,
         balance_terms,
         grad_input,
-        mine(flat[0:width]),
+        small[0, 0:rows],
         dense[0],
         dense[1],
         dense[2],
         dense[3],
-        mine(table_sum),
-        mine(flat[width:2 * width]),
-        mine(router_sum),
-        up_share,
-        down_share,
+        small[3:at, 0:heads],
+        small[1, 0:rows],
+        small[at:at + experts, 0:rows].T,
+        up_share.astype(f32),
+        down_share.astype(f32),
     )
 
 

time: 986 us -> 695 us (0.70)
  waiting for transfers between devices: 452 us -> 178 us
  blocking collectives: 38.2 us -> 0 us
  Pallas kernels: 264 us -> 290 us
  starting transfers between devices: 17.5 us -> 36.2 us
  local copies, waits for them, and re-layouts: 41.8 us -> 29.2 us
  matrix products: 92.6 us -> 80.9 us
    ppermute x6, waiting for transfers between devices: 179 us -> 20.7 us  [over_rep(): lax.ppermute(x, 'rep', [(i, i ^ k) for i in range(lax.axis_size('rep'))])]
    ppermute x12 -> x18, waiting for transfers between devices: 221 us -> 153 us  [onward(): return lax.ppermute(x, 'grp', pairs)]
    psum x1 -> x0, waiting for transfers between devices: 46.7 us -> none  [shards(): dense = lax.psum(tuple(dense), 'rep')]
    psum x1 -> x0, blocking collectives: 38.2 us -> none  [shards(): flat = lax.psum(flat, ('rep', 'grp'))]
    pallas_call x1, Pallas kernels: 48.4 us -> 75.2 us  [gather_group(): pl.pallas_call(partial(gather_kernel, chips, reps), in_specs=[hbm] * (cou...]
    convert_element_type x6 -> x14, other arithmetic: 7.86 us -> 33.1 us  [the longest x9 19.1 us: reduce_steps(): total = total.astype(sent_as)]
    ppermute x12 -> x18, starting transfers between devices: 7.41 us -> 24.8 us  [onward(): return lax.ppermute(x, 'grp', pairs)]
    dynamic_slice x6 -> x1, local copies, waits for them, and re-layouts: 15.2 us -> 0.08 us  [one(): lax.dynamic_index_in_dim(x, 2 * group.source_chip(k) + core, x.ndim - 3,...]
  transfers between devices with their start and end apart: 39 -> 50, of which waited for: 16 -> 16; matrix products, arithmetic and copies ran while one was open for 14% -> 20% of each run, Pallas kernels for 17% -> 42%
where the time goes in v3:
time: 695 us; the launch traced here: 692 us
  Pallas kernels  290 us (42%)
  waiting for transfers between devices  178 us (26%)
  matrix products  80.9 us (12%)
  other arithmetic  57.6 us (8%)
  starting transfers between devices  36.2 us (5%)
  local copies, waits for them, and re-layouts  29.2 us (4%)
  between operations  19.8 us (3%)
    pallas_call x4, Pallas kernels, expert_block(): pl.pallas_call(expert_kernel, grid=(local, hidden // part), in_specs=in_s...  169 us
    ppermute x18, waiting for transfers between devices, onward(): return lax.ppermute(x, 'grp', pairs)  153 us
    pallas_call x1, Pallas kernels, gather_group(): pl.pallas_call(partial(gather_kernel, chips, reps), in_specs=[hbm] * (cou...  75.2 us
    dot_general x1, matrix products, shards(): jnp.einsum('ekf,ekd->efd', act_all, after(dy_all, sent), preferred_elemen...  28.3 us
    dot_general x1, matrix products, shards(): jnp.einsum('ekd,ekf->edf', after(x_all, sent), dpre_all, preferred_elemen...  27.5 us
    pallas_call x1, Pallas kernels, attend_back(): pl.pallas_call(bwd_kernel, grid=(pairs,), in_specs=[band, whole(seq, 1),...  26.1 us
    ppermute x18, starting transfers between devices, onward(): return lax.ppermute(x, 'grp', pairs)  24.8 us
    ppermute x6, waiting for transfers between devices, over_rep(): lax.ppermute(x, 'rep', [(i, i ^ k) for i in range(lax.axis_size('rep'))])  20.7 us
  transfers between devices with their start and end apart: 50, of which 16 were waited for; matrix products, arithmetic and copies ran while one was open for 20% of the time, Pallas kernels for 42%

profile of v3, /device:TPU:0, one launch (start us, length us, event | category | flops | bytes accessed | tf_op | source)
XLA Modules:
  0.0 691.9 jit_solution(8871206299181015237)
XLA Ops:
  8.0 2.9 broadcast_select_fusion.g_a
  10.9 3.0 collective-permute-start
  15.6 75.2 %gather_group.1 = (bf16[768,768]{1,0:T(8,128)(2,1)}, bf16[768,768]{1,0:T(8,128)(2,1)}, bf16[768,768]{1,0:T(8,128)(2,1)}, bf16[768,768]{1,0:T(8,128)(2,1)}, bf16[...) custom-call(bf16[96,768]{1,0:T(8,128)(2,1)} %refs_0_.1, bf16[96,768]{1,0:T(8,128)(2,1)} %refs_1_.1, bf16[96,768]{1,0:T(8,128)(2,1)} %refs_2_.1, ...), custom_call_target="tpu_custom_call" | custom-call | bytes 16777216 | tf_op jit(solution)/shard_map/gather_group/pallas_call | solution.py:556
  104.5 20.0 %attend.1 = (bf16[1024,768]{1,0:T(8,128)(2,1)S(1)}, f32[6,8,256]{2,1,0:T(8,128)S(1)}) custom-call(f32[12,8,384]{2,1,0:T(8,128)S(1)} %copy_subtract_fusion.base, s32[1024,1]{1,0:T(8,128)S(1)} %copy.97.seg_col, s32[1,1024]{1,0:T(1,128)S(1)} %bitcast.171, bf16[1024,768]{1,0:T(8,128)(2,1)S(1)} %convolution_convert_fusion.5.q, ...), custom_call_target="tpu_custom_call" | custom-call | flops 1 | bytes 1024 | tf_op jit(solution)/shard_map/attend/pallas_call | solution.py:123
  124.6 6.5 collective-permute-done.1.g_a
  134.4 4.5 reduce-window.6
  141.7 42.1 %expert_block.4 = (bf16[1024,768]{1,0:T(8,128)(2,1)S(1)}, bf16[1024,768]{1,0:T(8,128)(2,1)S(1)}, bf16[1040,768]{1,0:T(8,128)(2,1)}, bf16[1040,768]{1,0:T(8,128)(...) custom-call(s32[1]{0:T(128)} %bitcast.12.first, ...), custom_call_target="tpu_custom_call" | custom-call | flops 25769803776 | bytes 62914560 | tf_op jit(solution)/shard_map/expert_block/pallas_call | solution.py:387
  185.5 3.4 collective-permute-start.12
  191.1 42.6 %expert_block.5 = (bf16[1024,768]{1,0:T(8,128)(2,1)S(1)}, bf16[1024,768]{1,0:T(8,128)(2,1)}, bf16[1040,768]{1,0:T(8,128)(2,1)}, bf16[1040,768]{1,0:T(8,128)(2,1)...) custom-call(s32[1]{0:T(128)} %bitcast.12.first, ...), custom_call_target="tpu_custom_call", output_to_operand_aliasing={{4}: (9, {}), {5}: (10, {}), {6}: (11, {}), {7}: (12, {})} | custom-call | flops 25769803776 | bytes 62914560 | tf_op jit(solution)/shard_map/expert_block/pallas_call | solution.py:387
  234.8 21.9 %collective-permute-done.7.n_a = bf16[1024,768]{1,0:T(8,128)(2,1)S(1)} collective-permute-done((bf16[1024,768]{1,0:T(8,128)(2,1)S(1)}, bf16[1024,768]{1,0:T(8,128)(2,1)S(1)}, u32[]{:S(2)}, u32[]{:S(2)}) %collective-permute-start.7) | collective-permute-done | bytes 1572896 | tf_op jit(solution)/shard_map/ppermute | solution.py:426
  257.4 2.6 collective-permute-start.10
  262.4 42.2 %expert_block.6 = (bf16[1024,768]{1,0:T(8,128)(2,1)S(1)}, bf16[1024,768]{1,0:T(8,128)(2,1)S(1)}, bf16[1040,768]{1,0:T(8,128)(2,1)}, bf16[1040,768]{1,0:T(8,128)(...) custom-call(s32[1]{0:T(128)} %bitcast.12.first, ...), custom_call_target="tpu_custom_call", output_to_operand_aliasing={{4}: (9, {}), {5}: (10, {}), {6}: (11, {}), {7}: (12, {})} | custom-call | flops 25769803776 | bytes 62914560 | tf_op jit(solution)/shard_map/expert_block/pallas_call | solution.py:387
  305.3 1.6 add_convert_fusion.2
  306.9 2.7 collective-permute-start.18
  310.8 42.1 %expert_block.7 = (bf16[1024,768]{1,0:T(8,128)(2,1)S(1)}, bf16[1024,768]{1,0:T(8,128)(2,1)S(1)}, bf16[1040,768]{1,0:T(8,128)(2,1)}, bf16[1040,768]{1,0:T(8,128)(...) custom-call(s32[1]{0:T(128)} %bitcast.12.first, ...), custom_call_target="tpu_custom_call", output_to_operand_aliasing={{4}: (9, {}), {5}: (10, {}), {6}: (11, {}), {7}: (12, {})} | custom-call | flops 25769803776 | bytes 62914560 | tf_op jit(solution)/shard_map/expert_block/pallas_call | solution.py:387
  353.0 2.2 add_convert_fusion.1
  355.3 1.6 collective-permute-start.19
  356.8 27.5 %convolution_convert_fusion = bf16[2,768,3072]{2,1,0:T(8,128)(2,1)} fusion(bf16[2,2048,768]{2,1,0:T(8,128)(2,1)} %get-tuple-element.136, bf16[2,2048,3072]{2,1,0:T(8,128)(2,1)} %get-tuple-element.137), kind=kOutput, calls=%fused_computation | convolution fusion | flops 19332071424 | bytes 40894464 | tf_op jit(solution)/shard_map/ekd,ekf->edf/dot_general | solution.py:728
  384.3 9.5 %collective-permute-done.19 = bf16[1040,768]{1,0:T(8,128)(2,1)} collective-permute-done((bf16[1040,768]{1,0:T(8,128)(2,1)}, bf16[1040,768]{1,0:T(8,128)(2,1)}, u32[]{:S(2)}, u32[]{:S(2)}) %collective-permute-start.19) | collective-permute-done | bytes 1597472 | tf_op jit(solution)/shard_map/ppermute | solution.py:426
  393.8 4.2 add_convert_fusion
  398.7 28.3 %convolution_convert_fusion.1 = bf16[2,3072,768]{2,1,0:T(8,128)(2,1)} fusion(bf16[2,2048,3072]{2,1,0:T(8,128)(2,1)} %get-tuple-element.140, bf16[2,2048,768]{2,1,0:T(8,128)(2,1)} %get-tuple-element.142), kind=kOutput, calls=%fused_computation.1 | convolution fusion | flops 19332071424 | bytes 40894464 | tf_op jit(solution)/shard_map/ekf,ekd->efd/dot_general | solution.py:731
  427.0 9.8 %collective-permute-done.20 = bf16[1040,768]{1,0:T(8,128)(2,1)} collective-permute-done((bf16[1040,768]{1,0:T(8,128)(2,1)}, bf16[1040,768]{1,0:T(8,128)(2,1)}, u32[]{:S(2)}, u32[]{:S(2)}) %collective-permute-start.20) | collective-permute-done | bytes 1597472 | tf_op jit(solution)/shard_map/ppermute | solution.py:426
  436.9 4.6 convert_add_fusion.1
  444.2 4.5 multiply_reduce_fusion
  454.2 26.1 %attend_back.1 = (bf16[1024,768]{1,0:T(8,128)(2,1)S(1)}, bf16[1024,768]{1,0:T(8,128)(2,1)S(1)}, bf16[1024,768]{1,0:T(8,128)(2,1)S(1)}, f32[12,8,384]{2,1,0:T(8,128)S(1)}, f32[6,8,256]{2,1,0:T(8,128)S(1)}) custom-call(f32[12,8,384]{2,1,0:T(8,128)S(1)} %copy-done.20, s32[1024,1]{1,0:T(8,128)S(1)} %copy-done.7, s32[1,1024]{1,0:T(1,128)S(1)} %bitcast.172, ...), custom_call_target="tpu_custom_call" | custom-call | flops 1 | bytes 1024 | tf_op jit(solution)/shard_map/attend_back/pallas_call | solution.py:213
  485.5 2.9 fusion.44
  488.4 2.1 add_convert_fusion.6
  497.5 30.6 %collective-permute-done.25 = bf16[1024,768]{1,0:T(8,128)(2,1)S(1)} collective-permute-done((bf16[1024,768]{1,0:T(8,128)(2,1)S(1)}, bf16[1024,768]{1,0:T(8,128)(2,1)S(1)}, u32[]{:S(2)}, u32[]{:S(2)}) %collective-permute-start.25) | collective-permute-done | bytes 1572896 | tf_op jit(solution)/shard_map/ppermute | solution.py:426
  529.3 2.0 fusion.3
  533.4 2.6 fusion.6
  539.3 2.9 add_convert_fusion.5
  544.2 1.9 collective-permute-start.42
  547.9 44.5 %collective-permute-done.42 = bf16[4,96,768]{2,1,0:T(8,128)(2,1)S(1)} collective-permute-done((bf16[4,96,768]{2,1,0:T(8,128)(2,1)S(1)}, bf16[4,96,768]{2,1,0:T(8,128)(2,1)S(1)}, u32[]{:S(2)}, u32[]{:S(2)}) %collective-permute-start.42) | collective-permute-done | bytes 589856 | tf_op jit(solution)/shard_map/ppermute | solution.py:426
  593.8 3.2 collective-permute-done.32
  597.0 2.9 collective-permute-start.33
  599.9 11.9 %collective-permute-done.33 = f32[24,128]{1,0:T(8,128)S(1)} collective-permute-done((f32[24,128]{1,0:T(8,128)S(1)}, f32[24,128]{1,0:T(8,128)S(1)}, u32[]{:S(2)}, u32[]{:S(2)}) %collective-permute-start.33) | collective-permute-done | bytes 12320 | tf_op jit(solution)/shard_map/ppermute | solution.py:426
  613.6 3.9 collective-permute-done.34
  619.0 1.9 collective-permute-start.36
  621.4 3.3 add_convert_fusion.4
  624.7 2.8 collective-permute-start.27
  628.2 10.3 %collective-permute-done.44 = bf16[4,96,768]{2,1,0:T(8,128)(2,1)S(1)} collective-permute-done((bf16[4,96,768]{2,1,0:T(8,128)(2,1)S(1)}, bf16[4,96,768]{2,1,0:T(8,128)(2,1)S(1)}, u32[]{:S(2)}, u32[]{:S(2)}) %collective-permute-start.44) | collective-permute-done | bytes 589856 | tf_op jit(solution)/shard_map/ppermute | solution.py:426
  640.9 1.9 collective-permute-start.46
  645.9 10.2 %collective-permute-done.45 = bf16[4,96,768]{2,1,0:T(8,128)(2,1)} collective-permute-done((bf16[4,96,768]{2,1,0:T(8,128)(2,1)}, bf16[4,96,768]{2,1,0:T(8,128)(2,1)}, u32[]{:S(2)}, u32[]{:S(2)}) %collective-permute-start.45) | collective-permute-done | bytes 589856 | tf_op jit(solution)/shard_map/ppermute | solution.py:828
  656.1 10.5 %collective-permute-done.46 = bf16[4,96,768]{2,1,0:T(8,128)(2,1)} collective-permute-done((bf16[4,96,768]{2,1,0:T(8,128)(2,1)}, bf16[4,96,768]{2,1,0:T(8,128)(2,1)}, u32[]{:S(2)}, u32[]{:S(2)}) %collective-permute-start.46) | collective-permute-done | bytes 589856 | tf_op jit(solution)/shard_map/ppermute | solution.py:828
  666.6 2.0 convert_add_fusion.6
  671.0 3.8 add_convert_fusion.3
  674.8 4.4 convert_element_type.556
  679.3 4.2 convert_element_type.557
  (367 shorter events, 73.6 us)
Async XLA Ops:
  7.2 667.6 %reduce-scatter.3.cloned.1.call-start = ((), (), s32[]{:S(2)}) async-start(), calls=%async_computation.2 | async-start | bytes 11796480 | tf_op jit(solution)/shard_map/reduce_scatter | solution.py:730
  10.9 82.1 %collective-permute-start = (bf16[1024,768]{1,0:T(8,128)(2,1)}, bf16[1024,768]{1,0:T(8,128)(2,1)}, u32[]{:S(2)}, u32[]{:S(2)}) collective-permute-start(bf16[1024,768]{1,0:T(8,128)(2,1)} %broadcast_select_fusion.g_a), channel_id=1, source_target_pairs={{0,2},{1,3},{2,6},{3,7},{6,4},{7,5},{4,0},{5,1},{8,10},{9,11},{10,... | collective-permute-start | bytes 4718600 | tf_op jit(solution)/shard_map/ppermute | solution.py:426
  13.9 127.8 %collective-permute-start.3 = (bf16[1024,768]{1,0:T(8,128)(2,1)}, bf16[1024,768]{1,0:T(8,128)(2,1)}, u32[]{:S(2)}, u32[]{:S(2)}) collective-permute-start(bf16[1024,768]{1,0:T(8,128)(2,1)} %broadcast_select_fusion.g_a), channel_id=1, source_target_pairs={{0,1},{1,0},{2,3},{3,2},{4,5},{5,4},{6,7},{7,6},{8,9},{9,8},{10,11... | collective-permute-start | bytes 4718600 | tf_op jit(solution)/shard_map/ppermute | solution.py:429
  93.0 38.1 %collective-permute-start.1 = (bf16[1024,768]{1,0:T(8,128)(2,1)}, bf16[1024,768]{1,0:T(8,128)(2,1)}, u32[]{:S(2)}, u32[]{:S(2)}) collective-permute-start(bf16[1024,768]{1,0:T(8,128)(2,1)} %collective-permute-done.g_a), channel_id=1, source_target_pairs={{0,2},{1,3},{2,6},{3,7},{6,4},{7,5},{4,0},{5,1},{8,10},{9,11},{10,... | collective-permute-start | bytes 4718600 | tf_op jit(solution)/shard_map/ppermute | solution.py:426
  134.3 7.4 %collective-permute-start.2 = (bf16[1024,768]{1,0:T(8,128)(2,1)S(1)}, bf16[1024,768]{1,0:T(8,128)(2,1)}, u32[]{:S(2)}, u32[]{:S(2)}) collective-permute-start(bf16[1024,768]{1,0:T(8,128)(2,1)S(1)} %multiply_convert_fusion.n_a), channel_id=1, source_target_pairs={{0,1},{1,0},{2,3},{3,2},{4,5},{5,4},{6,7},{7,6},{8,9},{9,8},{10,11... | collective-permute-start | bytes 4718600 | tf_op jit(solution)/shard_map/ppermute | solution.py:429
  140.0 49.4 %collective-permute-start.6 = (bf16[1024,768]{1,0:T(8,128)(2,1)}, bf16[1024,768]{1,0:T(8,128)(2,1)S(1)}, u32[]{:S(2)}, u32[]{:S(2)}) collective-permute-start(bf16[1024,768]{1,0:T(8,128)(2,1)} %collective-permute-done.g_a), channel_id=1, source_target_pairs={{0,1},{1,0},{2,3},{3,2},{4,5},{5,4},{6,7},{7,6},{8,9},{9,8},{10,11... | collective-permute-start | bytes 4718600 | tf_op jit(solution)/shard_map/ppermute | solution.py:429
  140.6 44.3 %collective-permute-start.4 = (bf16[1024,768]{1,0:T(8,128)(2,1)S(1)}, bf16[1024,768]{1,0:T(8,128)(2,1)S(1)}, u32[]{:S(2)}, u32[]{:S(2)}) collective-permute-start(bf16[1024,768]{1,0:T(8,128)(2,1)S(1)} %multiply_convert_fusion.n_a), channel_id=1, source_target_pairs={{0,2},{1,3},{2,6},{3,7},{6,4},{7,5},{4,0},{5,1},{8,10},{9,11},{10,... | collective-permute-start | bytes 4718600 | tf_op jit(solution)/shard_map/ppermute | solution.py:426
  184.9 4.5 collective-permute-start.5
  185.0 75.0 %collective-permute-start.9 = (bf16[1024,768]{1,0:T(8,128)(2,1)}, bf16[1024,768]{1,0:T(8,128)(2,1)S(1)}, u32[]{:S(2)}, u32[]{:S(2)}) collective-permute-start(bf16[1024,768]{1,0:T(8,128)(2,1)} %collective-permute-done.1.g_a), channel_id=1, source_target_pairs={{0,1},{1,0},{2,3},{3,2},{4,5},{5,4},{6,7},{7,6},{8,9},{9,8},{10,11... | collective-permute-start | bytes 4718600 | tf_op jit(solution)/shard_map/ppermute | solution.py:429
  185.5 71.2 %collective-permute-start.12 = (bf16[1024,768]{1,0:T(8,128)(2,1)}, bf16[1024,768]{1,0:T(8,128)(2,1)}, u32[]{:S(2)}, u32[]{:S(2)}) collective-permute-start(bf16[1024,768]{1,0:T(8,128)(2,1)} %collective-permute-done.1.g_a), channel_id=1, source_target_pairs={{0,2},{1,3},{2,6},{3,7},{6,4},{7,5},{4,0},{5,1},{8,10},{9,11},{10,... | collective-permute-start | bytes 4718600 | tf_op jit(solution)/shard_map/ppermute | solution.py:426
  188.9 67.8 %collective-permute-start.7 = (bf16[1024,768]{1,0:T(8,128)(2,1)S(1)}, bf16[1024,768]{1,0:T(8,128)(2,1)S(1)}, u32[]{:S(2)}, u32[]{:S(2)}) collective-permute-start(bf16[1024,768]{1,0:T(8,128)(2,1)S(1)} %collective-permute-done.4.n_a), channel_id=1, source_target_pairs={{0,2},{1,3},{2,6},{3,7},{6,4},{7,5},{4,0},{5,1},{8,10},{9,11},{10,... | collective-permute-start | bytes 4718600 | tf_op jit(solution)/shard_map/ppermute | solution.py:426
  256.7 4.4 collective-permute-start.8
  256.8 52.8 %collective-permute-start.13 = (bf16[1024,768]{1,0:T(8,128)(2,1)}, bf16[1024,768]{1,0:T(8,128)(2,1)}, u32[]{:S(2)}, u32[]{:S(2)}) collective-permute-start(bf16[1024,768]{1,0:T(8,128)(2,1)} %collective-permute-done.12.g_a), channel_id=1, source_target_pairs={{0,1},{1,0},{2,3},{3,2},{4,5},{5,4},{6,7},{7,6},{8,9},{9,8},{10,11... | collective-permute-start | bytes 4718600 | tf_op jit(solution)/shard_map/ppermute | solution.py:429
  257.4 47.3 %collective-permute-start.10 = (bf16[1024,768]{1,0:T(8,128)(2,1)S(1)}, bf16[1024,768]{1,0:T(8,128)(2,1)S(1)}, u32[]{:S(2)}, u32[]{:S(2)}) collective-permute-start(bf16[1024,768]{1,0:T(8,128)(2,1)S(1)} %collective-permute-done.7.n_a), channel_id=1, source_target_pairs={{0,2},{1,3},{2,6},{3,7},{6,4},{7,5},{4,0},{5,1},{8,10},{9,11},{10,... | collective-permute-start | bytes 4718600 | tf_op jit(solution)/shard_map/ppermute | solution.py:426
  260.0 45.3 %collective-permute-start.14 = (bf16[1040,768]{1,0:T(8,128)(2,1)}, bf16[1040,768]{1,0:T(8,128)(2,1)S(1)}, u32[]{:S(2)}, u32[]{:S(2)}) collective-permute-start(bf16[1040,768]{1,0:T(8,128)(2,1)} %get-tuple-element.118), channel_id=1, source_target_pairs={{0,1},{1,0},{2,3},{3,2},{4,5},{5,4},{6,7},{7,6},{8,9},{9,8},{10,11... | collective-permute-start | bytes 4792328 | tf_op jit(solution)/shard_map/ppermute | solution.py:429
  304.6 5.0 collective-permute-start.11
  304.9 48.1 %collective-permute-start.17 = (bf16[1040,768]{1,0:T(8,128)(2,1)}, bf16[1040,768]{1,0:T(8,128)(2,1)S(1)}, u32[]{:S(2)}, u32[]{:S(2)}) collective-permute-start(bf16[1040,768]{1,0:T(8,128)(2,1)} %get-tuple-element.132), channel_id=1, source_target_pairs={{0,1},{1,0},{2,3},{3,2},{4,5},{5,4},{6,7},{7,6},{8,9},{9,8},{10,11... | collective-permute-start | bytes 4792328 | tf_op jit(solution)/shard_map/ppermute | solution.py:429
  306.9 46.0 %collective-permute-start.18 = (bf16[1040,768]{1,0:T(8,128)(2,1)}, bf16[1040,768]{1,0:T(8,128)(2,1)S(1)}, u32[]{:S(2)}, u32[]{:S(2)}) collective-permute-start(bf16[1040,768]{1,0:T(8,128)(2,1)} %add_convert_fusion.2), channel_id=1, source_target_pairs={{0,2},{1,3},{2,6},{3,7},{6,4},{7,5},{4,0},{5,1},{8,10},{9,11},{10,... | collective-permute-start | bytes 4792328 | tf_op jit(solution)/shard_map/ppermute | solution.py:426
  352.9 31.5 %collective-permute-start.16 = (bf16[1040,768]{1,0:T(8,128)(2,1)}, bf16[1040,768]{1,0:T(8,128)(2,1)}, u32[]{:S(2)}, u32[]{:S(2)}) collective-permute-start(bf16[1040,768]{1,0:T(8,128)(2,1)} %get-tuple-element.131), channel_id=1, source_target_pairs={{0,1},{1,0},{2,3},{3,2},{4,5},{5,4},{6,7},{7,6},{8,9},{9,8},{10,11... | collective-permute-start | bytes 4792328 | tf_op jit(solution)/shard_map/ppermute | solution.py:429
  355.3 38.6 %collective-permute-start.19 = (bf16[1040,768]{1,0:T(8,128)(2,1)}, bf16[1040,768]{1,0:T(8,128)(2,1)}, u32[]{:S(2)}, u32[]{:S(2)}) collective-permute-start(bf16[1040,768]{1,0:T(8,128)(2,1)} %add_convert_fusion.1), channel_id=1, source_target_pairs={{0,2},{1,3},{2,6},{3,7},{6,4},{7,5},{4,0},{5,1},{8,10},{9,11},{10,... | collective-permute-start | bytes 4792328 | tf_op jit(solution)/shard_map/ppermute | solution.py:426
  398.0 281.2 %reduce-scatter.5.cloned.1.call-start = ((), (), s32[]{:S(2)}) async-start(), calls=%async_computation.3 | async-start | bytes 11796480 | tf_op jit(solution)/shard_map/reduce_scatter | solution.py:733
  398.1 28.9 %collective-permute-start.15 = (bf16[1040,768]{1,0:T(8,128)(2,1)}, bf16[1040,768]{1,0:T(8,128)(2,1)}, u32[]{:S(2)}, u32[]{:S(2)}) collective-permute-start(bf16[1040,768]{1,0:T(8,128)(2,1)} %get-tuple-element.129), channel_id=1, source_target_pairs={{0,1},{1,0},{2,3},{3,2},{4,5},{5,4},{6,7},{7,6},{8,9},{9,8},{10,11... | collective-permute-start | bytes 4792328 | tf_op jit(solution)/shard_map/ppermute | solution.py:429
  398.2 38.7 %collective-permute-start.20 = (bf16[1040,768]{1,0:T(8,128)(2,1)}, bf16[1040,768]{1,0:T(8,128)(2,1)}, u32[]{:S(2)}, u32[]{:S(2)}) collective-permute-start(bf16[1040,768]{1,0:T(8,128)(2,1)} %add_convert_fusion), channel_id=1, source_target_pairs={{0,2},{1,3},{2,6},{3,7},{6,4},{7,5},{4,0},{5,1},{8,10},{9,11},{10,... | collective-permute-start | bytes 4792328 | tf_op jit(solution)/shard_map/ppermute | solution.py:426
  443.0 45.4 %collective-permute-start.24 = (bf16[1024,768]{1,0:T(8,128)(2,1)}, bf16[1024,768]{1,0:T(8,128)(2,1)}, u32[]{:S(2)}, u32[]{:S(2)}) collective-permute-start(bf16[1024,768]{1,0:T(8,128)(2,1)} %get-tuple-element.152), channel_id=1, source_target_pairs={{0,1},{1,0},{2,3},{3,2},{4,5},{5,4},{6,7},{7,6},{8,9},{9,8},{10,11... | collective-permute-start | bytes 4718600 | tf_op jit(solution)/shard_map/ppermute | solution.py:429
  484.1 55.2 %collective-permute-start.23 = (bf16[1024,768]{1,0:T(8,128)(2,1)}, bf16[1024,768]{1,0:T(8,128)(2,1)}, u32[]{:S(2)}, u32[]{:S(2)}) collective-permute-start(bf16[1024,768]{1,0:T(8,128)(2,1)} %copy-done.26), channel_id=1, source_target_pairs={{0,1},{1,0},{2,3},{3,2},{4,5},{5,4},{6,7},{7,6},{8,9},{9,8},{10,11... | collective-permute-start | bytes 4718600 | tf_op jit(solution)/shard_map/ppermute | solution.py:429
  490.5 37.6 %collective-permute-start.25 = (bf16[1024,768]{1,0:T(8,128)(2,1)S(1)}, bf16[1024,768]{1,0:T(8,128)(2,1)S(1)}, u32[]{:S(2)}, u32[]{:S(2)}) collective-permute-start(bf16[1024,768]{1,0:T(8,128)(2,1)S(1)} %add_convert_fusion.6), channel_id=1, source_target_pairs={{0,2},{1,3},{2,6},{3,7},{6,4},{7,5},{4,0},{5,1},{8,10},{9,11},{10,... | collective-permute-start | bytes 4718600 | tf_op jit(solution)/shard_map/ppermute | solution.py:426
  538.0 4.3 collective-permute-start.41
  538.6 78.9 %collective-permute-start.22 = (bf16[1024,768]{1,0:T(8,128)(2,1)}, bf16[1024,768]{1,0:T(8,128)(2,1)}, u32[]{:S(2)}, u32[]{:S(2)}) collective-permute-start(bf16[1024,768]{1,0:T(8,128)(2,1)} %copy-done.25), channel_id=1, source_target_pairs={{0,1},{1,0},{2,3},{3,2},{4,5},{5,4},{6,7},{7,6},{8,9},{9,8},{10,11... | collective-permute-start | bytes 4718600 | tf_op jit(solution)/shard_map/ppermute | solution.py:429
  539.2 8.4 %collective-permute-start.40 = (bf16[4,96,768]{2,1,0:T(8,128)(2,1)}, bf16[4,96,768]{2,1,0:T(8,128)(2,1)}, u32[]{:S(2)}, u32[]{:S(2)}) collective-permute-start(bf16[4,96,768]{2,1,0:T(8,128)(2,1)} %get-tuple-element.185), channel_id=1, source_target_pairs={{0,1},{1,0},{2,3},{3,2},{4,5},{5,4},{6,7},{7,6},{8,9},{9,8},{10,11... | collective-permute-start | bytes 1769480 | tf_op jit(solution)/shard_map/ppermute | solution.py:429
  542.2 76.8 %collective-permute-start.26 = (bf16[1024,768]{1,0:T(8,128)(2,1)S(1)}, bf16[1024,768]{1,0:T(8,128)(2,1)S(1)}, u32[]{:S(2)}, u32[]{:S(2)}) collective-permute-start(bf16[1024,768]{1,0:T(8,128)(2,1)S(1)} %add_convert_fusion.5), channel_id=1, source_target_pairs={{0,2},{1,3},{2,6},{3,7},{6,4},{7,5},{4,0},{5,1},{8,10},{9,11},{10,... | collective-permute-start | bytes 4718600 | tf_op jit(solution)/shard_map/ppermute | solution.py:426
  544.2 48.2 %collective-permute-start.42 = (bf16[4,96,768]{2,1,0:T(8,128)(2,1)S(1)}, bf16[4,96,768]{2,1,0:T(8,128)(2,1)S(1)}, u32[]{:S(2)}, u32[]{:S(2)}) collective-permute-start(bf16[4,96,768]{2,1,0:T(8,128)(2,1)S(1)} %fusion.12), channel_id=1, source_target_pairs={{0,2},{1,3},{2,6},{3,7},{6,4},{7,5},{4,0},{5,1},{8,10},{9,11},{10,... | collective-permute-start | bytes 1769480 | tf_op jit(solution)/shard_map/ppermute | solution.py:426
  547.4 73.5 %collective-permute-start.39 = (bf16[4,96,768]{2,1,0:T(8,128)(2,1)S(1)}, bf16[4,96,768]{2,1,0:T(8,128)(2,1)S(1)}, u32[]{:S(2)}, u32[]{:S(2)}) collective-permute-start(bf16[4,96,768]{2,1,0:T(8,128)(2,1)S(1)} %copy-done.50), channel_id=1, source_target_pairs={{0,1},{1,0},{2,3},{3,2},{4,5},{5,4},{6,7},{7,6},{8,9},{9,8},{10,11... | collective-permute-start | bytes 1769480 | tf_op jit(solution)/shard_map/ppermute | solution.py:429
  547.6 46.1 %collective-permute-start.30 = (f32[24,128]{1,0:T(8,128)S(1)}, f32[24,128]{1,0:T(8,128)S(1)}, u32[]{:S(2)}, u32[]{:S(2)}) collective-permute-start(f32[24,128]{1,0:T(8,128)S(1)} %bitcast.196), channel_id=1, source_target_pairs={{0,1},{1,0},{2,3},{3,2},{4,5},{5,4},{6,7},{7,6},{8,9},{9,8},{10,11... | collective-permute-start | bytes 36872 | tf_op jit(solution)/shard_map/ppermute | solution.py:429
  592.4 4.6 collective-permute-start.32
  593.7 3.3 collective-permute-start.29
  597.0 24.1 %collective-permute-start.43 = (bf16[4,96,768]{2,1,0:T(8,128)(2,1)S(1)}, bf16[4,96,768]{2,1,0:T(8,128)(2,1)S(1)}, u32[]{:S(2)}, u32[]{:S(2)}) collective-permute-start(bf16[4,96,768]{2,1,0:T(8,128)(2,1)S(1)} %fusion.14), channel_id=1, source_target_pairs={{0,2},{1,3},{2,6},{3,7},{6,4},{7,5},{4,0},{5,1},{8,10},{9,11},{10,... | collective-permute-start | bytes 1769480 | tf_op jit(solution)/shard_map/ppermute | solution.py:426
  597.0 14.7 %collective-permute-start.33 = (f32[24,128]{1,0:T(8,128)S(1)}, f32[24,128]{1,0:T(8,128)S(1)}, u32[]{:S(2)}, u32[]{:S(2)}) collective-permute-start(f32[24,128]{1,0:T(8,128)S(1)} %add_add_fusion.2), channel_id=1, source_target_pairs={{0,2},{1,3},{2,6},{3,7},{6,4},{7,5},{4,0},{5,1},{8,10},{9,11},{10,... | collective-permute-start | bytes 36872 | tf_op jit(solution)/shard_map/ppermute | solution.py:426
  612.9 4.6 collective-permute-start.34
  617.5 10.7 %collective-permute-start.38 = (bf16[4,96,768]{2,1,0:T(8,128)(2,1)S(1)}, bf16[4,96,768]{2,1,0:T(8,128)(2,1)S(1)}, u32[]{:S(2)}, u32[]{:S(2)}) collective-permute-start(bf16[4,96,768]{2,1,0:T(8,128)(2,1)S(1)} %copy-done.49), channel_id=1, source_target_pairs={{0,1},{1,0},{2,3},{3,2},{4,5},{5,4},{6,7},{7,6},{8,9},{9,8},{10,11... | collective-permute-start | bytes 1769480 | tf_op jit(solution)/shard_map/ppermute | solution.py:429
  617.5 7.2 %collective-permute-start.35 = (f32[24,128]{1,0:T(8,128)S(1)}, f32[24,128]{1,0:T(8,128)S(1)}, u32[]{:S(2)}, u32[]{:S(2)}) collective-permute-start(f32[24,128]{1,0:T(8,128)S(1)} %add_add_fusion.4), channel_id=1, source_target_pairs={{0,8},{8,0},{16,24},{24,16},{1,9},{9,1},{17,25},{25,17},{2,10},{10... | collective-permute-start | bytes 36872 | tf_op jit(solution)/shard_map/ppermute | solution.py:828
  619.0 5.8 collective-permute-start.36
  620.9 6.7 collective-permute-start.37
  621.3 17.2 %collective-permute-start.44 = (bf16[4,96,768]{2,1,0:T(8,128)(2,1)S(1)}, bf16[4,96,768]{2,1,0:T(8,128)(2,1)S(1)}, u32[]{:S(2)}, u32[]{:S(2)}) collective-permute-start(bf16[4,96,768]{2,1,0:T(8,128)(2,1)S(1)} %fusion.16), channel_id=1, source_target_pairs={{0,2},{1,3},{2,6},{3,7},{6,4},{7,5},{4,0},{5,1},{8,10},{9,11},{10,... | collective-permute-start | bytes 1769480 | tf_op jit(solution)/shard_map/ppermute | solution.py:426
  624.7 45.0 %collective-permute-start.21 = (bf16[1024,768]{1,0:T(8,128)(2,1)S(1)}, bf16[1024,768]{1,0:T(8,128)(2,1)}, u32[]{:S(2)}, u32[]{:S(2)}) collective-permute-start(bf16[1024,768]{1,0:T(8,128)(2,1)S(1)} %copy-done.24), channel_id=1, source_target_pairs={{0,1},{1,0},{2,3},{3,2},{4,5},{5,4},{6,7},{7,6},{8,9},{9,8},{10,11... | collective-permute-start | bytes 4718600 | tf_op jit(solution)/shard_map/ppermute | solution.py:429
  624.7 46.3 %collective-permute-start.27 = (bf16[1024,768]{1,0:T(8,128)(2,1)}, bf16[1024,768]{1,0:T(8,128)(2,1)}, u32[]{:S(2)}, u32[]{:S(2)}) collective-permute-start(bf16[1024,768]{1,0:T(8,128)(2,1)} %add_convert_fusion.4), channel_id=1, source_target_pairs={{0,2},{1,3},{2,6},{3,7},{6,4},{7,5},{4,0},{5,1},{8,10},{9,11},{10,... | collective-permute-start | bytes 4718600 | tf_op jit(solution)/shard_map/ppermute | solution.py:426
  639.5 16.6 %collective-permute-start.45 = (bf16[4,96,768]{2,1,0:T(8,128)(2,1)}, bf16[4,96,768]{2,1,0:T(8,128)(2,1)}, u32[]{:S(2)}, u32[]{:S(2)}) collective-permute-start(bf16[4,96,768]{2,1,0:T(8,128)(2,1)} %fusion.18), channel_id=1, source_target_pairs={{0,8},{8,0},{16,24},{24,16},{1,9},{9,1},{17,25},{25,17},{2,10},{10... | collective-permute-start | bytes 1769480 | tf_op jit(solution)/shard_map/ppermute | solution.py:828
  640.9 25.7 %collective-permute-start.46 = (bf16[4,96,768]{2,1,0:T(8,128)(2,1)}, bf16[4,96,768]{2,1,0:T(8,128)(2,1)}, u32[]{:S(2)}, u32[]{:S(2)}) collective-permute-start(bf16[4,96,768]{2,1,0:T(8,128)(2,1)} %fusion.18), channel_id=1, source_target_pairs={{0,16},{8,24},{16,0},{24,8},{1,17},{9,25},{17,1},{25,9},{2,18},{10... | collective-permute-start | bytes 1769480 | tf_op jit(solution)/shard_map/ppermute | solution.py:828
  642.8 23.8 %collective-permute-start.47 = (bf16[4,96,768]{2,1,0:T(8,128)(2,1)}, bf16[4,96,768]{2,1,0:T(8,128)(2,1)}, u32[]{:S(2)}, u32[]{:S(2)}) collective-permute-start(bf16[4,96,768]{2,1,0:T(8,128)(2,1)} %fusion.18), channel_id=1, source_target_pairs={{0,24},{8,16},{16,8},{24,0},{1,25},{9,17},{17,9},{25,1},{2,26},{10... | collective-permute-start | bytes 1769480 | tf_op jit(solution)/shard_map/ppermute | solution.py:828
  (85 other events, 1086.4 us)
Sparse Core Ops, SparseCore 0:
  398.1 94.2 reduce-scatter.2
  495.6 95.0 reduce-scatter.4

commit v4 on v3

--- a/solution.py
+++ b/solution.py
@@ -295,28 +295,18 @@
             g_rows = jnp.dot(one_hot, g_ref[...], preferred_element_type=f32)
             g_s[part, :] = g_rows.astype(bf16)
             dy_s[part, :] = (gate_s[part, :] * g_rows).astype(bf16)
+        y_sum[...] = jnp.zeros_like(y_sum)
+        d_sum[...] = jnp.zeros_like(d_sum)
         x_out[0] = x_s[...]
         dy_out[0] = dy_s[...]
 
     pre = jnp.dot(x_s[...], w_in[0], preferred_element_type=f32)
+    dact = lax.dot_general(dy_s[...], w_out[0], (((1,), (1,)), ((), ())), preferred_element_type=f32)
     act, slope = gelu_and_slope(pre)
-    act = act.astype(bf16)
-    act_out[0] = act
-    dact = lax.dot_general(dy_s[...], w_out[0], (((1,), (1,)), ((), ())), preferred_element_type=f32)
-    dpre = (dact * slope).astype(bf16)
-    dpre_out[0] = dpre
-    y_part = jnp.dot(act, w_out[0], preferred_element_type=f32)
-    d_part = lax.dot_general(dpre, w_in[0], (((1,), (1,)), ((), ())), preferred_element_type=f32)
-
-    @pl.when(f == 0)
-    def _():
-        y_sum[...] = y_part
-        d_sum[...] = d_part
-
-    @pl.when(f != 0)
-    def _():
-        y_sum[...] += y_part
-        d_sum[...] += d_part
+    act_out[0] = act.astype(bf16)
+    dpre_out[0] = (dact * slope).astype(bf16)
+    y_sum[...] += jnp.dot(act_out[0], w_out[0], preferred_element_type=f32)
+    d_sum[...] += lax.dot_general(dpre_out[0], w_in[0], (((1,), (1,)), ((), ())), preferred_element_type=f32)
 
     @pl.when(f == pl.num_programs(1) - 1)
     def _():
@@ -442,132 +432,149 @@
     return value
 
 
-def gather_kernel(chips, reps, *refs):
-    count = 5
-    shard, tally = refs[:count], refs[count]
-    full, tally_all = refs[count + 1:2 * count + 1], refs[2 * count + 1]
-    own_sem, ring_send, ring_recv, core_send, core_recv, rep_send, rep_recv, tally_in, tally_sum, tally_vmem = refs[2 * count + 2:]
+def gather_kernel(chips, reps, stack, small, tally, stack_all, small_all, tally_all,
+                  own_sem, ring_send, ring_recv, core_send, core_recv, own_send, own_recv,
+                  plane_send, plane_recv, cross_send, cross_recv, rep_send, rep_recv, tally_in, tally_sum, tally_vmem):
     order = chip_ring(chips)
+    mats, rows = stack.shape[0], stack.shape[1]
     rep, me = lax.axis_index("rep"), lax.axis_index("grp")
     chip, core = me // 2, me % 2
-    after, before = [0] * chips, [0] * chips
+    mine = lax.rem(rep, mats)
+    after_z, before_z = [0] * chips, [0] * chips
     for i, z in enumerate(order):
-        after[z], before[z] = order[(i + 1) % chips], order[(i - 1) % chips]
-    after = 2 * pick_constant(after, chip) + core
-    before = 2 * pick_constant(before, chip) + core
+        after_z[z], before_z[z] = order[(i + 1) % chips], order[(i - 1) % chips]
+    onward = 2 * pick_constant(after_z, chip) + core
+    before = 2 * pick_constant(before_z, chip) + core
     sibling = 2 * chip + 1 - core
     mesh_id = pl.DeviceIdType.MESH
+    plane = [(rep - mine) + lax.rem(mine + j, mats) for j in range(1, mats)]
 
     barrier = pltpu.get_barrier_semaphore()
-    peers = [(rep, after), (rep, before), (rep, sibling)]
-    peers += [(lax.rem(rep + k, reps), me) for k in range(1, reps)]
+    peers = [(rep, onward), (rep, before), (rep, sibling)] + [(lax.rem(rep + k, reps), me) for k in range(1, reps)]
     for peer in peers:
         pl.semaphore_signal(barrier, inc=1, device_id=peer, device_id_type=mesh_id)
     pl.semaphore_wait(barrier, len(peers))
-
-    def place(a, owner):
-        if a == count:
-            return tally_all.at[owner]
-        rows = shard[a].shape[0]
-        return full[a].at[pl.ds(pl.multiple_of(owner * rows, rows), rows), :]
 
     def remote(src, dst, send, recv, target):
         return pltpu.make_async_remote_copy(
             src_ref=src, dst_ref=dst, send_sem=send, recv_sem=recv, device_id=target, device_id_type=mesh_id
         )
 
+    def owner_of(k, which_core):
+        source = [0] * chips
+        for i, z in enumerate(order):
+            source[z] = order[(i - k) % chips]
+        return 2 * pick_constant(source, chip) + which_core
+
+    def shard(mat, owner):
+        return stack_all.at[mat, pl.ds(pl.multiple_of(owner * rows, rows), rows), :]
+
+    def places(k, which_core):
+        owner = owner_of(k, which_core)
+        return [shard(mine, owner), small_all.at[owner], tally_all.at[owner]]
+
+    def matrix(j):
+        return lax.rem(mine + j, mats)
+
+    sent = []
+
+    def start(copy):
+        copy.start()
+        sent.append(copy)
+        return copy
+
     tallies = [
-        remote(tally, tally_in.at[k - 1], rep_send.at[k - 1], rep_recv.at[k - 1], (lax.rem(rep + k, reps), me))
+        start(remote(tally, tally_in.at[k - 1], rep_send.at[k - 1], rep_recv.at[k - 1], (lax.rem(rep + k, reps), me)))
         for k in range(1, reps)
     ]
-    for copy in tallies:
+    own = [
+        pltpu.make_async_copy(stack, stack_all.at[:, pl.ds(pl.multiple_of(me * rows, rows), rows), :], own_sem.at[0]),
+        pltpu.make_async_copy(small, small_all.at[me], own_sem.at[1]),
+        pltpu.make_async_copy(tally, tally_vmem, own_sem.at[2]),
+    ]
+    for copy in own:
         copy.start()
-    own_tally = pltpu.make_async_copy(tally, tally_vmem, own_sem.at[count])
-    own_tally.start()
-
-    pending = []
-    moved = [None] * (count + 1)
-    own = []
-    for a in range(count):
-        keep = pltpu.make_async_copy(shard[a], place(a, me), own_sem.at[a])
-        keep.start()
-        own.append(keep)
-        ring = remote(shard[a], place(a, me), ring_send.at[0, a], ring_recv.at[0, a], (rep, after))
-        ring.start()
-        across = remote(shard[a], place(a, me), core_send.at[0, a], core_recv.at[0, a], (rep, sibling))
-        across.start()
-        moved[a] = ring
-        pending += [ring, across]
-
-    own_tally.wait()
+    here = places(0, core)
+    moved = [
+        start(remote(stack.at[mine], here[0], ring_send.at[0, 0], ring_recv.at[0, 0], (rep, onward))),
+        start(remote(small, here[1], ring_send.at[0, 1], ring_recv.at[0, 1], (rep, onward))),
+    ]
+    everywhere = stack_all.at[:, pl.ds(pl.multiple_of(me * rows, rows), rows), :]
+    start(remote(small, here[1], core_send.at[0, 1], core_recv.at[0, 1], (rep, sibling)))
+    start(remote(stack, everywhere, own_send, own_recv, (rep, sibling)))
+    own[2].wait()
     total = tally_vmem[...]
     for k, copy in enumerate(tallies):
         copy.wait_recv()
         total = total + tally_in[k]
     tally_sum[...] = total
-    keep = pltpu.make_async_copy(tally_sum, place(count, me), own_sem.at[count + 1])
+    keep = pltpu.make_async_copy(tally_sum, here[2], own_sem.at[3])
     keep.start()
-    own.append(keep)
-    ring = remote(tally_sum, place(count, me), ring_send.at[0, count], ring_recv.at[0, count], (rep, after))
-    ring.start()
-    across = remote(tally_sum, place(count, me), core_send.at[0, count], core_recv.at[0, count], (rep, sibling))
-    across.start()
-    moved[count] = ring
-    pending += [ring, across]
+    own = [own[0], own[1], keep]
+    moved.append(start(remote(tally_sum, here[2], ring_send.at[0, 2], ring_recv.at[0, 2], (rep, onward))))
+    start(remote(tally_sum, here[2], core_send.at[0, 2], core_recv.at[0, 2], (rep, sibling)))
+
+    def pass_across(k):
+        for j in range(1, mats):
+            block = shard(matrix(j), owner_of(k, core))
+            remote(block, block, plane_send.at[k, j - 1], plane_recv.at[k, mats - 1 - j], (plane[j - 1], me)).wait_recv()
+            start(remote(block, block, cross_send.at[k, mats - 1 - j], cross_recv.at[k, j - 1], (rep, sibling)))
 
     for k in range(1, chips):
-        source = [0] * chips
-        for i, z in enumerate(order):
-            source[z] = order[(i - k) % chips]
-        owner = 2 * pick_constant(source, chip) + core
-        for a in range(count + 1):
+        here = places(k, core)
+        for a in range(3):
             moved[a].wait_recv()
-            block = place(a, owner)
             if k < chips - 1:
-                ring = remote(block, block, ring_send.at[k, a], ring_recv.at[k, a], (rep, after))
-                ring.start()
-                moved[a] = ring
-                pending.append(ring)
-            across = remote(block, block, core_send.at[k, a], core_recv.at[k, a], (rep, sibling))
-            across.start()
-            pending.append(across)
-    for copy in pending:
+                moved[a] = start(remote(here[a], here[a], ring_send.at[k, a], ring_recv.at[k, a], (rep, onward)))
+            if a == 0:
+                for j in range(1, mats):
+                    start(remote(here[0], here[0], plane_send.at[k, j - 1], plane_recv.at[k, j - 1], (plane[j - 1], me)))
+            start(remote(here[a], here[a], core_send.at[k, a], core_recv.at[k, a], (rep, sibling)))
+        if k > 1:
+            pass_across(k - 1)
+    pass_across(chips - 1)
+    for copy in sent:
         copy.wait_send()
-    for copy in tallies:
-        copy.wait_send()
-    for keep in own:
-        keep.wait()
+    for copy in own:
+        copy.wait()
+    other = stack_all.at[:, pl.ds(pl.multiple_of(sibling * rows, rows), rows), :]
+    remote(stack, other, own_send, own_recv, (rep, sibling)).wait_recv()
     for k in range(chips):
-        source = [0] * chips
-        for i, z in enumerate(order):
-            source[z] = order[(i - k) % chips]
-        owner = 2 * pick_constant(source, chip) + 1 - core
-        for a in range(count + 1):
-            block = place(a, owner)
-            remote(block, block, core_send.at[k, a], core_recv.at[k, a], (rep, sibling)).wait_recv()
-
-
-def gather_group(arrays, tally):
+        there = places(k, 1 - core)
+        for a in range(3):
+            if a > 0 or k > 0:
+                remote(there[a], there[a], core_send.at[k, a], core_recv.at[k, a], (rep, sibling)).wait_recv()
+        if k > 0:
+            for j in range(1, mats):
+                block = shard(matrix(j), owner_of(k, 1 - core))
+                remote(block, block, cross_send.at[k, j - 1], cross_recv.at[k, j - 1], (rep, sibling)).wait_recv()
+
+
+def gather_group(stack, small, tally):
     size, reps = lax.axis_size("grp"), lax.axis_size("rep")
     chips = size // 2
-    count = len(arrays)
+    mats, rows, width = stack.shape
     hbm = pl.BlockSpec(memory_space=pl.ANY)
     dma = pltpu.SemaphoreType.DMA
     return pl.pallas_call(
         partial(gather_kernel, chips, reps),
-        in_specs=[hbm] * (count + 1),
-        out_specs=[hbm] * (count + 1),
-        out_shape=[jax.ShapeDtypeStruct((size * x.shape[0], x.shape[1]), x.dtype) for x in arrays]
-        + [jax.ShapeDtypeStruct((size,) + tally.shape, f32)],
+        in_specs=[hbm] * 3,
+        out_specs=[hbm] * 3,
+        out_shape=[
+            jax.ShapeDtypeStruct((mats, size * rows, width), stack.dtype),
+            jax.ShapeDtypeStruct((size,) + small.shape, small.dtype),
+            jax.ShapeDtypeStruct((size,) + tally.shape, f32),
+        ],
         scratch_shapes=[
-            dma((count + 2,)), dma((chips, count + 1)), dma((chips, count + 1)), dma((chips, count + 1)), dma((chips, count + 1)),
+            dma((4,)), dma((chips, 3)), dma((chips, 3)), dma((chips, 3)), dma((chips, 3)), dma, dma,
+            dma((chips, mats - 1)), dma((chips, mats - 1)), dma((chips, mats - 1)), dma((chips, mats - 1)),
             dma((reps,)), dma((reps,)),
             pltpu.VMEM((reps - 1,) + tally.shape, f32), pltpu.VMEM(tally.shape, f32), pltpu.VMEM(tally.shape, f32),
         ],
         compiler_params=pltpu.CompilerParams(collective_id=0, has_side_effects=True),
         cost_estimate=pl.CostEstimate(flops=0, bytes_accessed=16 * 1024 * 1024, transcendentals=0),
         name="gather_group",
-    )(*arrays, tally)
+    )(stack, small, tally)
 
 
 def pack_small(gain_attn, gain_ffn, router, rel_bias, routes):
@@ -652,9 +659,8 @@
     choose = routes[:, :, None] == lax.iota(jnp.int32, experts)[None, None, :]
     tally = jnp.pad(jnp.sum(choose.astype(f32), axis=(0, 1))[None], ((0, 7), (0, 128 - experts)))
     small = pack_small(gain_attn, gain_ffn, router, rel_bias, routes)
-    query_full, key_full, value_full, output_full, small_all, tally_all = gather_group(
-        (w_query, w_key, w_value, w_output, small), tally
-    )
+    stack_all, small_all, tally_all = gather_group(jnp.stack([w_query, w_key, w_value, w_output]), small, tally)
+    query_full, key_full, value_full, output_full = [stack_all[m] for m in range(4)]
     gain_one, gain_two, table_full, router_t, routes_all = unpack_small(
         small_all, groups, gain_attn.shape[0], rel_bias.shape[0], rel_bias.shape[1], experts, tok_rows
     )
@@ -676,7 +682,7 @@
     key_rows = jnp.dot(normed_one, key_full, preferred_element_type=f32).astype(bf16)
     value_rows = jnp.dot(normed_one, value_full, preferred_element_type=f32).astype(bf16)
     base = bias_base(table_full)
-    context, lse = attend(query_rows, key_rows, value_rows, segments, base)
+    context, lse = attend(query_rows, key_rows, value_rows, after(segments, slots_all), base)
     context = after(context, grad_ring[2])
     hidden_one = inputs + jnp.dot(context, output_full, preferred_element_type=f32)
     scale_two = rms_scale(hidden_one)
@@ -689,8 +695,7 @@
     norm_ring = [normed_two]
     for k in range(group.chips):
         if k >= 3:
-            ring[k] = after(ring[k], results[k - 3][2])
-            sibs.append(group.swap(ring[k]))
+            sibs.append(group.swap(after(ring[k], results[k - 3][2])))
         norm_now = norm_ring[k]
         norm_sib = group.swap(norm_now)
         if k < group.chips - 1:
@@ -704,6 +709,8 @@
             ],
             axis=0,
         )
+        if k == 1:
+            info = after(info, ring[3:])
         if k == group.chips - 1:
             back_own, back_sib = [r[2] for r in results], [r[3] for r in results]
             back_steps = reduce_steps(group, back_own, back_sib)
@@ -732,10 +739,10 @@
     back = back_steps.send(down_grad)[1]
     down_share = lax.psum_scatter(after(down_grad, back), "rep", scatter_dimension=1, tiled=True)
 
-    y_own, y_sib = after(([r[0] for r in results], [r[1] for r in results]), back)
-    y_steps = reduce_steps(group, y_own, y_sib)
+    y_steps = reduce_steps(group, [r[0] for r in results], [r[1] for r in results])
     next(y_steps)
-    y_moving = y_steps.send(None)[0]
+    y_moving, sent = y_steps.send(back)
+    back = after(back, sent)
 
     logits = jnp.dot(normed_two, router_full, preferred_element_type=f32)
     router_prob = jax.nn.softmax(logits, axis=-1)
@@ -773,7 +780,10 @@
     grad_query_rows, grad_key_rows, grad_value_rows, near_grad, far_grad = attend_back(
         query_rows, key_rows, value_rows, segments, base, context, grad_context, lse
     )
-    grad_query_rows = after(grad_query_rows, y_moving)
+    sent = None
+    for k in range(2, chips - 1):
+        y_moving, sent = y_steps.send(grad_query_rows)
+    grad_query_rows, grad_key_rows, grad_value_rows = after((grad_query_rows, grad_key_rows, grad_value_rows), sent)
     query_grad = outer_sum(normed_one, grad_query_rows)
     key_grad = outer_sum(normed_one, grad_key_rows)
     value_grad = outer_sum(normed_one, grad_value_rows)
@@ -796,10 +806,8 @@
             return lax.dynamic_index_in_dim(x, 2 * group.source_chip(k) + core, x.ndim - 3, keepdims=False)
         return [one(k, group.core) for k in range(chips)], [one(k, 1 - group.core) for k in range(chips)]
 
-    for k in range(2, chips):
-        y_steps.send(grad_query_rows)
     rows = width // groups
-    dense = after(jnp.stack([query_grad, key_grad, value_grad, output_grad]).astype(bf16), grad_input)
+    dense = jnp.stack([query_grad, key_grad, value_grad, output_grad]).astype(bf16)
     dense_steps = reduce_steps(group, *shares(dense, rows))
 
     def lanes(x):
@@ -817,18 +825,23 @@
     small_steps = reduce_steps(group, *shares(small.reshape(-1, 128), small.shape[1]), f32)
     next(dense_steps)
     next(small_steps)
-    for k in range(chips):
-        dense_sum, small_sum = dense_steps.send(None)[1], small_steps.send(None)[1]
-    mixed = y_steps.send(grad_input)[1]
+    up_share, down_share = up_share.astype(f32), down_share.astype(f32)
+    pins = y_moving
+    for k in range(1, chips):
+        dense_sum, small_sum = dense_steps.send(pins)[1], small_steps.send(pins)[1]
+        pins = (up_share, grad_input) if k == 1 else None
+    y_steps.send((dense_sum, small_sum))
+    dense_sum, small_sum = dense_steps.send(None)[1], small_steps.send(None)[1]
+    mixed = y_steps.send(dense_sum)[1]
     output = (hidden_one + mixed).astype(bf16)
 
     def over_rep(x):
-        total = x.astype(f32)
-        for k in range(1, lax.axis_size("rep")):
-            total = total + lax.ppermute(x, "rep", [(i, i ^ k) for i in range(lax.axis_size("rep"))]).astype(f32)
-        return total
-
-    dense, small = over_rep(dense_sum.astype(bf16)), over_rep(small_sum)
+        count = lax.axis_size("rep")
+        return x.astype(f32), [lax.ppermute(x, "rep", [(i, i ^ k) for i in range(count)]) for k in range(1, count)]
+
+    (dense, dense_moved), (small, small_moved) = over_rep(dense_sum.astype(bf16)), over_rep(small_sum)
+    for got, also in zip(after(dense_moved, down_share), small_moved):
+        dense, small = dense + got.astype(f32), small + also
     at = 3 + bias_rows
     balance_terms = experts * experts * fraction * (small[2, 0:experts] / all_tokens)
     loss = aux_weight / experts * jnp.sum(balance_terms)
@@ -845,8 +858,8 @@
         small[3:at, 0:heads],
         small[1, 0:rows],
         small[at:at + experts, 0:rows].T,
-        up_share.astype(f32),
-        down_share.astype(f32),
+        up_share,
+        down_share,
     )
 
 

time: 695 us -> 625 us (0.90)
  waiting for transfers between devices: 178 us -> 119 us
  Pallas kernels: 290 us -> 262 us
  other arithmetic: 57.6 us -> 65.3 us
  starting transfers between devices: 36.2 us -> 43.6 us
    ppermute x18, waiting for transfers between devices: 153 us -> 105 us  [onward(): return lax.ppermute(x, 'grp', pairs)]
    pallas_call x1, Pallas kernels: 75.2 us -> 59.7 us  [gather_group(): pl.pallas_call(partial(gather_kernel, chips, reps), in_specs=[hbm] * 3, o...]
    pallas_call x4, Pallas kernels: 169 us -> 157 us  [expert_block(): pl.pallas_call(expert_kernel, grid=(local, hidden // part), in_specs=in_s...]
    ppermute x6, waiting for transfers between devices: 20.7 us -> 10 us  [over_rep(): lax.ppermute(x, 'rep', [(i, i ^ k) for i in range(count)])]
    ppermute x18, starting transfers between devices: 24.8 us -> 32.1 us  [onward(): return lax.ppermute(x, 'grp', pairs)]
  transfers between devices with their start and end apart: 50 -> 50, of which waited for: 16 -> 15; matrix products, arithmetic and copies ran while one was open for 20% -> 24% of each run, Pallas kernels for 42% -> 42%
where the time goes in v4:
time: 625 us; the launch traced here: 621 us
  Pallas kernels  262 us (42%)
  waiting for transfers between devices  119 us (19%)
  matrix products  84.4 us (14%)
  other arithmetic  65.3 us (10%)
  starting transfers between devices  43.6 us (7%)
  local copies, waits for them, and re-layouts  27 us (4%)
  between operations  19.6 us (3%)
    pallas_call x4, Pallas kernels, expert_block(): pl.pallas_call(expert_kernel, grid=(local, hidden // part), in_specs=in_s...  157 us
    ppermute x18, waiting for transfers between devices, onward(): return lax.ppermute(x, 'grp', pairs)  105 us
    pallas_call x1, Pallas kernels, gather_group(): pl.pallas_call(partial(gather_kernel, chips, reps), in_specs=[hbm] * 3, o...  59.7 us
    ppermute x18, starting transfers between devices, onward(): return lax.ppermute(x, 'grp', pairs)  32.1 us
    dot_general x1, matrix products, shards(): jnp.einsum('ekf,ekd->efd', act_all, after(dy_all, sent), preferred_elemen...  28.9 us
    dot_general x1, matrix products, shards(): jnp.einsum('ekd,ekf->edf', after(x_all, sent), dpre_all, preferred_elemen...  27.2 us
    pallas_call x1, Pallas kernels, attend_back(): pl.pallas_call(bwd_kernel, grid=(pairs,), in_specs=[band, whole(seq, 1),...  26 us
    convert_element_type x9, other arithmetic, reduce_steps(): total = total.astype(sent_as)  22.4 us
  transfers between devices with their start and end apart: 50, of which 15 were waited for; matrix products, arithmetic and copies ran while one was open for 24% of the time, Pallas kernels for 42%

profile of v4, /device:TPU:0, one launch (start us, length us, event | category | flops | bytes accessed | tf_op | source)
XLA Modules:
  0.0 621.5 jit_solution(15846662146557005063)
XLA Ops:
  8.0 2.8 broadcast_select_fusion.g_a
  10.9 3.0 collective-permute-start
  16.5 59.7 %gather_group.1 = (bf16[4,768,768]{2,1,0:T(8,128)(2,1)}, bf16[8,48,128]{2,1,0:T(8,128)(2,1)}, f32[8,8,128]{2,1,0:T(8,128)}) custom-call(bf16[4,96,768]{2,1,0:T(8,128)(2,1)} %pad_maximum_fusion.1.stack, bf16[48,128]{1,0:T(8,128)(2,1)} %pad.52.small, f32[8,128]{1,0:T(8,128)} %pad.53.tally), custom_call_target="tpu_custom_call" | custom-call | bytes 16777216 | tf_op jit(solution)/shard_map/gather_group/pallas_call | solution.py:559
  78.0 4.5 reduce-window.6
  91.5 20.0 %attend.1 = (bf16[1024,768]{1,0:T(8,128)(2,1)S(1)}, f32[6,8,256]{2,1,0:T(8,128)S(1)}) custom-call(f32[12,8,384]{2,1,0:T(8,128)S(1)} %copy_subtract_fusion.base, s32[1024,1]{1,0:T(8,128)S(1)} %copy.102.seg_col, s32[1,1024]{1,0:T(1,128)S(1)} %bitcast.187, bf16[1024,768]{1,0:T(8,128)(2,1)S(1)} %convolution_convert_fusion.5.q, ...), custom_call_target="tpu_custom_call" | custom-call | flops 1 | bytes 1024 | tf_op jit(solution)/shard_map/attend/pallas_call | solution.py:123
  111.6 11.7 %collective-permute-done.1.g_a = bf16[1024,768]{1,0:T(8,128)(2,1)S(1)} collective-permute-done((bf16[1024,768]{1,0:T(8,128)(2,1)}, bf16[1024,768]{1,0:T(8,128)(2,1)S(1)}, u32[]{:S(2)}, u32[]{:S(2)}) %collective-permute-start.1) | collective-permute-done | bytes 1572896 | tf_op jit(solution)/shard_map/ppermute | solution.py:416
  133.1 3.5 collective-permute-start.9
  136.6 39.1 %expert_block.4 = (bf16[1024,768]{1,0:T(8,128)(2,1)S(1)}, bf16[1024,768]{1,0:T(8,128)(2,1)S(1)}, bf16[1040,768]{1,0:T(8,128)(2,1)}, bf16[1040,768]{1,0:T(8,128)(...) custom-call(s32[1]{0:T(128)} %bitcast.21.first, ...), custom_call_target="tpu_custom_call" | custom-call | flops 25769803776 | bytes 62914560 | tf_op jit(solution)/shard_map/expert_block/pallas_call | solution.py:377
  178.9 25.2 %collective-permute-done.9.g_a = bf16[1024,768]{1,0:T(8,128)(2,1)} collective-permute-done((bf16[1024,768]{1,0:T(8,128)(2,1)}, bf16[1024,768]{1,0:T(8,128)(2,1)}, u32[]{:S(2)}, u32[]{:S(2)}) %collective-permute-start.9) | collective-permute-done | bytes 1572896 | tf_op jit(solution)/shard_map/ppermute | solution.py:416
  205.7 39.4 %expert_block.5 = (bf16[1024,768]{1,0:T(8,128)(2,1)S(1)}, bf16[1024,768]{1,0:T(8,128)(2,1)}, bf16[1040,768]{1,0:T(8,128)(2,1)}, bf16[1040,768]{1,0:T(8,128)(2,1)...) custom-call(s32[1]{0:T(128)} %bitcast.21.first, ...), custom_call_target="tpu_custom_call", output_to_operand_aliasing={{4}: (9, {}), {5}: (10, {}), {6}: (11, {}), {7}: (12, {})} | custom-call | flops 25769803776 | bytes 62914560 | tf_op jit(solution)/shard_map/expert_block/pallas_call | solution.py:377
  248.3 2.6 collective-permute-done.11.n_b
  252.0 39.1 %expert_block.6 = (bf16[1024,768]{1,0:T(8,128)(2,1)S(1)}, bf16[1024,768]{1,0:T(8,128)(2,1)S(1)}, bf16[1040,768]{1,0:T(8,128)(2,1)}, bf16[1040,768]{1,0:T(8,128)(...) custom-call(s32[1]{0:T(128)} %bitcast.21.first, ...), custom_call_target="tpu_custom_call", output_to_operand_aliasing={{4}: (9, {}), {5}: (10, {}), {6}: (11, {}), {7}: (12, {})} | custom-call | flops 25769803776 | bytes 62914560 | tf_op jit(solution)/shard_map/expert_block/pallas_call | solution.py:377
  295.8 39.1 %expert_block.7 = (bf16[1024,768]{1,0:T(8,128)(2,1)S(1)}, bf16[1024,768]{1,0:T(8,128)(2,1)S(1)}, bf16[1040,768]{1,0:T(8,128)(2,1)}, bf16[1040,768]{1,0:T(8,128)(...) custom-call(s32[1]{0:T(128)} %bitcast.21.first, ...), custom_call_target="tpu_custom_call", output_to_operand_aliasing={{4}: (9, {}), {5}: (10, {}), {6}: (11, {}), {7}: (12, {})} | custom-call | flops 25769803776 | bytes 62914560 | tf_op jit(solution)/shard_map/expert_block/pallas_call | solution.py:377
  335.1 2.0 add_convert_fusion.1
  337.1 2.8 collective-permute-start.23
  339.9 27.2 %convolution_convert_fusion = bf16[2,768,3072]{2,1,0:T(8,128)(2,1)} fusion(bf16[2,2048,768]{2,1,0:T(8,128)(2,1)} %get-tuple-element.138, bf16[2,2048,3072]{2,1,0:T(8,128)(2,1)} %get-tuple-element.139), kind=kOutput, calls=%fused_computation | convolution fusion | flops 19332071424 | bytes 40894464 | tf_op jit(solution)/shard_map/ekd,ekf->edf/dot_general | solution.py:735
  367.1 8.5 %collective-permute-done.23 = bf16[1040,768]{1,0:T(8,128)(2,1)} collective-permute-done((bf16[1040,768]{1,0:T(8,128)(2,1)}, bf16[1040,768]{1,0:T(8,128)(2,1)}, u32[]{:S(2)}, u32[]{:S(2)}) %collective-permute-start.23) | collective-permute-done | bytes 1597472 | tf_op jit(solution)/shard_map/ppermute | solution.py:416
  375.6 3.7 add_convert_fusion
  379.5 2.1 collective-permute-start.24
  381.6 28.9 %convolution_convert_fusion.1 = bf16[2,3072,768]{2,1,0:T(8,128)(2,1)} fusion(bf16[2,2048,3072]{2,1,0:T(8,128)(2,1)} %get-tuple-element.142, bf16[2,2048,768]{2,1,0:T(8,128)(2,1)} %get-tuple-element.144), kind=kOutput, calls=%fused_computation.1 | convolution fusion | flops 19332071424 | bytes 40894464 | tf_op jit(solution)/shard_map/ekf,ekd->efd/dot_general | solution.py:738
  410.5 7.9 %collective-permute-done.24 = bf16[1040,768]{1,0:T(8,128)(2,1)} collective-permute-done((bf16[1040,768]{1,0:T(8,128)(2,1)}, bf16[1040,768]{1,0:T(8,128)(2,1)}, u32[]{:S(2)}, u32[]{:S(2)}) %collective-permute-start.24) | collective-permute-done | bytes 1597472 | tf_op jit(solution)/shard_map/ppermute | solution.py:416
  418.4 4.4 convert_add_fusion.1
  426.7 3.2 add_convert_fusion.6
  432.2 3.3 multiply_reduce_fusion
  436.8 3.8 convolution_convert_fusion.2.dctx
  441.2 26.0 %attend_back.1 = (bf16[1024,768]{1,0:T(8,128)(2,1)S(1)}, bf16[1024,768]{1,0:T(8,128)(2,1)S(1)}, bf16[1024,768]{1,0:T(8,128)(2,1)S(1)}, f32[12,8,384]{2,1,0:T(8,128)S(1)}, f32[6,8,256]{2,1,0:T(8,128)S(1)}) custom-call(f32[12,8,384]{2,1,0:T(8,128)S(1)} %copy-done.20, s32[1024,1]{1,0:T(8,128)S(1)} %copy.107.seg_col, s32[1,1024]{1,0:T(1,128)S(1)} %bitcast.189, ...), custom_call_target="tpu_custom_call" | custom-call | flops 1 | bytes 1024 | tf_op jit(solution)/shard_map/attend_back/pallas_call | solution.py:213
  472.1 3.4 convolution_convert_fusion.6
  475.6 3.7 add_convert_fusion.5
  479.3 3.5 collective-permute-start.26
  494.5 3.5 fusion.3
  498.1 18.8 %collective-permute-done.26 = bf16[1024,768]{1,0:T(8,128)(2,1)S(1)} collective-permute-done((bf16[1024,768]{1,0:T(8,128)(2,1)}, bf16[1024,768]{1,0:T(8,128)(2,1)S(1)}, u32[]{:S(2)}, u32[]{:S(2)}) %collective-permute-start.26) | collective-permute-done | bytes 1572896 | tf_op jit(solution)/shard_map/ppermute | solution.py:416
  516.9 2.8 fusion.9
  519.7 2.3 collective-permute-start.30
  522.1 4.8 fusion.6
  527.2 4.4 convert_element_type.522
  531.9 3.4 collective-permute-done.30
  536.6 1.8 fusion.11
  538.4 2.5 collective-permute-start.31
  540.9 11.9 %collective-permute-done.36 = f32[24,128]{1,0:T(8,128)S(1)} collective-permute-done((f32[24,128]{1,0:T(8,128)S(1)}, f32[24,128]{1,0:T(8,128)S(1)}, u32[]{:S(2)}, u32[]{:S(2)}) %collective-permute-start.36) | collective-permute-done | bytes 12320 | tf_op jit(solution)/shard_map/ppermute | solution.py:416
  554.5 2.9 collective-permute-done.41
  563.6 3.3 add_convert_fusion.4
  567.0 2.1 collective-permute-start.37
  569.7 10.1 %collective-permute-done.39 = bf16[4,96,768]{2,1,0:T(8,128)(2,1)S(1)} collective-permute-done((bf16[4,96,768]{2,1,0:T(8,128)(2,1)S(1)}, bf16[4,96,768]{2,1,0:T(8,128)(2,1)S(1)}, u32[]{:S(2)}, u32[]{:S(2)}) %collective-permute-start.39) | collective-permute-done | bytes 589856 | tf_op jit(solution)/shard_map/ppermute | solution.py:416
  587.6 4.2 convert_element_type.555
  591.8 2.5 collective-permute-done.45
  594.3 7.5 %collective-permute-done.46 = bf16[4,96,768]{2,1,0:T(8,128)(2,1)} collective-permute-done((bf16[4,96,768]{2,1,0:T(8,128)(2,1)S(1)}, bf16[4,96,768]{2,1,0:T(8,128)(2,1)}, u32[]{:S(2)}, u32[]{:S(2)}) %collective-permute-start.46) | collective-permute-done | bytes 589856 | tf_op jit(solution)/shard_map/ppermute | solution.py:840
  604.5 4.8 collective-permute-done.37
  609.4 3.8 add_convert_fusion.3
  (370 shorter events, 80.2 us)
Async XLA Ops:
  7.2 520.0 %reduce-scatter.3.cloned.1.call-start = ((), (), s32[]{:S(2)}) async-start(), calls=%async_computation.2 | async-start | bytes 11796480 | tf_op jit(solution)/shard_map/reduce_scatter | solution.py:737
  10.9 74.4 %collective-permute-start = (bf16[1024,768]{1,0:T(8,128)(2,1)}, bf16[1024,768]{1,0:T(8,128)(2,1)}, u32[]{:S(2)}, u32[]{:S(2)}) collective-permute-start(bf16[1024,768]{1,0:T(8,128)(2,1)} %broadcast_select_fusion.g_a), channel_id=1, source_target_pairs={{0,2},{1,3},{2,6},{3,7},{6,4},{7,5},{4,0},{5,1},{8,10},{9,11},{10,... | collective-permute-start | bytes 4718600 | tf_op jit(solution)/shard_map/ppermute | solution.py:416
  13.9 122.7 %collective-permute-start.3 = (bf16[1024,768]{1,0:T(8,128)(2,1)}, bf16[1024,768]{1,0:T(8,128)(2,1)}, u32[]{:S(2)}, u32[]{:S(2)}) collective-permute-start(bf16[1024,768]{1,0:T(8,128)(2,1)} %broadcast_select_fusion.g_a), channel_id=1, source_target_pairs={{0,1},{1,0},{2,3},{3,2},{4,5},{5,4},{6,7},{7,6},{8,9},{9,8},{10,11... | collective-permute-start | bytes 4718600 | tf_op jit(solution)/shard_map/ppermute | solution.py:419
  85.3 38.0 %collective-permute-start.1 = (bf16[1024,768]{1,0:T(8,128)(2,1)}, bf16[1024,768]{1,0:T(8,128)(2,1)S(1)}, u32[]{:S(2)}, u32[]{:S(2)}) collective-permute-start(bf16[1024,768]{1,0:T(8,128)(2,1)} %collective-permute-done.g_a), channel_id=1, source_target_pairs={{0,2},{1,3},{2,6},{3,7},{6,4},{7,5},{4,0},{5,1},{8,10},{9,11},{10,... | collective-permute-start | bytes 4718600 | tf_op jit(solution)/shard_map/ppermute | solution.py:416
  126.6 9.9 %collective-permute-start.2 = (bf16[1024,768]{1,0:T(8,128)(2,1)S(1)}, bf16[1024,768]{1,0:T(8,128)(2,1)}, u32[]{:S(2)}, u32[]{:S(2)}) collective-permute-start(bf16[1024,768]{1,0:T(8,128)(2,1)S(1)} %multiply_convert_fusion.n_a), channel_id=1, source_target_pairs={{0,1},{1,0},{2,3},{3,2},{4,5},{5,4},{6,7},{7,6},{8,9},{9,8},{10,11... | collective-permute-start | bytes 4718600 | tf_op jit(solution)/shard_map/ppermute | solution.py:419
  131.6 72.5 %collective-permute-start.8 = (bf16[1024,768]{1,0:T(8,128)(2,1)}, bf16[1024,768]{1,0:T(8,128)(2,1)S(1)}, u32[]{:S(2)}, u32[]{:S(2)}) collective-permute-start(bf16[1024,768]{1,0:T(8,128)(2,1)} %collective-permute-done.g_a), channel_id=1, source_target_pairs={{0,1},{1,0},{2,3},{3,2},{4,5},{5,4},{6,7},{7,6},{8,9},{9,8},{10,11... | collective-permute-start | bytes 4718600 | tf_op jit(solution)/shard_map/ppermute | solution.py:419
  132.1 45.9 %collective-permute-start.5 = (bf16[1024,768]{1,0:T(8,128)(2,1)S(1)}, bf16[1024,768]{1,0:T(8,128)(2,1)S(1)}, u32[]{:S(2)}, u32[]{:S(2)}) collective-permute-start(bf16[1024,768]{1,0:T(8,128)(2,1)S(1)} %multiply_convert_fusion.n_a), channel_id=1, source_target_pairs={{0,2},{1,3},{2,6},{3,7},{6,4},{7,5},{4,0},{5,1},{8,10},{9,11},{10,... | collective-permute-start | bytes 4718600 | tf_op jit(solution)/shard_map/ppermute | solution.py:416
  133.1 71.0 %collective-permute-start.9 = (bf16[1024,768]{1,0:T(8,128)(2,1)}, bf16[1024,768]{1,0:T(8,128)(2,1)}, u32[]{:S(2)}, u32[]{:S(2)}) collective-permute-start(bf16[1024,768]{1,0:T(8,128)(2,1)} %copy-done.69), channel_id=1, source_target_pairs={{0,2},{1,3},{2,6},{3,7},{6,4},{7,5},{4,0},{5,1},{8,10},{9,11},{10,... | collective-permute-start | bytes 4718600 | tf_op jit(solution)/shard_map/ppermute | solution.py:416
  178.0 26.1 %collective-permute-start.7 = (bf16[1024,768]{1,0:T(8,128)(2,1)S(1)}, bf16[1024,768]{1,0:T(8,128)(2,1)S(1)}, u32[]{:S(2)}, u32[]{:S(2)}) collective-permute-start(bf16[1024,768]{1,0:T(8,128)(2,1)S(1)} %collective-permute-done.5.n_a), channel_id=1, source_target_pairs={{0,1},{1,0},{2,3},{3,2},{4,5},{5,4},{6,7},{7,6},{8,9},{9,8},{10,11... | collective-permute-start | bytes 4718600 | tf_op jit(solution)/shard_map/ppermute | solution.py:419
  178.1 70.2 %collective-permute-start.12 = (bf16[1024,768]{1,0:T(8,128)(2,1)S(1)}, bf16[1024,768]{1,0:T(8,128)(2,1)S(1)}, u32[]{:S(2)}, u32[]{:S(2)}) collective-permute-start(bf16[1024,768]{1,0:T(8,128)(2,1)S(1)} %copy-done.70), channel_id=1, source_target_pairs={{0,1},{1,0},{2,3},{3,2},{4,5},{5,4},{6,7},{7,6},{8,9},{9,8},{10,11... | collective-permute-start | bytes 4718600 | tf_op jit(solution)/shard_map/ppermute | solution.py:419
  178.6 67.7 %collective-permute-start.6 = (bf16[1024,768]{1,0:T(8,128)(2,1)S(1)}, bf16[1024,768]{1,0:T(8,128)(2,1)S(1)}, u32[]{:S(2)}, u32[]{:S(2)}) collective-permute-start(bf16[1024,768]{1,0:T(8,128)(2,1)S(1)} %collective-permute-done.5.n_a), channel_id=1, source_target_pairs={{0,2},{1,3},{2,6},{3,7},{6,4},{7,5},{4,0},{5,1},{8,10},{9,11},{10,... | collective-permute-start | bytes 4718600 | tf_op jit(solution)/shard_map/ppermute | solution.py:416
  246.3 4.5 collective-permute-start.11
  246.4 47.9 %collective-permute-start.14 = (bf16[1024,768]{1,0:T(8,128)(2,1)}, bf16[1024,768]{1,0:T(8,128)(2,1)}, u32[]{:S(2)}, u32[]{:S(2)}) collective-permute-start(bf16[1024,768]{1,0:T(8,128)(2,1)} %collective-permute-done.9.g_a), channel_id=1, source_target_pairs={{0,1},{1,0},{2,3},{3,2},{4,5},{5,4},{6,7},{7,6},{8,9},{9,8},{10,11... | collective-permute-start | bytes 4718600 | tf_op jit(solution)/shard_map/ppermute | solution.py:419
  246.9 44.2 %collective-permute-start.10 = (bf16[1024,768]{1,0:T(8,128)(2,1)S(1)}, bf16[1024,768]{1,0:T(8,128)(2,1)S(1)}, u32[]{:S(2)}, u32[]{:S(2)}) collective-permute-start(bf16[1024,768]{1,0:T(8,128)(2,1)S(1)} %collective-permute-done.6.n_a), channel_id=1, source_target_pairs={{0,2},{1,3},{2,6},{3,7},{6,4},{7,5},{4,0},{5,1},{8,10},{9,11},{10,... | collective-permute-start | bytes 4718600 | tf_op jit(solution)/shard_map/ppermute | solution.py:416
  248.3 43.6 %collective-permute-start.15 = (bf16[1040,768]{1,0:T(8,128)(2,1)}, bf16[1040,768]{1,0:T(8,128)(2,1)S(1)}, u32[]{:S(2)}, u32[]{:S(2)}) collective-permute-start(bf16[1040,768]{1,0:T(8,128)(2,1)} %get-tuple-element.119), channel_id=1, source_target_pairs={{0,1},{1,0},{2,3},{3,2},{4,5},{5,4},{6,7},{7,6},{8,9},{9,8},{10,11... | collective-permute-start | bytes 4792328 | tf_op jit(solution)/shard_map/ppermute | solution.py:419
  291.4 43.7 %collective-permute-start.21 = (bf16[1040,768]{1,0:T(8,128)(2,1)}, bf16[1040,768]{1,0:T(8,128)(2,1)S(1)}, u32[]{:S(2)}, u32[]{:S(2)}) collective-permute-start(bf16[1040,768]{1,0:T(8,128)(2,1)} %get-tuple-element.134), channel_id=1, source_target_pairs={{0,1},{1,0},{2,3},{3,2},{4,5},{5,4},{6,7},{7,6},{8,9},{9,8},{10,11... | collective-permute-start | bytes 4792328 | tf_op jit(solution)/shard_map/ppermute | solution.py:419
  292.7 42.3 %collective-permute-start.22 = (bf16[1040,768]{1,0:T(8,128)(2,1)S(1)}, bf16[1040,768]{1,0:T(8,128)(2,1)S(1)}, u32[]{:S(2)}, u32[]{:S(2)}) collective-permute-start(bf16[1040,768]{1,0:T(8,128)(2,1)S(1)} %add_convert_fusion.2), channel_id=1, source_target_pairs={{0,2},{1,3},{2,6},{3,7},{6,4},{7,5},{4,0},{5,1},{8,10},{9,11},{10,... | collective-permute-start | bytes 4792328 | tf_op jit(solution)/shard_map/ppermute | solution.py:416
  334.9 32.2 %collective-permute-start.20 = (bf16[1040,768]{1,0:T(8,128)(2,1)}, bf16[1040,768]{1,0:T(8,128)(2,1)}, u32[]{:S(2)}, u32[]{:S(2)}) collective-permute-start(bf16[1040,768]{1,0:T(8,128)(2,1)} %get-tuple-element.133), channel_id=1, source_target_pairs={{0,1},{1,0},{2,3},{3,2},{4,5},{5,4},{6,7},{7,6},{8,9},{9,8},{10,11... | collective-permute-start | bytes 4792328 | tf_op jit(solution)/shard_map/ppermute | solution.py:419
  337.1 38.5 %collective-permute-start.23 = (bf16[1040,768]{1,0:T(8,128)(2,1)}, bf16[1040,768]{1,0:T(8,128)(2,1)}, u32[]{:S(2)}, u32[]{:S(2)}) collective-permute-start(bf16[1040,768]{1,0:T(8,128)(2,1)} %add_convert_fusion.1), channel_id=1, source_target_pairs={{0,2},{1,3},{2,6},{3,7},{6,4},{7,5},{4,0},{5,1},{8,10},{9,11},{10,... | collective-permute-start | bytes 4792328 | tf_op jit(solution)/shard_map/ppermute | solution.py:416
  379.4 208.2 %reduce-scatter.5.cloned.1.call-start = ((), (), s32[]{:S(2)}) async-start(), calls=%async_computation.3 | async-start | bytes 11796480 | tf_op jit(solution)/shard_map/reduce_scatter | solution.py:740
  379.4 31.1 %collective-permute-start.19 = (bf16[1040,768]{1,0:T(8,128)(2,1)}, bf16[1040,768]{1,0:T(8,128)(2,1)}, u32[]{:S(2)}, u32[]{:S(2)}) collective-permute-start(bf16[1040,768]{1,0:T(8,128)(2,1)} %get-tuple-element.131), channel_id=1, source_target_pairs={{0,1},{1,0},{2,3},{3,2},{4,5},{5,4},{6,7},{7,6},{8,9},{9,8},{10,11... | collective-permute-start | bytes 4792328 | tf_op jit(solution)/shard_map/ppermute | solution.py:419
  379.5 38.9 %collective-permute-start.24 = (bf16[1040,768]{1,0:T(8,128)(2,1)}, bf16[1040,768]{1,0:T(8,128)(2,1)}, u32[]{:S(2)}, u32[]{:S(2)}) collective-permute-start(bf16[1040,768]{1,0:T(8,128)(2,1)} %add_convert_fusion), channel_id=1, source_target_pairs={{0,2},{1,3},{2,6},{3,7},{6,4},{7,5},{4,0},{5,1},{8,10},{9,11},{10,... | collective-permute-start | bytes 4792328 | tf_op jit(solution)/shard_map/ppermute | solution.py:416
  425.4 50.1 %collective-permute-start.17 = (bf16[1024,768]{1,0:T(8,128)(2,1)}, bf16[1024,768]{1,0:T(8,128)(2,1)}, u32[]{:S(2)}, u32[]{:S(2)}) collective-permute-start(bf16[1024,768]{1,0:T(8,128)(2,1)} %copy-done.26), channel_id=1, source_target_pairs={{0,1},{1,0},{2,3},{3,2},{4,5},{5,4},{6,7},{7,6},{8,9},{9,8},{10,11... | collective-permute-start | bytes 4718600 | tf_op jit(solution)/shard_map/ppermute | solution.py:419
  425.5 136.9 %collective-permute-start.16 = (bf16[1024,768]{1,0:T(8,128)(2,1)}, bf16[1024,768]{1,0:T(8,128)(2,1)}, u32[]{:S(2)}, u32[]{:S(2)}) collective-permute-start(bf16[1024,768]{1,0:T(8,128)(2,1)} %copy-done.25), channel_id=1, source_target_pairs={{0,1},{1,0},{2,3},{3,2},{4,5},{5,4},{6,7},{7,6},{8,9},{9,8},{10,11... | collective-permute-start | bytes 4718600 | tf_op jit(solution)/shard_map/ppermute | solution.py:419
  429.9 45.7 %collective-permute-start.25 = (bf16[1024,768]{1,0:T(8,128)(2,1)}, bf16[1024,768]{1,0:T(8,128)(2,1)}, u32[]{:S(2)}, u32[]{:S(2)}) collective-permute-start(bf16[1024,768]{1,0:T(8,128)(2,1)} %add_convert_fusion.6), channel_id=1, source_target_pairs={{0,2},{1,3},{2,6},{3,7},{6,4},{7,5},{4,0},{5,1},{8,10},{9,11},{10,... | collective-permute-start | bytes 4718600 | tf_op jit(solution)/shard_map/ppermute | solution.py:416
  479.3 37.6 %collective-permute-start.26 = (bf16[1024,768]{1,0:T(8,128)(2,1)}, bf16[1024,768]{1,0:T(8,128)(2,1)S(1)}, u32[]{:S(2)}, u32[]{:S(2)}) collective-permute-start(bf16[1024,768]{1,0:T(8,128)(2,1)} %add_convert_fusion.5), channel_id=1, source_target_pairs={{0,2},{1,3},{2,6},{3,7},{6,4},{7,5},{4,0},{5,1},{8,10},{9,11},{10,... | collective-permute-start | bytes 4718600 | tf_op jit(solution)/shard_map/ppermute | solution.py:416
  491.0 7.1 %collective-permute-start.29 = (bf16[4,96,768]{2,1,0:T(8,128)(2,1)}, bf16[4,96,768]{2,1,0:T(8,128)(2,1)}, u32[]{:S(2)}, u32[]{:S(2)}) collective-permute-start(bf16[4,96,768]{2,1,0:T(8,128)(2,1)} %get-tuple-element.191), channel_id=1, source_target_pairs={{0,1},{1,0},{2,3},{3,2},{4,5},{5,4},{6,7},{7,6},{8,9},{9,8},{10,11... | collective-permute-start | bytes 1769480 | tf_op jit(solution)/shard_map/ppermute | solution.py:419
  491.0 40.6 %collective-permute-start.28 = (bf16[4,96,768]{2,1,0:T(8,128)(2,1)}, bf16[4,96,768]{2,1,0:T(8,128)(2,1)}, u32[]{:S(2)}, u32[]{:S(2)}) collective-permute-start(bf16[4,96,768]{2,1,0:T(8,128)(2,1)} %get-tuple-element.192), channel_id=1, source_target_pairs={{0,1},{1,0},{2,3},{3,2},{4,5},{5,4},{6,7},{7,6},{8,9},{9,8},{10,11... | collective-permute-start | bytes 1769480 | tf_op jit(solution)/shard_map/ppermute | solution.py:419
  491.5 67.3 %collective-permute-start.27 = (bf16[4,96,768]{2,1,0:T(8,128)(2,1)}, bf16[4,96,768]{2,1,0:T(8,128)(2,1)}, u32[]{:S(2)}, u32[]{:S(2)}) collective-permute-start(bf16[4,96,768]{2,1,0:T(8,128)(2,1)} %get-tuple-element.193), channel_id=1, source_target_pairs={{0,1},{1,0},{2,3},{3,2},{4,5},{5,4},{6,7},{7,6},{8,9},{9,8},{10,11... | collective-permute-start | bytes 1769480 | tf_op jit(solution)/shard_map/ppermute | solution.py:419
  519.7 15.6 %collective-permute-start.30 = (bf16[4,96,768]{2,1,0:T(8,128)(2,1)}, bf16[4,96,768]{2,1,0:T(8,128)(2,1)}, u32[]{:S(2)}, u32[]{:S(2)}) collective-permute-start(bf16[4,96,768]{2,1,0:T(8,128)(2,1)} %fusion.9), channel_id=1, source_target_pairs={{0,2},{1,3},{2,6},{3,7},{6,4},{7,5},{4,0},{5,1},{8,10},{9,11},{10,... | collective-permute-start | bytes 1769480 | tf_op jit(solution)/shard_map/ppermute | solution.py:416
  522.0 4.9 collective-permute-start.34
  526.9 11.5 %collective-permute-start.33 = (f32[24,128]{1,0:T(8,128)S(1)}, f32[24,128]{1,0:T(8,128)S(1)}, u32[]{:S(2)}, u32[]{:S(2)}) collective-permute-start(f32[24,128]{1,0:T(8,128)S(1)} %bitcast.214), channel_id=1, source_target_pairs={{0,1},{1,0},{2,3},{3,2},{4,5},{5,4},{6,7},{7,6},{8,9},{9,8},{10,11... | collective-permute-start | bytes 36872 | tf_op jit(solution)/shard_map/ppermute | solution.py:419
  531.6 9.3 %collective-permute-start.32 = (f32[24,128]{1,0:T(8,128)S(1)}, f32[24,128]{1,0:T(8,128)S(1)}, u32[]{:S(2)}, u32[]{:S(2)}) collective-permute-start(f32[24,128]{1,0:T(8,128)S(1)} %bitcast.213), channel_id=1, source_target_pairs={{0,1},{1,0},{2,3},{3,2},{4,5},{5,4},{6,7},{7,6},{8,9},{9,8},{10,11... | collective-permute-start | bytes 36872 | tf_op jit(solution)/shard_map/ppermute | solution.py:419
  535.3 5.5 collective-permute-start.35
  538.4 21.2 %collective-permute-start.31 = (bf16[4,96,768]{2,1,0:T(8,128)(2,1)S(1)}, bf16[4,96,768]{2,1,0:T(8,128)(2,1)S(1)}, u32[]{:S(2)}, u32[]{:S(2)}) collective-permute-start(bf16[4,96,768]{2,1,0:T(8,128)(2,1)S(1)} %fusion.11), channel_id=1, source_target_pairs={{0,2},{1,3},{2,6},{3,7},{6,4},{7,5},{4,0},{5,1},{8,10},{9,11},{10,... | collective-permute-start | bytes 1769480 | tf_op jit(solution)/shard_map/ppermute | solution.py:416
  540.8 12.0 %collective-permute-start.36 = (f32[24,128]{1,0:T(8,128)S(1)}, f32[24,128]{1,0:T(8,128)S(1)}, u32[]{:S(2)}, u32[]{:S(2)}) collective-permute-start(f32[24,128]{1,0:T(8,128)S(1)} %add_add_fusion.3), channel_id=1, source_target_pairs={{0,2},{1,3},{2,6},{3,7},{6,4},{7,5},{4,0},{5,1},{8,10},{9,11},{10,... | collective-permute-start | bytes 36872 | tf_op jit(solution)/shard_map/ppermute | solution.py:416
  540.9 13.6 %collective-permute-start.40 = (f32[24,128]{1,0:T(8,128)S(1)}, f32[24,128]{1,0:T(8,128)S(1)}, u32[]{:S(2)}, u32[]{:S(2)}) collective-permute-start(f32[24,128]{1,0:T(8,128)S(1)} %bitcast.212), channel_id=1, source_target_pairs={{0,1},{1,0},{2,3},{3,2},{4,5},{5,4},{6,7},{7,6},{8,9},{9,8},{10,11... | collective-permute-start | bytes 36872 | tf_op jit(solution)/shard_map/ppermute | solution.py:419
  552.8 4.6 collective-permute-start.41
  554.5 15.2 %collective-permute-start.38 = (bf16[4,96,768]{2,1,0:T(8,128)(2,1)S(1)}, bf16[4,96,768]{2,1,0:T(8,128)(2,1)S(1)}, u32[]{:S(2)}, u32[]{:S(2)}) collective-permute-start(bf16[4,96,768]{2,1,0:T(8,128)(2,1)S(1)} %copy-done.47), channel_id=1, source_target_pairs={{0,1},{1,0},{2,3},{3,2},{4,5},{5,4},{6,7},{7,6},{8,9},{9,8},{10,11... | collective-permute-start | bytes 1769480 | tf_op jit(solution)/shard_map/ppermute | solution.py:419
  557.4 9.6 %collective-permute-start.42 = (f32[24,128]{1,0:T(8,128)S(1)}, f32[24,128]{1,0:T(8,128)S(1)}, u32[]{:S(2)}, u32[]{:S(2)}) collective-permute-start(f32[24,128]{1,0:T(8,128)S(1)} %add_add_fusion.2), channel_id=1, source_target_pairs={{0,8},{8,0},{16,24},{24,16},{1,9},{9,1},{17,25},{25,17},{2,10},{10... | collective-permute-start | bytes 36872 | tf_op jit(solution)/shard_map/ppermute | solution.py:840
  558.8 8.2 %collective-permute-start.43 = (f32[24,128]{1,0:T(8,128)S(1)}, f32[24,128]{1,0:T(8,128)S(1)}, u32[]{:S(2)}, u32[]{:S(2)}) collective-permute-start(f32[24,128]{1,0:T(8,128)S(1)} %add_add_fusion.2), channel_id=1, source_target_pairs={{0,16},{8,24},{16,0},{24,8},{1,17},{9,25},{17,1},{25,9},{2,18},{10... | collective-permute-start | bytes 36872 | tf_op jit(solution)/shard_map/ppermute | solution.py:840
  559.5 9.6 %collective-permute-start.44 = (f32[24,128]{1,0:T(8,128)S(1)}, f32[24,128]{1,0:T(8,128)S(1)}, u32[]{:S(2)}, u32[]{:S(2)}) collective-permute-start(f32[24,128]{1,0:T(8,128)S(1)} %add_add_fusion.2), channel_id=1, source_target_pairs={{0,24},{8,16},{16,8},{24,0},{1,25},{9,17},{17,9},{25,1},{2,26},{10... | collective-permute-start | bytes 36872 | tf_op jit(solution)/shard_map/ppermute | solution.py:840
  562.4 17.5 %collective-permute-start.39 = (bf16[4,96,768]{2,1,0:T(8,128)(2,1)S(1)}, bf16[4,96,768]{2,1,0:T(8,128)(2,1)S(1)}, u32[]{:S(2)}, u32[]{:S(2)}) collective-permute-start(bf16[4,96,768]{2,1,0:T(8,128)(2,1)S(1)} %fusion.13), channel_id=1, source_target_pairs={{0,2},{1,3},{2,6},{3,7},{6,4},{7,5},{4,0},{5,1},{8,10},{9,11},{10,... | collective-permute-start | bytes 1769480 | tf_op jit(solution)/shard_map/ppermute | solution.py:416
  567.0 37.5 %collective-permute-start.4 = (bf16[1024,768]{1,0:T(8,128)(2,1)S(1)}, bf16[1024,768]{1,0:T(8,128)(2,1)}, u32[]{:S(2)}, u32[]{:S(2)}) collective-permute-start(bf16[1024,768]{1,0:T(8,128)(2,1)S(1)} %copy-done.24), channel_id=1, source_target_pairs={{0,1},{1,0},{2,3},{3,2},{4,5},{5,4},{6,7},{7,6},{8,9},{9,8},{10,11... | collective-permute-start | bytes 4718600 | tf_op jit(solution)/shard_map/ppermute | solution.py:419
  567.0 42.4 %collective-permute-start.37 = (bf16[1024,768]{1,0:T(8,128)(2,1)}, bf16[1024,768]{1,0:T(8,128)(2,1)}, u32[]{:S(2)}, u32[]{:S(2)}) collective-permute-start(bf16[1024,768]{1,0:T(8,128)(2,1)} %add_convert_fusion.4), channel_id=1, source_target_pairs={{0,2},{1,3},{2,6},{3,7},{6,4},{7,5},{4,0},{5,1},{8,10},{9,11},{10,... | collective-permute-start | bytes 4718600 | tf_op jit(solution)/shard_map/ppermute | solution.py:416
  581.1 13.2 %collective-permute-start.45 = (bf16[4,96,768]{2,1,0:T(8,128)(2,1)S(1)}, bf16[4,96,768]{2,1,0:T(8,128)(2,1)S(1)}, u32[]{:S(2)}, u32[]{:S(2)}) collective-permute-start(bf16[4,96,768]{2,1,0:T(8,128)(2,1)S(1)} %fusion.8), channel_id=1, source_target_pairs={{0,8},{8,0},{16,24},{24,16},{1,9},{9,1},{17,25},{25,17},{2,10},{10... | collective-permute-start | bytes 1769480 | tf_op jit(solution)/shard_map/ppermute | solution.py:840
  582.6 19.2 %collective-permute-start.46 = (bf16[4,96,768]{2,1,0:T(8,128)(2,1)S(1)}, bf16[4,96,768]{2,1,0:T(8,128)(2,1)}, u32[]{:S(2)}, u32[]{:S(2)}) collective-permute-start(bf16[4,96,768]{2,1,0:T(8,128)(2,1)S(1)} %fusion.8), channel_id=1, source_target_pairs={{0,16},{8,24},{16,0},{24,8},{1,17},{9,25},{17,1},{25,9},{2,18},{10... | collective-permute-start | bytes 1769480 | tf_op jit(solution)/shard_map/ppermute | solution.py:840
  583.3 18.5 %collective-permute-start.47 = (bf16[4,96,768]{2,1,0:T(8,128)(2,1)S(1)}, bf16[4,96,768]{2,1,0:T(8,128)(2,1)}, u32[]{:S(2)}, u32[]{:S(2)}) collective-permute-start(bf16[4,96,768]{2,1,0:T(8,128)(2,1)S(1)} %fusion.8), channel_id=1, source_target_pairs={{0,24},{8,16},{16,8},{24,0},{1,25},{9,17},{17,9},{25,1},{2,26},{10... | collective-permute-start | bytes 1769480 | tf_op jit(solution)/shard_map/ppermute | solution.py:840
  (85 other events, 756.4 us)
Sparse Core Ops, SparseCore 0:
  379.5 95.4 reduce-scatter.2
  478.0 95.5 reduce-scatter.4

commit v5 on v4

--- a/solution.py
+++ b/solution.py
@@ -415,6 +415,13 @@
             pairs += [(2 * z, 2 * after), (2 * z + 1, 2 * after + 1)]
         return lax.ppermute(x, "grp", pairs)
 
+    def backward(self, x):
+        pairs = []
+        for i, z in enumerate(self.order):
+            before = self.order[(i - 1) % self.chips]
+            pairs += [(2 * z, 2 * before), (2 * z + 1, 2 * before + 1)]
+        return lax.ppermute(x, "grp", pairs)
+
     def swap(self, x):
         return lax.ppermute(x, "grp", [(i, i ^ 1) for i in range(self.size)])
 
@@ -628,6 +635,34 @@
     yield moving, total
 
 
+def reduce_both_ways(group, own, sibling):
+    half = group.chips // 2
+    ahead, behind, total = None, None, None
+    for k in list(range(half - 1, 0, -1)) + list(range(half, group.chips)) + [0]:
+        pins = yield ahead, behind, total
+        other = group.swap(sibling[k])
+        if k >= half:
+            other, ahead = after((other, ahead), pins)
+            arrived = [ahead]
+        elif k > 0:
+            other, behind = after((other, behind), pins)
+            arrived = [behind]
+        else:
+            other, ahead, behind = after((other, ahead, behind), pins)
+            arrived = [ahead, behind]
+        total = own[k].astype(f32) + other.astype(f32)
+        for block in arrived:
+            if block is not None:
+                total = total + block.astype(f32)
+        if k > 0:
+            total = total.astype(bf16)
+        if k >= half:
+            ahead = group.onward(total)
+        elif k > 0:
+            behind = group.backward(total)
+    yield ahead, behind, total
+
+
 def local_slots(routes_all, first, local):
     ids = first + lax.iota(jnp.int32, local)
     hot = jnp.any(routes_all[:, None, :, :] == ids[None, :, None, None], axis=2).astype(jnp.int32)
@@ -667,12 +702,13 @@
     router_full = router_t.T
     counts = jnp.sum(tally_all[:, 0, 0:experts], axis=0)
     first = (group.me * exp_local).astype(jnp.int32)
-    slots_all = local_slots(routes_all, first, exp_local)
 
     kept_grad = jnp.where((segments != 0)[:, None], cotangent, jnp.zeros_like(cotangent))
     grad_ring = [kept_grad]
-    for k in range(1, group.chips):
+    for k in range(1, group.chips - 1):
         grad_ring.append(group.onward(grad_ring[-1]))
+    grad_ring.append(group.backward(after(kept_grad, small_all)))
+    slots_all = local_slots(after(routes_all, grad_ring[1]), first, exp_local)
 
     inputs = tokens.astype(f32)
     scale_one = rms_scale(inputs)
@@ -683,7 +719,7 @@
     value_rows = jnp.dot(normed_one, value_full, preferred_element_type=f32).astype(bf16)
     base = bias_base(table_full)
     context, lse = attend(query_rows, key_rows, value_rows, after(segments, slots_all), base)
-    context = after(context, grad_ring[2])
+    context = after(context, grad_ring[-1])
     hidden_one = inputs + jnp.dot(context, output_full, preferred_element_type=f32)
     scale_two = rms_scale(hidden_one)
     normed_two = (hidden_one * scale_two * gain_two.astype(f32)).astype(bf16)
@@ -709,8 +745,8 @@
             ],
             axis=0,
         )
-        if k == 1:
-            info = after(info, ring[3:])
+        if k == 0:
+            info = after(info, ring[2])
         if k == group.chips - 1:
             back_own, back_sib = [r[2] for r in results], [r[3] for r in results]
             back_steps = reduce_steps(group, back_own, back_sib)
@@ -736,13 +772,15 @@
     sent = back_steps.send(up_grad)[1]
     up_share = lax.psum_scatter(after(up_grad, sent), "rep", scatter_dimension=1, tiled=True)
     down_grad = jnp.einsum("ekf,ekd->efd", act_all, after(dy_all, sent), preferred_element_type=f32).astype(bf16)
-    back = back_steps.send(down_grad)[1]
+
+    y_steps = reduce_both_ways(group, [r[0] for r in results], [r[1] for r in results])
+    next(y_steps)
+    sums = []
+    for k in range(chips - 2):
+        y_ahead, y_behind, sent = y_steps.send(down_grad)
+        sums.append(sent)
+    back = back_steps.send((down_grad, sums))[1]
     down_share = lax.psum_scatter(after(down_grad, back), "rep", scatter_dimension=1, tiled=True)
-
-    y_steps = reduce_steps(group, [r[0] for r in results], [r[1] for r in results])
-    next(y_steps)
-    y_moving, sent = y_steps.send(back)
-    back = after(back, sent)
 
     logits = jnp.dot(normed_two, router_full, preferred_element_type=f32)
     router_prob = jax.nn.softmax(logits, axis=-1)
@@ -780,10 +818,7 @@
     grad_query_rows, grad_key_rows, grad_value_rows, near_grad, far_grad = attend_back(
         query_rows, key_rows, value_rows, segments, base, context, grad_context, lse
     )
-    sent = None
-    for k in range(2, chips - 1):
-        y_moving, sent = y_steps.send(grad_query_rows)
-    grad_query_rows, grad_key_rows, grad_value_rows = after((grad_query_rows, grad_key_rows, grad_value_rows), sent)
+    grad_query_rows, grad_key_rows, grad_value_rows = after((grad_query_rows, grad_key_rows, grad_value_rows), y_behind)
     query_grad = outer_sum(normed_one, grad_query_rows)
     key_grad = outer_sum(normed_one, grad_key_rows)
     value_grad = outer_sum(normed_one, grad_value_rows)
@@ -826,13 +861,15 @@
     next(dense_steps)
     next(small_steps)
     up_share, down_share = up_share.astype(f32), down_share.astype(f32)
-    pins = y_moving
+    pins = y_ahead
     for k in range(1, chips):
-        dense_sum, small_sum = dense_steps.send(pins)[1], small_steps.send(pins)[1]
+        dense_sum = dense_steps.send(pins)[1]
+        small_sum = small_steps.send(dense_sum)[1]
         pins = (up_share, grad_input) if k == 1 else None
-    y_steps.send((dense_sum, small_sum))
-    dense_sum, small_sum = dense_steps.send(None)[1], small_steps.send(None)[1]
-    mixed = y_steps.send(dense_sum)[1]
+    y_steps.send(dense_sum)
+    dense_sum = dense_steps.send(None)[1]
+    small_sum = small_steps.send(dense_sum)[1]
+    mixed = y_steps.send(dense_sum)[2]
     output = (hidden_one + mixed).astype(bf16)
 
     def over_rep(x):

time: 625 us -> 620 us (level)
  matrix products: 84.4 us -> 97.6 us
  starting transfers between devices: 43.6 us -> 31.8 us
  waiting for transfers between devices: 119 us -> 109 us
    ppermute x18 -> x16, waiting for transfers between devices: 105 us -> 77.3 us  [onward(): return lax.ppermute(x, 'grp', pairs)]
    ppermute x18 -> x16, starting transfers between devices: 32.1 us -> 18.3 us  [onward(): return lax.ppermute(x, 'grp', pairs)]
    reduce_scatter x1, waiting for transfers between devices: 0.01 us -> 13.6 us  [shards(): lax.psum_scatter(after(down_grad, back), 'rep', scatter_dimension=1, tile...]
    dot_general x5, matrix products: 13.5 us -> 24.6 us  [back_proj(): lax.dot_general(grad_rows, weight, (((1,), (1,)), ((), ())), preferred_el...]
    convert_element_type x0 -> x3, other arithmetic: none -> 10.2 us  [reduce_both_ways(): total = total.astype(bf16)]
    convert_element_type x9 -> x6, other arithmetic: 22.4 us -> 13 us  [reduce_steps(): total = total.astype(sent_as)]
    unnamed x177 -> x157, local copies, waits for them, and re-layouts: 15.5 us -> 11.5 us
  transfers between devices with their start and end apart: 50 -> 50, of which waited for: 15 -> 16; matrix products, arithmetic and copies ran while one was open for 24% -> 27% of each run, Pallas kernels for 42% -> 43%
where the time goes in v5:
time: 620 us; the launch traced here: 611 us
  Pallas kernels  263 us (42%)
  waiting for transfers between devices  109 us (18%)
  matrix products  97.6 us (16%)
  other arithmetic  67.7 us (11%)
  starting transfers between devices  31.8 us (5%)
  local copies, waits for them, and re-layouts  23 us (4%)
  between operations  19.6 us (3%)
    pallas_call x4, Pallas kernels, expert_block(): pl.pallas_call(expert_kernel, grid=(local, hidden // part), in_specs=in_s...  157 us
    ppermute x16, waiting for transfers between devices, onward(): return lax.ppermute(x, 'grp', pairs)  77.3 us
    pallas_call x1, Pallas kernels, gather_group(): pl.pallas_call(partial(gather_kernel, chips, reps), in_specs=[hbm] * 3, o...  59.7 us
    dot_general x1, matrix products, shards(): jnp.einsum('ekf,ekd->efd', act_all, after(dy_all, sent), preferred_elemen...  29.1 us
    dot_general x1, matrix products, shards(): jnp.einsum('ekd,ekf->edf', after(x_all, sent), dpre_all, preferred_elemen...  27.3 us
    pallas_call x1, Pallas kernels, attend_back(): pl.pallas_call(bwd_kernel, grid=(pairs,), in_specs=[band, whole(seq, 1),...  26.2 us
    dot_general x5, matrix products, back_proj(): lax.dot_general(grad_rows, weight, (((1,), (1,)), ((), ())), preferred_el...  24.6 us
    pallas_call x1, Pallas kernels, attend(): pl.pallas_call(fwd_kernel, grid=(pairs,), in_specs=[pl.BlockSpec((2, 8, S...  20 us
  transfers between devices with their start and end apart: 50, of which 16 were waited for; matrix products, arithmetic and copies ran while one was open for 27% of the time, Pallas kernels for 43%

profile of v5, /device:TPU:0, one launch (start us, length us, event | category | flops | bytes accessed | tf_op | source)
XLA Modules:
  0.0 611.3 jit_solution(2244588890470913572)
XLA Ops:
  8.0 2.8 broadcast_select_fusion.g_a
  10.8 3.0 collective-permute-start
  16.5 59.7 %gather_group.1 = (bf16[4,768,768]{2,1,0:T(8,128)(2,1)}, bf16[8,48,128]{2,1,0:T(8,128)(2,1)}, f32[8,8,128]{2,1,0:T(8,128)}) custom-call(bf16[4,96,768]{2,1,0:T(8,128)(2,1)} %pad_maximum_fusion.1.stack, bf16[48,128]{1,0:T(8,128)(2,1)} %pad.52.small, f32[8,128]{1,0:T(8,128)} %pad.53.tally), custom_call_target="tpu_custom_call" | custom-call | bytes 16777216 | tf_op jit(solution)/shard_map/gather_group/pallas_call | solution.py:566
  76.2 1.8 collective-permute-start.1
  83.8 4.5 reduce-window.6
  89.3 3.3 convolution_convert_fusion.3.v
  92.6 3.2 convolution_convert_fusion.4.k
  97.3 20.0 %attend.1 = (bf16[1024,768]{1,0:T(8,128)(2,1)S(1)}, f32[6,8,256]{2,1,0:T(8,128)S(1)}) custom-call(f32[12,8,384]{2,1,0:T(8,128)S(1)} %copy_subtract_fusion.base, s32[1024,1]{1,0:T(8,128)S(1)} %copy.102.seg_col, s32[1,1024]{1,0:T(1,128)S(1)} %bitcast.189, bf16[1024,768]{1,0:T(8,128)(2,1)S(1)} %convolution_convert_fusion.5.q, ...), custom_call_target="tpu_custom_call" | custom-call | flops 1 | bytes 1024 | tf_op jit(solution)/shard_map/attend/pallas_call | solution.py:123
  125.6 2.2 collective-permute-start.6
  127.9 30.4 %collective-permute-done.4.g_a = bf16[1024,768]{1,0:T(8,128)(2,1)} collective-permute-done((bf16[1024,768]{1,0:T(8,128)(2,1)}, bf16[1024,768]{1,0:T(8,128)(2,1)}, u32[]{:S(2)}, u32[]{:S(2)}) %collective-permute-start.4) | collective-permute-done | bytes 1572896 | tf_op jit(solution)/shard_map/ppermute | solution.py:416
  158.3 39.0 %expert_block.4 = (bf16[1024,768]{1,0:T(8,128)(2,1)S(1)}, bf16[1024,768]{1,0:T(8,128)(2,1)S(1)}, bf16[1040,768]{1,0:T(8,128)(2,1)}, bf16[1040,768]{1,0:T(8,128)(...) custom-call(s32[1]{0:T(128)} %bitcast.21.first, ...), custom_call_target="tpu_custom_call" | custom-call | flops 25769803776 | bytes 62914560 | tf_op jit(solution)/shard_map/expert_block/pallas_call | solution.py:377
  200.7 2.3 collective-permute-done.8.n_b
  204.2 39.0 %expert_block.5 = (bf16[1024,768]{1,0:T(8,128)(2,1)S(1)}, bf16[1024,768]{1,0:T(8,128)(2,1)S(1)}, bf16[1040,768]{1,0:T(8,128)(2,1)}, bf16[1040,768]{1,0:T(8,128)(...) custom-call(s32[1]{0:T(128)} %bitcast.21.first, ...), custom_call_target="tpu_custom_call", output_to_operand_aliasing={{4}: (9, {}), {5}: (10, {}), {6}: (11, {}), {7}: (12, {})} | custom-call | flops 25769803776 | bytes 62914560 | tf_op jit(solution)/shard_map/expert_block/pallas_call | solution.py:377
  245.3 2.4 collective-permute-done.11.n_b
  248.9 39.4 %expert_block.6 = (bf16[1024,768]{1,0:T(8,128)(2,1)S(1)}, bf16[1024,768]{1,0:T(8,128)(2,1)S(1)}, bf16[1040,768]{1,0:T(8,128)(2,1)}, bf16[1040,768]{1,0:T(8,128)(...) custom-call(s32[1]{0:T(128)} %bitcast.21.first, ...), custom_call_target="tpu_custom_call", output_to_operand_aliasing={{4}: (9, {}), {5}: (10, {}), {6}: (11, {}), {7}: (12, {})} | custom-call | flops 25769803776 | bytes 62914560 | tf_op jit(solution)/shard_map/expert_block/pallas_call | solution.py:377
  293.0 39.6 %expert_block.7 = (bf16[1024,768]{1,0:T(8,128)(2,1)S(1)}, bf16[1024,768]{1,0:T(8,128)(2,1)}, bf16[1040,768]{1,0:T(8,128)(2,1)}, bf16[1040,768]{1,0:T(8,128)(2,1)...) custom-call(s32[1]{0:T(128)} %bitcast.21.first, ...), custom_call_target="tpu_custom_call", output_to_operand_aliasing={{4}: (9, {}), {5}: (10, {}), {6}: (11, {}), {7}: (12, {})} | custom-call | flops 25769803776 | bytes 62914560 | tf_op jit(solution)/shard_map/expert_block/pallas_call | solution.py:377
  332.8 1.9 add_convert_fusion.1
  334.7 1.9 collective-permute-start.21
  336.6 27.3 %convolution_convert_fusion = bf16[2,768,3072]{2,1,0:T(8,128)(2,1)} fusion(bf16[2,2048,768]{2,1,0:T(8,128)(2,1)} %get-tuple-element.144, bf16[2,2048,3072]{2,1,0:T(8,128)(2,1)} %get-tuple-element.145), kind=kOutput, calls=%fused_computation | convolution fusion | flops 19332071424 | bytes 40894464 | tf_op jit(solution)/shard_map/ekd,ekf->edf/dot_general | solution.py:771
  363.9 9.4 %collective-permute-done.21 = bf16[1040,768]{1,0:T(8,128)(2,1)} collective-permute-done((bf16[1040,768]{1,0:T(8,128)(2,1)}, bf16[1040,768]{1,0:T(8,128)(2,1)}, u32[]{:S(2)}, u32[]{:S(2)}) %collective-permute-start.21) | collective-permute-done | bytes 1597472 | tf_op jit(solution)/shard_map/ppermute | solution.py:416
  373.3 4.1 add_convert_fusion
  379.2 29.1 %convolution_convert_fusion.1 = bf16[2,3072,768]{2,1,0:T(8,128)(2,1)} fusion(bf16[2,2048,3072]{2,1,0:T(8,128)(2,1)} %get-tuple-element.136, bf16[2,2048,768]{2,1,0:T(8,128)(2,1)} %get-tuple-element.148), kind=kOutput, calls=%fused_computation.1 | convolution fusion | flops 19332071424 | bytes 40894464 | tf_op jit(solution)/shard_map/ekf,ekd->efd/dot_general | solution.py:774
  408.3 3.3 add_convert_fusion.5
  411.6 3.2 add_convert_fusion.6
  414.9 2.2 collective-permute-done.24
  417.1 4.4 convert_add_fusion.1
  424.1 2.2 collective-permute-start.22
  427.3 4.2 multiply_reduce_fusion
  432.9 3.8 convolution_convert_fusion.2.dctx
  437.2 26.2 %attend_back.1 = (bf16[1024,768]{1,0:T(8,128)(2,1)S(1)}, bf16[1024,768]{1,0:T(8,128)(2,1)S(1)}, bf16[1024,768]{1,0:T(8,128)(2,1)S(1)}, f32[12,8,384]{2,1,0:T(8,128)S(1)}, f32[6,8,256]{2,1,0:T(8,128)S(1)}) custom-call(f32[12,8,384]{2,1,0:T(8,128)S(1)} %copy-done.17, s32[1024,1]{1,0:T(8,128)S(1)} %copy.107.seg_col, s32[1,1024]{1,0:T(1,128)S(1)} %bitcast.191, ...), custom_call_target="tpu_custom_call" | custom-call | flops 1 | bytes 1024 | tf_op jit(solution)/shard_map/attend_back/pallas_call | solution.py:213
  473.8 4.9 fusion.21
  478.7 4.5 fusion.24
  483.7 7.2 %fusion.3 = (f32[768]{0:T(1024)S(1)}, f32[1024]{0:T(1024)S(1)}, f32[1024,768]{1,0:T(8,128)}) fusion(bf16[1024,768]{1,0:T(8,128)(2,1)} %param.34, f32[1024]{0:T(1024)S(1)} %copy-done.48, f32[768]{0:T(1024)S(1)} %copy-done.52, bf16[1024,768]{1,0:T(8,128)(2,1)S(1)} %copy-done.15, bf16[4,768,768]{2,1,0:T(8,128)(2,1)} %get-tuple-element.104, ...), kind=kOutput, calls=%fused_computation.15 | convolution fusion | flops 1215035648 | bytes 13776896 | tf_op jit(solution)/shard_map/dot_general | solution.py:617
  491.4 3.4 collective-permute-done.22
  494.9 2.2 fusion.9
  497.5 4.7 fusion.6
  502.2 4.4 convert_element_type.517
  506.7 6.9 %collective-permute-done.30 = bf16[4,96,768]{2,1,0:T(8,128)(2,1)} collective-permute-done((bf16[4,96,768]{2,1,0:T(8,128)(2,1)}, bf16[4,96,768]{2,1,0:T(8,128)(2,1)}, u32[]{:S(2)}, u32[]{:S(2)}) %collective-permute-start.30) | collective-permute-done | bytes 589856 | tf_op jit(solution)/shard_map/ppermute | solution.py:416
  516.7 2.9 collective-permute-start.39
  519.6 11.3 %collective-permute-done.39 = f32[24,128]{1,0:T(8,128)S(1)} collective-permute-done((f32[24,128]{1,0:T(8,128)S(1)}, f32[24,128]{1,0:T(8,128)S(1)}, u32[]{:S(2)}, u32[]{:S(2)}) %collective-permute-start.39) | collective-permute-done | bytes 12320 | tf_op jit(solution)/shard_map/ppermute | solution.py:416
  533.1 3.0 collective-permute-done.40
  536.1 2.7 collective-permute-start.41
  538.8 3.7 add_convert_fusion.4
  542.5 10.8 %collective-permute-done.34 = bf16[4,96,768]{2,1,0:T(8,128)(2,1)S(1)} collective-permute-done((bf16[4,96,768]{2,1,0:T(8,128)(2,1)S(1)}, bf16[4,96,768]{2,1,0:T(8,128)(2,1)S(1)}, u32[]{:S(2)}, u32[]{:S(2)}) %collective-permute-start.34) | collective-permute-done | bytes 589856 | tf_op jit(solution)/shard_map/ppermute | solution.py:416
  566.6 13.6 %reduce-scatter.5.cloned.1.call-done = bf16[2,768,768]{2,1,0:T(8,128)(2,1)} async-done(((bf16[2,3072,768]{2,1,0:T(8,128)(2,1)}), bf16[2,768,768]{2,1,0:T(8,128)(2,1)}) %reduce-scatter.5.cloned.1.call-update) | async-done | bytes 2359312 | tf_op jit(solution)/shard_map/reduce_scatter | solution.py:783
  580.2 4.2 convert_element_type.551
  584.4 10.3 %collective-permute-done.47 = bf16[4,96,768]{2,1,0:T(8,128)(2,1)} collective-permute-done((bf16[4,96,768]{2,1,0:T(8,128)(2,1)S(1)}, bf16[4,96,768]{2,1,0:T(8,128)(2,1)}, u32[]{:S(2)}, u32[]{:S(2)}) %collective-permute-start.47) | collective-permute-done | bytes 589856 | tf_op jit(solution)/shard_map/ppermute | solution.py:877
  598.2 4.7 add_convert_fusion.3
  (350 shorter events, 70.4 us)
Async XLA Ops:
  7.2 495.0 %reduce-scatter.3.cloned.1.call-start = ((), (), s32[]{:S(2)}) async-start(), calls=%async_computation.2 | async-start | bytes 11796480 | tf_op jit(solution)/shard_map/reduce_scatter | solution.py:773
  10.8 72.8 %collective-permute-start = (bf16[1024,768]{1,0:T(8,128)(2,1)}, bf16[1024,768]{1,0:T(8,128)(2,1)}, u32[]{:S(2)}, u32[]{:S(2)}) collective-permute-start(bf16[1024,768]{1,0:T(8,128)(2,1)} %broadcast_select_fusion.g_a), channel_id=1, source_target_pairs={{0,2},{1,3},{2,6},{3,7},{6,4},{7,5},{4,0},{5,1},{8,10},{9,11},{10,... | collective-permute-start | bytes 4718600 | tf_op jit(solution)/shard_map/ppermute | solution.py:416
  13.9 144.4 %collective-permute-start.3 = (bf16[1024,768]{1,0:T(8,128)(2,1)}, bf16[1024,768]{1,0:T(8,128)(2,1)}, u32[]{:S(2)}, u32[]{:S(2)}) collective-permute-start(bf16[1024,768]{1,0:T(8,128)(2,1)} %broadcast_select_fusion.g_a), channel_id=1, source_target_pairs={{0,1},{1,0},{2,3},{3,2},{4,5},{5,4},{6,7},{7,6},{8,9},{9,8},{10,11... | collective-permute-start | bytes 4718600 | tf_op jit(solution)/shard_map/ppermute | solution.py:426
  76.2 41.2 %collective-permute-start.1 = (bf16[1024,768]{1,0:T(8,128)(2,1)}, bf16[1024,768]{1,0:T(8,128)(2,1)}, u32[]{:S(2)}, u32[]{:S(2)}) collective-permute-start(bf16[1024,768]{1,0:T(8,128)(2,1)} %broadcast_select_fusion.g_a), channel_id=1, source_target_pairs={{0,4},{1,5},{2,0},{3,1},{6,2},{7,3},{4,6},{5,7},{8,12},{9,13},{10,... | collective-permute-start | bytes 4718600 | tf_op jit(solution)/shard_map/ppermute | solution.py:423
  119.6 38.7 %collective-permute-start.4 = (bf16[1024,768]{1,0:T(8,128)(2,1)}, bf16[1024,768]{1,0:T(8,128)(2,1)}, u32[]{:S(2)}, u32[]{:S(2)}) collective-permute-start(bf16[1024,768]{1,0:T(8,128)(2,1)} %collective-permute-done.g_a), channel_id=1, source_target_pairs={{0,2},{1,3},{2,6},{3,7},{6,4},{7,5},{4,0},{5,1},{8,10},{9,11},{10,... | collective-permute-start | bytes 4718600 | tf_op jit(solution)/shard_map/ppermute | solution.py:416
  120.8 37.5 %collective-permute-start.2 = (bf16[1024,768]{1,0:T(8,128)(2,1)S(1)}, bf16[1024,768]{1,0:T(8,128)(2,1)}, u32[]{:S(2)}, u32[]{:S(2)}) collective-permute-start(bf16[1024,768]{1,0:T(8,128)(2,1)S(1)} %multiply_convert_fusion.n_a), channel_id=1, source_target_pairs={{0,1},{1,0},{2,3},{3,2},{4,5},{5,4},{6,7},{7,6},{8,9},{9,8},{10,11... | collective-permute-start | bytes 4718600 | tf_op jit(solution)/shard_map/ppermute | solution.py:426
  125.6 74.0 %collective-permute-start.6 = (bf16[1024,768]{1,0:T(8,128)(2,1)S(1)}, bf16[1024,768]{1,0:T(8,128)(2,1)S(1)}, u32[]{:S(2)}, u32[]{:S(2)}) collective-permute-start(bf16[1024,768]{1,0:T(8,128)(2,1)S(1)} %multiply_convert_fusion.n_a), channel_id=1, source_target_pairs={{0,2},{1,3},{2,6},{3,7},{6,4},{7,5},{4,0},{5,1},{8,10},{9,11},{10,... | collective-permute-start | bytes 4718600 | tf_op jit(solution)/shard_map/ppermute | solution.py:416
  127.8 72.9 %collective-permute-start.9 = (bf16[1024,768]{1,0:T(8,128)(2,1)}, bf16[1024,768]{1,0:T(8,128)(2,1)S(1)}, u32[]{:S(2)}, u32[]{:S(2)}) collective-permute-start(bf16[1024,768]{1,0:T(8,128)(2,1)} %collective-permute-done.g_a), channel_id=1, source_target_pairs={{0,1},{1,0},{2,3},{3,2},{4,5},{5,4},{6,7},{7,6},{8,9},{9,8},{10,11... | collective-permute-start | bytes 4718600 | tf_op jit(solution)/shard_map/ppermute | solution.py:426
  199.6 3.4 collective-permute-start.8
  199.6 44.7 %collective-permute-start.7 = (bf16[1024,768]{1,0:T(8,128)(2,1)S(1)}, bf16[1024,768]{1,0:T(8,128)(2,1)S(1)}, u32[]{:S(2)}, u32[]{:S(2)}) collective-permute-start(bf16[1024,768]{1,0:T(8,128)(2,1)S(1)} %collective-permute-done.6.n_a), channel_id=1, source_target_pairs={{0,2},{1,3},{2,6},{3,7},{6,4},{7,5},{4,0},{5,1},{8,10},{9,11},{10,... | collective-permute-start | bytes 4718600 | tf_op jit(solution)/shard_map/ppermute | solution.py:416
  200.1 45.2 %collective-permute-start.12 = (bf16[1024,768]{1,0:T(8,128)(2,1)}, bf16[1024,768]{1,0:T(8,128)(2,1)S(1)}, u32[]{:S(2)}, u32[]{:S(2)}) collective-permute-start(bf16[1024,768]{1,0:T(8,128)(2,1)} %collective-permute-done.4.g_a), channel_id=1, source_target_pairs={{0,1},{1,0},{2,3},{3,2},{4,5},{5,4},{6,7},{7,6},{8,9},{9,8},{10,11... | collective-permute-start | bytes 4718600 | tf_op jit(solution)/shard_map/ppermute | solution.py:426
  244.3 3.4 collective-permute-start.11
  244.5 46.7 %collective-permute-start.14 = (bf16[1024,768]{1,0:T(8,128)(2,1)}, bf16[1024,768]{1,0:T(8,128)(2,1)}, u32[]{:S(2)}, u32[]{:S(2)}) collective-permute-start(bf16[1024,768]{1,0:T(8,128)(2,1)} %collective-permute-done.1.g_a), channel_id=1, source_target_pairs={{0,1},{1,0},{2,3},{3,2},{4,5},{5,4},{6,7},{7,6},{8,9},{9,8},{10,11... | collective-permute-start | bytes 4718600 | tf_op jit(solution)/shard_map/ppermute | solution.py:426
  244.9 43.4 %collective-permute-start.10 = (bf16[1024,768]{1,0:T(8,128)(2,1)S(1)}, bf16[1024,768]{1,0:T(8,128)(2,1)S(1)}, u32[]{:S(2)}, u32[]{:S(2)}) collective-permute-start(bf16[1024,768]{1,0:T(8,128)(2,1)S(1)} %collective-permute-done.7.n_a), channel_id=1, source_target_pairs={{0,2},{1,3},{2,6},{3,7},{6,4},{7,5},{4,0},{5,1},{8,10},{9,11},{10,... | collective-permute-start | bytes 4718600 | tf_op jit(solution)/shard_map/ppermute | solution.py:416
  245.3 43.7 %collective-permute-start.15 = (bf16[1040,768]{1,0:T(8,128)(2,1)}, bf16[1040,768]{1,0:T(8,128)(2,1)S(1)}, u32[]{:S(2)}, u32[]{:S(2)}) collective-permute-start(bf16[1040,768]{1,0:T(8,128)(2,1)} %get-tuple-element.126), channel_id=1, source_target_pairs={{0,1},{1,0},{2,3},{3,2},{4,5},{5,4},{6,7},{7,6},{8,9},{9,8},{10,11... | collective-permute-start | bytes 4792328 | tf_op jit(solution)/shard_map/ppermute | solution.py:426
  288.3 3.5 collective-permute-start.13
  288.5 44.3 %collective-permute-start.19 = (bf16[1040,768]{1,0:T(8,128)(2,1)}, bf16[1040,768]{1,0:T(8,128)(2,1)S(1)}, u32[]{:S(2)}, u32[]{:S(2)}) collective-permute-start(bf16[1040,768]{1,0:T(8,128)(2,1)} %get-tuple-element.140), channel_id=1, source_target_pairs={{0,1},{1,0},{2,3},{3,2},{4,5},{5,4},{6,7},{7,6},{8,9},{9,8},{10,11... | collective-permute-start | bytes 4792328 | tf_op jit(solution)/shard_map/ppermute | solution.py:426
  290.6 42.2 %collective-permute-start.20 = (bf16[1040,768]{1,0:T(8,128)(2,1)}, bf16[1040,768]{1,0:T(8,128)(2,1)S(1)}, u32[]{:S(2)}, u32[]{:S(2)}) collective-permute-start(bf16[1040,768]{1,0:T(8,128)(2,1)} %add_convert_fusion.2), channel_id=1, source_target_pairs={{0,2},{1,3},{2,6},{3,7},{6,4},{7,5},{4,0},{5,1},{8,10},{9,11},{10,... | collective-permute-start | bytes 4792328 | tf_op jit(solution)/shard_map/ppermute | solution.py:416
  332.6 31.3 %collective-permute-start.18 = (bf16[1040,768]{1,0:T(8,128)(2,1)}, bf16[1040,768]{1,0:T(8,128)(2,1)}, u32[]{:S(2)}, u32[]{:S(2)}) collective-permute-start(bf16[1040,768]{1,0:T(8,128)(2,1)} %get-tuple-element.139), channel_id=1, source_target_pairs={{0,1},{1,0},{2,3},{3,2},{4,5},{5,4},{6,7},{7,6},{8,9},{9,8},{10,11... | collective-permute-start | bytes 4792328 | tf_op jit(solution)/shard_map/ppermute | solution.py:426
  334.7 38.6 %collective-permute-start.21 = (bf16[1040,768]{1,0:T(8,128)(2,1)}, bf16[1040,768]{1,0:T(8,128)(2,1)}, u32[]{:S(2)}, u32[]{:S(2)}) collective-permute-start(bf16[1040,768]{1,0:T(8,128)(2,1)} %add_convert_fusion.1), channel_id=1, source_target_pairs={{0,2},{1,3},{2,6},{3,7},{6,4},{7,5},{4,0},{5,1},{8,10},{9,11},{10,... | collective-permute-start | bytes 4792328 | tf_op jit(solution)/shard_map/ppermute | solution.py:416
  377.4 202.8 %reduce-scatter.5.cloned.1.call-start = ((), (), s32[]{:S(2)}) async-start(), calls=%async_computation.3 | async-start | bytes 11796480 | tf_op jit(solution)/shard_map/reduce_scatter | solution.py:783
  377.5 37.4 %collective-permute-start.23 = (bf16[1040,768]{1,0:T(8,128)(2,1)}, bf16[1040,768]{1,0:T(8,128)(2,1)}, u32[]{:S(2)}, u32[]{:S(2)}) collective-permute-start(bf16[1040,768]{1,0:T(8,128)(2,1)} %get-tuple-element.150), channel_id=1, source_target_pairs={{0,1},{1,0},{2,3},{3,2},{4,5},{5,4},{6,7},{7,6},{8,9},{9,8},{10,11... | collective-permute-start | bytes 4792328 | tf_op jit(solution)/shard_map/ppermute | solution.py:426
  377.6 30.7 %collective-permute-start.25 = (bf16[1024,768]{1,0:T(8,128)(2,1)}, bf16[1024,768]{1,0:T(8,128)(2,1)}, u32[]{:S(2)}, u32[]{:S(2)}) collective-permute-start(bf16[1024,768]{1,0:T(8,128)(2,1)} %copy-done.22), channel_id=1, source_target_pairs={{0,1},{1,0},{2,3},{3,2},{4,5},{5,4},{6,7},{7,6},{8,9},{9,8},{10,11... | collective-permute-start | bytes 4718600 | tf_op jit(solution)/shard_map/ppermute | solution.py:426
  378.1 30.2 %collective-permute-start.17 = (bf16[1024,768]{1,0:T(8,128)(2,1)}, bf16[1024,768]{1,0:T(8,128)(2,1)}, u32[]{:S(2)}, u32[]{:S(2)}) collective-permute-start(bf16[1024,768]{1,0:T(8,128)(2,1)} %copy-done.23), channel_id=1, source_target_pairs={{0,1},{1,0},{2,3},{3,2},{4,5},{5,4},{6,7},{7,6},{8,9},{9,8},{10,11... | collective-permute-start | bytes 4718600 | tf_op jit(solution)/shard_map/ppermute | solution.py:426
  378.1 38.9 %collective-permute-start.24 = (bf16[1040,768]{1,0:T(8,128)(2,1)}, bf16[1040,768]{1,0:T(8,128)(2,1)}, u32[]{:S(2)}, u32[]{:S(2)}) collective-permute-start(bf16[1040,768]{1,0:T(8,128)(2,1)} %add_convert_fusion), channel_id=1, source_target_pairs={{0,2},{1,3},{2,6},{3,7},{6,4},{7,5},{4,0},{5,1},{8,10},{9,11},{10,... | collective-permute-start | bytes 4792328 | tf_op jit(solution)/shard_map/ppermute | solution.py:416
  423.9 112.2 %collective-permute-start.16 = (bf16[1024,768]{1,0:T(8,128)(2,1)}, bf16[1024,768]{1,0:T(8,128)(2,1)}, u32[]{:S(2)}, u32[]{:S(2)}) collective-permute-start(bf16[1024,768]{1,0:T(8,128)(2,1)} %get-tuple-element.133), channel_id=1, source_target_pairs={{0,1},{1,0},{2,3},{3,2},{4,5},{5,4},{6,7},{7,6},{8,9},{9,8},{10,11... | collective-permute-start | bytes 4718600 | tf_op jit(solution)/shard_map/ppermute | solution.py:426
  424.0 39.4 %collective-permute-start.26 = (bf16[1024,768]{1,0:T(8,128)(2,1)}, bf16[1024,768]{1,0:T(8,128)(2,1)}, u32[]{:S(2)}, u32[]{:S(2)}) collective-permute-start(bf16[1024,768]{1,0:T(8,128)(2,1)} %add_convert_fusion.5), channel_id=1, source_target_pairs={{0,4},{1,5},{2,0},{3,1},{6,2},{7,3},{4,6},{5,7},{8,12},{9,13},{10,... | collective-permute-start | bytes 4718600 | tf_op jit(solution)/shard_map/ppermute | solution.py:423
  424.1 70.8 %collective-permute-start.22 = (bf16[1024,768]{1,0:T(8,128)(2,1)}, bf16[1024,768]{1,0:T(8,128)(2,1)}, u32[]{:S(2)}, u32[]{:S(2)}) collective-permute-start(bf16[1024,768]{1,0:T(8,128)(2,1)} %add_convert_fusion.6), channel_id=1, source_target_pairs={{0,2},{1,3},{2,6},{3,7},{6,4},{7,5},{4,0},{5,1},{8,10},{9,11},{10,... | collective-permute-start | bytes 4718600 | tf_op jit(solution)/shard_map/ppermute | solution.py:416
  473.0 21.9 %collective-permute-start.29 = (bf16[4,96,768]{2,1,0:T(8,128)(2,1)}, bf16[4,96,768]{2,1,0:T(8,128)(2,1)}, u32[]{:S(2)}, u32[]{:S(2)}) collective-permute-start(bf16[4,96,768]{2,1,0:T(8,128)(2,1)} %get-tuple-element.201), channel_id=1, source_target_pairs={{0,1},{1,0},{2,3},{3,2},{4,5},{5,4},{6,7},{7,6},{8,9},{9,8},{10,11... | collective-permute-start | bytes 1769480 | tf_op jit(solution)/shard_map/ppermute | solution.py:426
  473.0 33.7 %collective-permute-start.28 = (bf16[4,96,768]{2,1,0:T(8,128)(2,1)}, bf16[4,96,768]{2,1,0:T(8,128)(2,1)}, u32[]{:S(2)}, u32[]{:S(2)}) collective-permute-start(bf16[4,96,768]{2,1,0:T(8,128)(2,1)} %get-tuple-element.202), channel_id=1, source_target_pairs={{0,1},{1,0},{2,3},{3,2},{4,5},{5,4},{6,7},{7,6},{8,9},{9,8},{10,11... | collective-permute-start | bytes 1769480 | tf_op jit(solution)/shard_map/ppermute | solution.py:426
  473.5 57.5 %collective-permute-start.27 = (bf16[4,96,768]{2,1,0:T(8,128)(2,1)}, bf16[4,96,768]{2,1,0:T(8,128)(2,1)}, u32[]{:S(2)}, u32[]{:S(2)}) collective-permute-start(bf16[4,96,768]{2,1,0:T(8,128)(2,1)} %get-tuple-element.203), channel_id=1, source_target_pairs={{0,1},{1,0},{2,3},{3,2},{4,5},{5,4},{6,7},{7,6},{8,9},{9,8},{10,11... | collective-permute-start | bytes 1769480 | tf_op jit(solution)/shard_map/ppermute | solution.py:426
  497.1 16.5 %collective-permute-start.30 = (bf16[4,96,768]{2,1,0:T(8,128)(2,1)}, bf16[4,96,768]{2,1,0:T(8,128)(2,1)}, u32[]{:S(2)}, u32[]{:S(2)}) collective-permute-start(bf16[4,96,768]{2,1,0:T(8,128)(2,1)} %fusion.9), channel_id=1, source_target_pairs={{0,2},{1,3},{2,6},{3,7},{6,4},{7,5},{4,0},{5,1},{8,10},{9,11},{10,... | collective-permute-start | bytes 1769480 | tf_op jit(solution)/shard_map/ppermute | solution.py:416
  515.2 16.2 %collective-permute-start.31 = (bf16[4,96,768]{2,1,0:T(8,128)(2,1)S(1)}, bf16[4,96,768]{2,1,0:T(8,128)(2,1)S(1)}, u32[]{:S(2)}, u32[]{:S(2)}) collective-permute-start(bf16[4,96,768]{2,1,0:T(8,128)(2,1)S(1)} %fusion.11), channel_id=1, source_target_pairs={{0,2},{1,3},{2,6},{3,7},{6,4},{7,5},{4,0},{5,1},{8,10},{9,11},{10,... | collective-permute-start | bytes 1769480 | tf_op jit(solution)/shard_map/ppermute | solution.py:416
  515.5 4.1 collective-permute-start.37
  516.7 14.3 %collective-permute-start.39 = (f32[24,128]{1,0:T(8,128)S(1)}, f32[24,128]{1,0:T(8,128)S(1)}, u32[]{:S(2)}, u32[]{:S(2)}) collective-permute-start(f32[24,128]{1,0:T(8,128)S(1)} %add.721), channel_id=1, source_target_pairs={{0,2},{1,3},{2,6},{3,7},{6,4},{7,5},{4,0},{5,1},{8,10},{9,11},{10,... | collective-permute-start | bytes 36872 | tf_op jit(solution)/shard_map/ppermute | solution.py:416
  519.6 77.7 %collective-permute-start.5 = (bf16[1024,768]{1,0:T(8,128)(2,1)S(1)}, bf16[1024,768]{1,0:T(8,128)(2,1)}, u32[]{:S(2)}, u32[]{:S(2)}) collective-permute-start(bf16[1024,768]{1,0:T(8,128)(2,1)S(1)} %copy-done.21), channel_id=1, source_target_pairs={{0,1},{1,0},{2,3},{3,2},{4,5},{5,4},{6,7},{7,6},{8,9},{9,8},{10,11... | collective-permute-start | bytes 4718600 | tf_op jit(solution)/shard_map/ppermute | solution.py:426
  530.9 11.5 %collective-permute-start.33 = (bf16[4,96,768]{2,1,0:T(8,128)(2,1)S(1)}, bf16[4,96,768]{2,1,0:T(8,128)(2,1)S(1)}, u32[]{:S(2)}, u32[]{:S(2)}) collective-permute-start(bf16[4,96,768]{2,1,0:T(8,128)(2,1)S(1)} %copy-done.40), channel_id=1, source_target_pairs={{0,1},{1,0},{2,3},{3,2},{4,5},{5,4},{6,7},{7,6},{8,9},{9,8},{10,11... | collective-permute-start | bytes 1769480 | tf_op jit(solution)/shard_map/ppermute | solution.py:426
  531.5 4.6 collective-permute-start.40
  533.0 21.6 %collective-permute-start.35 = (f32[24,128]{1,0:T(8,128)S(1)}, f32[24,128]{1,0:T(8,128)S(1)}, u32[]{:S(2)}, u32[]{:S(2)}) collective-permute-start(f32[24,128]{1,0:T(8,128)S(1)} %bitcast.214), channel_id=1, source_target_pairs={{0,1},{1,0},{2,3},{3,2},{4,5},{5,4},{6,7},{7,6},{8,9},{9,8},{10,11... | collective-permute-start | bytes 36872 | tf_op jit(solution)/shard_map/ppermute | solution.py:426
  536.1 17.2 %collective-permute-start.34 = (bf16[4,96,768]{2,1,0:T(8,128)(2,1)S(1)}, bf16[4,96,768]{2,1,0:T(8,128)(2,1)S(1)}, u32[]{:S(2)}, u32[]{:S(2)}) collective-permute-start(bf16[4,96,768]{2,1,0:T(8,128)(2,1)S(1)} %fusion.13), channel_id=1, source_target_pairs={{0,2},{1,3},{2,6},{3,7},{6,4},{7,5},{4,0},{5,1},{8,10},{9,11},{10,... | collective-permute-start | bytes 1769480 | tf_op jit(solution)/shard_map/ppermute | solution.py:416
  536.1 18.5 %collective-permute-start.41 = (f32[24,128]{1,0:T(8,128)S(1)}, f32[24,128]{1,0:T(8,128)S(1)}, u32[]{:S(2)}, u32[]{:S(2)}) collective-permute-start(f32[24,128]{1,0:T(8,128)S(1)} %add_add_fusion.3), channel_id=1, source_target_pairs={{0,2},{1,3},{2,6},{3,7},{6,4},{7,5},{4,0},{5,1},{8,10},{9,11},{10,... | collective-permute-start | bytes 36872 | tf_op jit(solution)/shard_map/ppermute | solution.py:416
  542.5 54.8 %collective-permute-start.32 = (bf16[1024,768]{1,0:T(8,128)(2,1)}, bf16[1024,768]{1,0:T(8,128)(2,1)}, u32[]{:S(2)}, u32[]{:S(2)}) collective-permute-start(bf16[1024,768]{1,0:T(8,128)(2,1)} %add_convert_fusion.4), channel_id=1, source_target_pairs={{0,2},{1,3},{2,6},{3,7},{6,4},{7,5},{4,0},{5,1},{8,10},{9,11},{10,... | collective-permute-start | bytes 4718600 | tf_op jit(solution)/shard_map/ppermute | solution.py:416
  554.6 4.1 collective-permute-start.42
  556.1 4.0 collective-permute-start.43
  556.7 4.9 collective-permute-start.44
  558.7 25.7 %collective-permute-start.45 = (bf16[4,96,768]{2,1,0:T(8,128)(2,1)S(1)}, bf16[4,96,768]{2,1,0:T(8,128)(2,1)S(1)}, u32[]{:S(2)}, u32[]{:S(2)}) collective-permute-start(bf16[4,96,768]{2,1,0:T(8,128)(2,1)S(1)} %fusion.8), channel_id=1, source_target_pairs={{0,8},{8,0},{16,24},{24,16},{1,9},{9,1},{17,25},{25,17},{2,10},{10... | collective-permute-start | bytes 1769480 | tf_op jit(solution)/shard_map/ppermute | solution.py:877
  560.2 24.2 %collective-permute-start.46 = (bf16[4,96,768]{2,1,0:T(8,128)(2,1)S(1)}, bf16[4,96,768]{2,1,0:T(8,128)(2,1)S(1)}, u32[]{:S(2)}, u32[]{:S(2)}) collective-permute-start(bf16[4,96,768]{2,1,0:T(8,128)(2,1)S(1)} %fusion.8), channel_id=1, source_target_pairs={{0,16},{8,24},{16,0},{24,8},{1,17},{9,25},{17,1},{25,9},{2,18},{10... | collective-permute-start | bytes 1769480 | tf_op jit(solution)/shard_map/ppermute | solution.py:877
  561.6 33.1 %collective-permute-start.47 = (bf16[4,96,768]{2,1,0:T(8,128)(2,1)S(1)}, bf16[4,96,768]{2,1,0:T(8,128)(2,1)}, u32[]{:S(2)}, u32[]{:S(2)}) collective-permute-start(bf16[4,96,768]{2,1,0:T(8,128)(2,1)S(1)} %fusion.8), channel_id=1, source_target_pairs={{0,24},{8,16},{16,8},{24,0},{1,25},{9,17},{17,9},{25,1},{2,26},{10... | collective-permute-start | bytes 1769480 | tf_op jit(solution)/shard_map/ppermute | solution.py:877
  (75 other events, 587.6 us)
Sparse Core Ops, SparseCore 0:
  377.6 93.7 reduce-scatter.2
  474.5 105.6 reduce-scatter.4

commit v6 on v5

--- a/solution.py
+++ b/solution.py
@@ -843,7 +843,7 @@
 
     rows = width // groups
     dense = jnp.stack([query_grad, key_grad, value_grad, output_grad]).astype(bf16)
-    dense_steps = reduce_steps(group, *shares(dense, rows))
+    dense_own, dense_sib = shares(dense, rows)
 
     def lanes(x):
         return jnp.pad(x, ((0, 0), (0, 0), (0, 128 - x.shape[2])))
@@ -857,18 +857,37 @@
         lanes(jnp.transpose(router_grad.T.reshape(experts, groups, rows), (1, 0, 2))),
     ], axis=1)
     small = jnp.pad(small, ((0, 0), (0, -small.shape[1] % 8), (0, 0)))
-    small_steps = reduce_steps(group, *shares(small.reshape(-1, 128), small.shape[1]), f32)
-    next(dense_steps)
-    next(small_steps)
+    small_own, small_sib = shares(small.reshape(-1, 128), small.shape[1])
+    lines = -(-small_own[0].size // width)
+
+    def pack_sums(matrices, rest):
+        rest = jnp.pad(rest.reshape(-1), (0, lines * width - rest.size)).reshape(lines, width)
+        high = lax.reduce_precision(rest, 8, 7)
+        parts = (matrices.reshape(-1, width), high, rest - high)
+        return jnp.concatenate([part.astype(bf16) for part in parts], axis=0)
+
+    def unpack_sums(block):
+        block = block.astype(f32)
+        rest = block[-2 * lines:-lines] + block[-lines:]
+        return block[:-2 * lines].reshape(dense_own[0].shape), rest.reshape(-1)[:small_own[0].size].reshape(small_own[0].shape)
+
     up_share, down_share = up_share.astype(f32), down_share.astype(f32)
-    pins = y_ahead
-    for k in range(1, chips):
-        dense_sum = dense_steps.send(pins)[1]
-        small_sum = small_steps.send(dense_sum)[1]
+    arriving, pins = None, y_ahead
+    for k in list(range(1, chips)) + [0]:
+        other, rest = group.swap(dense_sib[k]), group.swap(small_sib[k])
+        if pins is not None:
+            other = after(other, pins)
+        dense_sum = dense_own[k].astype(f32) + other.astype(f32)
+        small_sum = small_own[k] + rest
+        if arriving is not None:
+            more, rest = unpack_sums(arriving)
+            dense_sum, small_sum = dense_sum + more, small_sum + rest
+        if k > 0:
+            block = pack_sums(dense_sum, small_sum)
+            arriving = group.onward(block)
         pins = (up_share, grad_input) if k == 1 else None
-    y_steps.send(dense_sum)
-    dense_sum = dense_steps.send(None)[1]
-    small_sum = small_steps.send(dense_sum)[1]
+        if k == chips - 1:
+            y_steps.send(block)
     mixed = y_steps.send(dense_sum)[2]
     output = (hidden_one + mixed).astype(bf16)
 
@@ -876,9 +895,27 @@
         count = lax.axis_size("rep")
         return x.astype(f32), [lax.ppermute(x, "rep", [(i, i ^ k) for i in range(count)]) for k in range(1, count)]
 
-    (dense, dense_moved), (small, small_moved) = over_rep(dense_sum.astype(bf16)), over_rep(small_sum)
-    for got, also in zip(after(dense_moved, down_share), small_moved):
-        dense, small = dense + got.astype(f32), small + also
+    reps = lax.axis_size("rep")
+    small, small_moved = over_rep(small_sum)
+    if reps == dense_sum.shape[0]:
+        me = lax.axis_index("rep")
+        sent = dense_sum.astype(bf16)
+
+        def swap_with(k, x):
+            return lax.ppermute(x, "rep", [(i, i ^ k) for i in range(reps)])
+
+        mine = lax.dynamic_index_in_dim(dense_sum, me, 0, keepdims=False)
+        for k in range(1, reps):
+            mine = mine + swap_with(k, lax.dynamic_index_in_dim(sent, me ^ k, 0, keepdims=False)).astype(f32)
+        mine = mine.astype(bf16)
+        whole = jnp.stack([mine] + after([swap_with(k, mine) for k in range(1, reps)], output))
+        dense = [lax.dynamic_index_in_dim(whole, me ^ m, 0, keepdims=False).astype(f32) for m in range(reps)]
+    else:
+        dense, dense_moved = over_rep(dense_sum.astype(bf16))
+        for got in after(dense_moved, output):
+            dense = dense + got.astype(f32)
+    for also in small_moved:
+        small = small + also
     at = 3 + bias_rows
     balance_terms = experts * experts * fraction * (small[2, 0:experts] / all_tokens)
     loss = aux_weight / experts * jnp.sum(balance_terms)

time: 620 us -> 610 us (0.984)
  matrix products: 97.6 us -> 87.5 us
    ppermute x16 -> x13, waiting for transfers between devices: 77.3 us -> 91.3 us  [onward(): return lax.ppermute(x, 'grp', pairs)]
    reduce_scatter x1, waiting for transfers between devices: 13.6 us -> 0.01 us  [shards(): lax.psum_scatter(after(down_grad, back), 'rep', scatter_dimension=1, tile...]
    ppermute x6 -> x3, waiting for transfers between devices: 11.8 us -> 0.01 us  [over_rep(): lax.ppermute(x, 'rep', [(i, i ^ k) for i in range(count)])]
    dot_general x5, matrix products: 24.6 us -> 14.3 us  [back_proj(): lax.dot_general(grad_rows, weight, (((1,), (1,)), ((), ())), preferred_el...]
    convert_element_type x0 -> x12, other arithmetic: none -> 8.44 us  [the longest x6 4.57 us: pack_sums(): return jnp.concatenate([part.astype(bf16) for part in parts], axis=0)]
    ppermute x0 -> x6, starting transfers between devices: none -> 7.04 us  [swap_with(): return lax.ppermute(x, 'rep', [(i, i ^ k) for i in range(reps)])]
    ppermute x0 -> x6, waiting for transfers between devices: none -> 6.97 us  [swap_with(): return lax.ppermute(x, 'rep', [(i, i ^ k) for i in range(reps)])]
    convert_element_type x6 -> x3, other arithmetic: 13 us -> 7.63 us  [reduce_steps(): total = total.astype(sent_as)]
  transfers between devices with their start and end apart: 50 -> 50, of which waited for: 16 -> 15; matrix products, arithmetic and copies ran while one was open for 27% -> 27% of each run, Pallas kernels for 43% -> 44%
where the time goes in v6:
time: 610 us; the launch traced here: 601 us
  Pallas kernels  263 us (43%)
  waiting for transfers between devices  105 us (17%)
  matrix products  87.5 us (14%)
  other arithmetic  70.5 us (12%)
  starting transfers between devices  32.3 us (5%)
  local copies, waits for them, and re-layouts  23.9 us (4%)
  between operations  19.8 us (3%)
    pallas_call x4, Pallas kernels, expert_block(): pl.pallas_call(expert_kernel, grid=(local, hidden // part), in_specs=in_s...  157 us
    ppermute x13, waiting for transfers between devices, onward(): return lax.ppermute(x, 'grp', pairs)  91.3 us
    pallas_call x1, Pallas kernels, gather_group(): pl.pallas_call(partial(gather_kernel, chips, reps), in_specs=[hbm] * 3, o...  59.7 us
    dot_general x1, matrix products, shards(): jnp.einsum('ekf,ekd->efd', act_all, after(dy_all, sent), preferred_elemen...  29.1 us
    dot_general x1, matrix products, shards(): jnp.einsum('ekd,ekf->edf', after(x_all, sent), dpre_all, preferred_elemen...  27.5 us
    pallas_call x1, Pallas kernels, attend_back(): pl.pallas_call(bwd_kernel, grid=(pairs,), in_specs=[band, whole(seq, 1),...  26.2 us
    pallas_call x1, Pallas kernels, attend(): pl.pallas_call(fwd_kernel, grid=(pairs,), in_specs=[pl.BlockSpec((2, 8, S...  20 us
    ppermute x13, starting transfers between devices, onward(): return lax.ppermute(x, 'grp', pairs)  14.6 us
  transfers between devices with their start and end apart: 50, of which 15 were waited for; matrix products, arithmetic and copies ran while one was open for 27% of the time, Pallas kernels for 44%

profile of v6, /device:TPU:0, one launch (start us, length us, event | category | flops | bytes accessed | tf_op | source)
XLA Modules:
  0.0 601.2 jit_solution(14334335293384291051)
XLA Ops:
  8.5 2.8 broadcast_select_fusion.g_a
  11.4 3.0 collective-permute-start
  17.0 59.7 %gather_group.1 = (bf16[4,768,768]{2,1,0:T(8,128)(2,1)}, bf16[8,48,128]{2,1,0:T(8,128)(2,1)}, f32[8,8,128]{2,1,0:T(8,128)}) custom-call(bf16[4,96,768]{2,1,0:T(8,128)(2,1)} %pad_maximum_fusion.4.stack, bf16[48,128]{1,0:T(8,128)(2,1)} %pad.52.small, f32[8,128]{1,0:T(8,128)} %pad.53.tally), custom_call_target="tpu_custom_call" | custom-call | bytes 16777216 | tf_op jit(solution)/shard_map/gather_group/pallas_call | solution.py:566
  76.8 1.8 collective-permute-start.1
  82.5 1.6 fusion.2
  84.3 4.5 reduce-window.6
  89.8 3.3 convolution_convert_fusion.3.v
  93.1 3.2 convolution_convert_fusion.4.k
  97.9 20.0 %attend.1 = (bf16[1024,768]{1,0:T(8,128)(2,1)S(1)}, f32[6,8,256]{2,1,0:T(8,128)S(1)}) custom-call(f32[12,8,384]{2,1,0:T(8,128)S(1)} %copy_subtract_fusion.base, s32[1024,1]{1,0:T(8,128)S(1)} %copy.94.seg_col, s32[1,1024]{1,0:T(1,128)S(1)} %bitcast.210, bf16[1024,768]{1,0:T(8,128)(2,1)S(1)} %convolution_convert_fusion.5.q, ...), custom_call_target="tpu_custom_call" | custom-call | flops 1 | bytes 1024 | tf_op jit(solution)/shard_map/attend/pallas_call | solution.py:123
  126.1 2.2 collective-permute-start.6
  128.4 30.3 %collective-permute-done.4.g_a = bf16[1024,768]{1,0:T(8,128)(2,1)} collective-permute-done((bf16[1024,768]{1,0:T(8,128)(2,1)}, bf16[1024,768]{1,0:T(8,128)(2,1)}, u32[]{:S(2)}, u32[]{:S(2)}) %collective-permute-start.4) | collective-permute-done | bytes 1572896 | tf_op jit(solution)/shard_map/ppermute | solution.py:416
  158.8 39.0 %expert_block.4 = (bf16[1024,768]{1,0:T(8,128)(2,1)S(1)}, bf16[1024,768]{1,0:T(8,128)(2,1)S(1)}, bf16[1040,768]{1,0:T(8,128)(2,1)}, bf16[1040,768]{1,0:T(8,128)(...) custom-call(s32[1]{0:T(128)} %bitcast.21.first, ...), custom_call_target="tpu_custom_call" | custom-call | flops 25769803776 | bytes 62914560 | tf_op jit(solution)/shard_map/expert_block/pallas_call | solution.py:377
  201.2 2.3 collective-permute-done.8.n_b
  204.7 39.0 %expert_block.5 = (bf16[1024,768]{1,0:T(8,128)(2,1)S(1)}, bf16[1024,768]{1,0:T(8,128)(2,1)S(1)}, bf16[1040,768]{1,0:T(8,128)(2,1)}, bf16[1040,768]{1,0:T(8,128)(...) custom-call(s32[1]{0:T(128)} %bitcast.21.first, ...), custom_call_target="tpu_custom_call", output_to_operand_aliasing={{4}: (9, {}), {5}: (10, {}), {6}: (11, {}), {7}: (12, {})} | custom-call | flops 25769803776 | bytes 62914560 | tf_op jit(solution)/shard_map/expert_block/pallas_call | solution.py:377
  245.9 2.4 collective-permute-done.11.n_b
  249.4 39.1 %expert_block.6 = (bf16[1024,768]{1,0:T(8,128)(2,1)S(1)}, bf16[1024,768]{1,0:T(8,128)(2,1)S(1)}, bf16[1040,768]{1,0:T(8,128)(2,1)}, bf16[1040,768]{1,0:T(8,128)(...) custom-call(s32[1]{0:T(128)} %bitcast.21.first, ...), custom_call_target="tpu_custom_call", output_to_operand_aliasing={{4}: (9, {}), {5}: (10, {}), {6}: (11, {}), {7}: (12, {})} | custom-call | flops 25769803776 | bytes 62914560 | tf_op jit(solution)/shard_map/expert_block/pallas_call | solution.py:377
  289.2 1.6 add_convert_fusion.2
  293.2 39.6 %expert_block.7 = (bf16[1024,768]{1,0:T(8,128)(2,1)S(1)}, bf16[1024,768]{1,0:T(8,128)(2,1)}, bf16[1040,768]{1,0:T(8,128)(2,1)}, bf16[1040,768]{1,0:T(8,128)(2,1)...) custom-call(s32[1]{0:T(128)} %bitcast.21.first, ...), custom_call_target="tpu_custom_call", output_to_operand_aliasing={{4}: (9, {}), {5}: (10, {}), {6}: (11, {}), {7}: (12, {})} | custom-call | flops 25769803776 | bytes 62914560 | tf_op jit(solution)/shard_map/expert_block/pallas_call | solution.py:377
  333.0 1.9 add_convert_fusion.1
  334.9 1.9 collective-permute-start.21
  336.7 27.5 %convolution_convert_fusion = bf16[2,768,3072]{2,1,0:T(8,128)(2,1)} fusion(bf16[2,2048,768]{2,1,0:T(8,128)(2,1)} %get-tuple-element.136, bf16[2,2048,3072]{2,1,0:T(8,128)(2,1)} %get-tuple-element.137), kind=kOutput, calls=%fused_computation | convolution fusion | flops 19332071424 | bytes 40894464 | tf_op jit(solution)/shard_map/ekd,ekf->edf/dot_general | solution.py:771
  364.3 9.2 %collective-permute-done.21 = bf16[1040,768]{1,0:T(8,128)(2,1)} collective-permute-done((bf16[1040,768]{1,0:T(8,128)(2,1)}, bf16[1040,768]{1,0:T(8,128)(2,1)}, u32[]{:S(2)}, u32[]{:S(2)}) %collective-permute-start.21) | collective-permute-done | bytes 1597472 | tf_op jit(solution)/shard_map/ppermute | solution.py:416
  373.5 4.1 add_convert_fusion
  379.4 29.1 %convolution_convert_fusion.1 = bf16[2,3072,768]{2,1,0:T(8,128)(2,1)} fusion(bf16[2,2048,3072]{2,1,0:T(8,128)(2,1)} %get-tuple-element.128, bf16[2,2048,768]{2,1,0:T(8,128)(2,1)} %get-tuple-element.140), kind=kOutput, calls=%fused_computation.1 | convolution fusion | flops 19332071424 | bytes 40894464 | tf_op jit(solution)/shard_map/ekf,ekd->efd/dot_general | solution.py:774
  408.5 3.3 add_convert_fusion.5
  411.8 3.3 add_convert_fusion.6
  415.1 2.1 collective-permute-done.24
  417.3 4.4 convert_add_fusion.1
  424.2 2.1 collective-permute-start.22
  427.4 4.2 multiply_reduce_fusion
  433.0 3.8 convolution_convert_fusion.2.dctx
  437.3 26.2 %attend_back.1 = (bf16[1024,768]{1,0:T(8,128)(2,1)S(1)}, bf16[1024,768]{1,0:T(8,128)(2,1)S(1)}, bf16[1024,768]{1,0:T(8,128)(2,1)S(1)}, f32[12,8,384]{2,1,0:T(8,128)S(1)}, f32[6,8,256]{2,1,0:T(8,128)S(1)}) custom-call(f32[12,8,384]{2,1,0:T(8,128)S(1)} %copy-done.15, s32[1024,1]{1,0:T(8,128)S(1)} %copy.99.seg_col, s32[1,1024]{1,0:T(1,128)S(1)} %bitcast.212, ...), custom_call_target="tpu_custom_call" | custom-call | flops 1 | bytes 1024 | tf_op jit(solution)/shard_map/attend_back/pallas_call | solution.py:213
  475.4 3.5 fusion.7
  481.8 12.6 %collective-permute-done.22 = bf16[1024,768]{1,0:T(8,128)(2,1)} collective-permute-done((bf16[1024,768]{1,0:T(8,128)(2,1)}, bf16[1024,768]{1,0:T(8,128)(2,1)}, u32[]{:S(2)}, u32[]{:S(2)}) %collective-permute-start.22) | collective-permute-done | bytes 1572896 | tf_op jit(solution)/shard_map/ppermute | solution.py:416
  496.5 5.0 fusion.6
  501.5 10.7 %collective-permute-done.31 = bf16[392,768]{1,0:T(8,128)(2,1)S(1)} collective-permute-done((bf16[392,768]{1,0:T(8,128)(2,1)S(1)}, bf16[392,768]{1,0:T(8,128)(2,1)S(1)}, u32[]{:S(2)}, u32[]{:S(2)}) %collective-permute-start.31) | collective-permute-done | bytes 602144 | tf_op jit(solution)/shard_map/ppermute | solution.py:416
  512.5 4.7 convert_element_type.564
  519.4 14.6 %collective-permute-done.33 = bf16[392,768]{1,0:T(8,128)(2,1)S(1)} collective-permute-done((bf16[392,768]{1,0:T(8,128)(2,1)S(1)}, bf16[392,768]{1,0:T(8,128)(2,1)S(1)}, u32[]{:S(2)}, u32[]{:S(2)}) %collective-permute-start.33) | collective-permute-done | bytes 602144 | tf_op jit(solution)/shard_map/ppermute | solution.py:416
  535.1 1.6 fusion.13
  538.2 3.6 add_convert_fusion.4
  541.8 2.4 collective-permute-start.35
  544.2 11.2 %collective-permute-done.37 = bf16[392,768]{1,0:T(8,128)(2,1)} collective-permute-done((bf16[392,768]{1,0:T(8,128)(2,1)}, bf16[392,768]{1,0:T(8,128)(2,1)}, u32[]{:S(2)}, u32[]{:S(2)}) %collective-permute-start.37) | collective-permute-done | bytes 602144 | tf_op jit(solution)/shard_map/ppermute | solution.py:416
  559.7 1.6 collective-permute-start.41
  570.5 2.2 collective-permute-done.42
  573.4 4.0 collective-permute-done.44
  577.9 3.3 collective-permute-start.47
  581.1 4.4 convert_element_type.622
  586.0 4.6 add_convert_fusion.3
  (370 shorter events, 72.9 us)
Async XLA Ops:
  7.2 505.3 %reduce-scatter.3.cloned.1.call-start = ((), (), s32[]{:S(2)}) async-start(), calls=%async_computation.2 | async-start | bytes 11796480 | tf_op jit(solution)/shard_map/reduce_scatter | solution.py:773
  11.4 72.8 %collective-permute-start = (bf16[1024,768]{1,0:T(8,128)(2,1)}, bf16[1024,768]{1,0:T(8,128)(2,1)}, u32[]{:S(2)}, u32[]{:S(2)}) collective-permute-start(bf16[1024,768]{1,0:T(8,128)(2,1)} %broadcast_select_fusion.g_a), channel_id=1, source_target_pairs={{0,2},{1,3},{2,6},{3,7},{6,4},{7,5},{4,0},{5,1},{8,10},{9,11},{10,... | collective-permute-start | bytes 4718600 | tf_op jit(solution)/shard_map/ppermute | solution.py:416
  14.4 144.4 %collective-permute-start.3 = (bf16[1024,768]{1,0:T(8,128)(2,1)}, bf16[1024,768]{1,0:T(8,128)(2,1)}, u32[]{:S(2)}, u32[]{:S(2)}) collective-permute-start(bf16[1024,768]{1,0:T(8,128)(2,1)} %broadcast_select_fusion.g_a), channel_id=1, source_target_pairs={{0,1},{1,0},{2,3},{3,2},{4,5},{5,4},{6,7},{7,6},{8,9},{9,8},{10,11... | collective-permute-start | bytes 4718600 | tf_op jit(solution)/shard_map/ppermute | solution.py:426
  76.8 41.2 %collective-permute-start.1 = (bf16[1024,768]{1,0:T(8,128)(2,1)}, bf16[1024,768]{1,0:T(8,128)(2,1)}, u32[]{:S(2)}, u32[]{:S(2)}) collective-permute-start(bf16[1024,768]{1,0:T(8,128)(2,1)} %broadcast_select_fusion.g_a), channel_id=1, source_target_pairs={{0,4},{1,5},{2,0},{3,1},{6,2},{7,3},{4,6},{5,7},{8,12},{9,13},{10,... | collective-permute-start | bytes 4718600 | tf_op jit(solution)/shard_map/ppermute | solution.py:423
  120.1 38.7 %collective-permute-start.4 = (bf16[1024,768]{1,0:T(8,128)(2,1)}, bf16[1024,768]{1,0:T(8,128)(2,1)}, u32[]{:S(2)}, u32[]{:S(2)}) collective-permute-start(bf16[1024,768]{1,0:T(8,128)(2,1)} %collective-permute-done.g_a), channel_id=1, source_target_pairs={{0,2},{1,3},{2,6},{3,7},{6,4},{7,5},{4,0},{5,1},{8,10},{9,11},{10,... | collective-permute-start | bytes 4718600 | tf_op jit(solution)/shard_map/ppermute | solution.py:416
  121.3 37.5 %collective-permute-start.2 = (bf16[1024,768]{1,0:T(8,128)(2,1)S(1)}, bf16[1024,768]{1,0:T(8,128)(2,1)}, u32[]{:S(2)}, u32[]{:S(2)}) collective-permute-start(bf16[1024,768]{1,0:T(8,128)(2,1)S(1)} %multiply_convert_fusion.n_a), channel_id=1, source_target_pairs={{0,1},{1,0},{2,3},{3,2},{4,5},{5,4},{6,7},{7,6},{8,9},{9,8},{10,11... | collective-permute-start | bytes 4718600 | tf_op jit(solution)/shard_map/ppermute | solution.py:426
  126.1 73.9 %collective-permute-start.6 = (bf16[1024,768]{1,0:T(8,128)(2,1)S(1)}, bf16[1024,768]{1,0:T(8,128)(2,1)S(1)}, u32[]{:S(2)}, u32[]{:S(2)}) collective-permute-start(bf16[1024,768]{1,0:T(8,128)(2,1)S(1)} %multiply_convert_fusion.n_a), channel_id=1, source_target_pairs={{0,2},{1,3},{2,6},{3,7},{6,4},{7,5},{4,0},{5,1},{8,10},{9,11},{10,... | collective-permute-start | bytes 4718600 | tf_op jit(solution)/shard_map/ppermute | solution.py:416
  128.3 72.9 %collective-permute-start.9 = (bf16[1024,768]{1,0:T(8,128)(2,1)}, bf16[1024,768]{1,0:T(8,128)(2,1)S(1)}, u32[]{:S(2)}, u32[]{:S(2)}) collective-permute-start(bf16[1024,768]{1,0:T(8,128)(2,1)} %collective-permute-done.g_a), channel_id=1, source_target_pairs={{0,1},{1,0},{2,3},{3,2},{4,5},{5,4},{6,7},{7,6},{8,9},{9,8},{10,11... | collective-permute-start | bytes 4718600 | tf_op jit(solution)/shard_map/ppermute | solution.py:426
  200.1 44.7 %collective-permute-start.7 = (bf16[1024,768]{1,0:T(8,128)(2,1)S(1)}, bf16[1024,768]{1,0:T(8,128)(2,1)S(1)}, u32[]{:S(2)}, u32[]{:S(2)}) collective-permute-start(bf16[1024,768]{1,0:T(8,128)(2,1)S(1)} %collective-permute-done.6.n_a), channel_id=1, source_target_pairs={{0,2},{1,3},{2,6},{3,7},{6,4},{7,5},{4,0},{5,1},{8,10},{9,11},{10,... | collective-permute-start | bytes 4718600 | tf_op jit(solution)/shard_map/ppermute | solution.py:416
  200.6 45.3 %collective-permute-start.12 = (bf16[1024,768]{1,0:T(8,128)(2,1)}, bf16[1024,768]{1,0:T(8,128)(2,1)S(1)}, u32[]{:S(2)}, u32[]{:S(2)}) collective-permute-start(bf16[1024,768]{1,0:T(8,128)(2,1)} %collective-permute-done.4.g_a), channel_id=1, source_target_pairs={{0,1},{1,0},{2,3},{3,2},{4,5},{5,4},{6,7},{7,6},{8,9},{9,8},{10,11... | collective-permute-start | bytes 4718600 | tf_op jit(solution)/shard_map/ppermute | solution.py:426
  244.8 3.4 collective-permute-start.11
  245.0 46.3 %collective-permute-start.14 = (bf16[1024,768]{1,0:T(8,128)(2,1)}, bf16[1024,768]{1,0:T(8,128)(2,1)}, u32[]{:S(2)}, u32[]{:S(2)}) collective-permute-start(bf16[1024,768]{1,0:T(8,128)(2,1)} %collective-permute-done.1.g_a), channel_id=1, source_target_pairs={{0,1},{1,0},{2,3},{3,2},{4,5},{5,4},{6,7},{7,6},{8,9},{9,8},{10,11... | collective-permute-start | bytes 4718600 | tf_op jit(solution)/shard_map/ppermute | solution.py:426
  245.5 43.0 %collective-permute-start.10 = (bf16[1024,768]{1,0:T(8,128)(2,1)S(1)}, bf16[1024,768]{1,0:T(8,128)(2,1)S(1)}, u32[]{:S(2)}, u32[]{:S(2)}) collective-permute-start(bf16[1024,768]{1,0:T(8,128)(2,1)S(1)} %collective-permute-done.7.n_a), channel_id=1, source_target_pairs={{0,2},{1,3},{2,6},{3,7},{6,4},{7,5},{4,0},{5,1},{8,10},{9,11},{10,... | collective-permute-start | bytes 4718600 | tf_op jit(solution)/shard_map/ppermute | solution.py:416
  245.9 43.3 %collective-permute-start.15 = (bf16[1040,768]{1,0:T(8,128)(2,1)}, bf16[1040,768]{1,0:T(8,128)(2,1)S(1)}, u32[]{:S(2)}, u32[]{:S(2)}) collective-permute-start(bf16[1040,768]{1,0:T(8,128)(2,1)} %get-tuple-element.118), channel_id=1, source_target_pairs={{0,1},{1,0},{2,3},{3,2},{4,5},{5,4},{6,7},{7,6},{8,9},{9,8},{10,11... | collective-permute-start | bytes 4792328 | tf_op jit(solution)/shard_map/ppermute | solution.py:426
  288.5 3.5 collective-permute-start.13
  288.8 44.2 %collective-permute-start.19 = (bf16[1040,768]{1,0:T(8,128)(2,1)}, bf16[1040,768]{1,0:T(8,128)(2,1)S(1)}, u32[]{:S(2)}, u32[]{:S(2)}) collective-permute-start(bf16[1040,768]{1,0:T(8,128)(2,1)} %get-tuple-element.132), channel_id=1, source_target_pairs={{0,1},{1,0},{2,3},{3,2},{4,5},{5,4},{6,7},{7,6},{8,9},{9,8},{10,11... | collective-permute-start | bytes 4792328 | tf_op jit(solution)/shard_map/ppermute | solution.py:426
  290.8 42.1 %collective-permute-start.20 = (bf16[1040,768]{1,0:T(8,128)(2,1)}, bf16[1040,768]{1,0:T(8,128)(2,1)S(1)}, u32[]{:S(2)}, u32[]{:S(2)}) collective-permute-start(bf16[1040,768]{1,0:T(8,128)(2,1)} %add_convert_fusion.2), channel_id=1, source_target_pairs={{0,2},{1,3},{2,6},{3,7},{6,4},{7,5},{4,0},{5,1},{8,10},{9,11},{10,... | collective-permute-start | bytes 4792328 | tf_op jit(solution)/shard_map/ppermute | solution.py:416
  332.7 31.5 %collective-permute-start.18 = (bf16[1040,768]{1,0:T(8,128)(2,1)}, bf16[1040,768]{1,0:T(8,128)(2,1)}, u32[]{:S(2)}, u32[]{:S(2)}) collective-permute-start(bf16[1040,768]{1,0:T(8,128)(2,1)} %get-tuple-element.131), channel_id=1, source_target_pairs={{0,1},{1,0},{2,3},{3,2},{4,5},{5,4},{6,7},{7,6},{8,9},{9,8},{10,11... | collective-permute-start | bytes 4792328 | tf_op jit(solution)/shard_map/ppermute | solution.py:426
  334.9 38.6 %collective-permute-start.21 = (bf16[1040,768]{1,0:T(8,128)(2,1)}, bf16[1040,768]{1,0:T(8,128)(2,1)}, u32[]{:S(2)}, u32[]{:S(2)}) collective-permute-start(bf16[1040,768]{1,0:T(8,128)(2,1)} %add_convert_fusion.1), channel_id=1, source_target_pairs={{0,2},{1,3},{2,6},{3,7},{6,4},{7,5},{4,0},{5,1},{8,10},{9,11},{10,... | collective-permute-start | bytes 4792328 | tf_op jit(solution)/shard_map/ppermute | solution.py:416
  377.6 203.5 %reduce-scatter.5.cloned.1.call-start = ((), (), s32[]{:S(2)}) async-start(), calls=%async_computation.3 | async-start | bytes 11796480 | tf_op jit(solution)/shard_map/reduce_scatter | solution.py:783
  377.7 37.4 %collective-permute-start.23 = (bf16[1040,768]{1,0:T(8,128)(2,1)}, bf16[1040,768]{1,0:T(8,128)(2,1)}, u32[]{:S(2)}, u32[]{:S(2)}) collective-permute-start(bf16[1040,768]{1,0:T(8,128)(2,1)} %get-tuple-element.142), channel_id=1, source_target_pairs={{0,1},{1,0},{2,3},{3,2},{4,5},{5,4},{6,7},{7,6},{8,9},{9,8},{10,11... | collective-permute-start | bytes 4792328 | tf_op jit(solution)/shard_map/ppermute | solution.py:426
  377.8 30.8 %collective-permute-start.25 = (bf16[1024,768]{1,0:T(8,128)(2,1)}, bf16[1024,768]{1,0:T(8,128)(2,1)}, u32[]{:S(2)}, u32[]{:S(2)}) collective-permute-start(bf16[1024,768]{1,0:T(8,128)(2,1)} %copy-done.20), channel_id=1, source_target_pairs={{0,1},{1,0},{2,3},{3,2},{4,5},{5,4},{6,7},{7,6},{8,9},{9,8},{10,11... | collective-permute-start | bytes 4718600 | tf_op jit(solution)/shard_map/ppermute | solution.py:426
  378.2 30.3 %collective-permute-start.17 = (bf16[1024,768]{1,0:T(8,128)(2,1)}, bf16[1024,768]{1,0:T(8,128)(2,1)}, u32[]{:S(2)}, u32[]{:S(2)}) collective-permute-start(bf16[1024,768]{1,0:T(8,128)(2,1)} %copy-done.21), channel_id=1, source_target_pairs={{0,1},{1,0},{2,3},{3,2},{4,5},{5,4},{6,7},{7,6},{8,9},{9,8},{10,11... | collective-permute-start | bytes 4718600 | tf_op jit(solution)/shard_map/ppermute | solution.py:426
  378.3 38.9 %collective-permute-start.24 = (bf16[1040,768]{1,0:T(8,128)(2,1)}, bf16[1040,768]{1,0:T(8,128)(2,1)}, u32[]{:S(2)}, u32[]{:S(2)}) collective-permute-start(bf16[1040,768]{1,0:T(8,128)(2,1)} %add_convert_fusion), channel_id=1, source_target_pairs={{0,2},{1,3},{2,6},{3,7},{6,4},{7,5},{4,0},{5,1},{8,10},{9,11},{10,... | collective-permute-start | bytes 4792328 | tf_op jit(solution)/shard_map/ppermute | solution.py:416
  424.1 39.4 %collective-permute-start.26 = (bf16[1024,768]{1,0:T(8,128)(2,1)}, bf16[1024,768]{1,0:T(8,128)(2,1)}, u32[]{:S(2)}, u32[]{:S(2)}) collective-permute-start(bf16[1024,768]{1,0:T(8,128)(2,1)} %add_convert_fusion.5), channel_id=1, source_target_pairs={{0,4},{1,5},{2,0},{3,1},{6,2},{7,3},{4,6},{5,7},{8,12},{9,13},{10,... | collective-permute-start | bytes 4718600 | tf_op jit(solution)/shard_map/ppermute | solution.py:423
  424.2 70.1 %collective-permute-start.22 = (bf16[1024,768]{1,0:T(8,128)(2,1)}, bf16[1024,768]{1,0:T(8,128)(2,1)}, u32[]{:S(2)}, u32[]{:S(2)}) collective-permute-start(bf16[1024,768]{1,0:T(8,128)(2,1)} %add_convert_fusion.6), channel_id=1, source_target_pairs={{0,2},{1,3},{2,6},{3,7},{6,4},{7,5},{4,0},{5,1},{8,10},{9,11},{10,... | collective-permute-start | bytes 4718600 | tf_op jit(solution)/shard_map/ppermute | solution.py:416
  472.5 21.8 %collective-permute-start.29 = (bf16[4,96,768]{2,1,0:T(8,128)(2,1)}, bf16[4,96,768]{2,1,0:T(8,128)(2,1)}, u32[]{:S(2)}, u32[]{:S(2)}) collective-permute-start(bf16[4,96,768]{2,1,0:T(8,128)(2,1)} %get-tuple-element.187), channel_id=1, source_target_pairs={{0,1},{1,0},{2,3},{3,2},{4,5},{5,4},{6,7},{7,6},{8,9},{9,8},{10,11... | collective-permute-start | bytes 1769480 | tf_op jit(solution)/shard_map/ppermute | solution.py:426
  495.9 16.4 %collective-permute-start.31 = (bf16[392,768]{1,0:T(8,128)(2,1)S(1)}, bf16[392,768]{1,0:T(8,128)(2,1)S(1)}, u32[]{:S(2)}, u32[]{:S(2)}) collective-permute-start(bf16[392,768]{1,0:T(8,128)(2,1)S(1)} %pad_maximum_fusion.1), channel_id=1, source_target_pairs={{0,2},{1,3},{2,6},{3,7},{6,4},{7,5},{4,0},{5,1},{8,10},{9,11},{10,... | collective-permute-start | bytes 1806344 | tf_op jit(solution)/shard_map/ppermute | solution.py:416
  496.0 21.2 %collective-permute-start.28 = (bf16[4,96,768]{2,1,0:T(8,128)(2,1)S(1)}, bf16[4,96,768]{2,1,0:T(8,128)(2,1)}, u32[]{:S(2)}, u32[]{:S(2)}) collective-permute-start(bf16[4,96,768]{2,1,0:T(8,128)(2,1)S(1)} %get-tuple-element.188), channel_id=1, source_target_pairs={{0,1},{1,0},{2,3},{3,2},{4,5},{5,4},{6,7},{7,6},{8,9},{9,8},{10,11... | collective-permute-start | bytes 1769480 | tf_op jit(solution)/shard_map/ppermute | solution.py:426
  496.0 16.3 %collective-permute-start.32 = (f32[24,128]{1,0:T(8,128)S(1)}, f32[24,128]{1,0:T(8,128)S(1)}, u32[]{:S(2)}, u32[]{:S(2)}) collective-permute-start(f32[24,128]{1,0:T(8,128)S(1)} %bitcast.247), channel_id=1, source_target_pairs={{0,1},{1,0},{2,3},{3,2},{4,5},{5,4},{6,7},{7,6},{8,9},{9,8},{10,11... | collective-permute-start | bytes 36872 | tf_op jit(solution)/shard_map/ppermute | solution.py:426
  518.7 15.4 %collective-permute-start.33 = (bf16[392,768]{1,0:T(8,128)(2,1)S(1)}, bf16[392,768]{1,0:T(8,128)(2,1)S(1)}, u32[]{:S(2)}, u32[]{:S(2)}) collective-permute-start(bf16[392,768]{1,0:T(8,128)(2,1)S(1)} %pad_maximum_fusion.2), channel_id=1, source_target_pairs={{0,2},{1,3},{2,6},{3,7},{6,4},{7,5},{4,0},{5,1},{8,10},{9,11},{10,... | collective-permute-start | bytes 1806344 | tf_op jit(solution)/shard_map/ppermute | solution.py:416
  518.7 19.5 %collective-permute-start.16 = (bf16[1024,768]{1,0:T(8,128)(2,1)}, bf16[1024,768]{1,0:T(8,128)(2,1)}, u32[]{:S(2)}, u32[]{:S(2)}) collective-permute-start(bf16[1024,768]{1,0:T(8,128)(2,1)} %get-tuple-element.125), channel_id=1, source_target_pairs={{0,1},{1,0},{2,3},{3,2},{4,5},{5,4},{6,7},{7,6},{8,9},{9,8},{10,11... | collective-permute-start | bytes 4718600 | tf_op jit(solution)/shard_map/ppermute | solution.py:426
  518.8 15.5 %collective-permute-start.27 = (bf16[4,96,768]{2,1,0:T(8,128)(2,1)S(1)}, bf16[4,96,768]{2,1,0:T(8,128)(2,1)S(1)}, u32[]{:S(2)}, u32[]{:S(2)}) collective-permute-start(bf16[4,96,768]{2,1,0:T(8,128)(2,1)S(1)} %get-tuple-element.189), channel_id=1, source_target_pairs={{0,1},{1,0},{2,3},{3,2},{4,5},{5,4},{6,7},{7,6},{8,9},{9,8},{10,11... | collective-permute-start | bytes 1769480 | tf_op jit(solution)/shard_map/ppermute | solution.py:426
  519.3 14.8 %collective-permute-start.34 = (f32[24,128]{1,0:T(8,128)S(1)}, f32[24,128]{1,0:T(8,128)S(1)}, u32[]{:S(2)}, u32[]{:S(2)}) collective-permute-start(f32[24,128]{1,0:T(8,128)S(1)} %bitcast.246), channel_id=1, source_target_pairs={{0,1},{1,0},{2,3},{3,2},{4,5},{5,4},{6,7},{7,6},{8,9},{9,8},{10,11... | collective-permute-start | bytes 36872 | tf_op jit(solution)/shard_map/ppermute | solution.py:426
  537.6 17.7 %collective-permute-start.37 = (bf16[392,768]{1,0:T(8,128)(2,1)}, bf16[392,768]{1,0:T(8,128)(2,1)}, u32[]{:S(2)}, u32[]{:S(2)}) collective-permute-start(bf16[392,768]{1,0:T(8,128)(2,1)} %pad_maximum_fusion.3), channel_id=1, source_target_pairs={{0,2},{1,3},{2,6},{3,7},{6,4},{7,5},{4,0},{5,1},{8,10},{9,11},{10,... | collective-permute-start | bytes 1806344 | tf_op jit(solution)/shard_map/ppermute | solution.py:416
  537.6 47.9 %collective-permute-start.5 = (bf16[1024,768]{1,0:T(8,128)(2,1)S(1)}, bf16[1024,768]{1,0:T(8,128)(2,1)}, u32[]{:S(2)}, u32[]{:S(2)}) collective-permute-start(bf16[1024,768]{1,0:T(8,128)(2,1)S(1)} %copy-done.19), channel_id=1, source_target_pairs={{0,1},{1,0},{2,3},{3,2},{4,5},{5,4},{6,7},{7,6},{8,9},{9,8},{10,11... | collective-permute-start | bytes 4718600 | tf_op jit(solution)/shard_map/ppermute | solution.py:426
  537.6 22.1 %collective-permute-start.36 = (bf16[4,96,768]{2,1,0:T(8,128)(2,1)}, bf16[4,96,768]{2,1,0:T(8,128)(2,1)}, u32[]{:S(2)}, u32[]{:S(2)}) collective-permute-start(bf16[4,96,768]{2,1,0:T(8,128)(2,1)} %get-tuple-element.186), channel_id=1, source_target_pairs={{0,1},{1,0},{2,3},{3,2},{4,5},{5,4},{6,7},{7,6},{8,9},{9,8},{10,11... | collective-permute-start | bytes 1769480 | tf_op jit(solution)/shard_map/ppermute | solution.py:426
  538.1 18.4 %collective-permute-start.38 = (f32[24,128]{1,0:T(8,128)S(1)}, f32[24,128]{1,0:T(8,128)S(1)}, u32[]{:S(2)}, u32[]{:S(2)}) collective-permute-start(f32[24,128]{1,0:T(8,128)S(1)} %bitcast.245), channel_id=1, source_target_pairs={{0,1},{1,0},{2,3},{3,2},{4,5},{5,4},{6,7},{7,6},{8,9},{9,8},{10,11... | collective-permute-start | bytes 36872 | tf_op jit(solution)/shard_map/ppermute | solution.py:426
  541.8 44.2 %collective-permute-start.35 = (bf16[1024,768]{1,0:T(8,128)(2,1)}, bf16[1024,768]{1,0:T(8,128)(2,1)}, u32[]{:S(2)}, u32[]{:S(2)}) collective-permute-start(bf16[1024,768]{1,0:T(8,128)(2,1)} %add_convert_fusion.4), channel_id=1, source_target_pairs={{0,2},{1,3},{2,6},{3,7},{6,4},{7,5},{4,0},{5,1},{8,10},{9,11},{10,... | collective-permute-start | bytes 4718600 | tf_op jit(solution)/shard_map/ppermute | solution.py:416
  556.6 7.0 %collective-permute-start.39 = (f32[24,128]{1,0:T(8,128)S(1)}, f32[24,128]{1,0:T(8,128)S(1)}, u32[]{:S(2)}, u32[]{:S(2)}) collective-permute-start(f32[24,128]{1,0:T(8,128)S(1)} %add_add_fusion.2), channel_id=1, source_target_pairs={{0,8},{8,0},{16,24},{24,16},{1,9},{9,1},{17,25},{25,17},{2,10},{10... | collective-permute-start | bytes 36872 | tf_op jit(solution)/shard_map/ppermute | solution.py:896
  558.1 6.9 %collective-permute-start.40 = (f32[24,128]{1,0:T(8,128)S(1)}, f32[24,128]{1,0:T(8,128)S(1)}, u32[]{:S(2)}, u32[]{:S(2)}) collective-permute-start(f32[24,128]{1,0:T(8,128)S(1)} %add_add_fusion.2), channel_id=1, source_target_pairs={{0,16},{8,24},{16,0},{24,8},{1,17},{9,25},{17,1},{25,9},{2,18},{10... | collective-permute-start | bytes 36872 | tf_op jit(solution)/shard_map/ppermute | solution.py:896
  559.7 5.8 collective-permute-start.41
  563.6 9.1 %collective-permute-start.42 = (bf16[96,768]{1,0:T(8,128)(2,1)}, bf16[96,768]{1,0:T(8,128)(2,1)S(1)}, u32[]{:S(2)}, u32[]{:S(2)}) collective-permute-start(bf16[96,768]{1,0:T(8,128)(2,1)} %get-tuple-element.196), channel_id=1, source_target_pairs={{0,8},{8,0},{16,24},{24,16},{1,9},{9,1},{17,25},{25,17},{2,10},{10... | collective-permute-start | bytes 442376 | tf_op jit(solution)/shard_map/ppermute | solution.py:905
  565.0 8.5 %collective-permute-start.43 = (bf16[96,768]{1,0:T(8,128)(2,1)}, bf16[96,768]{1,0:T(8,128)(2,1)S(1)}, u32[]{:S(2)}, u32[]{:S(2)}) collective-permute-start(bf16[96,768]{1,0:T(8,128)(2,1)} %get-tuple-element.198), channel_id=1, source_target_pairs={{0,16},{8,24},{16,0},{24,8},{1,17},{9,25},{17,1},{25,9},{2,18},{10... | collective-permute-start | bytes 442376 | tf_op jit(solution)/shard_map/ppermute | solution.py:905
  565.5 12.0 %collective-permute-start.44 = (bf16[96,768]{1,0:T(8,128)(2,1)S(1)}, bf16[96,768]{1,0:T(8,128)(2,1)S(1)}, u32[]{:S(2)}, u32[]{:S(2)}) collective-permute-start(bf16[96,768]{1,0:T(8,128)(2,1)S(1)} %get-tuple-element.197), channel_id=1, source_target_pairs={{0,24},{8,16},{16,8},{24,0},{1,25},{9,17},{17,9},{25,1},{2,26},{10... | collective-permute-start | bytes 442376 | tf_op jit(solution)/shard_map/ppermute | solution.py:905
  577.6 13.1 %collective-permute-start.45 = (bf16[96,768]{1,0:T(8,128)(2,1)S(1)}, bf16[96,768]{1,0:T(8,128)(2,1)S(1)}, u32[]{:S(2)}, u32[]{:S(2)}) collective-permute-start(bf16[96,768]{1,0:T(8,128)(2,1)S(1)} %fusion.42), channel_id=1, source_target_pairs={{0,8},{8,0},{16,24},{24,16},{1,9},{9,1},{17,25},{25,17},{2,10},{10... | collective-permute-start | bytes 442376 | tf_op jit(solution)/shard_map/ppermute | solution.py:905
  577.8 12.8 %collective-permute-start.46 = (bf16[96,768]{1,0:T(8,128)(2,1)S(1)}, bf16[96,768]{1,0:T(8,128)(2,1)}, u32[]{:S(2)}, u32[]{:S(2)}) collective-permute-start(bf16[96,768]{1,0:T(8,128)(2,1)S(1)} %fusion.42), channel_id=1, source_target_pairs={{0,16},{8,24},{16,0},{24,8},{1,17},{9,25},{17,1},{25,9},{2,18},{10... | collective-permute-start | bytes 442376 | tf_op jit(solution)/shard_map/ppermute | solution.py:905
  577.9 12.8 %collective-permute-start.47 = (bf16[96,768]{1,0:T(8,128)(2,1)S(1)}, bf16[96,768]{1,0:T(8,128)(2,1)}, u32[]{:S(2)}, u32[]{:S(2)}) collective-permute-start(bf16[96,768]{1,0:T(8,128)(2,1)S(1)} %fusion.42), channel_id=1, source_target_pairs={{0,24},{8,16},{16,8},{24,0},{1,25},{9,17},{17,9},{25,1},{2,26},{10... | collective-permute-start | bytes 442376 | tf_op jit(solution)/shard_map/ppermute | solution.py:905
  (73 other events, 544.7 us)
Sparse Core Ops, SparseCore 0:
  377.7 93.8 reduce-scatter.2
  474.7 100.7 reduce-scatter.4

commit v7 on v6

--- a/solution.py
+++ b/solution.py
@@ -264,7 +264,7 @@
 
 def expert_kernel(first, n_a, n_b, g_a, g_b, info, router_t, w_in, w_out, *rest):
     (y_a, y_b, r_a, r_b, act_out, dpre_out, x_out, dy_out,
-     hot, x_s, g_s, dy_s, gate_s, y_sum, d_sum, y_all, d_all, dgate_c) = rest[-18:]
+     hot, x_s, g_s, dy_s, gate_s, y_sum, d_sum, yd_all, gates, dgate_c) = rest[-18:]
     e, f = pl.program_id(0), pl.program_id(1)
     rows, width = n_a.shape
     cap = x_s.shape[0] // 2
@@ -274,9 +274,6 @@
     @pl.when((e == 0) & (f == 0))
     def _():
         dgate_c[...] = jnp.zeros_like(dgate_c)
-
-    @pl.when(f == 0)
-    def _():
         for s, (n_ref, g_ref) in enumerate(sources):
             logits = lax.dot_general(router_t[...], n_ref[...], (((1,), (1,)), ((), ())), preferred_element_type=f32)
             ids = lax.broadcasted_iota(jnp.int32, logits.shape, 0)
@@ -284,7 +281,13 @@
             prob = power / jnp.sum(power, axis=0, keepdims=True)
             chosen = (ids == info[4 * s + 2:4 * s + 3, :]) | (ids == info[4 * s + 3:4 * s + 4, :])
             both = jnp.sum(jnp.where(chosen, prob, 0.0), axis=0, keepdims=True)
-            gate_row = jnp.sum(jnp.where(ids == expert, prob, 0.0), axis=0, keepdims=True) / both
+            gates[s] = prob / both
+
+    @pl.when(f == 0)
+    def _():
+        for s, (n_ref, g_ref) in enumerate(sources):
+            ids = lax.broadcasted_iota(jnp.int32, gates.shape[1:], 0)
+            gate_row = jnp.sum(jnp.where(ids == expert, gates[s], 0.0), axis=0, keepdims=True)
             slot_row = jnp.where(e == 0, info[4 * s:4 * s + 1, :], info[4 * s + 1:4 * s + 2, :])
             match = slot_row == lax.broadcasted_iota(jnp.int32, (cap, rows), 0)
             one_hot = jnp.where(match, 1.0, 0.0).astype(bf16)
@@ -317,8 +320,8 @@
         for s in range(2):
             part = slice(s * cap, (s + 1) * cap)
             here = pl.ds(pl.multiple_of(e * cap, cap), cap)
-            y_all[s, here, :] = y_rows[part]
-            d_all[s, here, :] = d_rows[part]
+            yd_all[s, here, 0:width] = y_rows[part]
+            yd_all[s, here, width:] = d_rows[part]
             slot_row = jnp.where(e == 0, info[4 * s:4 * s + 1, :], info[4 * s + 1:4 * s + 2, :])
             match = slot_row == lax.broadcasted_iota(jnp.int32, (cap, rows), 0)
             row = jnp.sum(jnp.where(match, dgate[part], 0.0), axis=0, keepdims=True)
@@ -330,8 +333,9 @@
     def _():
         turn = (((0,), (0,)), ((), ()))
         for s, (y_ref, r_ref) in enumerate(((y_a, r_a), (y_b, r_b))):
-            y_ref[...] = lax.dot_general(hot[s], y_all[s], turn, preferred_element_type=f32).astype(bf16)
-            r_ref[0:rows, :] = lax.dot_general(hot[s], d_all[s], turn, preferred_element_type=f32).astype(bf16)
+            sums = lax.dot_general(hot[s], yd_all[s], turn, preferred_element_type=f32).astype(bf16)
+            y_ref[...] = sums[:, 0:width]
+            r_ref[0:rows, :] = sums[:, width:]
             value = dgate_c[TOP * s:TOP * s + TOP, :]
             high = value.astype(bf16)
             value = value - high.astype(f32)
@@ -385,7 +389,7 @@
             pltpu.VMEM((2 * cap, width), bf16), pltpu.VMEM((2 * cap, width), bf16), pltpu.VMEM((2 * cap, width), bf16),
             pltpu.VMEM((2 * cap, 1), f32),
             pltpu.VMEM((2 * cap, width), f32), pltpu.VMEM((2 * cap, width), f32),
-            pltpu.VMEM((2, local * cap, width), bf16), pltpu.VMEM((2, local * cap, width), bf16),
+            pltpu.VMEM((2, local * cap, 2 * width), bf16), pltpu.VMEM((2,) + (router_t.shape[0], rows), f32),
             pltpu.VMEM((8, rows), f32),
         ],
         input_output_aliases=alias,

time: 610 us -> 606 us (level)
  transfers between devices with their start and end apart: 50 -> 50, of which waited for: 15 -> 15; matrix products, arithmetic and copies ran while one was open for 27% -> 27% of each run, Pallas kernels for 44% -> 43%
where the time goes in v7:
time: 606 us; the launch traced here: 597 us
  Pallas kernels  259 us (43%)
  waiting for transfers between devices  105 us (17%)
  matrix products  87.5 us (14%)
  other arithmetic  70.5 us (12%)
  starting transfers between devices  32.4 us (5%)
  local copies, waits for them, and re-layouts  23.9 us (4%)
  between operations  19.8 us (3%)
    pallas_call x4, Pallas kernels, expert_block(): pl.pallas_call(expert_kernel, grid=(local, hidden // part), in_specs=in_s...  153 us
    ppermute x13, waiting for transfers between devices, onward(): return lax.ppermute(x, 'grp', pairs)  91.4 us
    pallas_call x1, Pallas kernels, gather_group(): pl.pallas_call(partial(gather_kernel, chips, reps), in_specs=[hbm] * 3, o...  59.7 us
    dot_general x1, matrix products, shards(): jnp.einsum('ekf,ekd->efd', act_all, after(dy_all, sent), preferred_elemen...  29.1 us
    dot_general x1, matrix products, shards(): jnp.einsum('ekd,ekf->edf', after(x_all, sent), dpre_all, preferred_elemen...  27.5 us
    pallas_call x1, Pallas kernels, attend_back(): pl.pallas_call(bwd_kernel, grid=(pairs,), in_specs=[band, whole(seq, 1),...  26.2 us
    pallas_call x1, Pallas kernels, attend(): pl.pallas_call(fwd_kernel, grid=(pairs,), in_specs=[pl.BlockSpec((2, 8, S...  20 us
    ppermute x13, starting transfers between devices, onward(): return lax.ppermute(x, 'grp', pairs)  14.7 us
  transfers between devices with their start and end apart: 50, of which 15 were waited for; matrix products, arithmetic and copies ran while one was open for 27% of the time, Pallas kernels for 43%

profile of v7, /device:TPU:0, one launch (start us, length us, event | category | flops | bytes accessed | tf_op | source)
XLA Modules:
  0.0 597.3 jit_solution(1699296886182812113)
XLA Ops:
  8.5 2.8 broadcast_select_fusion.g_a
  11.4 3.0 collective-permute-start
  17.0 59.7 %gather_group.1 = (bf16[4,768,768]{2,1,0:T(8,128)(2,1)}, bf16[8,48,128]{2,1,0:T(8,128)(2,1)}, f32[8,8,128]{2,1,0:T(8,128)}) custom-call(bf16[4,96,768]{2,1,0:T(8,128)(2,1)} %pad_maximum_fusion.4.stack, bf16[48,128]{1,0:T(8,128)(2,1)} %pad.52.small, f32[8,128]{1,0:T(8,128)} %pad.53.tally), custom_call_target="tpu_custom_call" | custom-call | bytes 16777216 | tf_op jit(solution)/shard_map/gather_group/pallas_call | solution.py:570
  76.8 1.8 collective-permute-start.1
  84.3 4.5 reduce-window.6
  89.8 3.3 convolution_convert_fusion.3.v
  93.1 3.2 convolution_convert_fusion.4.k
  97.9 20.0 %attend.1 = (bf16[1024,768]{1,0:T(8,128)(2,1)S(1)}, f32[6,8,256]{2,1,0:T(8,128)S(1)}) custom-call(f32[12,8,384]{2,1,0:T(8,128)S(1)} %copy_subtract_fusion.base, s32[1024,1]{1,0:T(8,128)S(1)} %copy.94.seg_col, s32[1,1024]{1,0:T(1,128)S(1)} %bitcast.210, bf16[1024,768]{1,0:T(8,128)(2,1)S(1)} %convolution_convert_fusion.5.q, ...), custom_call_target="tpu_custom_call" | custom-call | flops 1 | bytes 1024 | tf_op jit(solution)/shard_map/attend/pallas_call | solution.py:123
  126.1 2.2 collective-permute-start.6
  128.4 30.3 %collective-permute-done.4.g_a = bf16[1024,768]{1,0:T(8,128)(2,1)} collective-permute-done((bf16[1024,768]{1,0:T(8,128)(2,1)}, bf16[1024,768]{1,0:T(8,128)(2,1)}, u32[]{:S(2)}, u32[]{:S(2)}) %collective-permute-start.4) | collective-permute-done | bytes 1572896 | tf_op jit(solution)/shard_map/ppermute | solution.py:420
  158.8 38.0 %expert_block.4 = (bf16[1024,768]{1,0:T(8,128)(2,1)S(1)}, bf16[1024,768]{1,0:T(8,128)(2,1)S(1)}, bf16[1040,768]{1,0:T(8,128)(2,1)}, bf16[1040,768]{1,0:T(8,128)(...) custom-call(s32[1]{0:T(128)} %bitcast.21.first, ...), custom_call_target="tpu_custom_call" | custom-call | flops 25769803776 | bytes 62914560 | tf_op jit(solution)/shard_map/expert_block/pallas_call | solution.py:381
  200.2 2.3 collective-permute-done.8.n_b
  203.7 38.0 %expert_block.5 = (bf16[1024,768]{1,0:T(8,128)(2,1)S(1)}, bf16[1024,768]{1,0:T(8,128)(2,1)S(1)}, bf16[1040,768]{1,0:T(8,128)(2,1)}, bf16[1040,768]{1,0:T(8,128)(...) custom-call(s32[1]{0:T(128)} %bitcast.21.first, ...), custom_call_target="tpu_custom_call", output_to_operand_aliasing={{4}: (9, {}), {5}: (10, {}), {6}: (11, {}), {7}: (12, {})} | custom-call | flops 25769803776 | bytes 62914560 | tf_op jit(solution)/shard_map/expert_block/pallas_call | solution.py:381
  243.9 2.4 collective-permute-done.11.n_b
  247.5 38.1 %expert_block.6 = (bf16[1024,768]{1,0:T(8,128)(2,1)S(1)}, bf16[1024,768]{1,0:T(8,128)(2,1)S(1)}, bf16[1040,768]{1,0:T(8,128)(2,1)}, bf16[1040,768]{1,0:T(8,128)(...) custom-call(s32[1]{0:T(128)} %bitcast.21.first, ...), custom_call_target="tpu_custom_call", output_to_operand_aliasing={{4}: (9, {}), {5}: (10, {}), {6}: (11, {}), {7}: (12, {})} | custom-call | flops 25769803776 | bytes 62914560 | tf_op jit(solution)/shard_map/expert_block/pallas_call | solution.py:381
  286.3 1.6 add_convert_fusion.2
  290.2 38.6 %expert_block.7 = (bf16[1024,768]{1,0:T(8,128)(2,1)S(1)}, bf16[1024,768]{1,0:T(8,128)(2,1)}, bf16[1040,768]{1,0:T(8,128)(2,1)}, bf16[1040,768]{1,0:T(8,128)(2,1)...) custom-call(s32[1]{0:T(128)} %bitcast.21.first, ...), custom_call_target="tpu_custom_call", output_to_operand_aliasing={{4}: (9, {}), {5}: (10, {}), {6}: (11, {}), {7}: (12, {})} | custom-call | flops 25769803776 | bytes 62914560 | tf_op jit(solution)/shard_map/expert_block/pallas_call | solution.py:381
  329.1 1.9 add_convert_fusion.1
  331.0 1.9 collective-permute-start.21
  332.9 27.5 %convolution_convert_fusion = bf16[2,768,3072]{2,1,0:T(8,128)(2,1)} fusion(bf16[2,2048,768]{2,1,0:T(8,128)(2,1)} %get-tuple-element.136, bf16[2,2048,3072]{2,1,0:T(8,128)(2,1)} %get-tuple-element.137), kind=kOutput, calls=%fused_computation | convolution fusion | flops 19332071424 | bytes 40894464 | tf_op jit(solution)/shard_map/ekd,ekf->edf/dot_general | solution.py:775
  360.4 9.2 %collective-permute-done.21 = bf16[1040,768]{1,0:T(8,128)(2,1)} collective-permute-done((bf16[1040,768]{1,0:T(8,128)(2,1)}, bf16[1040,768]{1,0:T(8,128)(2,1)}, u32[]{:S(2)}, u32[]{:S(2)}) %collective-permute-start.21) | collective-permute-done | bytes 1597472 | tf_op jit(solution)/shard_map/ppermute | solution.py:420
  369.6 4.1 add_convert_fusion
  375.5 29.1 %convolution_convert_fusion.1 = bf16[2,3072,768]{2,1,0:T(8,128)(2,1)} fusion(bf16[2,2048,3072]{2,1,0:T(8,128)(2,1)} %get-tuple-element.128, bf16[2,2048,768]{2,1,0:T(8,128)(2,1)} %get-tuple-element.140), kind=kOutput, calls=%fused_computation.1 | convolution fusion | flops 19332071424 | bytes 40894464 | tf_op jit(solution)/shard_map/ekf,ekd->efd/dot_general | solution.py:778
  404.6 3.3 add_convert_fusion.5
  407.9 3.3 add_convert_fusion.6
  411.2 2.2 collective-permute-done.24
  413.4 4.4 convert_add_fusion.1
  420.3 2.1 collective-permute-start.22
  423.6 4.2 multiply_reduce_fusion
  429.1 3.8 convolution_convert_fusion.2.dctx
  433.4 26.2 %attend_back.1 = (bf16[1024,768]{1,0:T(8,128)(2,1)S(1)}, bf16[1024,768]{1,0:T(8,128)(2,1)S(1)}, bf16[1024,768]{1,0:T(8,128)(2,1)S(1)}, f32[12,8,384]{2,1,0:T(8,128)S(1)}, f32[6,8,256]{2,1,0:T(8,128)S(1)}) custom-call(f32[12,8,384]{2,1,0:T(8,128)S(1)} %copy-done.15, s32[1024,1]{1,0:T(8,128)S(1)} %copy.99.seg_col, s32[1,1024]{1,0:T(1,128)S(1)} %bitcast.212, ...), custom_call_target="tpu_custom_call" | custom-call | flops 1 | bytes 1024 | tf_op jit(solution)/shard_map/attend_back/pallas_call | solution.py:213
  471.6 3.5 fusion.7
  477.9 12.5 %collective-permute-done.22 = bf16[1024,768]{1,0:T(8,128)(2,1)} collective-permute-done((bf16[1024,768]{1,0:T(8,128)(2,1)}, bf16[1024,768]{1,0:T(8,128)(2,1)}, u32[]{:S(2)}, u32[]{:S(2)}) %collective-permute-start.22) | collective-permute-done | bytes 1572896 | tf_op jit(solution)/shard_map/ppermute | solution.py:420
  492.6 5.0 fusion.6
  497.6 10.7 %collective-permute-done.31 = bf16[392,768]{1,0:T(8,128)(2,1)S(1)} collective-permute-done((bf16[392,768]{1,0:T(8,128)(2,1)S(1)}, bf16[392,768]{1,0:T(8,128)(2,1)S(1)}, u32[]{:S(2)}, u32[]{:S(2)}) %collective-permute-start.31) | collective-permute-done | bytes 602144 | tf_op jit(solution)/shard_map/ppermute | solution.py:420
  508.6 4.7 convert_element_type.564
  515.5 14.7 %collective-permute-done.33 = bf16[392,768]{1,0:T(8,128)(2,1)S(1)} collective-permute-done((bf16[392,768]{1,0:T(8,128)(2,1)S(1)}, bf16[392,768]{1,0:T(8,128)(2,1)S(1)}, u32[]{:S(2)}, u32[]{:S(2)}) %collective-permute-start.33) | collective-permute-done | bytes 602144 | tf_op jit(solution)/shard_map/ppermute | solution.py:420
  531.2 1.6 fusion.13
  534.3 3.6 add_convert_fusion.4
  537.9 2.4 collective-permute-start.35
  540.3 11.2 %collective-permute-done.37 = bf16[392,768]{1,0:T(8,128)(2,1)} collective-permute-done((bf16[392,768]{1,0:T(8,128)(2,1)}, bf16[392,768]{1,0:T(8,128)(2,1)}, u32[]{:S(2)}, u32[]{:S(2)}) %collective-permute-start.37) | collective-permute-done | bytes 602144 | tf_op jit(solution)/shard_map/ppermute | solution.py:420
  555.8 1.6 collective-permute-start.41
  561.6 1.6 collective-permute-start.44
  566.6 2.2 collective-permute-done.42
  569.5 4.0 collective-permute-done.44
  573.9 3.3 collective-permute-start.47
  577.2 4.4 convert_element_type.622
  582.2 4.6 add_convert_fusion.3
  (370 shorter events, 72.8 us)
Async XLA Ops:
  7.2 501.4 %reduce-scatter.3.cloned.1.call-start = ((), (), s32[]{:S(2)}) async-start(), calls=%async_computation.2 | async-start | bytes 11796480 | tf_op jit(solution)/shard_map/reduce_scatter | solution.py:777
  11.4 72.8 %collective-permute-start = (bf16[1024,768]{1,0:T(8,128)(2,1)}, bf16[1024,768]{1,0:T(8,128)(2,1)}, u32[]{:S(2)}, u32[]{:S(2)}) collective-permute-start(bf16[1024,768]{1,0:T(8,128)(2,1)} %broadcast_select_fusion.g_a), channel_id=1, source_target_pairs={{0,2},{1,3},{2,6},{3,7},{6,4},{7,5},{4,0},{5,1},{8,10},{9,11},{10,... | collective-permute-start | bytes 4718600 | tf_op jit(solution)/shard_map/ppermute | solution.py:420
  14.4 144.4 %collective-permute-start.3 = (bf16[1024,768]{1,0:T(8,128)(2,1)}, bf16[1024,768]{1,0:T(8,128)(2,1)}, u32[]{:S(2)}, u32[]{:S(2)}) collective-permute-start(bf16[1024,768]{1,0:T(8,128)(2,1)} %broadcast_select_fusion.g_a), channel_id=1, source_target_pairs={{0,1},{1,0},{2,3},{3,2},{4,5},{5,4},{6,7},{7,6},{8,9},{9,8},{10,11... | collective-permute-start | bytes 4718600 | tf_op jit(solution)/shard_map/ppermute | solution.py:430
  76.8 41.2 %collective-permute-start.1 = (bf16[1024,768]{1,0:T(8,128)(2,1)}, bf16[1024,768]{1,0:T(8,128)(2,1)}, u32[]{:S(2)}, u32[]{:S(2)}) collective-permute-start(bf16[1024,768]{1,0:T(8,128)(2,1)} %broadcast_select_fusion.g_a), channel_id=1, source_target_pairs={{0,4},{1,5},{2,0},{3,1},{6,2},{7,3},{4,6},{5,7},{8,12},{9,13},{10,... | collective-permute-start | bytes 4718600 | tf_op jit(solution)/shard_map/ppermute | solution.py:427
  120.1 38.7 %collective-permute-start.4 = (bf16[1024,768]{1,0:T(8,128)(2,1)}, bf16[1024,768]{1,0:T(8,128)(2,1)}, u32[]{:S(2)}, u32[]{:S(2)}) collective-permute-start(bf16[1024,768]{1,0:T(8,128)(2,1)} %collective-permute-done.g_a), channel_id=1, source_target_pairs={{0,2},{1,3},{2,6},{3,7},{6,4},{7,5},{4,0},{5,1},{8,10},{9,11},{10,... | collective-permute-start | bytes 4718600 | tf_op jit(solution)/shard_map/ppermute | solution.py:420
  121.3 37.5 %collective-permute-start.2 = (bf16[1024,768]{1,0:T(8,128)(2,1)S(1)}, bf16[1024,768]{1,0:T(8,128)(2,1)}, u32[]{:S(2)}, u32[]{:S(2)}) collective-permute-start(bf16[1024,768]{1,0:T(8,128)(2,1)S(1)} %multiply_convert_fusion.n_a), channel_id=1, source_target_pairs={{0,1},{1,0},{2,3},{3,2},{4,5},{5,4},{6,7},{7,6},{8,9},{9,8},{10,11... | collective-permute-start | bytes 4718600 | tf_op jit(solution)/shard_map/ppermute | solution.py:430
  126.1 73.0 %collective-permute-start.6 = (bf16[1024,768]{1,0:T(8,128)(2,1)S(1)}, bf16[1024,768]{1,0:T(8,128)(2,1)S(1)}, u32[]{:S(2)}, u32[]{:S(2)}) collective-permute-start(bf16[1024,768]{1,0:T(8,128)(2,1)S(1)} %multiply_convert_fusion.n_a), channel_id=1, source_target_pairs={{0,2},{1,3},{2,6},{3,7},{6,4},{7,5},{4,0},{5,1},{8,10},{9,11},{10,... | collective-permute-start | bytes 4718600 | tf_op jit(solution)/shard_map/ppermute | solution.py:420
  128.3 71.9 %collective-permute-start.9 = (bf16[1024,768]{1,0:T(8,128)(2,1)}, bf16[1024,768]{1,0:T(8,128)(2,1)S(1)}, u32[]{:S(2)}, u32[]{:S(2)}) collective-permute-start(bf16[1024,768]{1,0:T(8,128)(2,1)} %collective-permute-done.g_a), channel_id=1, source_target_pairs={{0,1},{1,0},{2,3},{3,2},{4,5},{5,4},{6,7},{7,6},{8,9},{9,8},{10,11... | collective-permute-start | bytes 4718600 | tf_op jit(solution)/shard_map/ppermute | solution.py:430
  199.1 3.4 collective-permute-start.8
  199.2 43.7 %collective-permute-start.7 = (bf16[1024,768]{1,0:T(8,128)(2,1)S(1)}, bf16[1024,768]{1,0:T(8,128)(2,1)S(1)}, u32[]{:S(2)}, u32[]{:S(2)}) collective-permute-start(bf16[1024,768]{1,0:T(8,128)(2,1)S(1)} %collective-permute-done.6.n_a), channel_id=1, source_target_pairs={{0,2},{1,3},{2,6},{3,7},{6,4},{7,5},{4,0},{5,1},{8,10},{9,11},{10,... | collective-permute-start | bytes 4718600 | tf_op jit(solution)/shard_map/ppermute | solution.py:420
  199.6 44.3 %collective-permute-start.12 = (bf16[1024,768]{1,0:T(8,128)(2,1)}, bf16[1024,768]{1,0:T(8,128)(2,1)S(1)}, u32[]{:S(2)}, u32[]{:S(2)}) collective-permute-start(bf16[1024,768]{1,0:T(8,128)(2,1)} %collective-permute-done.4.g_a), channel_id=1, source_target_pairs={{0,1},{1,0},{2,3},{3,2},{4,5},{5,4},{6,7},{7,6},{8,9},{9,8},{10,11... | collective-permute-start | bytes 4718600 | tf_op jit(solution)/shard_map/ppermute | solution.py:430
  243.1 45.4 %collective-permute-start.14 = (bf16[1024,768]{1,0:T(8,128)(2,1)}, bf16[1024,768]{1,0:T(8,128)(2,1)}, u32[]{:S(2)}, u32[]{:S(2)}) collective-permute-start(bf16[1024,768]{1,0:T(8,128)(2,1)} %collective-permute-done.1.g_a), channel_id=1, source_target_pairs={{0,1},{1,0},{2,3},{3,2},{4,5},{5,4},{6,7},{7,6},{8,9},{9,8},{10,11... | collective-permute-start | bytes 4718600 | tf_op jit(solution)/shard_map/ppermute | solution.py:430
  243.5 42.1 %collective-permute-start.10 = (bf16[1024,768]{1,0:T(8,128)(2,1)S(1)}, bf16[1024,768]{1,0:T(8,128)(2,1)S(1)}, u32[]{:S(2)}, u32[]{:S(2)}) collective-permute-start(bf16[1024,768]{1,0:T(8,128)(2,1)S(1)} %collective-permute-done.7.n_a), channel_id=1, source_target_pairs={{0,2},{1,3},{2,6},{3,7},{6,4},{7,5},{4,0},{5,1},{8,10},{9,11},{10,... | collective-permute-start | bytes 4718600 | tf_op jit(solution)/shard_map/ppermute | solution.py:420
  243.9 42.4 %collective-permute-start.15 = (bf16[1040,768]{1,0:T(8,128)(2,1)}, bf16[1040,768]{1,0:T(8,128)(2,1)S(1)}, u32[]{:S(2)}, u32[]{:S(2)}) collective-permute-start(bf16[1040,768]{1,0:T(8,128)(2,1)} %get-tuple-element.118), channel_id=1, source_target_pairs={{0,1},{1,0},{2,3},{3,2},{4,5},{5,4},{6,7},{7,6},{8,9},{9,8},{10,11... | collective-permute-start | bytes 4792328 | tf_op jit(solution)/shard_map/ppermute | solution.py:430
  285.6 3.5 collective-permute-start.13
  285.8 43.3 %collective-permute-start.19 = (bf16[1040,768]{1,0:T(8,128)(2,1)}, bf16[1040,768]{1,0:T(8,128)(2,1)S(1)}, u32[]{:S(2)}, u32[]{:S(2)}) collective-permute-start(bf16[1040,768]{1,0:T(8,128)(2,1)} %get-tuple-element.132), channel_id=1, source_target_pairs={{0,1},{1,0},{2,3},{3,2},{4,5},{5,4},{6,7},{7,6},{8,9},{9,8},{10,11... | collective-permute-start | bytes 4792328 | tf_op jit(solution)/shard_map/ppermute | solution.py:430
  287.9 41.2 %collective-permute-start.20 = (bf16[1040,768]{1,0:T(8,128)(2,1)}, bf16[1040,768]{1,0:T(8,128)(2,1)S(1)}, u32[]{:S(2)}, u32[]{:S(2)}) collective-permute-start(bf16[1040,768]{1,0:T(8,128)(2,1)} %add_convert_fusion.2), channel_id=1, source_target_pairs={{0,2},{1,3},{2,6},{3,7},{6,4},{7,5},{4,0},{5,1},{8,10},{9,11},{10,... | collective-permute-start | bytes 4792328 | tf_op jit(solution)/shard_map/ppermute | solution.py:420
  328.9 31.5 %collective-permute-start.18 = (bf16[1040,768]{1,0:T(8,128)(2,1)}, bf16[1040,768]{1,0:T(8,128)(2,1)}, u32[]{:S(2)}, u32[]{:S(2)}) collective-permute-start(bf16[1040,768]{1,0:T(8,128)(2,1)} %get-tuple-element.131), channel_id=1, source_target_pairs={{0,1},{1,0},{2,3},{3,2},{4,5},{5,4},{6,7},{7,6},{8,9},{9,8},{10,11... | collective-permute-start | bytes 4792328 | tf_op jit(solution)/shard_map/ppermute | solution.py:430
  331.0 38.6 %collective-permute-start.21 = (bf16[1040,768]{1,0:T(8,128)(2,1)}, bf16[1040,768]{1,0:T(8,128)(2,1)}, u32[]{:S(2)}, u32[]{:S(2)}) collective-permute-start(bf16[1040,768]{1,0:T(8,128)(2,1)} %add_convert_fusion.1), channel_id=1, source_target_pairs={{0,2},{1,3},{2,6},{3,7},{6,4},{7,5},{4,0},{5,1},{8,10},{9,11},{10,... | collective-permute-start | bytes 4792328 | tf_op jit(solution)/shard_map/ppermute | solution.py:420
  373.8 203.4 %reduce-scatter.5.cloned.1.call-start = ((), (), s32[]{:S(2)}) async-start(), calls=%async_computation.3 | async-start | bytes 11796480 | tf_op jit(solution)/shard_map/reduce_scatter | solution.py:787
  373.8 37.4 %collective-permute-start.23 = (bf16[1040,768]{1,0:T(8,128)(2,1)}, bf16[1040,768]{1,0:T(8,128)(2,1)}, u32[]{:S(2)}, u32[]{:S(2)}) collective-permute-start(bf16[1040,768]{1,0:T(8,128)(2,1)} %get-tuple-element.142), channel_id=1, source_target_pairs={{0,1},{1,0},{2,3},{3,2},{4,5},{5,4},{6,7},{7,6},{8,9},{9,8},{10,11... | collective-permute-start | bytes 4792328 | tf_op jit(solution)/shard_map/ppermute | solution.py:430
  373.9 30.7 %collective-permute-start.25 = (bf16[1024,768]{1,0:T(8,128)(2,1)}, bf16[1024,768]{1,0:T(8,128)(2,1)}, u32[]{:S(2)}, u32[]{:S(2)}) collective-permute-start(bf16[1024,768]{1,0:T(8,128)(2,1)} %copy-done.20), channel_id=1, source_target_pairs={{0,1},{1,0},{2,3},{3,2},{4,5},{5,4},{6,7},{7,6},{8,9},{9,8},{10,11... | collective-permute-start | bytes 4718600 | tf_op jit(solution)/shard_map/ppermute | solution.py:430
  374.4 30.3 %collective-permute-start.17 = (bf16[1024,768]{1,0:T(8,128)(2,1)}, bf16[1024,768]{1,0:T(8,128)(2,1)}, u32[]{:S(2)}, u32[]{:S(2)}) collective-permute-start(bf16[1024,768]{1,0:T(8,128)(2,1)} %copy-done.21), channel_id=1, source_target_pairs={{0,1},{1,0},{2,3},{3,2},{4,5},{5,4},{6,7},{7,6},{8,9},{9,8},{10,11... | collective-permute-start | bytes 4718600 | tf_op jit(solution)/shard_map/ppermute | solution.py:430
  374.5 38.9 %collective-permute-start.24 = (bf16[1040,768]{1,0:T(8,128)(2,1)}, bf16[1040,768]{1,0:T(8,128)(2,1)}, u32[]{:S(2)}, u32[]{:S(2)}) collective-permute-start(bf16[1040,768]{1,0:T(8,128)(2,1)} %add_convert_fusion), channel_id=1, source_target_pairs={{0,2},{1,3},{2,6},{3,7},{6,4},{7,5},{4,0},{5,1},{8,10},{9,11},{10,... | collective-permute-start | bytes 4792328 | tf_op jit(solution)/shard_map/ppermute | solution.py:420
  420.2 39.4 %collective-permute-start.26 = (bf16[1024,768]{1,0:T(8,128)(2,1)}, bf16[1024,768]{1,0:T(8,128)(2,1)}, u32[]{:S(2)}, u32[]{:S(2)}) collective-permute-start(bf16[1024,768]{1,0:T(8,128)(2,1)} %add_convert_fusion.5), channel_id=1, source_target_pairs={{0,4},{1,5},{2,0},{3,1},{6,2},{7,3},{4,6},{5,7},{8,12},{9,13},{10,... | collective-permute-start | bytes 4718600 | tf_op jit(solution)/shard_map/ppermute | solution.py:427
  420.3 70.1 %collective-permute-start.22 = (bf16[1024,768]{1,0:T(8,128)(2,1)}, bf16[1024,768]{1,0:T(8,128)(2,1)}, u32[]{:S(2)}, u32[]{:S(2)}) collective-permute-start(bf16[1024,768]{1,0:T(8,128)(2,1)} %add_convert_fusion.6), channel_id=1, source_target_pairs={{0,2},{1,3},{2,6},{3,7},{6,4},{7,5},{4,0},{5,1},{8,10},{9,11},{10,... | collective-permute-start | bytes 4718600 | tf_op jit(solution)/shard_map/ppermute | solution.py:420
  468.6 21.8 %collective-permute-start.29 = (bf16[4,96,768]{2,1,0:T(8,128)(2,1)}, bf16[4,96,768]{2,1,0:T(8,128)(2,1)}, u32[]{:S(2)}, u32[]{:S(2)}) collective-permute-start(bf16[4,96,768]{2,1,0:T(8,128)(2,1)} %get-tuple-element.187), channel_id=1, source_target_pairs={{0,1},{1,0},{2,3},{3,2},{4,5},{5,4},{6,7},{7,6},{8,9},{9,8},{10,11... | collective-permute-start | bytes 1769480 | tf_op jit(solution)/shard_map/ppermute | solution.py:430
  492.0 16.4 %collective-permute-start.31 = (bf16[392,768]{1,0:T(8,128)(2,1)S(1)}, bf16[392,768]{1,0:T(8,128)(2,1)S(1)}, u32[]{:S(2)}, u32[]{:S(2)}) collective-permute-start(bf16[392,768]{1,0:T(8,128)(2,1)S(1)} %pad_maximum_fusion.1), channel_id=1, source_target_pairs={{0,2},{1,3},{2,6},{3,7},{6,4},{7,5},{4,0},{5,1},{8,10},{9,11},{10,... | collective-permute-start | bytes 1806344 | tf_op jit(solution)/shard_map/ppermute | solution.py:420
  492.1 21.2 %collective-permute-start.28 = (bf16[4,96,768]{2,1,0:T(8,128)(2,1)S(1)}, bf16[4,96,768]{2,1,0:T(8,128)(2,1)}, u32[]{:S(2)}, u32[]{:S(2)}) collective-permute-start(bf16[4,96,768]{2,1,0:T(8,128)(2,1)S(1)} %get-tuple-element.188), channel_id=1, source_target_pairs={{0,1},{1,0},{2,3},{3,2},{4,5},{5,4},{6,7},{7,6},{8,9},{9,8},{10,11... | collective-permute-start | bytes 1769480 | tf_op jit(solution)/shard_map/ppermute | solution.py:430
  492.1 16.3 %collective-permute-start.32 = (f32[24,128]{1,0:T(8,128)S(1)}, f32[24,128]{1,0:T(8,128)S(1)}, u32[]{:S(2)}, u32[]{:S(2)}) collective-permute-start(f32[24,128]{1,0:T(8,128)S(1)} %bitcast.247), channel_id=1, source_target_pairs={{0,1},{1,0},{2,3},{3,2},{4,5},{5,4},{6,7},{7,6},{8,9},{9,8},{10,11... | collective-permute-start | bytes 36872 | tf_op jit(solution)/shard_map/ppermute | solution.py:430
  514.8 15.4 %collective-permute-start.33 = (bf16[392,768]{1,0:T(8,128)(2,1)S(1)}, bf16[392,768]{1,0:T(8,128)(2,1)S(1)}, u32[]{:S(2)}, u32[]{:S(2)}) collective-permute-start(bf16[392,768]{1,0:T(8,128)(2,1)S(1)} %pad_maximum_fusion.2), channel_id=1, source_target_pairs={{0,2},{1,3},{2,6},{3,7},{6,4},{7,5},{4,0},{5,1},{8,10},{9,11},{10,... | collective-permute-start | bytes 1806344 | tf_op jit(solution)/shard_map/ppermute | solution.py:420
  514.8 19.5 %collective-permute-start.16 = (bf16[1024,768]{1,0:T(8,128)(2,1)}, bf16[1024,768]{1,0:T(8,128)(2,1)}, u32[]{:S(2)}, u32[]{:S(2)}) collective-permute-start(bf16[1024,768]{1,0:T(8,128)(2,1)} %get-tuple-element.125), channel_id=1, source_target_pairs={{0,1},{1,0},{2,3},{3,2},{4,5},{5,4},{6,7},{7,6},{8,9},{9,8},{10,11... | collective-permute-start | bytes 4718600 | tf_op jit(solution)/shard_map/ppermute | solution.py:430
  514.9 15.5 %collective-permute-start.27 = (bf16[4,96,768]{2,1,0:T(8,128)(2,1)S(1)}, bf16[4,96,768]{2,1,0:T(8,128)(2,1)S(1)}, u32[]{:S(2)}, u32[]{:S(2)}) collective-permute-start(bf16[4,96,768]{2,1,0:T(8,128)(2,1)S(1)} %get-tuple-element.189), channel_id=1, source_target_pairs={{0,1},{1,0},{2,3},{3,2},{4,5},{5,4},{6,7},{7,6},{8,9},{9,8},{10,11... | collective-permute-start | bytes 1769480 | tf_op jit(solution)/shard_map/ppermute | solution.py:430
  515.4 14.9 %collective-permute-start.34 = (f32[24,128]{1,0:T(8,128)S(1)}, f32[24,128]{1,0:T(8,128)S(1)}, u32[]{:S(2)}, u32[]{:S(2)}) collective-permute-start(f32[24,128]{1,0:T(8,128)S(1)} %bitcast.246), channel_id=1, source_target_pairs={{0,1},{1,0},{2,3},{3,2},{4,5},{5,4},{6,7},{7,6},{8,9},{9,8},{10,11... | collective-permute-start | bytes 36872 | tf_op jit(solution)/shard_map/ppermute | solution.py:430
  533.7 17.7 %collective-permute-start.37 = (bf16[392,768]{1,0:T(8,128)(2,1)}, bf16[392,768]{1,0:T(8,128)(2,1)}, u32[]{:S(2)}, u32[]{:S(2)}) collective-permute-start(bf16[392,768]{1,0:T(8,128)(2,1)} %pad_maximum_fusion.3), channel_id=1, source_target_pairs={{0,2},{1,3},{2,6},{3,7},{6,4},{7,5},{4,0},{5,1},{8,10},{9,11},{10,... | collective-permute-start | bytes 1806344 | tf_op jit(solution)/shard_map/ppermute | solution.py:420
  533.7 47.8 %collective-permute-start.5 = (bf16[1024,768]{1,0:T(8,128)(2,1)S(1)}, bf16[1024,768]{1,0:T(8,128)(2,1)}, u32[]{:S(2)}, u32[]{:S(2)}) collective-permute-start(bf16[1024,768]{1,0:T(8,128)(2,1)S(1)} %copy-done.19), channel_id=1, source_target_pairs={{0,1},{1,0},{2,3},{3,2},{4,5},{5,4},{6,7},{7,6},{8,9},{9,8},{10,11... | collective-permute-start | bytes 4718600 | tf_op jit(solution)/shard_map/ppermute | solution.py:430
  533.7 22.1 %collective-permute-start.36 = (bf16[4,96,768]{2,1,0:T(8,128)(2,1)}, bf16[4,96,768]{2,1,0:T(8,128)(2,1)}, u32[]{:S(2)}, u32[]{:S(2)}) collective-permute-start(bf16[4,96,768]{2,1,0:T(8,128)(2,1)} %get-tuple-element.186), channel_id=1, source_target_pairs={{0,1},{1,0},{2,3},{3,2},{4,5},{5,4},{6,7},{7,6},{8,9},{9,8},{10,11... | collective-permute-start | bytes 1769480 | tf_op jit(solution)/shard_map/ppermute | solution.py:430
  534.2 18.4 %collective-permute-start.38 = (f32[24,128]{1,0:T(8,128)S(1)}, f32[24,128]{1,0:T(8,128)S(1)}, u32[]{:S(2)}, u32[]{:S(2)}) collective-permute-start(f32[24,128]{1,0:T(8,128)S(1)} %bitcast.245), channel_id=1, source_target_pairs={{0,1},{1,0},{2,3},{3,2},{4,5},{5,4},{6,7},{7,6},{8,9},{9,8},{10,11... | collective-permute-start | bytes 36872 | tf_op jit(solution)/shard_map/ppermute | solution.py:430
  537.9 44.3 %collective-permute-start.35 = (bf16[1024,768]{1,0:T(8,128)(2,1)}, bf16[1024,768]{1,0:T(8,128)(2,1)}, u32[]{:S(2)}, u32[]{:S(2)}) collective-permute-start(bf16[1024,768]{1,0:T(8,128)(2,1)} %add_convert_fusion.4), channel_id=1, source_target_pairs={{0,2},{1,3},{2,6},{3,7},{6,4},{7,5},{4,0},{5,1},{8,10},{9,11},{10,... | collective-permute-start | bytes 4718600 | tf_op jit(solution)/shard_map/ppermute | solution.py:420
  552.7 7.0 %collective-permute-start.39 = (f32[24,128]{1,0:T(8,128)S(1)}, f32[24,128]{1,0:T(8,128)S(1)}, u32[]{:S(2)}, u32[]{:S(2)}) collective-permute-start(f32[24,128]{1,0:T(8,128)S(1)} %add_add_fusion.2), channel_id=1, source_target_pairs={{0,8},{8,0},{16,24},{24,16},{1,9},{9,1},{17,25},{25,17},{2,10},{10... | collective-permute-start | bytes 36872 | tf_op jit(solution)/shard_map/ppermute | solution.py:900
  554.2 6.9 %collective-permute-start.40 = (f32[24,128]{1,0:T(8,128)S(1)}, f32[24,128]{1,0:T(8,128)S(1)}, u32[]{:S(2)}, u32[]{:S(2)}) collective-permute-start(f32[24,128]{1,0:T(8,128)S(1)} %add_add_fusion.2), channel_id=1, source_target_pairs={{0,16},{8,24},{16,0},{24,8},{1,17},{9,25},{17,1},{25,9},{2,18},{10... | collective-permute-start | bytes 36872 | tf_op jit(solution)/shard_map/ppermute | solution.py:900
  555.8 5.8 collective-permute-start.41
  559.7 9.1 %collective-permute-start.42 = (bf16[96,768]{1,0:T(8,128)(2,1)}, bf16[96,768]{1,0:T(8,128)(2,1)S(1)}, u32[]{:S(2)}, u32[]{:S(2)}) collective-permute-start(bf16[96,768]{1,0:T(8,128)(2,1)} %get-tuple-element.196), channel_id=1, source_target_pairs={{0,8},{8,0},{16,24},{24,16},{1,9},{9,1},{17,25},{25,17},{2,10},{10... | collective-permute-start | bytes 442376 | tf_op jit(solution)/shard_map/ppermute | solution.py:909
  561.1 8.4 %collective-permute-start.43 = (bf16[96,768]{1,0:T(8,128)(2,1)}, bf16[96,768]{1,0:T(8,128)(2,1)S(1)}, u32[]{:S(2)}, u32[]{:S(2)}) collective-permute-start(bf16[96,768]{1,0:T(8,128)(2,1)} %get-tuple-element.198), channel_id=1, source_target_pairs={{0,16},{8,24},{16,0},{24,8},{1,17},{9,25},{17,1},{25,9},{2,18},{10... | collective-permute-start | bytes 442376 | tf_op jit(solution)/shard_map/ppermute | solution.py:909
  561.6 12.0 %collective-permute-start.44 = (bf16[96,768]{1,0:T(8,128)(2,1)S(1)}, bf16[96,768]{1,0:T(8,128)(2,1)S(1)}, u32[]{:S(2)}, u32[]{:S(2)}) collective-permute-start(bf16[96,768]{1,0:T(8,128)(2,1)S(1)} %get-tuple-element.197), channel_id=1, source_target_pairs={{0,24},{8,16},{16,8},{24,0},{1,25},{9,17},{17,9},{25,1},{2,26},{10... | collective-permute-start | bytes 442376 | tf_op jit(solution)/shard_map/ppermute | solution.py:909
  573.6 13.2 %collective-permute-start.45 = (bf16[96,768]{1,0:T(8,128)(2,1)S(1)}, bf16[96,768]{1,0:T(8,128)(2,1)S(1)}, u32[]{:S(2)}, u32[]{:S(2)}) collective-permute-start(bf16[96,768]{1,0:T(8,128)(2,1)S(1)} %fusion.42), channel_id=1, source_target_pairs={{0,8},{8,0},{16,24},{24,16},{1,9},{9,1},{17,25},{25,17},{2,10},{10... | collective-permute-start | bytes 442376 | tf_op jit(solution)/shard_map/ppermute | solution.py:909
  573.9 12.9 %collective-permute-start.46 = (bf16[96,768]{1,0:T(8,128)(2,1)S(1)}, bf16[96,768]{1,0:T(8,128)(2,1)}, u32[]{:S(2)}, u32[]{:S(2)}) collective-permute-start(bf16[96,768]{1,0:T(8,128)(2,1)S(1)} %fusion.42), channel_id=1, source_target_pairs={{0,16},{8,24},{16,0},{24,8},{1,17},{9,25},{17,1},{25,9},{2,18},{10... | collective-permute-start | bytes 442376 | tf_op jit(solution)/shard_map/ppermute | solution.py:909
  573.9 12.9 %collective-permute-start.47 = (bf16[96,768]{1,0:T(8,128)(2,1)S(1)}, bf16[96,768]{1,0:T(8,128)(2,1)}, u32[]{:S(2)}, u32[]{:S(2)}) collective-permute-start(bf16[96,768]{1,0:T(8,128)(2,1)S(1)} %fusion.42), channel_id=1, source_target_pairs={{0,24},{8,16},{16,8},{24,0},{1,25},{9,17},{17,9},{25,1},{2,26},{10... | collective-permute-start | bytes 442376 | tf_op jit(solution)/shard_map/ppermute | solution.py:909
  (73 other events, 543.0 us)
Sparse Core Ops, SparseCore 0:
  373.9 93.7 reduce-scatter.2
  470.8 100.6 reduce-scatter.4

commit v8 on v7

--- a/solution.py
+++ b/solution.py
@@ -749,7 +749,7 @@
             ],
             axis=0,
         )
-        if k == 0:
+        if k == 1:
             info = after(info, ring[2])
         if k == group.chips - 1:
             back_own, back_sib = [r[2] for r in results], [r[3] for r in results]

time: 606 us -> 604 us (level)
  waiting for transfers between devices: 105 us -> 98.7 us
    unnamed x153 -> x155, local copies, waits for them, and re-layouts: 11.5 us -> 12.4 us
  transfers between devices with their start and end apart: 50 -> 50, of which waited for: 15 -> 14; matrix products, arithmetic and copies ran while one was open for 27% -> 27% of each run, Pallas kernels for 43% -> 44%
where the time goes in v8:
time: 604 us; the launch traced here: 595 us
  Pallas kernels  259 us (43%)
  waiting for transfers between devices  98.7 us (16%)
  matrix products  87.3 us (14%)
  other arithmetic  70.4 us (12%)
  starting transfers between devices  34.8 us (6%)
  local copies, waits for them, and re-layouts  24.9 us (4%)
  between operations  19.8 us (3%)
    pallas_call x4, Pallas kernels, expert_block(): pl.pallas_call(expert_kernel, grid=(local, hidden // part), in_specs=in_s...  153 us
    ppermute x13, waiting for transfers between devices, onward(): return lax.ppermute(x, 'grp', pairs)  86.7 us
    pallas_call x1, Pallas kernels, gather_group(): pl.pallas_call(partial(gather_kernel, chips, reps), in_specs=[hbm] * 3, o...  59.7 us
    dot_general x1, matrix products, shards(): jnp.einsum('ekf,ekd->efd', act_all, after(dy_all, sent), preferred_elemen...  29.1 us
    dot_general x1, matrix products, shards(): jnp.einsum('ekd,ekf->edf', after(x_all, sent), dpre_all, preferred_elemen...  27.3 us
    pallas_call x1, Pallas kernels, attend_back(): pl.pallas_call(bwd_kernel, grid=(pairs,), in_specs=[band, whole(seq, 1),...  26.2 us
    pallas_call x1, Pallas kernels, attend(): pl.pallas_call(fwd_kernel, grid=(pairs,), in_specs=[pl.BlockSpec((2, 8, S...  20 us
    ppermute x13, starting transfers between devices, onward(): return lax.ppermute(x, 'grp', pairs)  16.2 us
  transfers between devices with their start and end apart: 50, of which 14 were waited for; matrix products, arithmetic and copies ran while one was open for 27% of the time, Pallas kernels for 44%

profile of v8, /device:TPU:0, one launch (start us, length us, event | category | flops | bytes accessed | tf_op | source)
XLA Modules:
  0.0 594.9 jit_solution(16904932255644022984)
XLA Ops:
  8.5 2.8 broadcast_select_fusion.g_a
  11.4 3.0 collective-permute-start
  17.0 59.7 %gather_group.1 = (bf16[4,768,768]{2,1,0:T(8,128)(2,1)}, bf16[8,48,128]{2,1,0:T(8,128)(2,1)}, f32[8,8,128]{2,1,0:T(8,128)}) custom-call(bf16[4,96,768]{2,1,0:T(8,128)(2,1)} %pad_maximum_fusion.4.stack, bf16[48,128]{1,0:T(8,128)(2,1)} %pad.52.small, f32[8,128]{1,0:T(8,128)} %pad.53.tally), custom_call_target="tpu_custom_call" | custom-call | bytes 16777216 | tf_op jit(solution)/shard_map/gather_group/pallas_call | solution.py:570
  76.8 1.8 collective-permute-start.1
  84.3 4.5 reduce-window.6
  89.8 3.3 convolution_convert_fusion.3.v
  93.1 3.2 convolution_convert_fusion.4.k
  97.9 20.0 %attend.1 = (bf16[1024,768]{1,0:T(8,128)(2,1)S(1)}, f32[6,8,256]{2,1,0:T(8,128)S(1)}) custom-call(f32[12,8,384]{2,1,0:T(8,128)S(1)} %copy_subtract_fusion.base, s32[1024,1]{1,0:T(8,128)S(1)} %copy.94.seg_col, s32[1,1024]{1,0:T(1,128)S(1)} %bitcast.210, bf16[1024,768]{1,0:T(8,128)(2,1)S(1)} %convolution_convert_fusion.5.q, ...), custom_call_target="tpu_custom_call" | custom-call | flops 1 | bytes 1024 | tf_op jit(solution)/shard_map/attend/pallas_call | solution.py:123
  126.5 2.7 collective-permute-start.9
  129.3 38.0 %expert_block.4 = (bf16[1024,768]{1,0:T(8,128)(2,1)S(1)}, bf16[1024,768]{1,0:T(8,128)(2,1)S(1)}, bf16[1040,768]{1,0:T(8,128)(2,1)}, bf16[1040,768]{1,0:T(8,128)(...) custom-call(s32[1]{0:T(128)} %bitcast.21.first, ...), custom_call_target="tpu_custom_call" | custom-call | flops 25769803776 | bytes 62914560 | tf_op jit(solution)/shard_map/expert_block/pallas_call | solution.py:381
  170.2 2.2 collective-permute-start.6
  172.4 25.6 %collective-permute-done.9.g_a = bf16[1024,768]{1,0:T(8,128)(2,1)S(1)} collective-permute-done((bf16[1024,768]{1,0:T(8,128)(2,1)}, bf16[1024,768]{1,0:T(8,128)(2,1)S(1)}, u32[]{:S(2)}, u32[]{:S(2)}) %collective-permute-start.9) | collective-permute-done | bytes 1572896 | tf_op jit(solution)/shard_map/ppermute | solution.py:420
  199.8 38.0 %expert_block.5 = (bf16[1024,768]{1,0:T(8,128)(2,1)S(1)}, bf16[1024,768]{1,0:T(8,128)(2,1)S(1)}, bf16[1040,768]{1,0:T(8,128)(2,1)}, bf16[1040,768]{1,0:T(8,128)(...) custom-call(s32[1]{0:T(128)} %bitcast.21.first, ...), custom_call_target="tpu_custom_call", output_to_operand_aliasing={{4}: (9, {}), {5}: (10, {}), {6}: (11, {}), {7}: (12, {})} | custom-call | flops 25769803776 | bytes 62914560 | tf_op jit(solution)/shard_map/expert_block/pallas_call | solution.py:381
  240.3 3.0 collective-permute-done.11.n_b
  244.5 38.4 %expert_block.6 = (bf16[1024,768]{1,0:T(8,128)(2,1)S(1)}, bf16[1024,768]{1,0:T(8,128)(2,1)S(1)}, bf16[1040,768]{1,0:T(8,128)(2,1)}, bf16[1040,768]{1,0:T(8,128)(...) custom-call(s32[1]{0:T(128)} %bitcast.21.first, ...), custom_call_target="tpu_custom_call", output_to_operand_aliasing={{4}: (9, {}), {5}: (10, {}), {6}: (11, {}), {7}: (12, {})} | custom-call | flops 25769803776 | bytes 62914560 | tf_op jit(solution)/shard_map/expert_block/pallas_call | solution.py:381
  283.7 1.6 add_convert_fusion.2
  287.7 38.6 %expert_block.7 = (bf16[1024,768]{1,0:T(8,128)(2,1)S(1)}, bf16[1024,768]{1,0:T(8,128)(2,1)}, bf16[1040,768]{1,0:T(8,128)(2,1)}, bf16[1040,768]{1,0:T(8,128)(2,1)...) custom-call(s32[1]{0:T(128)} %bitcast.21.first, ...), custom_call_target="tpu_custom_call", output_to_operand_aliasing={{4}: (9, {}), {5}: (10, {}), {6}: (11, {}), {7}: (12, {})} | custom-call | flops 25769803776 | bytes 62914560 | tf_op jit(solution)/shard_map/expert_block/pallas_call | solution.py:381
  326.7 1.9 add_convert_fusion.1
  328.6 1.9 collective-permute-start.21
  330.5 27.3 %convolution_convert_fusion = bf16[2,768,3072]{2,1,0:T(8,128)(2,1)} fusion(bf16[2,2048,768]{2,1,0:T(8,128)(2,1)} %get-tuple-element.136, bf16[2,2048,3072]{2,1,0:T(8,128)(2,1)} %get-tuple-element.137), kind=kOutput, calls=%fused_computation | convolution fusion | flops 19332071424 | bytes 40894464 | tf_op jit(solution)/shard_map/ekd,ekf->edf/dot_general | solution.py:775
  357.8 9.3 %collective-permute-done.21 = bf16[1040,768]{1,0:T(8,128)(2,1)} collective-permute-done((bf16[1040,768]{1,0:T(8,128)(2,1)}, bf16[1040,768]{1,0:T(8,128)(2,1)}, u32[]{:S(2)}, u32[]{:S(2)}) %collective-permute-start.21) | collective-permute-done | bytes 1597472 | tf_op jit(solution)/shard_map/ppermute | solution.py:420
  367.0 4.1 add_convert_fusion
  373.3 29.1 %convolution_convert_fusion.1 = bf16[2,3072,768]{2,1,0:T(8,128)(2,1)} fusion(bf16[2,2048,3072]{2,1,0:T(8,128)(2,1)} %get-tuple-element.128, bf16[2,2048,768]{2,1,0:T(8,128)(2,1)} %get-tuple-element.140), kind=kOutput, calls=%fused_computation.1 | convolution fusion | flops 19332071424 | bytes 40894464 | tf_op jit(solution)/shard_map/ekf,ekd->efd/dot_general | solution.py:778
  402.4 3.2 add_convert_fusion.5
  405.7 3.3 add_convert_fusion.6
  409.0 1.8 collective-permute-done.24
  410.8 4.2 convert_add_fusion.1
  417.8 1.9 collective-permute-start.22
  420.8 4.2 multiply_reduce_fusion
  426.4 3.8 convolution_convert_fusion.2.dctx
  430.7 26.2 %attend_back.1 = (bf16[1024,768]{1,0:T(8,128)(2,1)S(1)}, bf16[1024,768]{1,0:T(8,128)(2,1)S(1)}, bf16[1024,768]{1,0:T(8,128)(2,1)S(1)}, f32[12,8,384]{2,1,0:T(8,128)S(1)}, f32[6,8,256]{2,1,0:T(8,128)S(1)}) custom-call(f32[12,8,384]{2,1,0:T(8,128)S(1)} %copy-done.15, s32[1024,1]{1,0:T(8,128)S(1)} %copy.99.seg_col, s32[1,1024]{1,0:T(1,128)S(1)} %bitcast.212, ...), custom_call_target="tpu_custom_call" | custom-call | flops 1 | bytes 1024 | tf_op jit(solution)/shard_map/attend_back/pallas_call | solution.py:213
  468.8 3.5 fusion.7
  475.2 12.9 %collective-permute-done.22 = bf16[1024,768]{1,0:T(8,128)(2,1)} collective-permute-done((bf16[1024,768]{1,0:T(8,128)(2,1)}, bf16[1024,768]{1,0:T(8,128)(2,1)}, u32[]{:S(2)}, u32[]{:S(2)}) %collective-permute-start.22) | collective-permute-done | bytes 1572896 | tf_op jit(solution)/shard_map/ppermute | solution.py:420
  490.2 5.0 fusion.6
  495.2 10.7 %collective-permute-done.31 = bf16[392,768]{1,0:T(8,128)(2,1)S(1)} collective-permute-done((bf16[392,768]{1,0:T(8,128)(2,1)S(1)}, bf16[392,768]{1,0:T(8,128)(2,1)S(1)}, u32[]{:S(2)}, u32[]{:S(2)}) %collective-permute-start.31) | collective-permute-done | bytes 602144 | tf_op jit(solution)/shard_map/ppermute | solution.py:420
  506.2 4.7 convert_element_type.564
  513.1 14.7 %collective-permute-done.33 = bf16[392,768]{1,0:T(8,128)(2,1)S(1)} collective-permute-done((bf16[392,768]{1,0:T(8,128)(2,1)S(1)}, bf16[392,768]{1,0:T(8,128)(2,1)S(1)}, u32[]{:S(2)}, u32[]{:S(2)}) %collective-permute-start.33) | collective-permute-done | bytes 602144 | tf_op jit(solution)/shard_map/ppermute | solution.py:420
  528.8 1.6 fusion.13
  531.9 3.6 add_convert_fusion.4
  535.5 2.2 collective-permute-start.35
  537.7 11.4 %collective-permute-done.37 = bf16[392,768]{1,0:T(8,128)(2,1)} collective-permute-done((bf16[392,768]{1,0:T(8,128)(2,1)}, bf16[392,768]{1,0:T(8,128)(2,1)}, u32[]{:S(2)}, u32[]{:S(2)}) %collective-permute-start.37) | collective-permute-done | bytes 602144 | tf_op jit(solution)/shard_map/ppermute | solution.py:420
  550.3 1.6 collective-permute-start.39
  553.4 1.6 collective-permute-start.41
  564.2 2.2 collective-permute-done.42
  567.2 4.1 collective-permute-done.44
  571.5 3.4 collective-permute-start.47
  574.9 4.4 convert_element_type.622
  579.7 4.6 add_convert_fusion.3
  (372 shorter events, 74.2 us)
Async XLA Ops:
  7.2 499.0 %reduce-scatter.3.cloned.1.call-start = ((), (), s32[]{:S(2)}) async-start(), calls=%async_computation.2 | async-start | bytes 11796480 | tf_op jit(solution)/shard_map/reduce_scatter | solution.py:777
  11.4 72.8 %collective-permute-start = (bf16[1024,768]{1,0:T(8,128)(2,1)}, bf16[1024,768]{1,0:T(8,128)(2,1)}, u32[]{:S(2)}, u32[]{:S(2)}) collective-permute-start(bf16[1024,768]{1,0:T(8,128)(2,1)} %broadcast_select_fusion.g_a), channel_id=1, source_target_pairs={{0,2},{1,3},{2,6},{3,7},{6,4},{7,5},{4,0},{5,1},{8,10},{9,11},{10,... | collective-permute-start | bytes 4718600 | tf_op jit(solution)/shard_map/ppermute | solution.py:420
  14.4 114.9 %collective-permute-start.3 = (bf16[1024,768]{1,0:T(8,128)(2,1)}, bf16[1024,768]{1,0:T(8,128)(2,1)}, u32[]{:S(2)}, u32[]{:S(2)}) collective-permute-start(bf16[1024,768]{1,0:T(8,128)(2,1)} %broadcast_select_fusion.g_a), channel_id=1, source_target_pairs={{0,1},{1,0},{2,3},{3,2},{4,5},{5,4},{6,7},{7,6},{8,9},{9,8},{10,11... | collective-permute-start | bytes 4718600 | tf_op jit(solution)/shard_map/ppermute | solution.py:430
  76.8 41.2 %collective-permute-start.1 = (bf16[1024,768]{1,0:T(8,128)(2,1)}, bf16[1024,768]{1,0:T(8,128)(2,1)}, u32[]{:S(2)}, u32[]{:S(2)}) collective-permute-start(bf16[1024,768]{1,0:T(8,128)(2,1)} %broadcast_select_fusion.g_a), channel_id=1, source_target_pairs={{0,4},{1,5},{2,0},{3,1},{6,2},{7,3},{4,6},{5,7},{8,12},{9,13},{10,... | collective-permute-start | bytes 4718600 | tf_op jit(solution)/shard_map/ppermute | solution.py:427
  121.3 8.0 %collective-permute-start.2 = (bf16[1024,768]{1,0:T(8,128)(2,1)S(1)}, bf16[1024,768]{1,0:T(8,128)(2,1)}, u32[]{:S(2)}, u32[]{:S(2)}) collective-permute-start(bf16[1024,768]{1,0:T(8,128)(2,1)S(1)} %multiply_convert_fusion.n_a), channel_id=1, source_target_pairs={{0,1},{1,0},{2,3},{3,2},{4,5},{5,4},{6,7},{7,6},{8,9},{9,8},{10,11... | collective-permute-start | bytes 4718600 | tf_op jit(solution)/shard_map/ppermute | solution.py:430
  126.2 43.5 %collective-permute-start.5 = (bf16[1024,768]{1,0:T(8,128)(2,1)S(1)}, bf16[1024,768]{1,0:T(8,128)(2,1)S(1)}, u32[]{:S(2)}, u32[]{:S(2)}) collective-permute-start(bf16[1024,768]{1,0:T(8,128)(2,1)S(1)} %multiply_convert_fusion.n_a), channel_id=1, source_target_pairs={{0,2},{1,3},{2,6},{3,7},{6,4},{7,5},{4,0},{5,1},{8,10},{9,11},{10,... | collective-permute-start | bytes 4718600 | tf_op jit(solution)/shard_map/ppermute | solution.py:420
  126.5 71.6 %collective-permute-start.9 = (bf16[1024,768]{1,0:T(8,128)(2,1)}, bf16[1024,768]{1,0:T(8,128)(2,1)S(1)}, u32[]{:S(2)}, u32[]{:S(2)}) collective-permute-start(bf16[1024,768]{1,0:T(8,128)(2,1)} %collective-permute-done.g_a), channel_id=1, source_target_pairs={{0,2},{1,3},{2,6},{3,7},{6,4},{7,5},{4,0},{5,1},{8,10},{9,11},{10,... | collective-permute-start | bytes 4718600 | tf_op jit(solution)/shard_map/ppermute | solution.py:420
  129.2 68.8 %collective-permute-start.8 = (bf16[1024,768]{1,0:T(8,128)(2,1)}, bf16[1024,768]{1,0:T(8,128)(2,1)S(1)}, u32[]{:S(2)}, u32[]{:S(2)}) collective-permute-start(bf16[1024,768]{1,0:T(8,128)(2,1)} %collective-permute-done.g_a), channel_id=1, source_target_pairs={{0,1},{1,0},{2,3},{3,2},{4,5},{5,4},{6,7},{7,6},{8,9},{9,8},{10,11... | collective-permute-start | bytes 4718600 | tf_op jit(solution)/shard_map/ppermute | solution.py:430
  169.7 28.4 %collective-permute-start.7 = (bf16[1024,768]{1,0:T(8,128)(2,1)S(1)}, bf16[1024,768]{1,0:T(8,128)(2,1)S(1)}, u32[]{:S(2)}, u32[]{:S(2)}) collective-permute-start(bf16[1024,768]{1,0:T(8,128)(2,1)S(1)} %collective-permute-done.5.n_a), channel_id=1, source_target_pairs={{0,1},{1,0},{2,3},{3,2},{4,5},{5,4},{6,7},{7,6},{8,9},{9,8},{10,11... | collective-permute-start | bytes 4718600 | tf_op jit(solution)/shard_map/ppermute | solution.py:430
  170.2 68.8 %collective-permute-start.6 = (bf16[1024,768]{1,0:T(8,128)(2,1)S(1)}, bf16[1024,768]{1,0:T(8,128)(2,1)S(1)}, u32[]{:S(2)}, u32[]{:S(2)}) collective-permute-start(bf16[1024,768]{1,0:T(8,128)(2,1)S(1)} %collective-permute-done.5.n_a), channel_id=1, source_target_pairs={{0,2},{1,3},{2,6},{3,7},{6,4},{7,5},{4,0},{5,1},{8,10},{9,11},{10,... | collective-permute-start | bytes 4718600 | tf_op jit(solution)/shard_map/ppermute | solution.py:420
  198.0 42.3 %collective-permute-start.12 = (bf16[1024,768]{1,0:T(8,128)(2,1)S(1)}, bf16[1024,768]{1,0:T(8,128)(2,1)S(1)}, u32[]{:S(2)}, u32[]{:S(2)}) collective-permute-start(bf16[1024,768]{1,0:T(8,128)(2,1)S(1)} %collective-permute-done.9.g_a), channel_id=1, source_target_pairs={{0,1},{1,0},{2,3},{3,2},{4,5},{5,4},{6,7},{7,6},{8,9},{9,8},{10,11... | collective-permute-start | bytes 4718600 | tf_op jit(solution)/shard_map/ppermute | solution.py:430
  239.0 4.4 collective-permute-start.11
  239.5 46.0 %collective-permute-start.14 = (bf16[1024,768]{1,0:T(8,128)(2,1)}, bf16[1024,768]{1,0:T(8,128)(2,1)}, u32[]{:S(2)}, u32[]{:S(2)}) collective-permute-start(bf16[1024,768]{1,0:T(8,128)(2,1)} %collective-permute-done.1.g_a), channel_id=1, source_target_pairs={{0,1},{1,0},{2,3},{3,2},{4,5},{5,4},{6,7},{7,6},{8,9},{9,8},{10,11... | collective-permute-start | bytes 4718600 | tf_op jit(solution)/shard_map/ppermute | solution.py:430
  239.6 43.4 %collective-permute-start.10 = (bf16[1024,768]{1,0:T(8,128)(2,1)S(1)}, bf16[1024,768]{1,0:T(8,128)(2,1)S(1)}, u32[]{:S(2)}, u32[]{:S(2)}) collective-permute-start(bf16[1024,768]{1,0:T(8,128)(2,1)S(1)} %collective-permute-done.6.n_a), channel_id=1, source_target_pairs={{0,2},{1,3},{2,6},{3,7},{6,4},{7,5},{4,0},{5,1},{8,10},{9,11},{10,... | collective-permute-start | bytes 4718600 | tf_op jit(solution)/shard_map/ppermute | solution.py:420
  239.8 43.9 %collective-permute-start.15 = (bf16[1040,768]{1,0:T(8,128)(2,1)}, bf16[1040,768]{1,0:T(8,128)(2,1)S(1)}, u32[]{:S(2)}, u32[]{:S(2)}) collective-permute-start(bf16[1040,768]{1,0:T(8,128)(2,1)} %get-tuple-element.118), channel_id=1, source_target_pairs={{0,1},{1,0},{2,3},{3,2},{4,5},{5,4},{6,7},{7,6},{8,9},{9,8},{10,11... | collective-permute-start | bytes 4792328 | tf_op jit(solution)/shard_map/ppermute | solution.py:430
  283.5 43.3 %collective-permute-start.19 = (bf16[1040,768]{1,0:T(8,128)(2,1)}, bf16[1040,768]{1,0:T(8,128)(2,1)S(1)}, u32[]{:S(2)}, u32[]{:S(2)}) collective-permute-start(bf16[1040,768]{1,0:T(8,128)(2,1)} %get-tuple-element.132), channel_id=1, source_target_pairs={{0,1},{1,0},{2,3},{3,2},{4,5},{5,4},{6,7},{7,6},{8,9},{9,8},{10,11... | collective-permute-start | bytes 4792328 | tf_op jit(solution)/shard_map/ppermute | solution.py:430
  285.3 41.4 %collective-permute-start.20 = (bf16[1040,768]{1,0:T(8,128)(2,1)}, bf16[1040,768]{1,0:T(8,128)(2,1)S(1)}, u32[]{:S(2)}, u32[]{:S(2)}) collective-permute-start(bf16[1040,768]{1,0:T(8,128)(2,1)} %add_convert_fusion.2), channel_id=1, source_target_pairs={{0,2},{1,3},{2,6},{3,7},{6,4},{7,5},{4,0},{5,1},{8,10},{9,11},{10,... | collective-permute-start | bytes 4792328 | tf_op jit(solution)/shard_map/ppermute | solution.py:420
  326.3 31.5 %collective-permute-start.18 = (bf16[1040,768]{1,0:T(8,128)(2,1)}, bf16[1040,768]{1,0:T(8,128)(2,1)}, u32[]{:S(2)}, u32[]{:S(2)}) collective-permute-start(bf16[1040,768]{1,0:T(8,128)(2,1)} %get-tuple-element.131), channel_id=1, source_target_pairs={{0,1},{1,0},{2,3},{3,2},{4,5},{5,4},{6,7},{7,6},{8,9},{9,8},{10,11... | collective-permute-start | bytes 4792328 | tf_op jit(solution)/shard_map/ppermute | solution.py:430
  328.6 38.4 %collective-permute-start.21 = (bf16[1040,768]{1,0:T(8,128)(2,1)}, bf16[1040,768]{1,0:T(8,128)(2,1)}, u32[]{:S(2)}, u32[]{:S(2)}) collective-permute-start(bf16[1040,768]{1,0:T(8,128)(2,1)} %add_convert_fusion.1), channel_id=1, source_target_pairs={{0,2},{1,3},{2,6},{3,7},{6,4},{7,5},{4,0},{5,1},{8,10},{9,11},{10,... | collective-permute-start | bytes 4792328 | tf_op jit(solution)/shard_map/ppermute | solution.py:420
  371.2 203.7 %reduce-scatter.5.cloned.1.call-start = ((), (), s32[]{:S(2)}) async-start(), calls=%async_computation.3 | async-start | bytes 11796480 | tf_op jit(solution)/shard_map/reduce_scatter | solution.py:787
  371.2 37.8 %collective-permute-start.23 = (bf16[1040,768]{1,0:T(8,128)(2,1)}, bf16[1040,768]{1,0:T(8,128)(2,1)}, u32[]{:S(2)}, u32[]{:S(2)}) collective-permute-start(bf16[1040,768]{1,0:T(8,128)(2,1)} %get-tuple-element.142), channel_id=1, source_target_pairs={{0,1},{1,0},{2,3},{3,2},{4,5},{5,4},{6,7},{7,6},{8,9},{9,8},{10,11... | collective-permute-start | bytes 4792328 | tf_op jit(solution)/shard_map/ppermute | solution.py:430
  371.3 31.1 %collective-permute-start.25 = (bf16[1024,768]{1,0:T(8,128)(2,1)}, bf16[1024,768]{1,0:T(8,128)(2,1)}, u32[]{:S(2)}, u32[]{:S(2)}) collective-permute-start(bf16[1024,768]{1,0:T(8,128)(2,1)} %copy-done.20), channel_id=1, source_target_pairs={{0,1},{1,0},{2,3},{3,2},{4,5},{5,4},{6,7},{7,6},{8,9},{9,8},{10,11... | collective-permute-start | bytes 4718600 | tf_op jit(solution)/shard_map/ppermute | solution.py:430
  371.8 30.7 %collective-permute-start.17 = (bf16[1024,768]{1,0:T(8,128)(2,1)}, bf16[1024,768]{1,0:T(8,128)(2,1)}, u32[]{:S(2)}, u32[]{:S(2)}) collective-permute-start(bf16[1024,768]{1,0:T(8,128)(2,1)} %copy-done.21), channel_id=1, source_target_pairs={{0,1},{1,0},{2,3},{3,2},{4,5},{5,4},{6,7},{7,6},{8,9},{9,8},{10,11... | collective-permute-start | bytes 4718600 | tf_op jit(solution)/shard_map/ppermute | solution.py:430
  371.9 38.9 %collective-permute-start.24 = (bf16[1040,768]{1,0:T(8,128)(2,1)}, bf16[1040,768]{1,0:T(8,128)(2,1)}, u32[]{:S(2)}, u32[]{:S(2)}) collective-permute-start(bf16[1040,768]{1,0:T(8,128)(2,1)} %add_convert_fusion), channel_id=1, source_target_pairs={{0,2},{1,3},{2,6},{3,7},{6,4},{7,5},{4,0},{5,1},{8,10},{9,11},{10,... | collective-permute-start | bytes 4792328 | tf_op jit(solution)/shard_map/ppermute | solution.py:420
  417.5 39.4 %collective-permute-start.26 = (bf16[1024,768]{1,0:T(8,128)(2,1)}, bf16[1024,768]{1,0:T(8,128)(2,1)}, u32[]{:S(2)}, u32[]{:S(2)}) collective-permute-start(bf16[1024,768]{1,0:T(8,128)(2,1)} %add_convert_fusion.5), channel_id=1, source_target_pairs={{0,4},{1,5},{2,0},{3,1},{6,2},{7,3},{4,6},{5,7},{8,12},{9,13},{10,... | collective-permute-start | bytes 4718600 | tf_op jit(solution)/shard_map/ppermute | solution.py:427
  417.8 70.2 %collective-permute-start.22 = (bf16[1024,768]{1,0:T(8,128)(2,1)}, bf16[1024,768]{1,0:T(8,128)(2,1)}, u32[]{:S(2)}, u32[]{:S(2)}) collective-permute-start(bf16[1024,768]{1,0:T(8,128)(2,1)} %add_convert_fusion.6), channel_id=1, source_target_pairs={{0,2},{1,3},{2,6},{3,7},{6,4},{7,5},{4,0},{5,1},{8,10},{9,11},{10,... | collective-permute-start | bytes 4718600 | tf_op jit(solution)/shard_map/ppermute | solution.py:420
  465.9 22.1 %collective-permute-start.29 = (bf16[4,96,768]{2,1,0:T(8,128)(2,1)}, bf16[4,96,768]{2,1,0:T(8,128)(2,1)}, u32[]{:S(2)}, u32[]{:S(2)}) collective-permute-start(bf16[4,96,768]{2,1,0:T(8,128)(2,1)} %get-tuple-element.187), channel_id=1, source_target_pairs={{0,1},{1,0},{2,3},{3,2},{4,5},{5,4},{6,7},{7,6},{8,9},{9,8},{10,11... | collective-permute-start | bytes 1769480 | tf_op jit(solution)/shard_map/ppermute | solution.py:430
  489.6 16.3 %collective-permute-start.31 = (bf16[392,768]{1,0:T(8,128)(2,1)S(1)}, bf16[392,768]{1,0:T(8,128)(2,1)S(1)}, u32[]{:S(2)}, u32[]{:S(2)}) collective-permute-start(bf16[392,768]{1,0:T(8,128)(2,1)S(1)} %pad_maximum_fusion.1), channel_id=1, source_target_pairs={{0,2},{1,3},{2,6},{3,7},{6,4},{7,5},{4,0},{5,1},{8,10},{9,11},{10,... | collective-permute-start | bytes 1806344 | tf_op jit(solution)/shard_map/ppermute | solution.py:420
  489.7 21.2 %collective-permute-start.28 = (bf16[4,96,768]{2,1,0:T(8,128)(2,1)S(1)}, bf16[4,96,768]{2,1,0:T(8,128)(2,1)}, u32[]{:S(2)}, u32[]{:S(2)}) collective-permute-start(bf16[4,96,768]{2,1,0:T(8,128)(2,1)S(1)} %get-tuple-element.188), channel_id=1, source_target_pairs={{0,1},{1,0},{2,3},{3,2},{4,5},{5,4},{6,7},{7,6},{8,9},{9,8},{10,11... | collective-permute-start | bytes 1769480 | tf_op jit(solution)/shard_map/ppermute | solution.py:430
  489.7 16.3 %collective-permute-start.32 = (f32[24,128]{1,0:T(8,128)S(1)}, f32[24,128]{1,0:T(8,128)S(1)}, u32[]{:S(2)}, u32[]{:S(2)}) collective-permute-start(f32[24,128]{1,0:T(8,128)S(1)} %bitcast.247), channel_id=1, source_target_pairs={{0,1},{1,0},{2,3},{3,2},{4,5},{5,4},{6,7},{7,6},{8,9},{9,8},{10,11... | collective-permute-start | bytes 36872 | tf_op jit(solution)/shard_map/ppermute | solution.py:430
  512.3 15.4 %collective-permute-start.33 = (bf16[392,768]{1,0:T(8,128)(2,1)S(1)}, bf16[392,768]{1,0:T(8,128)(2,1)S(1)}, u32[]{:S(2)}, u32[]{:S(2)}) collective-permute-start(bf16[392,768]{1,0:T(8,128)(2,1)S(1)} %pad_maximum_fusion.2), channel_id=1, source_target_pairs={{0,2},{1,3},{2,6},{3,7},{6,4},{7,5},{4,0},{5,1},{8,10},{9,11},{10,... | collective-permute-start | bytes 1806344 | tf_op jit(solution)/shard_map/ppermute | solution.py:420
  512.4 19.5 %collective-permute-start.16 = (bf16[1024,768]{1,0:T(8,128)(2,1)}, bf16[1024,768]{1,0:T(8,128)(2,1)}, u32[]{:S(2)}, u32[]{:S(2)}) collective-permute-start(bf16[1024,768]{1,0:T(8,128)(2,1)} %get-tuple-element.125), channel_id=1, source_target_pairs={{0,1},{1,0},{2,3},{3,2},{4,5},{5,4},{6,7},{7,6},{8,9},{9,8},{10,11... | collective-permute-start | bytes 4718600 | tf_op jit(solution)/shard_map/ppermute | solution.py:430
  512.5 15.5 %collective-permute-start.27 = (bf16[4,96,768]{2,1,0:T(8,128)(2,1)S(1)}, bf16[4,96,768]{2,1,0:T(8,128)(2,1)S(1)}, u32[]{:S(2)}, u32[]{:S(2)}) collective-permute-start(bf16[4,96,768]{2,1,0:T(8,128)(2,1)S(1)} %get-tuple-element.189), channel_id=1, source_target_pairs={{0,1},{1,0},{2,3},{3,2},{4,5},{5,4},{6,7},{7,6},{8,9},{9,8},{10,11... | collective-permute-start | bytes 1769480 | tf_op jit(solution)/shard_map/ppermute | solution.py:430
  513.0 14.9 %collective-permute-start.34 = (f32[24,128]{1,0:T(8,128)S(1)}, f32[24,128]{1,0:T(8,128)S(1)}, u32[]{:S(2)}, u32[]{:S(2)}) collective-permute-start(f32[24,128]{1,0:T(8,128)S(1)} %bitcast.246), channel_id=1, source_target_pairs={{0,1},{1,0},{2,3},{3,2},{4,5},{5,4},{6,7},{7,6},{8,9},{9,8},{10,11... | collective-permute-start | bytes 36872 | tf_op jit(solution)/shard_map/ppermute | solution.py:430
  531.3 17.7 %collective-permute-start.37 = (bf16[392,768]{1,0:T(8,128)(2,1)}, bf16[392,768]{1,0:T(8,128)(2,1)}, u32[]{:S(2)}, u32[]{:S(2)}) collective-permute-start(bf16[392,768]{1,0:T(8,128)(2,1)} %pad_maximum_fusion.3), channel_id=1, source_target_pairs={{0,2},{1,3},{2,6},{3,7},{6,4},{7,5},{4,0},{5,1},{8,10},{9,11},{10,... | collective-permute-start | bytes 1806344 | tf_op jit(solution)/shard_map/ppermute | solution.py:420
  531.3 48.0 %collective-permute-start.4 = (bf16[1024,768]{1,0:T(8,128)(2,1)S(1)}, bf16[1024,768]{1,0:T(8,128)(2,1)}, u32[]{:S(2)}, u32[]{:S(2)}) collective-permute-start(bf16[1024,768]{1,0:T(8,128)(2,1)S(1)} %copy-done.19), channel_id=1, source_target_pairs={{0,1},{1,0},{2,3},{3,2},{4,5},{5,4},{6,7},{7,6},{8,9},{9,8},{10,11... | collective-permute-start | bytes 4718600 | tf_op jit(solution)/shard_map/ppermute | solution.py:430
  531.3 22.1 %collective-permute-start.36 = (bf16[4,96,768]{2,1,0:T(8,128)(2,1)}, bf16[4,96,768]{2,1,0:T(8,128)(2,1)}, u32[]{:S(2)}, u32[]{:S(2)}) collective-permute-start(bf16[4,96,768]{2,1,0:T(8,128)(2,1)} %get-tuple-element.186), channel_id=1, source_target_pairs={{0,1},{1,0},{2,3},{3,2},{4,5},{5,4},{6,7},{7,6},{8,9},{9,8},{10,11... | collective-permute-start | bytes 1769480 | tf_op jit(solution)/shard_map/ppermute | solution.py:430
  531.8 18.4 %collective-permute-start.38 = (f32[24,128]{1,0:T(8,128)S(1)}, f32[24,128]{1,0:T(8,128)S(1)}, u32[]{:S(2)}, u32[]{:S(2)}) collective-permute-start(f32[24,128]{1,0:T(8,128)S(1)} %bitcast.245), channel_id=1, source_target_pairs={{0,1},{1,0},{2,3},{3,2},{4,5},{5,4},{6,7},{7,6},{8,9},{9,8},{10,11... | collective-permute-start | bytes 36872 | tf_op jit(solution)/shard_map/ppermute | solution.py:430
  535.5 44.2 %collective-permute-start.35 = (bf16[1024,768]{1,0:T(8,128)(2,1)}, bf16[1024,768]{1,0:T(8,128)(2,1)}, u32[]{:S(2)}, u32[]{:S(2)}) collective-permute-start(bf16[1024,768]{1,0:T(8,128)(2,1)} %add_convert_fusion.4), channel_id=1, source_target_pairs={{0,2},{1,3},{2,6},{3,7},{6,4},{7,5},{4,0},{5,1},{8,10},{9,11},{10,... | collective-permute-start | bytes 4718600 | tf_op jit(solution)/shard_map/ppermute | solution.py:420
  550.3 7.0 %collective-permute-start.39 = (f32[24,128]{1,0:T(8,128)S(1)}, f32[24,128]{1,0:T(8,128)S(1)}, u32[]{:S(2)}, u32[]{:S(2)}) collective-permute-start(f32[24,128]{1,0:T(8,128)S(1)} %add_add_fusion.2), channel_id=1, source_target_pairs={{0,8},{8,0},{16,24},{24,16},{1,9},{9,1},{17,25},{25,17},{2,10},{10... | collective-permute-start | bytes 36872 | tf_op jit(solution)/shard_map/ppermute | solution.py:900
  551.9 6.9 %collective-permute-start.40 = (f32[24,128]{1,0:T(8,128)S(1)}, f32[24,128]{1,0:T(8,128)S(1)}, u32[]{:S(2)}, u32[]{:S(2)}) collective-permute-start(f32[24,128]{1,0:T(8,128)S(1)} %add_add_fusion.2), channel_id=1, source_target_pairs={{0,16},{8,24},{16,0},{24,8},{1,17},{9,25},{17,1},{25,9},{2,18},{10... | collective-permute-start | bytes 36872 | tf_op jit(solution)/shard_map/ppermute | solution.py:900
  553.4 5.8 collective-permute-start.41
  557.2 9.1 %collective-permute-start.42 = (bf16[96,768]{1,0:T(8,128)(2,1)}, bf16[96,768]{1,0:T(8,128)(2,1)S(1)}, u32[]{:S(2)}, u32[]{:S(2)}) collective-permute-start(bf16[96,768]{1,0:T(8,128)(2,1)} %get-tuple-element.196), channel_id=1, source_target_pairs={{0,8},{8,0},{16,24},{24,16},{1,9},{9,1},{17,25},{25,17},{2,10},{10... | collective-permute-start | bytes 442376 | tf_op jit(solution)/shard_map/ppermute | solution.py:909
  558.8 8.4 %collective-permute-start.43 = (bf16[96,768]{1,0:T(8,128)(2,1)}, bf16[96,768]{1,0:T(8,128)(2,1)S(1)}, u32[]{:S(2)}, u32[]{:S(2)}) collective-permute-start(bf16[96,768]{1,0:T(8,128)(2,1)} %get-tuple-element.198), channel_id=1, source_target_pairs={{0,16},{8,24},{16,0},{24,8},{1,17},{9,25},{17,1},{25,9},{2,18},{10... | collective-permute-start | bytes 442376 | tf_op jit(solution)/shard_map/ppermute | solution.py:909
  559.2 12.1 %collective-permute-start.44 = (bf16[96,768]{1,0:T(8,128)(2,1)S(1)}, bf16[96,768]{1,0:T(8,128)(2,1)S(1)}, u32[]{:S(2)}, u32[]{:S(2)}) collective-permute-start(bf16[96,768]{1,0:T(8,128)(2,1)S(1)} %get-tuple-element.197), channel_id=1, source_target_pairs={{0,24},{8,16},{16,8},{24,0},{1,25},{9,17},{17,9},{25,1},{2,26},{10... | collective-permute-start | bytes 442376 | tf_op jit(solution)/shard_map/ppermute | solution.py:909
  571.3 13.0 %collective-permute-start.45 = (bf16[96,768]{1,0:T(8,128)(2,1)S(1)}, bf16[96,768]{1,0:T(8,128)(2,1)S(1)}, u32[]{:S(2)}, u32[]{:S(2)}) collective-permute-start(bf16[96,768]{1,0:T(8,128)(2,1)S(1)} %fusion.42), channel_id=1, source_target_pairs={{0,8},{8,0},{16,24},{24,16},{1,9},{9,1},{17,25},{25,17},{2,10},{10... | collective-permute-start | bytes 442376 | tf_op jit(solution)/shard_map/ppermute | solution.py:909
  571.5 12.8 %collective-permute-start.46 = (bf16[96,768]{1,0:T(8,128)(2,1)S(1)}, bf16[96,768]{1,0:T(8,128)(2,1)}, u32[]{:S(2)}, u32[]{:S(2)}) collective-permute-start(bf16[96,768]{1,0:T(8,128)(2,1)S(1)} %fusion.42), channel_id=1, source_target_pairs={{0,16},{8,24},{16,0},{24,8},{1,17},{9,25},{17,1},{25,9},{2,18},{10... | collective-permute-start | bytes 442376 | tf_op jit(solution)/shard_map/ppermute | solution.py:909
  571.5 12.8 %collective-permute-start.47 = (bf16[96,768]{1,0:T(8,128)(2,1)S(1)}, bf16[96,768]{1,0:T(8,128)(2,1)}, u32[]{:S(2)}, u32[]{:S(2)}) collective-permute-start(bf16[96,768]{1,0:T(8,128)(2,1)S(1)} %fusion.42), channel_id=1, source_target_pairs={{0,24},{8,16},{16,8},{24,0},{1,25},{9,17},{17,9},{25,1},{2,26},{10... | collective-permute-start | bytes 442376 | tf_op jit(solution)/shard_map/ppermute | solution.py:909
  (74 other events, 584.6 us)
Sparse Core Ops, SparseCore 0:
  371.3 94.0 reduce-scatter.2
  468.5 100.6 reduce-scatter.4
